TPU v7x, 32 devices: a whole 2x2x4 slice. The times are simulated.
32 devices in a mesh: layer: 4 (over y, x), latent: 4 (over z), dp: 2 (over core).
Axes of the slice: x: 2, y: 2, z: 4, core: 2. Of those that a mesh axis runs over, the one named last changes fastest.
Arguments:
- pre_codes: bfloat16 [4, 1024, 2, 128], P('layer', ('latent', 'dp')), may hold values from -6 to 6
- block_ids: int32 [4, 1024, 2], P('layer', ('latent', 'dp')), may hold values from 0 to 63, as said below
- activations: bfloat16 [4, 1024, 4096], P('layer', ('latent', 'dp')), may hold values from -6 to 6
- target: bfloat16 [1024, 4096], P(('latent', 'dp')), may hold values from -6 to 6
- decoder: bfloat16 [4, 8192, 4096], P('layer', 'latent'), may hold values from -0.25 to 0.25
Outputs:
- decoder_grad: bfloat16 [4, 8192, 4096], P('layer', 'latent', 'dp')
- encoder_grad: bfloat16 [4, 8192, 4096], P('layer', 'latent', 'dp')
Inputs may be any that keep to these rules, and one draw needn't show every extreme that they name: `block_ids`: the 2 block numbers of a token in one layer are distinct. Among the tokens of one device in one layer (aligned blocks of 128 tokens), each block number is named at most 8 times, and in every layer some block number is named exactly 8 times by the tokens of every device.
All inputs are finite; a program needn't handle non-finite values.
Results may differ from a plain program's by a relative error of at most 0.0053.
Values may be sent and summed in bfloat16 or wider, within the bound.
No kernel may reach another device: no remote copies, remote signals or barrier semaphores. Data moves between devices by JAX's collectives and lax.ppermute only.
A program may use at most 192 MiB of HBM per device.

v0:
```python
import jax
import jax.numpy as jnp
from jax import lax
from jax.sharding import PartitionSpec as P


def local_contrib(received_pre, weights, lat_count, local_blocks):
    code_vals = jnp.maximum(received_pre, jnp.zeros((), received_pre.dtype))
    slot_span = received_pre.shape[1]
    block_size = received_pre.shape[2]
    grouped = code_vals.reshape(lat_count, local_blocks, slot_span, block_size)
    contrib = jnp.einsum("sbcl,bld->sbcd", grouped, weights, preferred_element_type=jnp.float32)
    contrib = contrib.astype(jnp.bfloat16).reshape(
        lat_count * local_blocks, slot_span, weights.shape[2]
    )
    return lax.all_to_all(contrib, "latent", split_axis=0, concat_axis=0, tiled=True)


def per_device(pre_codes, block_ids, activations, target, decoder):
    lat_count = lax.axis_size("latent")
    tok_count = activations.shape[1]
    model_width = activations.shape[2]
    active_count = block_ids.shape[2]
    block_size = pre_codes.shape[3]
    lat_rows = decoder.shape[1]
    local_blocks = lat_rows // block_size
    all_blocks = local_blocks * lat_count
    capacity = 2 * tok_count * active_count // all_blocks
    slot_count = all_blocks * capacity
    pair_count = tok_count * active_count
    pair_block = block_ids[0].T.reshape(pair_count)
    member = (pair_block[:, None] == jnp.arange(all_blocks, dtype=jnp.int32)[None, :]).astype(
        jnp.int32
    )
    before = jnp.cumsum(member, axis=0) - member
    pair_rank = jnp.sum(before * member, axis=1)
    target_slot = pair_block * capacity + pair_rank
    slot_pair = (jnp.arange(slot_count, dtype=jnp.int32)[:, None] == target_slot[None, :]).astype(
        jnp.bfloat16
    )
    slot_token = jnp.sum(slot_pair.reshape(slot_count, active_count, tok_count), axis=1)
    pre_pairs = jnp.transpose(pre_codes[0], (1, 0, 2)).reshape(pair_count, block_size)
    pre_slots = jnp.dot(slot_pair, pre_pairs, preferred_element_type=jnp.float32).astype(
        jnp.bfloat16
    )
    pre_slots = pre_slots.reshape(all_blocks, capacity, block_size)
    inputs = activations[0]
    weights = decoder[0].reshape(local_blocks, block_size, model_width)
    input_slots = jnp.dot(slot_token, inputs, preferred_element_type=jnp.float32).astype(
        jnp.bfloat16
    )
    input_slots = input_slots.reshape(all_blocks, capacity, model_width)
    pieces = (
        lax.all_to_all(pre_slots, "latent", split_axis=0, concat_axis=0, tiled=True),
        lax.all_to_all(input_slots, "latent", split_axis=0, concat_axis=0, tiled=True),
    )
    returned = local_contrib(pieces[0], weights, lat_count, local_blocks)
    returned, received_pre, received_inputs = (returned, pieces[0], pieces[1])
    part_sum = jnp.einsum(
        "st,sd->td",
        slot_token,
        returned.reshape(slot_count, model_width),
        preferred_element_type=jnp.float32,
    )
    rebuilt = lax.psum(part_sum, "layer")
    errors = ((rebuilt - target.astype(jnp.float32)) / tok_count).astype(jnp.bfloat16)
    error_slots = jnp.dot(slot_token, errors, preferred_element_type=jnp.float32).astype(
        jnp.bfloat16
    )
    error_slots = error_slots.reshape(all_blocks, capacity, model_width)
    received_errors = lax.all_to_all(error_slots, "latent", split_axis=0, concat_axis=0, tiled=True)
    pre_blocks = received_pre.reshape(lat_count, local_blocks, capacity, block_size)
    code_blocks = jnp.maximum(pre_blocks, jnp.zeros((), pre_blocks.dtype))
    error_blocks = received_errors.reshape(lat_count, local_blocks, capacity, model_width)
    input_blocks = received_inputs.reshape(lat_count, local_blocks, capacity, model_width)
    code_grad = jnp.einsum(
        "sbcd,bld->sbcl", error_blocks, weights, preferred_element_type=jnp.float32
    )
    pre_grad = jnp.where(pre_blocks > 0, code_grad, jnp.zeros((), jnp.float32)).astype(jnp.bfloat16)
    dec_term = jnp.einsum(
        "sbcl,sbcd->bld", code_blocks, error_blocks, preferred_element_type=jnp.float32
    )
    enc_term = jnp.einsum(
        "sbcl,sbcd->bld", pre_grad, input_blocks, preferred_element_type=jnp.float32
    )
    dec_term = dec_term.reshape(lat_rows, model_width)
    enc_term = enc_term.reshape(lat_rows, model_width)
    dec_half, enc_half = (
        lax.psum_scatter(dec_term, "dp", scatter_dimension=1, tiled=True),
        lax.psum_scatter(enc_term, "dp", scatter_dimension=1, tiled=True),
    )
    return (dec_half.astype(jnp.bfloat16)[None], enc_half.astype(jnp.bfloat16)[None])


def solution(mesh):
    placed = (
        P("layer", ("latent", "dp"), None, None),
        P("layer", ("latent", "dp"), None),
        P("layer", ("latent", "dp"), None),
        P(("latent", "dp"), None),
        P("layer", "latent", None),
    )
    return jax.shard_map(
        per_device,
        mesh=mesh,
        in_specs=placed,
        out_specs=(P("layer", "latent", "dp"), P("layer", "latent", "dp")),
        check_vma=False,
    )
```

profile of v0, /device:TPU:1, one launch (start us, length us, event | category | flops | bytes accessed | tf_op | source)
XLA Modules:
  0.0 456.2 jit_solution(12432365145437703422)
XLA Ops:
  7.2 0.9 copy.16
  8.1 0.7 fusion.19
  8.8 0.6 reduce-window.6
  9.6 0.8 fusion.18
  10.4 0.7 multiply_add_fusion
  11.4 10.0 %all_to_all.20 = bf16[64,8,128]{2,1,0:T(8,128)(2,1)S(1)} all-to-all(bf16[64,8,128]{2,1,0:T(8,128)(2,1)S(1)} %fusion.8), channel_id=1, replica_groups=mesh['layer'=4,'latent'=4,'dp'=2] {'latent'}, dimensions={0} | all-to-all | bytes 262144 | tf_op jit(solution)/shard_map/all_to_all | solution.py:54
  21.4 8.1 %fusion = bf16[4,16,8,4096]{3,2,0,1:T(8,128)(2,1)S(1)} fusion(bf16[16,128,4096,1]{2,1,3,0:T(8,128)(2,1)} %bitcast.87, bf16[4,16,8,128]{3,2,1,0:T(8,128)(2,1)S(1)} %bitcast.90), kind=kOutput, calls=%fused_computation.5 | convolution fusion | flops 538968064 | bytes 21102592 | tf_op jit(solution)/shard_map/sbcl,bld->sbcd/dot_general | solution.py:12
  29.5 2.3 copy.18
  31.8 5.0 %all-to-all-start.1 = ((bf16[64,8,4096]{2,1,0:T(8,128)(2,1)}), bf16[64,8,4096]{2,1,0:T(8,128)(2,1)}, u32[]{:S(2)}, u32[]{:S(2)}) async-start(bf16[64,8,4096]{2,1,0:T(8,128)(2,1)} %bitcast.89), calls=%async_computation.1 | async-start | bytes 8388608 | tf_op jit(solution)/shard_map/all_to_all | solution.py:16
  36.9 3.3 fusion.2
  40.1 89.3 %all-to-all-done.1 = bf16[64,8,4096]{2,1,0:T(8,128)(2,1)} async-done(((bf16[64,8,4096]{2,1,0:T(8,128)(2,1)}), bf16[64,8,4096]{2,1,0:T(8,128)(2,1)}, u32[]{:S(2)}, u32[]{:S(2)}) %all-to-all-start.1) | async-done | bytes 4194336 | tf_op jit(solution)/shard_map/all_to_all | solution.py:16
  129.4 4.9 %all-to-all-start.3 = ((bf16[64,8,4096]{2,1,0:T(8,128)(2,1)}), bf16[64,8,4096]{2,1,0:T(8,128)(2,1)}, u32[]{:S(2)}, u32[]{:S(2)}) async-start(bf16[64,8,4096]{2,1,0:T(8,128)(2,1)} %fusion.2), calls=%async_computation.4 | async-start | bytes 8388608 | tf_op jit(solution)/shard_map/all_to_all | solution.py:55
  134.4 4.3 fusion.3
  138.7 72.0 %all-reduce.2.cloned.1.call-done = f32[128,4096]{1,0:T(8,128)} async-done(((f32[128,4096]{1,0:T(8,128)}), f32[128,4096]{1,0:T(8,128)}) %all-reduce.2.cloned.1.call-update) | async-done | bytes 2097168 | tf_op jit(solution)/shard_map/psum | solution.py:65
  210.7 4.9 %fusion.1 = bf16[64,8,4096]{2,1,0:T(8,128)(2,1)} fusion(bf16[512,128]{1,0:T(8,128)(2,1)S(1)} %fusion.12, f32[128,4096]{1,0:T(8,128)} %all-reduce.2.cloned.1.call-done, bf16[128,4096]{1,0:T(8,128)(2,1)S(1)} %copy-done.2), kind=kOutput, calls=%fused_computation.6 | convolution fusion | flops 541065216 | bytes 7471104 | tf_op jit(solution)/shard_map/dot_general | solution.py:67
  215.6 11.4 %all-to-all-done.3 = bf16[64,8,4096]{2,1,0:T(8,128)(2,1)} async-done(((bf16[64,8,4096]{2,1,0:T(8,128)(2,1)}), bf16[64,8,4096]{2,1,0:T(8,128)(2,1)}, u32[]{:S(2)}, u32[]{:S(2)}) %all-to-all-start.3) | async-done | bytes 4194336 | tf_op jit(solution)/shard_map/all_to_all | solution.py:55
  227.0 4.8 %all-to-all-start.2 = ((bf16[64,8,4096]{2,1,0:T(8,128)(2,1)}), bf16[64,8,4096]{2,1,0:T(8,128)(2,1)}, u32[]{:S(2)}, u32[]{:S(2)}) async-start(bf16[64,8,4096]{2,1,0:T(8,128)(2,1)} %fusion.1), calls=%async_computation.2 | async-start | bytes 8388608 | tf_op jit(solution)/shard_map/all_to_all | solution.py:71
  231.9 92.6 %all-to-all-done.2 = bf16[64,8,4096]{2,1,0:T(8,128)(2,1)} async-done(((bf16[64,8,4096]{2,1,0:T(8,128)(2,1)}), bf16[64,8,4096]{2,1,0:T(8,128)(2,1)}, u32[]{:S(2)}, u32[]{:S(2)}) %all-to-all-start.2) | async-done | bytes 4194336 | tf_op jit(solution)/shard_map/all_to_all | solution.py:71
  324.5 21.6 %fusion.7 = f32[16,128,4096,1]{2,1,0,3:T(8,128)} fusion(bf16[4,16,8,4096]{3,2,1,0:T(8,128)(2,1)} %bitcast.28, pred[4,16,8,128]{3,2,1,0:T(8,128)(4,1)S(1)} %bitcast.92, bf16[4,16,8,4096]{3,2,1,0:T(8,128)(2,1)} %bitcast.19, bf16[16,128,4096,1]{2,1,0,3:T(8,128)(2,1)} %bitcast.88), kind=kOutput, calls=%fused_computation.15 | convolution fusion | flops 1073872896 | bytes 58785792 | tf_op jit(solution)/shard_map/sbcl,sbcd->bld/dot_general | solution.py:83
  346.4 26.1 %fusion.22 = f32[16,128,4096,1]{2,1,0,3:T(8,128)} fusion(bf16[4,16,8,128]{3,2,1,0:T(8,128)(2,1)S(1)} %bitcast.91, bf16[4,16,8,4096]{3,2,1,0:T(8,128)(2,1)} %bitcast.19), kind=kOutput, calls=%fused_computation.41 | convolution fusion | flops 536870912 | bytes 37879808 | tf_op jit(solution)/shard_map/sbcl,sbcd->bld/dot_general | solution.py:80
  372.5 19.3 %reduce-scatter.5.cloned.1.call-done = f32[2048,2048]{1,0:T(8,128)} async-done(((f32[2048,4096]{1,0:T(8,128)}), f32[2048,2048]{1,0:T(8,128)}) %reduce-scatter.5.cloned.1.call-update) | async-done | bytes 16777232 | tf_op jit(solution)/shard_map/reduce_scatter | solution.py:90
  391.8 9.1 %convert_bitcast_fusion = bf16[1,2048,2048]{2,1,0:T(8,128)(2,1)} fusion(f32[2048,2048]{1,0:T(8,128)} %reduce-scatter.5.cloned.1.call-done), kind=kLoop, calls=%fused_computation | loop fusion | flops 4194304 | bytes 25165824 | tf_op jit(solution)/shard_map/broadcast_in_dim | solution.py:92
  400.8 39.7 %reduce-scatter.3.cloned.1.call-done = f32[2048,2048]{1,0:T(8,128)} async-done(((f32[2048,4096]{1,0:T(8,128)}), f32[2048,2048]{1,0:T(8,128)}) %reduce-scatter.3.cloned.1.call-update) | async-done | bytes 16777232 | tf_op jit(solution)/shard_map/reduce_scatter | solution.py:89
  440.6 9.1 %convert_bitcast_fusion.1 = bf16[1,2048,2048]{2,1,0:T(8,128)(2,1)} fusion(f32[2048,2048]{1,0:T(8,128)} %reduce-scatter.3.cloned.1.call-done), kind=kLoop, calls=%fused_computation.1 | loop fusion | flops 4194304 | bytes 25165824 | tf_op jit(solution)/shard_map/broadcast_in_dim | solution.py:92
  (22 shorter events, 1.0 us)
Async XLA Ops:
  7.2 29.7 %copy-start = (bf16[1,128,4096]{2,1,0:T(8,128)(2,1)S(1)}, bf16[1,128,4096]{2,1,0:T(8,128)(2,1)}, u32[]{:S(2)}) copy-start(bf16[1,128,4096]{2,1,0:T(8,128)(2,1)} %param.7) | copy-start | bytes 3145732
  31.8 5.0 %copy-start.3 = (s32[1,128,2]{1,2,0:T(2,128)S(1)}, s32[1,128,2]{1,2,0:T(2,128)}, u32[]{:S(2)}) copy-start(s32[1,128,2]{1,2,0:T(2,128)} %param.6) | copy-start | bytes 3076
  31.8 97.7 %all-to-all-start.1 = ((bf16[64,8,4096]{2,1,0:T(8,128)(2,1)}), bf16[64,8,4096]{2,1,0:T(8,128)(2,1)}, u32[]{:S(2)}, u32[]{:S(2)}) async-start(bf16[64,8,4096]{2,1,0:T(8,128)(2,1)} %bitcast.89), calls=%async_computation.1 | async-start | bytes 8388608 | tf_op jit(solution)/shard_map/all_to_all | solution.py:16
  129.4 97.5 %all-to-all-start.3 = ((bf16[64,8,4096]{2,1,0:T(8,128)(2,1)}), bf16[64,8,4096]{2,1,0:T(8,128)(2,1)}, u32[]{:S(2)}, u32[]{:S(2)}) async-start(bf16[64,8,4096]{2,1,0:T(8,128)(2,1)} %fusion.2), calls=%async_computation.4 | async-start | bytes 8388608 | tf_op jit(solution)/shard_map/all_to_all | solution.py:55
  134.3 76.4 %copy-start.2 = (bf16[128,4096]{1,0:T(8,128)(2,1)S(1)}, bf16[128,4096]{1,0:T(8,128)(2,1)}, u32[]{:S(2)}) copy-start(bf16[128,4096]{1,0:T(8,128)(2,1)} %param.8) | copy-start | bytes 3145732
  134.3 76.4 %all-reduce.2.cloned.1.call-start = ((), (), s32[]{:S(2)}) async-start(), calls=%async_computation.6 | async-start | bytes 4194304 | tf_op jit(solution)/shard_map/psum | solution.py:65
  227.0 97.5 %all-to-all-start.2 = ((bf16[64,8,4096]{2,1,0:T(8,128)(2,1)}), bf16[64,8,4096]{2,1,0:T(8,128)(2,1)}, u32[]{:S(2)}, u32[]{:S(2)}) async-start(bf16[64,8,4096]{2,1,0:T(8,128)(2,1)} %fusion.1), calls=%async_computation.2 | async-start | bytes 8388608 | tf_op jit(solution)/shard_map/all_to_all | solution.py:71
  231.9 159.9 %reduce-scatter.5.cloned.1.call-start = ((), (), s32[]{:S(2)}) async-start(), calls=%async_computation.8 | async-start | bytes 50331648 | tf_op jit(solution)/shard_map/reduce_scatter | solution.py:90
  346.1 94.4 %reduce-scatter.3.cloned.1.call-start = ((), (), s32[]{:S(2)}) async-start(), calls=%async_computation.7 | async-start | bytes 50331648 | tf_op jit(solution)/shard_map/reduce_scatter | solution.py:89
  440.6 9.2 %copy-start.1 = (bf16[1,128,4096]{2,1,0:T(8,128)(2,1)S(1)}, bf16[1,128,4096]{2,1,0:T(8,128)(2,1)}, u32[]{:S(2)}) copy-start(bf16[1,128,4096]{2,1,0:T(8,128)(2,1)} %param.7) | copy-start | bytes 3145732
Sparse Core Ops, SparseCore 0:
  138.8 71.8 all-reduce.1
  346.3 45.4 reduce-scatter.4
  394.2 46.3 reduce-scatter.2
where the time goes:
time: 457 us; the launch traced here: 456 us
  waiting for transfers between devices  324 us (71%)
  matrix products  68.4 us (15%)
  other arithmetic  21.1 us (5%)
  starting transfers between devices  15 us (3%)
  between operations  13.8 us (3%)
  blocking collectives  10 us (2%)
    all_to_all x1, waiting for transfers between devices, per_device(): lax.all_to_all(error_slots, 'latent', split_axis=0, concat_axis=0, tiled=...  92.6 us
    all_to_all x1, waiting for transfers between devices, local_contrib(): lax.all_to_all(contrib, 'latent', split_axis=0, concat_axis=0, tiled=True)  89.3 us
    psum x1, waiting for transfers between devices, per_device(): rebuilt = lax.psum(part_sum, 'layer')  72 us
    reduce_scatter x1, waiting for transfers between devices, per_device(): lax.psum_scatter(dec_term, 'dp', scatter_dimension=1, tiled=True)  39.7 us
    dot_general x1, matrix products, per_device(): jnp.einsum('sbcl,sbcd->bld', code_blocks, error_blocks, preferred_element...  26.1 us
    dot_general x1, matrix products, per_device(): jnp.einsum('sbcl,sbcd->bld', pre_grad, input_blocks, preferred_element_ty...  21.6 us
    reduce_scatter x1, waiting for transfers between devices, per_device(): lax.psum_scatter(enc_term, 'dp', scatter_dimension=1, tiled=True)  19.3 us
    all_to_all x1, waiting for transfers between devices, per_device(): lax.all_to_all(input_slots, 'latent', split_axis=0, concat_axis=0, tiled=...  11.4 us
  transfers between devices with their start and end apart: 6, of which 6 were waited for; matrix products, arithmetic and copies ran while one was open for 10% of the time, Pallas kernels for 0%

commit v1 on v0

--- a/solution.py
+++ b/solution.py
@@ -1,7 +1,14 @@
+import functools
+
 import jax
 import jax.numpy as jnp
 from jax import lax
+from jax.experimental import pallas as pl
+from jax.experimental.pallas import tpu as pltpu
 from jax.sharding import PartitionSpec as P
+
+PAIRS = 1
+VMEM_BYTES = 48 * 1024 * 1024
 
 
 def local_contrib(received_pre, weights, lat_count, local_blocks):
@@ -16,7 +23,7 @@
     return lax.all_to_all(contrib, "latent", split_axis=0, concat_axis=0, tiled=True)
 
 
-def per_device(pre_codes, block_ids, activations, target, decoder):
+def slot_plan(pre_codes, block_ids, activations, target, decoder):
     lat_count = lax.axis_size("latent")
     tok_count = activations.shape[1]
     model_width = activations.shape[2]
@@ -92,6 +99,453 @@
     return (dec_half.astype(jnp.bfloat16)[None], enc_half.astype(jnp.bfloat16)[None])
 
 
+def shift(value, axis, step):
+    count = lax.axis_size(axis)
+    return lax.ppermute(value, axis, [(i, (i + step) % count) for i in range(count)])
+
+
+def flip(value, axis, bit):
+    count = lax.axis_size(axis)
+    return lax.ppermute(value, axis, [(i, i ^ bit) for i in range(count)])
+
+
+def hop(value, axis, step, least):
+    count = lax.axis_size(axis)
+    if step > 0:
+        pairs = [(i, i + 1) for i in range(least, count - 1)]
+    else:
+        pairs = [(i, i - 1) for i in range(1, count - least)]
+    return lax.ppermute(value, axis, pairs)
+
+
+def gather_line(own, axis):
+    count = lax.axis_size(axis)
+    up, down = [own], [own]
+    for step in range(1, count):
+        up.append(hop(up[-1], axis, 1, step - 1))
+        down.append(hop(down[-1], axis, -1, step - 1))
+    return [own] + [down[k] + up[count - k] for k in range(1, count)]
+
+
+def spread_rows(ids, rows, first, count):
+    out = []
+    for i in range(count):
+        block = (first + i).astype(jnp.float32)
+        value = jnp.where(ids[1:2] == block, rows[1], 0.0)
+        out.append(jnp.where(ids[0:1] == block, rows[0], value).astype(jnp.bfloat16))
+    return jnp.concatenate(out, axis=0)
+
+
+def forward_kernel(groups, blocks, place_ref, message_ref, weight_ref, out_ref, codes, id_map):
+    tok = message_ref.shape[2]
+    pad = message_ref.shape[1] - 2 * tok
+
+    @pl.when(pl.program_id(0) == 0)
+    def _():
+        first = place_ref[0].astype(jnp.float32)
+        rows = [message_ref[g, 2 * tok:2 * tok + pad, :].astype(jnp.float32) for g in range(groups)]
+        fill = tok - groups * pad
+        if fill:
+            rows.append(jnp.zeros((fill, tok), jnp.float32))
+        table = jnp.concatenate(rows, axis=0).T - first
+        for g in range(groups):
+            for j in range(2):
+                at = g * pad + j
+                id_map[g, j] = jnp.broadcast_to(table[:, at:at + 1], (tok, tok))
+
+        def block_step(b, carry):
+            block = b.astype(jnp.float32)
+            at = pl.multiple_of(b * tok, tok)
+            for g in range(groups):
+                pre0 = jnp.maximum(message_ref[g, 0:tok, :].astype(jnp.float32), 0.0)
+                pre1 = jnp.maximum(message_ref[g, tok:2 * tok, :].astype(jnp.float32), 0.0)
+                value = jnp.where(id_map[g, 1] == block, pre1, 0.0)
+                value = jnp.where(id_map[g, 0] == block, pre0, value)
+                codes[g * tok:(g + 1) * tok, pl.ds(at, tok)] = value.astype(jnp.bfloat16)
+            return carry
+
+        lax.fori_loop(0, blocks, block_step, 0)
+
+    step_rows = 2 * tok
+
+    def row_step(i, carry):
+        at = pl.multiple_of(i * step_rows, step_rows)
+        out_ref[0, pl.ds(at, step_rows), :] = jnp.dot(
+            codes[pl.ds(at, step_rows), :], weight_ref[0], preferred_element_type=jnp.float32
+        ).astype(jnp.bfloat16)
+        return carry
+
+    lax.fori_loop(0, codes.shape[0] // step_rows, row_step, 0)
+
+
+def forward(message, decoder, place, columns, width):
+    groups, _, tok = message.shape
+    lat_rows = decoder.shape[1]
+    steps = columns.shape[0]
+    scalars = jnp.concatenate([place[None], columns]).astype(jnp.int32)
+    return pl.pallas_call(
+        functools.partial(forward_kernel, groups, lat_rows // tok),
+        out_shape=jax.ShapeDtypeStruct((steps, groups * tok, width), jnp.bfloat16),
+        grid_spec=pltpu.PrefetchScalarGridSpec(
+            num_scalar_prefetch=1,
+            grid=(steps,),
+            in_specs=[
+                pl.BlockSpec(message.shape, lambda i, s: (0, 0, 0)),
+                pl.BlockSpec((1, lat_rows, width), lambda i, s: (0, 0, s[i + 1])),
+            ],
+            out_specs=pl.BlockSpec((1, groups * tok, width), lambda i, s: (i, 0, 0)),
+            scratch_shapes=[
+                pltpu.VMEM((groups * tok, lat_rows), jnp.bfloat16),
+                pltpu.VMEM((groups, 2, tok, tok), jnp.float32),
+            ],
+        ),
+        compiler_params=pltpu.CompilerParams(vmem_limit_bytes=VMEM_BYTES),
+        cost_estimate=pl.CostEstimate(
+            flops=2 * steps * groups * tok * lat_rows * width,
+            bytes_accessed=2 * steps * (groups * tok + lat_rows) * width,
+            transcendentals=0,
+        ),
+        name="forward",
+    )(scalars, message, decoder)
+
+
+def spread_into(target, ids, rows, first, size):
+    def build(b, carry):
+        at = pl.multiple_of(b * size, size)
+        target[pl.ds(at, size), :] = spread_rows(ids, rows, first + b, 1)
+        return carry
+
+    lax.fori_loop(0, target.shape[0] // size, build, 0)
+
+
+def take_piece(pieces, now):
+    for i, piece in enumerate(pieces):
+
+        @pl.when(pl.program_id(0) == i)
+        def _(piece=piece):
+            now[...] = piece[...]
+
+
+def code_grad_kernel(size, place_ref, ids_ref, weight_ref, *refs):
+    pieces, (grad_ref, now) = refs[:-2], refs[-2:]
+    take_piece(pieces, now)
+    several = 4 * size if weight_ref.shape[1] % (4 * size) == 0 else size
+
+    @pl.when(pl.program_id(0) == 0)
+    def _():
+        grad_ref[...] = jnp.zeros_like(grad_ref)
+
+    def step(i, carry):
+        at = pl.multiple_of(i * several, several)
+        grad = lax.dot_general(
+            weight_ref[0, pl.ds(at, several), :],
+            now[...],
+            (((1,), (1,)), ((), ())),
+            preferred_element_type=jnp.float32,
+        )
+        add0, add1 = 0.0, 0.0
+        for n in range(several // size):
+            block = (place_ref[0] + i * (several // size) + n).astype(jnp.float32)
+            part = grad[n * size:(n + 1) * size]
+            add0 = jnp.where(ids_ref[0:1] == block, part, add0)
+            add1 = jnp.where(ids_ref[1:2] == block, part, add1)
+        grad_ref[0] += add0
+        grad_ref[1] += add1
+        return carry
+
+    lax.fori_loop(0, weight_ref.shape[1] // several, step, 0)
+
+
+def code_grad(pieces, ids, decoder, first, columns, size):
+    lat_rows = decoder.shape[1]
+    tokens, width = pieces[0].shape
+    scalars = jnp.concatenate([first[None], columns]).astype(jnp.int32)
+    whole = pl.BlockSpec((tokens, width), lambda i, s: (0, 0))
+    return pl.pallas_call(
+        functools.partial(code_grad_kernel, size),
+        out_shape=jax.ShapeDtypeStruct((2, size, tokens), jnp.float32),
+        grid_spec=pltpu.PrefetchScalarGridSpec(
+            num_scalar_prefetch=1,
+            grid=(len(pieces),),
+            in_specs=[
+                pl.BlockSpec(ids.shape, lambda i, s: (0, 0)),
+                pl.BlockSpec((1, lat_rows, width), lambda i, s: (0, 0, s[i + 1])),
+            ]
+            + [whole] * len(pieces),
+            out_specs=pl.BlockSpec((2, size, tokens), lambda i, s: (0, 0, 0)),
+            scratch_shapes=[pltpu.VMEM((tokens, width), jnp.bfloat16)],
+        ),
+        compiler_params=pltpu.CompilerParams(vmem_limit_bytes=VMEM_BYTES),
+        cost_estimate=pl.CostEstimate(
+            flops=2 * len(pieces) * tokens * lat_rows * width,
+            bytes_accessed=2 * len(pieces) * (tokens + lat_rows) * width,
+            transcendentals=0,
+        ),
+        name="code_grad",
+    )(scalars, ids, decoder, *pieces)
+
+
+def decoder_kernel(size, place_ref, ids_ref, pre_ref, *refs):
+    pieces, (out_ref, now, codes) = refs[:-3], refs[-3:]
+    take_piece(pieces, now)
+
+    @pl.when(pl.program_id(0) == 0)
+    def _():
+        rows = [jnp.maximum(pre_ref[j].astype(jnp.float32), 0.0) for j in range(2)]
+        spread_into(codes, ids_ref[...], rows, place_ref[0], size)
+
+    several = 2 * size if codes.shape[0] % (2 * size) == 0 else size
+
+    def step(i, carry):
+        at = pl.multiple_of(i * several, several)
+        out_ref[pl.ds(at, several), :] = jnp.dot(
+            codes[pl.ds(at, several), :], now[...], preferred_element_type=jnp.float32
+        ).astype(jnp.bfloat16)
+        return carry
+
+    lax.fori_loop(0, codes.shape[0] // several, step, 0)
+
+
+def decoder_kernel_onto(size, place_ref, ids_ref, pre_ref, held_ref, *refs):
+    decoder_kernel(size, place_ref, ids_ref, pre_ref, *refs)
+
+
+def decoder_part(pieces, ids, pre_lanes, first, columns, lat_rows, half, held):
+    _, size, tokens = pre_lanes.shape
+    width = pieces[0].shape[1]
+    scalars = jnp.concatenate([first[None], columns]).astype(jnp.int32)
+    whole = pl.BlockSpec((tokens, width), lambda i, s: (0, 0))
+    return pl.pallas_call(
+        functools.partial(decoder_kernel if held is None else decoder_kernel_onto, size),
+        out_shape=jax.ShapeDtypeStruct((lat_rows, half), jnp.bfloat16),
+        grid_spec=pltpu.PrefetchScalarGridSpec(
+            num_scalar_prefetch=1,
+            grid=(len(pieces),),
+            in_specs=[
+                pl.BlockSpec(ids.shape, lambda i, s: (0, 0)),
+                pl.BlockSpec(pre_lanes.shape, lambda i, s: (0, 0, 0)),
+            ]
+            + ([] if held is None else [pl.BlockSpec(memory_space=pl.ANY)])
+            + [whole] * len(pieces),
+            out_specs=pl.BlockSpec((lat_rows, width), lambda i, s: (0, s[i + 1])),
+            scratch_shapes=[
+                pltpu.VMEM((tokens, width), jnp.bfloat16),
+                pltpu.VMEM((lat_rows, tokens), jnp.bfloat16),
+            ],
+        ),
+        compiler_params=pltpu.CompilerParams(vmem_limit_bytes=VMEM_BYTES),
+        input_output_aliases={} if held is None else {3: 0},
+        cost_estimate=pl.CostEstimate(
+            flops=2 * len(pieces) * tokens * lat_rows * width,
+            bytes_accessed=2 * len(pieces) * (tokens + lat_rows) * width,
+            transcendentals=0,
+        ),
+        name="decoder_part",
+    )(scalars, ids, pre_lanes, *([] if held is None else [held]), *pieces)
+
+
+def encoder_kernel(size, place_ref, ids_ref, pre_ref, *refs):
+    out_ref, grads = refs[-2:]
+    parts = [r for r in refs[:-2] if r.dtype == jnp.float32]
+    acts = [r for r in refs[:-2] if r.dtype == jnp.bfloat16]
+
+    @pl.when(pl.program_id(0) == 0)
+    def _():
+        rows = []
+        for j in range(2):
+            total = parts[0][j]
+            for part in parts[1:]:
+                total = total + part[j]
+            rows.append(jnp.where(pre_ref[j].astype(jnp.float32) > 0, total, 0.0))
+        spread_into(grads, ids_ref[...], rows, place_ref[0], size)
+
+    several = 2 * size if grads.shape[0] % (2 * size) == 0 else size
+
+    def step(i, carry):
+        at = pl.multiple_of(i * several, several)
+        total = 0.0
+        for k, act in enumerate(acts):
+            span = act.shape[0]
+            total = total + jnp.dot(
+                grads[pl.ds(at, several), k * span:(k + 1) * span], act[...], preferred_element_type=jnp.float32
+            )
+        out_ref[pl.ds(at, several), :] = total.astype(jnp.bfloat16)
+        return carry
+
+    lax.fori_loop(0, grads.shape[0] // several, step, 0)
+
+
+def encoder_part(parts, acts, ids, pre_lanes, first, lat_rows, half):
+    _, size, tokens = pre_lanes.shape
+    tile = 256 if half % 256 == 0 else half
+    scalars = first[None].astype(jnp.int32)
+    whole = pl.BlockSpec(pre_lanes.shape, lambda i, s: (0, 0, 0))
+    return pl.pallas_call(
+        functools.partial(encoder_kernel, size),
+        out_shape=jax.ShapeDtypeStruct((lat_rows, half), jnp.bfloat16),
+        grid_spec=pltpu.PrefetchScalarGridSpec(
+            num_scalar_prefetch=1,
+            grid=(half // tile,),
+            in_specs=[pl.BlockSpec(ids.shape, lambda i, s: (0, 0)), whole]
+            + [whole] * len(parts)
+            + [pl.BlockSpec((act.shape[0], tile), lambda i, s: (0, i)) for act in acts],
+            out_specs=pl.BlockSpec((lat_rows, tile), lambda i, s: (0, i)),
+            scratch_shapes=[pltpu.VMEM((lat_rows, tokens), jnp.bfloat16)],
+        ),
+        compiler_params=pltpu.CompilerParams(vmem_limit_bytes=VMEM_BYTES),
+        cost_estimate=pl.CostEstimate(
+            flops=2 * tokens * lat_rows * half,
+            bytes_accessed=2 * (tokens + lat_rows) * half,
+            transcendentals=0,
+        ),
+        name="encoder_part",
+    )(scalars, ids, pre_lanes, *parts, *acts)
+
+
+def dense_plan(pre_codes, block_ids, activations, target, decoder):
+    lay_count = lax.axis_size("layer")
+    lat_count = lax.axis_size("latent")
+    dp_count = lax.axis_size("dp")
+    lay_here = lax.axis_index("layer")
+    lat_here = lax.axis_index("latent")
+    dp_here = lax.axis_index("dp")
+    tok_count = activations.shape[1]
+    model_width = activations.shape[2]
+    active_count = block_ids.shape[2]
+    block_size = pre_codes.shape[3]
+    lat_rows = decoder.shape[1]
+    local_blocks = lat_rows // block_size
+    half = model_width // dp_count
+    group = dp_count * tok_count
+    tokens = lat_count * group
+    bits = [1 << i for i in range(lay_count.bit_length() - 1)]
+    chunks = 2 * PAIRS
+    width = half // (chunks * lay_count)
+    f32, bf16 = jnp.float32, jnp.bfloat16
+    first = lat_here * local_blocks
+
+    def columns(rows, which):
+        return lax.dynamic_slice_in_dim(rows, which * half, half, axis=1)
+
+    pre_rows = jnp.swapaxes(pre_codes[0], 0, 1).reshape(active_count * tok_count, block_size)
+    id_rows = jnp.pad(block_ids[0].T, ((0, 16 - active_count), (0, 0))).astype(bf16)
+    own = jnp.concatenate([pre_rows, id_rows], axis=0)
+    message = jnp.stack([own] + [shift(own, "latent", -k) for k in range(1, lat_count)])
+    message = jnp.stack([message, flip(message, "dp", 1)], axis=1)
+    message = message.reshape(lat_count * dp_count, own.shape[0], block_size)
+
+    acts = jnp.concatenate(
+        [columns(activations[0], dp_here), flip(columns(activations[0], 1 - dp_here), "dp", 1)]
+    )
+    acts = gather_line(acts, "latent")
+
+    goal = target.reshape(tok_count, dp_count, chunks, lay_count, width)
+
+    def goal_of(which):
+        cut = lax.dynamic_index_in_dim(goal, which, 1, False)
+        return lax.dynamic_index_in_dim(cut, lay_here, 2, False)
+
+    goals = jnp.concatenate([goal_of(dp_here), flip(goal_of(1 - dp_here), "dp", 1)])
+
+    def order_of(chunk):
+        return bits if chunk % 2 == 0 else bits[::-1]
+
+    def rows_of(order, fixed):
+        out = [fixed]
+        for bit in order:
+            out = out + [r | bit for r in out]
+        return out
+
+    def places(names, offset):
+        return jnp.stack([offset + chunk * lay_count + (lay_here ^ r) for chunk, r in names])
+
+    def weight_places(names):
+        return places(names, dp_here * (half // width))
+
+    every = range(chunks)
+    sent_names = [(c, r) for c in every for r in rows_of(order_of(c)[1:], order_of(c)[0])]
+    kept_names = [(c, r) for c in every for r in rows_of(order_of(c)[1:], 0)]
+    per = lay_count // 2
+    sent = forward(message, decoder, first, weight_places(sent_names), width)
+    kept = forward(message, decoder, first, weight_places(kept_names), width)
+
+    def reduce_layer(chunk):
+        order = order_of(chunk)
+        got = flip(sent[chunk * per:(chunk + 1) * per], "layer", order[0])
+        terms = [got, kept[chunk * per:(chunk + 1) * per]]
+        for bit in order[1:]:
+            size = terms[0].shape[0] // 2
+            far = sum(term[size:].astype(f32) for term in terms).astype(bf16)
+            terms = [term[:size] for term in terms] + [flip(far, "layer", bit)]
+        return sum(term[0].astype(f32) for term in terms)
+
+    def reduce_latent(total, chunk):
+        cut = total.reshape(lat_count, group, width)
+        out = cut[0]
+        for k in range(1, lat_count):
+            out = out + shift(cut[k].astype(bf16), "latent", k).astype(f32)
+        want = goals[:, chunk].astype(f32)
+        return ((out - want) / tok_count).astype(bf16)
+
+    pieces = {}
+    for chunk in every:
+        own_errors = reduce_latent(reduce_layer(chunk), chunk)
+        rows = jnp.concatenate([own_errors] + [shift(own_errors, "latent", -k) for k in range(1, lat_count)], axis=0)
+        pieces[chunk, 0] = rows
+        done = [0]
+        for bit in order_of(chunk)[::-1]:
+            for r in done:
+                pieces[chunk, r | bit] = flip(pieces[chunk, r], "layer", bit)
+            done = done + [r | bit for r in done]
+
+    cut = message.reshape(tokens // tok_count, own.shape[0], block_size)
+    pre_lanes = cut[:, :active_count * tok_count].reshape(-1, active_count, tok_count, block_size)
+    pre_lanes = jnp.transpose(pre_lanes, (1, 3, 0, 2)).reshape(active_count, block_size, tokens)
+    ids = cut[:, active_count * tok_count:active_count * tok_count + active_count]
+    ids = jnp.swapaxes(ids, 0, 1).reshape(active_count, tokens).astype(f32)
+
+    grads = []
+    dec = None
+    for r in range(lay_count):
+        names = [(c, r ^ 0) for c in every]
+        here = [pieces[name] for name in names]
+        grads.append(code_grad(here, ids, decoder, first, weight_places(names), block_size))
+        dec = decoder_part(here, ids, pre_lanes, first, places(names, 0), lat_rows, half, dec)
+    grad = sum(grads)
+    enc = encoder_part([grad, swap_cores(flip(grad, "dp", 1), tok_count)], acts, ids, pre_lanes, first, lat_rows, half)
+    return dec[None], enc[None]
+
+
+def swap_cores(value, tok_count):
+    cut = value.reshape(value.shape[:-1] + (-1, 2, tok_count))
+    return cut[..., ::-1, :].reshape(value.shape)
+
+
+def per_device(pre_codes, block_ids, activations, target, decoder):
+    lat_count = lax.axis_size("latent")
+    lay_count = lax.axis_size("layer")
+    dp_count = lax.axis_size("dp")
+    tok_count = activations.shape[1]
+    model_width = activations.shape[2]
+    active_count = block_ids.shape[2]
+    block_size = pre_codes.shape[3]
+    all_blocks = decoder.shape[1] // block_size * lat_count
+    slots = 2 * tok_count * active_count // lat_count
+    dense = (
+        slots >= tok_count
+        and dp_count == 2
+        and active_count == 2
+        and lay_count > 1
+        and lay_count & (lay_count - 1) == 0
+        and tok_count == block_size
+        and lat_count * dp_count * 16 <= tok_count
+        and model_width % (dp_count * 2 * PAIRS * lay_count * 128) == 0
+        and all_blocks <= 256
+    )
+    plan = dense_plan if dense else slot_plan
+    return plan(pre_codes, block_ids, activations, target, decoder)
+
+
 def solution(mesh):
     placed = (
         P("layer", ("latent", "dp"), None, None),

time: 457 us -> 311 us (0.68)
  waiting for transfers between devices: 324 us -> 89.4 us
  Pallas kernels: 0 us -> 104 us
  matrix products: 68.4 us -> 0 us
  starting transfers between devices: 15 us -> 70.1 us
  local copies, waits for them, and re-layouts: 3.44 us -> 25.9 us
  between operations: 13.8 us -> 0.97 us
  blocking collectives: 10 us -> 0 us
    all_to_all x3 -> x0, waiting for transfers between devices: 193 us -> none  [the longest x1 92.6 us: per_device(): lax.all_to_all(error_slots, 'latent', split_axis=0, concat_axis=0, tiled=...]
    pallas_call x0 -> x11, Pallas kernels: none -> 104 us  [the longest x4 30 us: decoder_part(): pl.pallas_call(functools.partial(decoder_kernel if held is None else deco...]
    ppermute x0 -> x35, waiting for transfers between devices: none -> 89.4 us  [the longest x15 54.3 us: shift(): lax.ppermute(value, axis, [(i, (i + step) % count) for i in range(count)])]
    psum x1 -> x0, waiting for transfers between devices: 72 us -> none  [per_device(): rebuilt = lax.psum(part_sum, 'layer')]
    ppermute x0 -> x35, starting transfers between devices: none -> 70.1 us  [the longest x15 36.8 us: shift(): lax.ppermute(value, axis, [(i, (i + step) % count) for i in range(count)])]
    dot_general x7 -> x0, matrix products: 68.4 us -> none  [the longest x1 26.1 us: per_device(): jnp.einsum('sbcl,sbcd->bld', code_blocks, error_blocks, preferred_element...]
    reduce_scatter x2 -> x0, waiting for transfers between devices: 59.1 us -> none  [the longest x1 39.7 us: per_device(): lax.psum_scatter(dec_term, 'dp', scatter_dimension=1, tiled=True)]
    broadcast_in_dim x2 -> x0, other arithmetic: 18.2 us -> none  [the longest x1 9.15 us: per_device(): dec_half.astype(jnp.bfloat16)[None]]
  transfers between devices with their start and end apart: 6 -> 35, of which waited for: 6 -> 13; matrix products, arithmetic and copies ran while one was open for 10% -> 9% of each run, Pallas kernels for 0% -> 22%
where the time goes in v1:
time: 311 us; the launch traced here: 309 us
  Pallas kernels  104 us (33%)
  waiting for transfers between devices  89.4 us (29%)
  starting transfers between devices  70.1 us (23%)
  local copies, waits for them, and re-layouts  25.9 us (8%)
  other arithmetic  18.1 us (6%)
    ppermute x15, waiting for transfers between devices, shift(): lax.ppermute(value, axis, [(i, (i + step) % count) for i in range(count)])  54.3 us
    ppermute x15, starting transfers between devices, shift(): lax.ppermute(value, axis, [(i, (i + step) % count) for i in range(count)])  36.8 us
    pallas_call x4, Pallas kernels, decoder_part(): pl.pallas_call(functools.partial(decoder_kernel if held is None else deco...  30 us
    ppermute x14, waiting for transfers between devices, flip(): return lax.ppermute(value, axis, [(i, i ^ bit) for i in range(count)])  29.6 us
    pallas_call x4, Pallas kernels, code_grad(): pl.pallas_call(functools.partial(code_grad_kernel, size), out_shape=jax.S...  25.7 us
    pallas_call x1, Pallas kernels, encoder_part(): pl.pallas_call(functools.partial(encoder_kernel, size), out_shape=jax.Sha...  25 us
    pallas_call x2, Pallas kernels, forward(): pl.pallas_call(functools.partial(forward_kernel, groups, lat_rows // tok)...  23.7 us
    ppermute x14, starting transfers between devices, flip(): return lax.ppermute(value, axis, [(i, i ^ bit) for i in range(count)])  21.6 us
  transfers between devices with their start and end apart: 35, of which 13 were waited for; matrix products, arithmetic and copies ran while one was open for 9% of the time, Pallas kernels for 22%

profile of v1, /device:TPU:1, one launch (start us, length us, event | category | flops | bytes accessed | tf_op | source)
XLA Modules:
  0.0 308.8 jit_solution(11503224404930918331)
XLA Ops:
  14.2 11.9 %forward.2 = bf16[4,1024,256]{2,1,0:T(8,128)(2,1)S(1)} custom-call(s32[5]{0:T(128)S(1)} %concatenate.50.place_ref, bf16[8,272,128]{2,1,0:T(8,128)(2,1)S(1)} %bitcast.105, bf16[1,2048,4096]{2,1,0:T(8,128)(2,1)} %weight_ref.11), custom_call_target="tpu_custom_call" | custom-call | flops 4294967296 | bytes 6291456 | tf_op jit(solution)/shard_map/forward/pallas_call | solution.py:186
  30.1 11.9 %forward.3 = bf16[4,1024,256]{2,1,0:T(8,128)(2,1)S(1)} custom-call(s32[5]{0:T(128)S(1)} %concatenate.51.place_ref, bf16[8,272,128]{2,1,0:T(8,128)(2,1)S(1)} %bitcast.106, bf16[1,2048,4096]{2,1,0:T(8,128)(2,1)} %weight_ref.11), custom_call_target="tpu_custom_call" | custom-call | flops 4294967296 | bytes 6291456 | tf_op jit(solution)/shard_map/forward/pallas_call | solution.py:186
  42.0 10.2 %collective-permute-done.13 = bf16[2,1024,256]{2,1,0:T(8,128)(2,1)} collective-permute-done((bf16[2,1024,256]{2,1,0:T(8,128)(2,1)}, bf16[2,1024,256]{2,1,0:T(8,128)(2,1)}, u32[]{:S(2)}, u32[]{:S(2)}) %collective-permute-start.13) | collective-permute-done | bytes 1048608 | tf_op jit(solution)/shard_map/ppermute | solution.py:109
  57.5 8.2 %collective-permute-done.14 = bf16[1,1024,256]{2,1,0:T(8,128)(2,1)} collective-permute-done((bf16[1,1024,256]{2,1,0:T(8,128)(2,1)S(1)}, bf16[1,1024,256]{2,1,0:T(8,128)(2,1)}, u32[]{:S(2)}, u32[]{:S(2)}) %collective-permute-start.14) | collective-permute-done | bytes 524320 | tf_op jit(solution)/shard_map/ppermute | solution.py:109
  70.9 4.3 %collective-permute-start.30 = (bf16[256,2048]{1,0:T(8,128)(2,1)}, bf16[256,2048]{1,0:T(8,128)(2,1)}, u32[]{:S(2)}, u32[]{:S(2)}) collective-permute-start(bf16[256,2048]{1,0:T(8,128)(2,1)} %pad_maximum_fusion.refs_2_), channel_id=1, source_target_pairs={{0,2},{2,4},{4,6},{1,3},{3,5},{5,7},{8,10},{10,12},{12,14},{9,11},... | collective-permute-start | bytes 3145736 | tf_op jit(solution)/shard_map/ppermute | solution.py:118
  89.1 5.5 %collective-permute-done.30 = bf16[256,2048]{1,0:T(8,128)(2,1)} collective-permute-done((bf16[256,2048]{1,0:T(8,128)(2,1)}, bf16[256,2048]{1,0:T(8,128)(2,1)}, u32[]{:S(2)}, u32[]{:S(2)}) %collective-permute-start.30) | collective-permute-done | bytes 1048608 | tf_op jit(solution)/shard_map/ppermute | solution.py:118
  94.6 4.1 %collective-permute-start.8 = (bf16[256,256]{1,0:T(8,128)(2,1)S(1)}, bf16[256,256]{1,0:T(8,128)(2,1)S(1)}, u32[]{:S(2)}, u32[]{:S(2)}) collective-permute-start(bf16[256,256]{1,0:T(8,128)(2,1)S(1)} %get-tuple-element.17), channel_id=1, source_target_pairs={{0,6},{2,0},{4,2},{6,4},{1,7},{3,1},{5,3},{7,5},{8,14},{10,8},{12,... | collective-permute-start | bytes 393224 | tf_op jit(solution)/shard_map/ppermute | solution.py:104
  98.7 14.4 %collective-permute-done.17 = bf16[256,256]{1,0:T(8,128)(2,1)S(1)} collective-permute-done((bf16[256,256]{1,0:T(8,128)(2,1)S(1)}, bf16[256,256]{1,0:T(8,128)(2,1)S(1)}, u32[]{:S(2)}, u32[]{:S(2)}) %collective-permute-start.17) | collective-permute-done | bytes 131104 | tf_op jit(solution)/shard_map/ppermute | solution.py:104
  113.1 6.9 %collective-permute-done.16 = bf16[256,256]{1,0:T(8,128)(2,1)S(1)} collective-permute-done((bf16[256,256]{1,0:T(8,128)(2,1)S(1)}, bf16[256,256]{1,0:T(8,128)(2,1)S(1)}, u32[]{:S(2)}, u32[]{:S(2)}) %collective-permute-start.16) | collective-permute-done | bytes 131104 | tf_op jit(solution)/shard_map/ppermute | solution.py:104
  121.7 9.5 %collective-permute-done.7 = bf16[256,256]{1,0:T(8,128)(2,1)S(1)} collective-permute-done((bf16[256,256]{1,0:T(8,128)(2,1)S(1)}, bf16[256,256]{1,0:T(8,128)(2,1)S(1)}, u32[]{:S(2)}, u32[]{:S(2)}) %collective-permute-start.7) | collective-permute-done | bytes 131104 | tf_op jit(solution)/shard_map/ppermute | solution.py:104
  138.8 14.3 %collective-permute-start.12 = (bf16[256,256]{1,0:T(8,128)(2,1)S(1)}, bf16[256,256]{1,0:T(8,128)(2,1)S(1)}, u32[]{:S(2)}, u32[]{:S(2)}) collective-permute-start(bf16[256,256]{1,0:T(8,128)(2,1)S(1)} %get-tuple-element.22), channel_id=1, source_target_pairs={{0,2},{2,4},{4,6},{6,0},{1,3},{3,5},{5,7},{7,1},{8,10},{10,12},{12... | collective-permute-start | bytes 393224 | tf_op jit(solution)/shard_map/ppermute | solution.py:104
  160.0 17.3 %collective-permute-done.11 = bf16[256,256]{1,0:T(8,128)(2,1)S(1)} collective-permute-done((bf16[256,256]{1,0:T(8,128)(2,1)S(1)}, bf16[256,256]{1,0:T(8,128)(2,1)S(1)}, u32[]{:S(2)}, u32[]{:S(2)}) %collective-permute-start.11) | collective-permute-done | bytes 131104 | tf_op jit(solution)/shard_map/ppermute | solution.py:104
  180.4 8.3 %collective-permute-done.23.refs_0_ = bf16[1024,256]{1,0:T(8,128)(2,1)S(1)} collective-permute-done((bf16[1024,256]{1,0:T(8,128)(2,1)S(1)}, bf16[1024,256]{1,0:T(8,128)(2,1)S(1)}, u32[]{:S(2)}, u32[]{:S(2)}) %collective-permute-start.23) | collective-permute-done | bytes 524320 | tf_op jit(solution)/shard_map/ppermute | solution.py:109
  190.1 6.4 %code_grad.4 = f32[2,128,1024]{2,1,0:T(8,128)S(1)} custom-call(s32[3]{0:T(128)S(1)} %get-tuple-element.26.place_ref, f32[2,1024]{1,0:T(2,128)S(1)} %convert_bitcast_fusion.ids_ref, bf16[1,2048,4096]{2,1,0:T(8,128)(2,1)} %weight_ref.11, bf16[1024,256]{1,0:T(8,128)(2,1)S(1)} %pad_maximum_fusion.2.refs_0_, bf16[1024,256]{1,0:T(8,128)(2,1)S(1)} %pad_maximum_fusion.3.refs_1_), custom_call_target="tpu_custom_call" | custom-call | flops 2147483648 | bytes 3145728 | tf_op jit(solution)/shard_map/code_grad/pallas_call | solution.py:264
  201.3 6.4 %code_grad.6 = f32[2,128,1024]{2,1,0:T(8,128)S(1)} custom-call(s32[3]{0:T(128)S(1)} %get-tuple-element.28.place_ref, f32[2,1024]{1,0:T(2,128)S(1)} %convert_bitcast_fusion.ids_ref, bf16[1,2048,4096]{2,1,0:T(8,128)(2,1)} %weight_ref.11, bf16[1024,256]{1,0:T(8,128)(2,1)S(1)} %collective-permute-done.23.refs_0_, ...), custom_call_target="tpu_custom_call" | custom-call | flops 2147483648 | bytes 3145728 | tf_op jit(solution)/shard_map/code_grad/pallas_call | solution.py:264
  207.8 6.4 %code_grad.5 = f32[2,128,1024]{2,1,0:T(8,128)S(1)} custom-call(s32[3]{0:T(128)S(1)} %get-tuple-element.27.place_ref, f32[2,1024]{1,0:T(2,128)S(1)} %convert_bitcast_fusion.ids_ref, bf16[1,2048,4096]{2,1,0:T(8,128)(2,1)} %weight_ref.11, bf16[1024,256]{1,0:T(8,128)(2,1)S(1)} %collective-permute-done.21.refs_0_, ...), custom_call_target="tpu_custom_call" | custom-call | flops 2147483648 | bytes 3145728 | tf_op jit(solution)/shard_map/code_grad/pallas_call | solution.py:264
  214.3 6.4 %code_grad.7 = f32[2,128,1024]{2,1,0:T(8,128)S(1)} custom-call(s32[3]{0:T(128)S(1)} %pad_add_fusion.7.place_ref, f32[2,1024]{1,0:T(2,128)S(1)} %convert_bitcast_fusion.ids_ref, bf16[1,2048,4096]{2,1,0:T(8,128)(2,1)} %weight_ref.11, bf16[1024,256]{1,0:T(8,128)(2,1)S(1)} %collective-permute-done.25.refs_0_, bf16[1024,256]{1,0:T(8,128)(2,1)S(1)} %collective-permute-done.26.refs_1_), custom_call_target="tpu_custom_call" | custom-call | flops 2147483648 | bytes 3145728 | tf_op jit(solution)/shard_map/code_grad/pallas_call | solution.py:264
  222.1 5.9 %collective-permute-start.27 = (f32[2,128,1024]{2,1,0:T(8,128)}, f32[2,128,1024]{2,1,0:T(8,128)}, u32[]{:S(2)}, u32[]{:S(2)}) collective-permute-start(f32[2,128,1024]{2,1,0:T(8,128)} %add_add_fusion.refs_0_), channel_id=1, source_target_pairs={{0,1},{1,0},{2,3},{3,2},{4,5},{5,4},{6,7},{7,6},{8,9},{9,8},{10,11... | collective-permute-start | bytes 3145736 | tf_op jit(solution)/shard_map/ppermute | solution.py:109
  235.4 7.5 %decoder_part.4.held_ref = bf16[2048,2048]{1,0:T(8,128)(2,1)} custom-call(s32[3]{0:T(128)S(1)} %pad_add_fusion.3.place_ref, f32[2,1024]{1,0:T(2,128)S(1)} %convert_bitcast_fusion.ids_ref, bf16[2,128,1024]{2,1,0:T(8,128)(2,1)S(1)} %reshape.83.pre_ref, bf16[1024,256]{1,0:T(8,128)(2,1)S(1)} %pad_maximum_fusion.2.refs_0_, ...), custom_call_target="tpu_custom_call" | custom-call | flops 2147483648 | bytes 3145728 | tf_op jit(solution)/shard_map/decoder_part/pallas_call | solution.py:318
  242.9 7.5 %decoder_part.5.held_ref = bf16[2048,2048]{1,0:T(8,128)(2,1)} custom-call(s32[3]{0:T(128)S(1)} %pad_add_fusion.2.place_ref, f32[2,1024]{1,0:T(2,128)S(1)} %convert_bitcast_fusion.ids_ref, bf16[2,128,1024]{2,1,0:T(8,128)(2,1)S(1)} %reshape.83.pre_ref, bf16[2048,2048]{1,0:T(8,128)(2,1)} %decoder_part.4.held_ref, ...), custom_call_target="tpu_custom_call", output_to_operand_aliasing={{}: (3, {})} | custom-call | flops 2147483648 | bytes 3145728 | tf_op jit(solution)/shard_map/decoder_part/pallas_call | solution.py:318
  250.4 7.5 %decoder_part.6.held_ref = bf16[2048,2048]{1,0:T(8,128)(2,1)} custom-call(s32[3]{0:T(128)S(1)} %get-tuple-element.25.place_ref, f32[2,1024]{1,0:T(2,128)S(1)} %convert_bitcast_fusion.ids_ref, bf16[2,128,1024]{2,1,0:T(8,128)(2,1)S(1)} %reshape.83.pre_ref, bf16[2048,2048]{1,0:T(8,128)(2,1)} %decoder_part.5.held_ref, ...), custom_call_target="tpu_custom_call", output_to_operand_aliasing={{}: (3, {})} | custom-call | flops 2147483648 | bytes 3145728 | tf_op jit(solution)/shard_map/decoder_part/pallas_call | solution.py:318
  262.8 7.5 %decoder_part.7 = bf16[2048,2048]{1,0:T(8,128)(2,1)} custom-call(s32[3]{0:T(128)S(1)} %pad_add_fusion.place_ref, f32[2,1024]{1,0:T(2,128)S(1)} %convert_bitcast_fusion.ids_ref, bf16[2,128,1024]{2,1,0:T(8,128)(2,1)S(1)} %reshape.83.pre_ref, bf16[2048,2048]{1,0:T(8,128)(2,1)} %decoder_part.6.held_ref, ...), custom_call_target="tpu_custom_call", output_to_operand_aliasing={{}: (3, {})} | custom-call | flops 2147483648 | bytes 3145728 | tf_op jit(solution)/shard_map/decoder_part/pallas_call | solution.py:318
  273.4 6.1 %rev.3 = f32[2,128,4,2,128]{4,3,2,1,0:T(2,128)} reverse(f32[2,128,4,2,128]{4,3,2,1,0:T(2,128)} %reshape.85), dimensions={3} | reverse | bytes 2097152 | tf_op jit(solution)/shard_map/rev | solution.py:521
  283.8 25.0 %encoder_part.1 = bf16[2048,2048]{1,0:T(8,128)(2,1)} custom-call(s32[1]{0:T(128)} %bitcast.place_ref, f32[2,1024]{1,0:T(2,128)S(1)} %convert_bitcast_fusion.ids_ref, bf16[2,128,1024]{2,1,0:T(8,128)(2,1)S(1)} %reshape.83.pre_ref, f32[2,128,1024]{2,1,0:T(8,128)} %add_add_fusion.refs_0_, f32[2,128,1024]{2,1,0:T(8,128)S(1)} %copy-done.7, ...), custom_call_target="tpu_custom_call" | custom-call | flops 8589934592 | bytes 12582912 | tf_op jit(solution)/shard_map/encoder_part/pallas_call | solution.py:383
  (113 shorter events, 88.3 us)
Async XLA Ops:
  27.5 24.7 %collective-permute-start.13 = (bf16[2,1024,256]{2,1,0:T(8,128)(2,1)}, bf16[2,1024,256]{2,1,0:T(8,128)(2,1)}, u32[]{:S(2)}, u32[]{:S(2)}) collective-permute-start(bf16[2,1024,256]{2,1,0:T(8,128)(2,1)} %get-tuple-element.7), channel_id=1, source_target_pairs={{0,16},{8,24},{16,0},{24,8},{1,17},{9,25},{17,1},{25,9},{2,18},{10... | collective-permute-start | bytes 3145736 | tf_op jit(solution)/shard_map/ppermute | solution.py:109
  28.9 28.6 %collective-permute-start.4 = (bf16[2,1024,256]{2,1,0:T(8,128)(2,1)}, bf16[2,1024,256]{2,1,0:T(8,128)(2,1)}, u32[]{:S(2)}, u32[]{:S(2)}) collective-permute-start(bf16[2,1024,256]{2,1,0:T(8,128)(2,1)} %get-tuple-element.8), channel_id=1, source_target_pairs={{0,8},{8,0},{16,24},{24,16},{1,9},{9,1},{17,25},{25,17},{2,10},{10... | collective-permute-start | bytes 3145736 | tf_op jit(solution)/shard_map/ppermute | solution.py:109
  68.6 18.7 %collective-permute-start.5 = (bf16[1,1024,256]{2,1,0:T(8,128)(2,1)}, bf16[1,1024,256]{2,1,0:T(8,128)(2,1)}, u32[]{:S(2)}, u32[]{:S(2)}) collective-permute-start(bf16[1,1024,256]{2,1,0:T(8,128)(2,1)} %get-tuple-element.6), channel_id=1, source_target_pairs={{0,16},{8,24},{16,0},{24,8},{1,17},{9,25},{17,1},{25,9},{2,18},{10... | collective-permute-start | bytes 1572872 | tf_op jit(solution)/shard_map/ppermute | solution.py:109
  70.9 23.7 %collective-permute-start.30 = (bf16[256,2048]{1,0:T(8,128)(2,1)}, bf16[256,2048]{1,0:T(8,128)(2,1)}, u32[]{:S(2)}, u32[]{:S(2)}) collective-permute-start(bf16[256,2048]{1,0:T(8,128)(2,1)} %pad_maximum_fusion.refs_2_), channel_id=1, source_target_pairs={{0,2},{2,4},{4,6},{1,3},{3,5},{5,7},{8,10},{10,12},{12,14},{9,11},... | collective-permute-start | bytes 3145736 | tf_op jit(solution)/shard_map/ppermute | solution.py:118
  82.4 53.3 %collective-permute-start.29 = (bf16[256,2048]{1,0:T(8,128)(2,1)}, bf16[256,2048]{1,0:T(8,128)(2,1)}, u32[]{:S(2)}, u32[]{:S(2)}) collective-permute-start(bf16[256,2048]{1,0:T(8,128)(2,1)} %pad_maximum_fusion.refs_2_), channel_id=1, source_target_pairs={{2,0},{4,2},{6,4},{3,1},{5,3},{7,5},{10,8},{12,10},{14,12},{11,9},... | collective-permute-start | bytes 3145736 | tf_op jit(solution)/shard_map/ppermute | solution.py:118
  83.7 29.4 %collective-permute-start.17 = (bf16[256,256]{1,0:T(8,128)(2,1)S(1)}, bf16[256,256]{1,0:T(8,128)(2,1)S(1)}, u32[]{:S(2)}, u32[]{:S(2)}) collective-permute-start(bf16[256,256]{1,0:T(8,128)(2,1)S(1)} %get-tuple-element.14), channel_id=1, source_target_pairs={{0,6},{2,0},{4,2},{6,4},{1,7},{3,1},{5,3},{7,5},{8,14},{10,8},{12,... | collective-permute-start | bytes 393224 | tf_op jit(solution)/shard_map/ppermute | solution.py:104
  87.3 32.8 %collective-permute-start.16 = (bf16[256,256]{1,0:T(8,128)(2,1)S(1)}, bf16[256,256]{1,0:T(8,128)(2,1)S(1)}, u32[]{:S(2)}, u32[]{:S(2)}) collective-permute-start(bf16[256,256]{1,0:T(8,128)(2,1)S(1)} %get-tuple-element.15), channel_id=1, source_target_pairs={{0,4},{2,6},{4,0},{6,2},{1,5},{3,7},{5,1},{7,3},{8,12},{10,14},{12... | collective-permute-start | bytes 393224 | tf_op jit(solution)/shard_map/ppermute | solution.py:104
  88.7 31.4 %collective-permute-start.15 = (bf16[256,256]{1,0:T(8,128)(2,1)S(1)}, bf16[256,256]{1,0:T(8,128)(2,1)S(1)}, u32[]{:S(2)}, u32[]{:S(2)}) collective-permute-start(bf16[256,256]{1,0:T(8,128)(2,1)S(1)} %get-tuple-element.13), channel_id=1, source_target_pairs={{0,2},{2,4},{4,6},{6,0},{1,3},{3,5},{5,7},{7,1},{8,10},{10,12},{12... | collective-permute-start | bytes 393224 | tf_op jit(solution)/shard_map/ppermute | solution.py:104
  94.6 27.1 %collective-permute-start.8 = (bf16[256,256]{1,0:T(8,128)(2,1)S(1)}, bf16[256,256]{1,0:T(8,128)(2,1)S(1)}, u32[]{:S(2)}, u32[]{:S(2)}) collective-permute-start(bf16[256,256]{1,0:T(8,128)(2,1)S(1)} %get-tuple-element.17), channel_id=1, source_target_pairs={{0,6},{2,0},{4,2},{6,4},{1,7},{3,1},{5,3},{7,5},{8,14},{10,8},{12,... | collective-permute-start | bytes 393224 | tf_op jit(solution)/shard_map/ppermute | solution.py:104
  120.0 59.1 %collective-permute-start.31 = (bf16[256,2048]{1,0:T(8,128)(2,1)}, bf16[256,2048]{1,0:T(8,128)(2,1)}, u32[]{:S(2)}, u32[]{:S(2)}) collective-permute-start(bf16[256,2048]{1,0:T(8,128)(2,1)} %collective-permute-done.30), channel_id=1, source_target_pairs={{2,4},{4,6},{3,5},{5,7},{10,12},{12,14},{11,13},{13,15},{18,20},{2... | collective-permute-start | bytes 3145736 | tf_op jit(solution)/shard_map/ppermute | solution.py:118
  132.5 20.6 %collective-permute-start.19 = (bf16[256,256]{1,0:T(8,128)(2,1)S(1)}, bf16[256,256]{1,0:T(8,128)(2,1)S(1)}, u32[]{:S(2)}, u32[]{:S(2)}) collective-permute-start(bf16[256,256]{1,0:T(8,128)(2,1)S(1)} %get-tuple-element.21), channel_id=1, source_target_pairs={{0,4},{2,6},{4,0},{6,2},{1,5},{3,7},{5,1},{7,3},{8,12},{10,14},{12... | collective-permute-start | bytes 393224 | tf_op jit(solution)/shard_map/ppermute | solution.py:104
  132.5 22.4 %collective-permute-start.18 = (bf16[256,256]{1,0:T(8,128)(2,1)S(1)}, bf16[256,256]{1,0:T(8,128)(2,1)S(1)}, u32[]{:S(2)}, u32[]{:S(2)}) collective-permute-start(bf16[256,256]{1,0:T(8,128)(2,1)S(1)} %get-tuple-element.21), channel_id=1, source_target_pairs={{0,6},{2,0},{4,2},{6,4},{1,7},{3,1},{5,3},{7,5},{8,14},{10,8},{12,... | collective-permute-start | bytes 393224 | tf_op jit(solution)/shard_map/ppermute | solution.py:104
  135.7 60.8 %collective-permute-start.33 = (bf16[256,2048]{1,0:T(8,128)(2,1)}, bf16[256,2048]{1,0:T(8,128)(2,1)}, u32[]{:S(2)}, u32[]{:S(2)}) collective-permute-start(bf16[256,2048]{1,0:T(8,128)(2,1)} %collective-permute-done.29), channel_id=1, source_target_pairs={{2,0},{4,2},{3,1},{5,3},{10,8},{12,10},{11,9},{13,11},{18,16},{20,... | collective-permute-start | bytes 3145736 | tf_op jit(solution)/shard_map/ppermute | solution.py:118
  138.8 20.0 %collective-permute-start.12 = (bf16[256,256]{1,0:T(8,128)(2,1)S(1)}, bf16[256,256]{1,0:T(8,128)(2,1)S(1)}, u32[]{:S(2)}, u32[]{:S(2)}) collective-permute-start(bf16[256,256]{1,0:T(8,128)(2,1)S(1)} %get-tuple-element.22), channel_id=1, source_target_pairs={{0,2},{2,4},{4,6},{6,0},{1,3},{3,5},{5,7},{7,1},{8,10},{10,12},{12... | collective-permute-start | bytes 393224 | tf_op jit(solution)/shard_map/ppermute | solution.py:104
  153.1 24.3 %collective-permute-start.11 = (bf16[256,256]{1,0:T(8,128)(2,1)S(1)}, bf16[256,256]{1,0:T(8,128)(2,1)S(1)}, u32[]{:S(2)}, u32[]{:S(2)}) collective-permute-start(bf16[256,256]{1,0:T(8,128)(2,1)S(1)} %get-tuple-element.22), channel_id=1, source_target_pairs={{0,4},{2,6},{4,0},{6,2},{1,5},{3,7},{5,1},{7,3},{8,12},{10,14},{12... | collective-permute-start | bytes 393224 | tf_op jit(solution)/shard_map/ppermute | solution.py:104
  155.0 22.4 %collective-permute-start.10 = (bf16[256,256]{1,0:T(8,128)(2,1)S(1)}, bf16[256,256]{1,0:T(8,128)(2,1)S(1)}, u32[]{:S(2)}, u32[]{:S(2)}) collective-permute-start(bf16[256,256]{1,0:T(8,128)(2,1)S(1)} %get-tuple-element.22), channel_id=1, source_target_pairs={{0,6},{2,0},{4,2},{6,4},{1,7},{3,1},{5,3},{7,5},{8,14},{10,8},{12,... | collective-permute-start | bytes 393224 | tf_op jit(solution)/shard_map/ppermute | solution.py:104
  158.7 31.1 %collective-permute-start.22 = (bf16[1024,256]{1,0:T(8,128)(2,1)S(1)}, bf16[1024,256]{1,0:T(8,128)(2,1)S(1)}, u32[]{:S(2)}, u32[]{:S(2)}) collective-permute-start(bf16[1024,256]{1,0:T(8,128)(2,1)S(1)} %pad_maximum_fusion.3.refs_1_), channel_id=1, source_target_pairs={{0,8},{8,0},{16,24},{24,16},{1,9},{9,1},{17,25},{25,17},{2,10},{10... | collective-permute-start | bytes 1572872 | tf_op jit(solution)/shard_map/ppermute | solution.py:109
  177.8 22.0 %collective-permute-start.24 = (bf16[1024,256]{1,0:T(8,128)(2,1)S(1)}, bf16[1024,256]{1,0:T(8,128)(2,1)S(1)}, u32[]{:S(2)}, u32[]{:S(2)}) collective-permute-start(bf16[1024,256]{1,0:T(8,128)(2,1)S(1)} %pad_maximum_fusion.3.refs_1_), channel_id=1, source_target_pairs={{0,16},{8,24},{16,0},{24,8},{1,17},{9,25},{17,1},{25,9},{2,18},{10... | collective-permute-start | bytes 1572872 | tf_op jit(solution)/shard_map/ppermute | solution.py:109
  179.2 28.6 %collective-permute-start.21 = (bf16[1024,256]{1,0:T(8,128)(2,1)S(1)}, bf16[1024,256]{1,0:T(8,128)(2,1)S(1)}, u32[]{:S(2)}, u32[]{:S(2)}) collective-permute-start(bf16[1024,256]{1,0:T(8,128)(2,1)S(1)} %pad_maximum_fusion.2.refs_0_), channel_id=1, source_target_pairs={{0,8},{8,0},{16,24},{24,16},{1,9},{9,1},{17,25},{25,17},{2,10},{10... | collective-permute-start | bytes 1572872 | tf_op jit(solution)/shard_map/ppermute | solution.py:109
  188.6 25.6 %collective-permute-start.25 = (bf16[1024,256]{1,0:T(8,128)(2,1)S(1)}, bf16[1024,256]{1,0:T(8,128)(2,1)S(1)}, u32[]{:S(2)}, u32[]{:S(2)}) collective-permute-start(bf16[1024,256]{1,0:T(8,128)(2,1)S(1)} %collective-permute-done.23.refs_0_), channel_id=1, source_target_pairs={{0,8},{8,0},{16,24},{24,16},{1,9},{9,1},{17,25},{25,17},{2,10},{10... | collective-permute-start | bytes 1572872 | tf_op jit(solution)/shard_map/ppermute | solution.py:109
  189.8 24.4 %collective-permute-start.26 = (bf16[1024,256]{1,0:T(8,128)(2,1)S(1)}, bf16[1024,256]{1,0:T(8,128)(2,1)S(1)}, u32[]{:S(2)}, u32[]{:S(2)}) collective-permute-start(bf16[1024,256]{1,0:T(8,128)(2,1)S(1)} %collective-permute-done.22.refs_1_), channel_id=1, source_target_pairs={{0,16},{8,24},{16,0},{24,8},{1,17},{9,25},{17,1},{25,9},{2,18},{10... | collective-permute-start | bytes 1572872 | tf_op jit(solution)/shard_map/ppermute | solution.py:109
  196.5 61.4 %collective-permute-start.32 = (bf16[256,2048]{1,0:T(8,128)(2,1)}, bf16[256,2048]{1,0:T(8,128)(2,1)}, u32[]{:S(2)}, u32[]{:S(2)}) collective-permute-start(bf16[256,2048]{1,0:T(8,128)(2,1)} %collective-permute-done.31), channel_id=1, source_target_pairs={{4,6},{5,7},{12,14},{13,15},{20,22},{21,23},{28,30},{29,31}} | collective-permute-start | bytes 3145736 | tf_op jit(solution)/shard_map/ppermute | solution.py:118
  199.9 60.0 %collective-permute-start.34 = (bf16[256,2048]{1,0:T(8,128)(2,1)}, bf16[256,2048]{1,0:T(8,128)(2,1)}, u32[]{:S(2)}, u32[]{:S(2)}) collective-permute-start(bf16[256,2048]{1,0:T(8,128)(2,1)} %collective-permute-done.33), channel_id=1, source_target_pairs={{2,0},{3,1},{10,8},{11,9},{18,16},{19,17},{26,24},{27,25}} | collective-permute-start | bytes 3145736 | tf_op jit(solution)/shard_map/ppermute | solution.py:118
  222.1 48.2 %collective-permute-start.27 = (f32[2,128,1024]{2,1,0:T(8,128)}, f32[2,128,1024]{2,1,0:T(8,128)}, u32[]{:S(2)}, u32[]{:S(2)}) collective-permute-start(f32[2,128,1024]{2,1,0:T(8,128)} %add_add_fusion.refs_0_), channel_id=1, source_target_pairs={{0,1},{1,0},{2,3},{3,2},{4,5},{5,4},{6,7},{7,6},{8,9},{9,8},{10,11... | collective-permute-start | bytes 3145736 | tf_op jit(solution)/shard_map/ppermute | solution.py:109
  (19 other events, 146.5 us)

commit v2 on v0

--- a/solution.py
+++ b/solution.py
@@ -1,7 +1,14 @@
+import functools
+
 import jax
 import jax.numpy as jnp
 from jax import lax
+from jax.experimental import pallas as pl
+from jax.experimental.pallas import tpu as pltpu
 from jax.sharding import PartitionSpec as P
+
+PAIRS = 2
+VMEM_BYTES = 40 * 1024 * 1024
 
 
 def local_contrib(received_pre, weights, lat_count, local_blocks):
@@ -16,7 +23,7 @@
     return lax.all_to_all(contrib, "latent", split_axis=0, concat_axis=0, tiled=True)
 
 
-def per_device(pre_codes, block_ids, activations, target, decoder):
+def slot_plan(pre_codes, block_ids, activations, target, decoder):
     lat_count = lax.axis_size("latent")
     tok_count = activations.shape[1]
     model_width = activations.shape[2]
@@ -92,6 +99,455 @@
     return (dec_half.astype(jnp.bfloat16)[None], enc_half.astype(jnp.bfloat16)[None])
 
 
+def flip(value, axis, bit):
+    count = lax.axis_size(axis)
+    return lax.ppermute(value, axis, [(i, i ^ bit) for i in range(count)])
+
+
+def hop(value, axis, step, least):
+    count = lax.axis_size(axis)
+    if step > 0:
+        pairs = [(i, i + 1) for i in range(least, count - 1)]
+    else:
+        pairs = [(i, i - 1) for i in range(1, count - least)]
+    return lax.ppermute(value, axis, pairs)
+
+
+def after(value, *others):
+    return lax.optimization_barrier((value,) + others)[0]
+
+
+def params():
+    return pltpu.CompilerParams(vmem_limit_bytes=VMEM_BYTES)
+
+
+def cost(rows, depth, columns):
+    return pl.CostEstimate(
+        flops=2 * rows * depth * columns,
+        bytes_accessed=2 * (rows * depth + depth * columns + rows * columns),
+        transcendentals=0,
+    )
+
+
+def resident(shape):
+    return pl.BlockSpec(shape, lambda i, s: (0,) * len(shape))
+
+
+def forward_kernel(groups, blocks, scalar_ref, message_ref, weight_ref, *refs):
+    outs, (codes, id_map, pre) = refs[:4], refs[4:]
+    tok = message_ref.shape[2]
+    pad = message_ref.shape[1] - 2 * tok
+    half = outs[0].shape[2]
+    step = pl.program_id(0)
+
+    @pl.when(step == 0)
+    def _():
+        first = scalar_ref[0].astype(jnp.float32)
+        rows = [message_ref[g, 2 * tok:2 * tok + pad, :].astype(jnp.float32) for g in range(groups)]
+        fill = tok - groups * pad
+        if fill:
+            rows.append(jnp.zeros((fill, tok), jnp.float32))
+        table = jnp.concatenate(rows, axis=0).T - first
+        for g in range(groups):
+            pre[g] = jnp.maximum(message_ref[g, 0:2 * tok, :], jnp.zeros((), jnp.bfloat16))
+            for j in range(2):
+                at = g * pad + j
+                wide = jnp.broadcast_to(table[:, at:at + 1], (tok, tok))
+                id_map[g, j * tok:(j + 1) * tok, :] = wide.astype(jnp.bfloat16)
+
+        def block_step(b, carry):
+            block = b.astype(jnp.float32).astype(jnp.bfloat16)
+            at = pl.multiple_of(b * tok, tok)
+            for g in range(groups):
+                value = jnp.where(id_map[g, tok:2 * tok, :] == block, pre[g, tok:2 * tok, :], jnp.zeros((), jnp.bfloat16))
+                value = jnp.where(id_map[g, 0:tok, :] == block, pre[g, 0:tok, :], value)
+                codes[g * tok:(g + 1) * tok, pl.ds(at, tok)] = value
+            return carry
+
+        lax.fori_loop(0, blocks, block_step, 0)
+
+    step_rows = 4 * tok if codes.shape[0] % (4 * tok) == 0 else tok
+    stores = {0: (0, 2), 1: (0, 3), 2: (1, 2), 3: (1, 3)}
+
+    def row_step(i, carry):
+        at = pl.multiple_of(i * step_rows, step_rows)
+        rows = pl.ds(at, step_rows)
+        value = jnp.dot(codes[rows, :], weight_ref[0], preferred_element_type=jnp.float32).astype(jnp.bfloat16)
+        for n, (to_a, to_b) in {0: (0, 2), 1: (0, 3), 2: (1, 2), 3: (1, 3)}.items():
+
+            @pl.when(step == n)
+            def _(to_a=to_a, to_b=to_b):
+                outs[to_a][0, rows, :] = value[:, :half]
+                outs[to_b][0, rows, :] = value[:, half:]
+
+        return carry
+
+    lax.fori_loop(0, codes.shape[0] // step_rows, row_step, 0)
+
+
+def forward(message, decoder, first, columns, width):
+    groups, _, tok = message.shape
+    lat_rows = decoder.shape[1]
+    rows = groups * tok
+    scalars = jnp.concatenate([first[None], columns]).astype(jnp.int32)
+    part = jax.ShapeDtypeStruct((2, rows, width // 2), jnp.bfloat16)
+    block = (1, rows, width // 2)
+    return pl.pallas_call(
+        functools.partial(forward_kernel, groups, lat_rows // tok),
+        out_shape=[part] * 4,
+        grid_spec=pltpu.PrefetchScalarGridSpec(
+            num_scalar_prefetch=1,
+            grid=(4,),
+            in_specs=[
+                resident(message.shape),
+                pl.BlockSpec((1, lat_rows, width), lambda i, s: (0, 0, s[i + 1])),
+            ],
+            out_specs=[
+                pl.BlockSpec(block, lambda i, s: (jnp.where(i < 1, 1, 0), 0, 0)),
+                pl.BlockSpec(block, lambda i, s: (jnp.where(i < 3, 1, 0), 0, 0)),
+                pl.BlockSpec(block, lambda i, s: (jnp.where(i < 2, 1, 0), 0, 0)),
+                pl.BlockSpec(block, lambda i, s: (jnp.where(i < 3, 1, 0), 0, 0)),
+            ],
+            scratch_shapes=[
+                pltpu.VMEM((rows, lat_rows), jnp.bfloat16),
+                pltpu.VMEM((groups, 2 * tok, tok), jnp.bfloat16),
+                pltpu.VMEM((groups, 2 * tok, tok), jnp.bfloat16),
+            ],
+        ),
+        compiler_params=params(),
+        cost_estimate=cost(rows, lat_rows, 4 * width),
+        name="forward",
+    )(scalars, message, decoder)
+
+
+def layer_sum_kernel(got_a, kept_a, far_a, got_b, kept_b, far_b, sent_ref, held_ref):
+    half = got_a.shape[2]
+    rows = sent_ref.shape[1]
+    for side, (got, kept, far) in enumerate(((got_a, kept_a, far_a), (got_b, kept_b, far_b))):
+        lanes = slice(side * half, (side + 1) * half)
+        for n in range(2 * sent_ref.shape[0]):
+            at = slice(n * rows, (n + 1) * rows)
+            total = got[0, at, :].astype(jnp.float32) + kept[0, at, :].astype(jnp.float32)
+            total = total + far[0, at, :].astype(jnp.float32)
+            if n % 2:
+                sent_ref[n // 2, :, lanes] = total.astype(jnp.bfloat16)
+            else:
+                held_ref[n // 2, :, lanes] = total
+
+
+def layer_sum(terms_a, terms_b, blocks):
+    _, rows, half = terms_a[0].shape
+    cut = (blocks // 2, rows // blocks, 2 * half)
+    return pl.pallas_call(
+        layer_sum_kernel,
+        out_shape=[jax.ShapeDtypeStruct(cut, jnp.bfloat16), jax.ShapeDtypeStruct(cut, jnp.float32)],
+        grid=(1,),
+        in_specs=[
+            pl.BlockSpec((1, rows, half), lambda i: (0, 0, 0)) for _ in range(6)
+        ],
+        out_specs=[pl.BlockSpec(cut, lambda i: (0, 0, 0))] * 2,
+        compiler_params=params(),
+        cost_estimate=cost(rows, 4, half),
+        name="layer_sum",
+    )(*terms_a, *terms_b)
+
+
+def spread_into(target, ids_ref, rows_refs, first, size):
+    low = ids_ref.shape[1]
+
+    def build(b, carry):
+        at = pl.multiple_of(b * size, size)
+        block = (first + b).astype(jnp.float32).astype(jnp.bfloat16)
+        here = [ids_ref[j] == block for j in range(2)]
+        for n in range(size // low):
+            rows = slice(n * low, (n + 1) * low)
+            value = jnp.where(here[1], rows_refs[1][rows, :], jnp.zeros((), jnp.bfloat16))
+            target[pl.ds(at + n * low, low), :] = jnp.where(here[0], rows_refs[0][rows, :], value)
+        return carry
+
+    lax.fori_loop(0, target.shape[0] // size, build, 0)
+
+
+def lanes_of(refs):
+    return refs[0][...] if len(refs) == 1 else jnp.concatenate([r[...] for r in refs], axis=1)
+
+
+def code_grad_kernel(size, shape, scalar_ref, ids_ref, *refs):
+    grad_ref = refs[-1]
+    weights, pieces = refs[:len(shape)], refs[len(shape):-1]
+
+    @pl.when(pl.program_id(0) == 0)
+    def _():
+        grad_ref[...] = jnp.zeros_like(grad_ref)
+
+    weight = jnp.concatenate([w[0] for w in weights], axis=1)
+    grad = lax.dot_general(
+        weight, lanes_of(pieces), (((1,), (1,)), ((), ())), preferred_element_type=jnp.float32
+    )
+    several = weight.shape[0] // size
+    add0, add1 = 0.0, 0.0
+    for n in range(several):
+        block = (scalar_ref[0] + pl.program_id(0) * several + n).astype(jnp.float32)
+        part = grad[n * size:(n + 1) * size]
+        add0 = jnp.where(ids_ref[0:1] == block, part, add0)
+        add1 = jnp.where(ids_ref[1:2] == block, part, add1)
+    grad_ref[0] += add0
+    grad_ref[1] += add1
+
+
+def code_grad(pieces, ids, decoder, first, columns, size):
+    lat_rows = decoder.shape[1]
+    tokens = pieces[0][0].shape[0]
+    width = sum(p.shape[1] for p in pieces[0])
+    scalars = jnp.concatenate([first[None], columns]).astype(jnp.int32)
+    flat = [p for piece in pieces for p in piece]
+    several = 4 * size if lat_rows % (4 * size) == 0 else size
+    return pl.pallas_call(
+        functools.partial(code_grad_kernel, size, [len(p) for p in pieces]),
+        out_shape=jax.ShapeDtypeStruct((2, size, tokens), jnp.float32),
+        grid_spec=pltpu.PrefetchScalarGridSpec(
+            num_scalar_prefetch=1,
+            grid=(lat_rows // several,),
+            in_specs=[resident(ids.shape)]
+            + [pl.BlockSpec((1, several, width), lambda i, s, n=n: (0, i, s[n + 1])) for n in range(len(pieces))]
+            + [resident(p.shape) for p in flat],
+            out_specs=resident((2, size, tokens)),
+        ),
+        compiler_params=params(),
+        cost_estimate=cost(lat_rows, len(pieces) * width, tokens),
+        name="code_grad",
+    )(scalars, ids, *[decoder] * len(pieces), *flat)
+
+
+def decoder_kernel(size, shape, skip, scalar_ref, ids_ref, codes_ref, *refs):
+    refs = refs[skip:]
+    pieces, (out_ref, now, codes) = refs[:-3], refs[-3:]
+    at = 0
+    for i, count in enumerate(shape):
+
+        @pl.when(pl.program_id(0) == i)
+        def _(at=at, count=count):
+            now[...] = lanes_of(pieces[at:at + count])
+
+        at += count
+
+    @pl.when(pl.program_id(0) == 0)
+    def _():
+        spread_into(codes, ids_ref, [codes_ref.at[0], codes_ref.at[1]], scalar_ref[0], size)
+
+    several = 8 * size if codes.shape[0] % (8 * size) == 0 else size
+
+    def step(i, carry):
+        rows = pl.ds(pl.multiple_of(i * several, several), several)
+        out_ref[rows, :] = jnp.dot(codes[rows, :], now[...], preferred_element_type=jnp.float32).astype(jnp.bfloat16)
+        return carry
+
+    lax.fori_loop(0, codes.shape[0] // several, step, 0)
+
+
+def decoder_part(pieces, ids, code_lanes, first, columns, lat_rows, half, held):
+    _, size, tokens = code_lanes.shape
+    width = sum(p.shape[1] for p in pieces[0])
+    scalars = jnp.concatenate([first[None], columns]).astype(jnp.int32)
+    flat = [p for piece in pieces for p in piece]
+    onto = [] if held is None else [held]
+    return pl.pallas_call(
+        functools.partial(decoder_kernel, size, [len(p) for p in pieces], len(onto)),
+        out_shape=jax.ShapeDtypeStruct((lat_rows, half), jnp.bfloat16),
+        grid_spec=pltpu.PrefetchScalarGridSpec(
+            num_scalar_prefetch=1,
+            grid=(len(pieces),),
+            in_specs=[resident(ids.shape), resident(code_lanes.shape)]
+            + [pl.BlockSpec(memory_space=pl.ANY) for _ in onto]
+            + [resident(p.shape) for p in flat],
+            out_specs=pl.BlockSpec((lat_rows, width), lambda i, s: (0, s[i + 1])),
+            scratch_shapes=[
+                pltpu.VMEM((tokens, width), jnp.bfloat16),
+                pltpu.VMEM((lat_rows, tokens), jnp.bfloat16),
+            ],
+        ),
+        compiler_params=params(),
+        input_output_aliases={3: 0} if onto else {},
+        cost_estimate=cost(lat_rows, tokens, len(pieces) * width),
+        name="decoder_part",
+    )(scalars, ids, code_lanes, *onto, *flat)
+
+
+def pre_grad_kernel(size, tok, scalar_ref, ids_ref, pre_ref, own_ref, theirs_ref, out_ref, rows):
+    for j in range(2):
+        for at in range(0, pre_ref.shape[2], 2 * tok):
+            for core in range(2):
+                here = slice(at + core * tok, at + (core + 1) * tok)
+                there = slice(at + (1 - core) * tok, at + (2 - core) * tok)
+                total = own_ref[j, :, here] + theirs_ref[j, :, there]
+                rows[j, :, here] = jnp.where(pre_ref[j, :, here].astype(jnp.float32) > 0, total, 0.0).astype(jnp.bfloat16)
+    spread_into(out_ref, ids_ref, [rows.at[0], rows.at[1]], scalar_ref[0], size)
+
+
+def pre_grad_spread(own, theirs, ids, pre_lanes, first, lat_rows, tok):
+    _, size, tokens = pre_lanes.shape
+    scalars = first[None].astype(jnp.int32)
+    return pl.pallas_call(
+        functools.partial(pre_grad_kernel, size, tok),
+        out_shape=jax.ShapeDtypeStruct((lat_rows, tokens), jnp.bfloat16),
+        grid_spec=pltpu.PrefetchScalarGridSpec(
+            num_scalar_prefetch=1,
+            grid=(1,),
+            in_specs=[resident(ids.shape)] + [resident(pre_lanes.shape)] * 3,
+            out_specs=resident((lat_rows, tokens)),
+            scratch_shapes=[pltpu.VMEM((2, size, tokens), jnp.bfloat16)],
+        ),
+        compiler_params=params(),
+        cost_estimate=cost(lat_rows, 2, tokens),
+        name="pre_grad_spread",
+    )(scalars, ids, pre_lanes, own, theirs)
+
+
+def dense_plan(pre_codes, block_ids, activations, target, decoder):
+    lay_count = lax.axis_size("layer")
+    lat_count = lax.axis_size("latent")
+    dp_count = lax.axis_size("dp")
+    lay_here = lax.axis_index("layer")
+    lat_here = lax.axis_index("latent")
+    dp_here = lax.axis_index("dp")
+    tok_count = activations.shape[1]
+    model_width = activations.shape[2]
+    active_count = block_ids.shape[2]
+    block_size = pre_codes.shape[3]
+    lat_rows = decoder.shape[1]
+    local_blocks = lat_rows // block_size
+    half = model_width // dp_count
+    group = dp_count * tok_count
+    tokens = lat_count * group
+    width = half // (PAIRS * lay_count)
+    side = width // 2
+    f32, bf16 = jnp.float32, jnp.bfloat16
+    first = lat_here * local_blocks
+
+    def columns(rows, which):
+        return lax.dynamic_slice_in_dim(rows, which * half, half, axis=1)
+
+    pre_rows = jnp.swapaxes(pre_codes[0], 0, 1).reshape(active_count * tok_count, block_size)
+    id_rows = jnp.pad(block_ids[0].T, ((0, 16 - active_count), (0, 0))).astype(bf16)
+    own = jnp.concatenate([pre_rows, id_rows], axis=0)
+    message = jnp.stack([own] + [flip(own, "latent", r) for r in range(1, lat_count)])
+
+    acts = jnp.concatenate(
+        [columns(activations[0], dp_here), flip(columns(activations[0], 1 - dp_here), "dp", 1)]
+    )
+    up, down = [acts], [acts]
+
+    def next_hops():
+        step = len(up)
+        up.append(hop(up[-1], "latent", 1, step - 1))
+        down.append(hop(down[-1], "latent", -1, step - 1))
+
+    next_hops()
+    message = jnp.stack([message, flip(message, "dp", 1)], axis=1)
+    message = message.reshape(lat_count * dp_count, own.shape[0], block_size)
+
+    goal = target.reshape(tok_count, dp_count, PAIRS, lay_count, width)
+
+    def goal_of(which):
+        cut = lax.dynamic_index_in_dim(goal, which, 1, False)
+        return lax.dynamic_index_in_dim(cut, lay_here, 2, False)
+
+    goals = jnp.concatenate([goal_of(dp_here), flip(goal_of(1 - dp_here), "dp", 1)])
+
+    def places(pair, names, offset):
+        return jnp.stack([offset + pair * lay_count + (lay_here ^ r) for r in names])
+
+    def weight_places(pair, names):
+        return places(pair, names, dp_here * (half // width))
+
+    parts = [forward(message, decoder, first, weight_places(p, (3, 1, 2, 0)), width) for p in range(PAIRS)]
+    got = [(flip(parts[p][0], "layer", 1), flip(parts[p][2], "layer", 2)) for p in range(PAIRS)]
+    up[1], down[1], got[0] = lax.optimization_barrier((up[1], down[1], got[0]))
+
+    def add(one, two):
+        return (one.astype(f32) + two.astype(f32)).astype(bf16)
+
+    lat_bits = [1 << i for i in range(lat_count.bit_length() - 1)]
+    own_errors = []
+    for p in range(PAIRS):
+        kept = parts[p][1], parts[p][3]
+        far = [flip(add(got[p][n][1:], kept[n][1:]), "layer", 2 - n) for n in range(2)]
+        sent, held = layer_sum((got[p][0], kept[0], far[0]), (got[p][1], kept[1], far[1]), lat_count)
+        near = flip(sent, "latent", 1)
+        terms = [held, near]
+        for bit in lat_bits[1:]:
+            cut = [t.reshape((-1, 2) + t.shape[1:]) for t in terms]
+            out = sum(c[:, 1].astype(f32) for c in cut).astype(bf16)
+            terms = [c[:, 0] for c in cut] + [flip(out, "latent", bit)]
+        total = sum(t[0].astype(f32) for t in terms)
+        own_errors.append(((total - goals[:, p].astype(f32)) / tok_count).astype(bf16))
+
+    if lat_count > 2:
+        up[1], down[1], own_errors[-1] = lax.optimization_barrier((up[1], down[1], own_errors[-1]))
+    while len(up) < lat_count:
+        next_hops()
+
+    pieces = []
+    for p in range(PAIRS):
+        rows = own_errors[p][None]
+        for bit in lat_bits[:0:-1]:
+            rows = jnp.stack([rows, flip(rows, "latent", bit)], axis=1).reshape((-1,) + rows.shape[1:])
+        rows = jnp.stack([rows, flip(rows, "latent", 1)], axis=1).reshape(tokens, width)
+        one, two = flip(rows, "layer", 1), flip(rows, "layer", 2)
+        three = (flip(two[:, :side], "layer", 1), flip(one[:, side:], "layer", 2))
+        pieces.append([(rows,), (one,), (two,), three])
+
+    cut = message.reshape(tokens // tok_count, own.shape[0], block_size)
+    pre_lanes = cut[:, :active_count * tok_count].reshape(-1, active_count, tok_count, block_size)
+    pre_lanes = jnp.transpose(pre_lanes, (1, 3, 0, 2)).reshape(active_count, block_size, tokens)
+    code_lanes = jnp.maximum(pre_lanes, jnp.zeros((), bf16))
+    ids = cut[:, active_count * tok_count:active_count * tok_count + active_count]
+    ids = jnp.swapaxes(ids, 0, 1).reshape(active_count, tokens)
+    ids_wide = jnp.broadcast_to(ids[:, None, :], (active_count, 16, tokens))
+    ids = ids.astype(f32)
+
+    grads = []
+    dec = None
+    for p in range(PAIRS):
+        for names in ((0, 1, 2, 3),) if p < PAIRS - 1 else ((0, 1, 2), (3,)):
+            here = [pieces[p][r] for r in names]
+            grads.append(code_grad(here, ids, decoder, first, weight_places(p, names), block_size))
+            dec = decoder_part(here, ids_wide, code_lanes, first, places(p, names, 0), lat_rows, half, dec)
+    grad = sum(grads)
+    pre_grad = pre_grad_spread(grad, flip(grad, "dp", 1), ids_wide, pre_lanes, first, lat_rows, tok_count)
+    along = [acts] + [down[k] + up[lat_count - k] for k in range(1, lat_count)]
+    along = jnp.stack(along)
+    along = [lax.dynamic_index_in_dim(along, lax.rem((lat_here ^ r) - lat_here + lat_count, lat_count), 0, False) for r in range(lat_count)]
+    enc = jnp.dot(pre_grad, jnp.concatenate(along), preferred_element_type=f32).astype(bf16)
+    return dec[None], enc[None]
+
+
+def per_device(pre_codes, block_ids, activations, target, decoder):
+    lat_count = lax.axis_size("latent")
+    lay_count = lax.axis_size("layer")
+    dp_count = lax.axis_size("dp")
+    tok_count = activations.shape[1]
+    model_width = activations.shape[2]
+    active_count = block_ids.shape[2]
+    block_size = pre_codes.shape[3]
+    all_blocks = decoder.shape[1] // block_size * lat_count
+    slots = 2 * tok_count * active_count // lat_count
+    dense = (
+        slots >= tok_count
+        and dp_count == 2
+        and active_count == 2
+        and lay_count == 4
+        and lat_count > 1
+        and lat_count & (lat_count - 1) == 0
+        and tok_count == block_size
+        and lat_count * dp_count * 16 <= tok_count
+        and model_width % (dp_count * 2 * PAIRS * lay_count * 128) == 0
+        and all_blocks <= 256
+    )
+    plan = dense_plan if dense else slot_plan
+    return plan(pre_codes, block_ids, activations, target, decoder)
+
+
 def solution(mesh):
     placed = (
         P("layer", ("latent", "dp"), None, None),

time: 457 us -> 223 us (0.49)
  waiting for transfers between devices: 324 us -> 81 us
  Pallas kernels: 0 us -> 62 us
  matrix products: 68.4 us -> 10.8 us
  starting transfers between devices: 15 us -> 41.1 us
  between operations: 13.8 us -> 1.1 us
  local copies, waits for them, and re-layouts: 3.44 us -> 14.2 us
  other arithmetic: 21.1 us -> 10.5 us
  blocking collectives: 10 us -> 0 us
    all_to_all x3 -> x0, waiting for transfers between devices: 193 us -> none  [the longest x1 92.6 us: per_device(): lax.all_to_all(error_slots, 'latent', split_axis=0, concat_axis=0, tiled=...]
    ppermute x0 -> x37, waiting for transfers between devices: none -> 81 us  [the longest x31 81 us: flip(): return lax.ppermute(value, axis, [(i, i ^ bit) for i in range(count)])]
    psum x1 -> x0, waiting for transfers between devices: 72 us -> none  [per_device(): rebuilt = lax.psum(part_sum, 'layer')]
    pallas_call x0 -> x11, Pallas kernels: none -> 62 us  [the longest x2 22.4 us: forward(): pl.pallas_call(functools.partial(forward_kernel, groups, lat_rows // tok)...]
    reduce_scatter x2 -> x0, waiting for transfers between devices: 59.1 us -> none  [the longest x1 39.7 us: per_device(): lax.psum_scatter(dec_term, 'dp', scatter_dimension=1, tiled=True)]
    dot_general x7 -> x1, matrix products: 68.4 us -> 10.8 us  [dense_plan(): jnp.dot(pre_grad, jnp.concatenate(along), preferred_element_type=f32)]
    ppermute x0 -> x37, starting transfers between devices: none -> 41.1 us  [the longest x31 30.3 us: flip(): return lax.ppermute(value, axis, [(i, i ^ bit) for i in range(count)])]
    broadcast_in_dim x2 -> x0, other arithmetic: 18.2 us -> none  [the longest x1 9.15 us: per_device(): dec_half.astype(jnp.bfloat16)[None]]
  transfers between devices with their start and end apart: 6 -> 37, of which waited for: 6 -> 16; matrix products, arithmetic and copies ran while one was open for 10% -> 9% of each run, Pallas kernels for 0% -> 28%
where the time goes in v2:
time: 223 us; the launch traced here: 221 us
  waiting for transfers between devices  81 us (36%)
  Pallas kernels  62 us (28%)
  starting transfers between devices  41.1 us (18%)
  local copies, waits for them, and re-layouts  14.2 us (6%)
  matrix products  10.8 us (5%)
  other arithmetic  10.5 us (5%)
    ppermute x31, waiting for transfers between devices, flip(): return lax.ppermute(value, axis, [(i, i ^ bit) for i in range(count)])  81 us
    ppermute x31, starting transfers between devices, flip(): return lax.ppermute(value, axis, [(i, i ^ bit) for i in range(count)])  30.3 us
    pallas_call x2, Pallas kernels, forward(): pl.pallas_call(functools.partial(forward_kernel, groups, lat_rows // tok)...  22.4 us
    pallas_call x3, Pallas kernels, decoder_part(): pl.pallas_call(functools.partial(decoder_kernel, size, [len(p) for p in p...  18.6 us
    pallas_call x3, Pallas kernels, code_grad(): pl.pallas_call(functools.partial(code_grad_kernel, size, [len(p) for p in...  17.8 us
    dot_general x1, matrix products, dense_plan(): jnp.dot(pre_grad, jnp.concatenate(along), preferred_element_type=f32)  10.8 us
    ppermute x6, starting transfers between devices, hop(): return lax.ppermute(value, axis, pairs)  10.7 us
    unnamed x27, local copies, waits for them, and re-layouts  6.75 us
  transfers between devices with their start and end apart: 37, of which 16 were waited for; matrix products, arithmetic and copies ran while one was open for 9% of the time, Pallas kernels for 28%

profile of v2, /device:TPU:1, one launch (start us, length us, event | category | flops | bytes accessed | tf_op | source)
XLA Modules:
  0.0 220.6 jit_solution(7529762816096553494)
XLA Ops:
  2.2 3.2 %collective-permute-start.1 = (bf16[272,128]{1,0:T(8,128)(2,1)S(1)}, bf16[272,128]{1,0:T(8,128)(2,1)S(1)}, u32[]{:S(2)}, u32[]{:S(2)}) collective-permute-start(bf16[272,128]{1,0:T(8,128)(2,1)S(1)} %get-tuple-element.55), channel_id=1, source_target_pairs={{0,4},{2,6},{4,0},{6,2},{1,5},{3,7},{5,1},{7,3},{8,12},{10,14},{12... | collective-permute-start | bytes 208904 | tf_op jit(solution)/shard_map/ppermute | solution.py:104
  9.1 2.6 %collective-permute-done.2 = bf16[272,128]{1,0:T(8,128)(2,1)S(1)} collective-permute-done((bf16[272,128]{1,0:T(8,128)(2,1)S(1)}, bf16[272,128]{1,0:T(8,128)(2,1)S(1)}, u32[]{:S(2)}, u32[]{:S(2)}) %collective-permute-start.2) | collective-permute-done | bytes 69664 | tf_op jit(solution)/shard_map/ppermute | solution.py:104
  16.3 11.1 %forward.3 = (bf16[2,1024,128]{2,1,0:T(8,128)(2,1)S(1)}, bf16[2,1024,128]{2,1,0:T(8,128)(2,1)S(1)}, bf16[2,1024,128]{2,1,0:T(8,128)(2,1)}, bf16[2,1024,128]{2,1,0:T(8,128)(2,1)S(1)}) custom-call(s32[5]{0:T(128)S(1)} %concatenate.44.scalar_ref, bf16[8,272,128]{2,1,0:T(8,128)(2,1)S(1)} %bitcast.137, bf16[1,2048,4096]{2,1,0:T(8,128)(2,1)} %refs_0_.5), custom_call_target="tpu_custom_call" | custom-call | flops 4294967296 | bytes 10485760 | tf_op jit(solution)/shard_map/forward/pallas_call | solution.py:195
  34.8 5.0 %collective-permute-start.5 = (bf16[256,2048]{1,0:T(8,128)(2,1)}, bf16[256,2048]{1,0:T(8,128)(2,1)}, u32[]{:S(2)}, u32[]{:S(2)}) collective-permute-start(bf16[256,2048]{1,0:T(8,128)(2,1)} %get-tuple-element.43), channel_id=1, source_target_pairs={{0,2},{2,4},{4,6},{1,3},{3,5},{5,7},{8,10},{10,12},{12,14},{9,11},... | collective-permute-start | bytes 3145736 | tf_op jit(solution)/shard_map/ppermute | solution.py:113
  42.5 11.3 %forward.2 = (bf16[2,1024,128]{2,1,0:T(8,128)(2,1)}, bf16[2,1024,128]{2,1,0:T(8,128)(2,1)S(1)}, bf16[2,1024,128]{2,1,0:T(8,128)(2,1)}, bf16[2,1024,128]{2,1,0:T(8,128)(2,1)S(1)}) custom-call(s32[5]{0:T(128)S(1)} %concatenate.42.scalar_ref, bf16[8,272,128]{2,1,0:T(8,128)(2,1)S(1)} %bitcast.138, bf16[1,2048,4096]{2,1,0:T(8,128)(2,1)} %refs_0_.5), custom_call_target="tpu_custom_call" | custom-call | flops 4294967296 | bytes 10485760 | tf_op jit(solution)/shard_map/forward/pallas_call | solution.py:195
  57.1 2.6 %reshape.184 = bf16[128,2,2,4,256]{4,3,2,1,0:T(4,128)(2,1)} reshape(bf16[128,4096]{1,0:T(8,128)(2,1)} %param.8) | data formatting | bytes 2097152 | tf_op jit(solution)/shard_map/reshape | solution.py:449
  61.5 10.1 %collective-permute-done.23.far_b = bf16[1,1024,128]{2,1,0:T(8,128)(2,1)} collective-permute-done((bf16[1,1024,128]{2,1,0:T(8,128)(2,1)}, bf16[1,1024,128]{2,1,0:T(8,128)(2,1)}, u32[]{:S(2)}, u32[]{:S(2)}) %collective-permute-start.23) | collective-permute-done | bytes 262176 | tf_op jit(solution)/shard_map/ppermute | solution.py:104
  71.7 2.4 %collective-permute-start.13 = (bf16[128,2,256]{2,0,1:T(8,128)(2,1)S(1)}, bf16[128,2,256]{2,0,1:T(8,128)(2,1)S(1)}, u32[]{:S(2)}, u32[]{:S(2)}) collective-permute-start(bf16[128,2,256]{2,0,1:T(8,128)(2,1)S(1)} %bitcast.170), channel_id=1, source_target_pairs={{0,1},{1,0},{2,3},{3,2},{4,5},{5,4},{6,7},{7,6},{8,9},{9,8},{10,11... | collective-permute-start | bytes 393224 | tf_op jit(solution)/shard_map/ppermute | solution.py:104
  80.1 5.2 %collective-permute-done.24 = bf16[2,256,256]{2,1,0:T(8,128)(2,1)S(1)} collective-permute-done((bf16[2,256,256]{2,1,0:T(8,128)(2,1)S(1)}, bf16[2,256,256]{2,1,0:T(8,128)(2,1)S(1)}, u32[]{:S(2)}, u32[]{:S(2)}) %collective-permute-start.24) | collective-permute-done | bytes 262176 | tf_op jit(solution)/shard_map/ppermute | solution.py:104
  89.8 4.7 %collective-permute-done.25 = bf16[1,256,256]{2,1,0:T(8,128)(2,1)S(1)} collective-permute-done((bf16[1,256,256]{2,1,0:T(8,128)(2,1)S(1)}, bf16[1,256,256]{2,1,0:T(8,128)(2,1)S(1)}, u32[]{:S(2)}, u32[]{:S(2)}) %collective-permute-start.25) | collective-permute-done | bytes 131104 | tf_op jit(solution)/shard_map/ppermute | solution.py:104
  94.8 7.2 %collective-permute-done.26 = bf16[1,256,256]{2,1,0:T(8,128)(2,1)S(1)} collective-permute-done((bf16[1,256,256]{2,1,0:T(8,128)(2,1)S(1)}, bf16[1,256,256]{2,1,0:T(8,128)(2,1)S(1)}, u32[]{:S(2)}, u32[]{:S(2)}) %collective-permute-start.26) | collective-permute-done | bytes 131104 | tf_op jit(solution)/shard_map/ppermute | solution.py:104
  106.0 7.2 %collective-permute-done.27 = bf16[2,256,256]{2,1,0:T(8,128)(2,1)} collective-permute-done((bf16[2,256,256]{2,1,0:T(8,128)(2,1)}, bf16[2,256,256]{2,1,0:T(8,128)(2,1)}, u32[]{:S(2)}, u32[]{:S(2)}) %collective-permute-start.27) | collective-permute-done | bytes 262176 | tf_op jit(solution)/shard_map/ppermute | solution.py:104
  114.8 24.5 %collective-permute-done.14 = bf16[1,256,256]{2,1,0:T(8,128)(2,1)S(1)} collective-permute-done((bf16[1,256,256]{2,1,0:T(8,128)(2,1)S(1)}, bf16[1,256,256]{2,1,0:T(8,128)(2,1)S(1)}, u32[]{:S(2)}, u32[]{:S(2)}) %collective-permute-start.14) | collective-permute-done | bytes 131104 | tf_op jit(solution)/shard_map/ppermute | solution.py:104
  140.3 2.6 %collective-permute-start.28 = (bf16[1024,256]{1,0:T(8,128)(2,1)S(1)}, bf16[1024,256]{1,0:T(8,128)(2,1)S(1)}, u32[]{:S(2)}, u32[]{:S(2)}) collective-permute-start(bf16[1024,256]{1,0:T(8,128)(2,1)S(1)} %bitcast.142), channel_id=1, source_target_pairs={{0,8},{8,0},{16,24},{24,16},{1,9},{9,1},{17,25},{25,17},{2,10},{10... | collective-permute-start | bytes 1572872 | tf_op jit(solution)/shard_map/ppermute | solution.py:104
  142.9 2.9 %collective-permute-done.15 = bf16[2,256,256]{2,1,0:T(8,128)(2,1)S(1)} collective-permute-done((bf16[2,256,256]{2,1,0:T(8,128)(2,1)S(1)}, bf16[2,256,256]{2,1,0:T(8,128)(2,1)S(1)}, u32[]{:S(2)}, u32[]{:S(2)}) %collective-permute-start.15) | collective-permute-done | bytes 262176 | tf_op jit(solution)/shard_map/ppermute | solution.py:104
  148.5 5.8 %collective-permute-done.28.refs_2_.refs_4_ = bf16[1024,256]{1,0:T(8,128)(2,1)S(1)} collective-permute-done((bf16[1024,256]{1,0:T(8,128)(2,1)S(1)}, bf16[1024,256]{1,0:T(8,128)(2,1)S(1)}, u32[]{:S(2)}, u32[]{:S(2)}) %collective-permute-start.28) | collective-permute-done | bytes 524320 | tf_op jit(solution)/shard_map/ppermute | solution.py:104
  155.5 6.2 %code_grad.4 = f32[2,128,1024]{2,1,0:T(8,128)S(1)} custom-call(s32[4]{0:T(128)S(1)} %get-tuple-element.59.scalar_ref, f32[2,1024]{1,0:T(2,128)S(1)} %get-tuple-element.46.ids_ref, bf16[1,2048,4096]{2,1,0:T(8,128)(2,1)} %refs_0_.5, bf16[1,2048,4096]{2,1,0:T(8,128)(2,1)} %refs_0_.5, bf16[1,2048,4096]{2,1,0:T(8,128)(2,1)} %refs_0_.5, ...), custom_call_target="tpu_custom_call" | custom-call | flops 3221225472 | bytes 8912896 | tf_op jit(solution)/shard_map/code_grad/pallas_call | solution.py:305
  167.1 4.1 %collective-permute-done.30.refs_1_ = bf16[1024,128]{1,0:T(8,128)(2,1)S(1)} collective-permute-done((bf16[1024,128]{1,0:T(8,128)(2,1)S(1)}, bf16[1024,128]{1,0:T(8,128)(2,1)S(1)}, u32[]{:S(2)}, u32[]{:S(2)}) %collective-permute-start.30) | collective-permute-done | bytes 262176 | tf_op jit(solution)/shard_map/ppermute | solution.py:104
  172.1 4.2 %code_grad.5 = f32[2,128,1024]{2,1,0:T(8,128)S(1)} custom-call(s32[2]{0:T(128)S(1)} %get-tuple-element.57.scalar_ref, f32[2,1024]{1,0:T(2,128)S(1)} %get-tuple-element.46.ids_ref, bf16[1,2048,4096]{2,1,0:T(8,128)(2,1)} %refs_0_.5, bf16[1024,128]{1,0:T(8,128)(2,1)S(1)} %collective-permute-done.30.refs_1_, bf16[1024,128]{1,0:T(8,128)(2,1)S(1)} %collective-permute-done.31.refs_2_), custom_call_target="tpu_custom_call" | custom-call | flops 1073741824 | bytes 5767168 | tf_op jit(solution)/shard_map/code_grad/pallas_call | solution.py:305
  176.8 7.4 %code_grad.3 = f32[2,128,1024]{2,1,0:T(8,128)S(1)} custom-call(s32[5]{0:T(128)S(1)} %concatenate.45.scalar_ref, f32[2,1024]{1,0:T(2,128)S(1)} %get-tuple-element.46.ids_ref, bf16[1,2048,4096]{2,1,0:T(8,128)(2,1)} %refs_0_.5, bf16[1,2048,4096]{2,1,0:T(8,128)(2,1)} %refs_0_.5, bf16[1,2048,4096]{2,1,0:T(8,128)(2,1)} %refs_0_.5, bf16[1,2048,4096]{2,1,0:T(8,128)(2,1)} %refs_0_.5, ...), custom_call_target="tpu_custom_call" | custom-call | flops 4294967296 | bytes 10485760 | tf_op jit(solution)/shard_map/code_grad/pallas_call | solution.py:305
  186.6 8.2 %decoder_part.3.refs_0_ = bf16[2048,2048]{1,0:T(8,128)(2,1)} custom-call(s32[5]{0:T(128)S(1)} %concatenate.40.scalar_ref, bf16[2,16,1024]{2,1,0:T(8,128)(2,1)S(1)} %broadcast_in_dim.14.ids_ref, bf16[2,128,1024]{2,1,0:T(8,128)(2,1)S(1)} %broadcast_maximum_fusion.codes_ref, bf16[1024,256]{1,0:T(8,128)(2,1)S(1)} %bitcast.148, ...), custom_call_target="tpu_custom_call" | custom-call | flops 4294967296 | bytes 10485760 | tf_op jit(solution)/shard_map/decoder_part/pallas_call | solution.py:354
  194.8 6.7 %decoder_part.4.refs_0_ = bf16[2048,2048]{1,0:T(8,128)(2,1)} custom-call(s32[4]{0:T(128)S(1)} %get-tuple-element.58.scalar_ref, bf16[2,16,1024]{2,1,0:T(8,128)(2,1)S(1)} %broadcast_in_dim.14.ids_ref, bf16[2,128,1024]{2,1,0:T(8,128)(2,1)S(1)} %broadcast_maximum_fusion.codes_ref, ...), custom_call_target="tpu_custom_call", output_to_operand_aliasing={{}: (3, {})} | custom-call | flops 3221225472 | bytes 8912896 | tf_op jit(solution)/shard_map/decoder_part/pallas_call | solution.py:354
  201.6 3.7 %decoder_part.5 = bf16[2048,2048]{1,0:T(8,128)(2,1)} custom-call(s32[2]{0:T(128)S(1)} %get-tuple-element.56.scalar_ref, bf16[2,16,1024]{2,1,0:T(8,128)(2,1)S(1)} %broadcast_in_dim.14.ids_ref, bf16[2,128,1024]{2,1,0:T(8,128)(2,1)S(1)} %broadcast_maximum_fusion.codes_ref, bf16[2048,2048]{1,0:T(8,128)(2,1)} %decoder_part.4.refs_0_, ...), custom_call_target="tpu_custom_call", output_to_operand_aliasing={{}: (3, {})} | custom-call | flops 1073741824 | bytes 5767168 | tf_op jit(solution)/shard_map/decoder_part/pallas_call | solution.py:354
  209.8 10.8 %convert_bitcast_fusion = bf16[1,2048,2048]{2,1,0:T(8,128)(2,1)} fusion(bf16[2048,1024]{1,0:T(8,128)(2,1)S(1)} %pre_grad_spread.1, bf16[1024,2048]{1,0:T(8,128)(2,1)S(1)} %bitcast_dynamic-update-slice_fusion), kind=kOutput, calls=%fused_computation | convolution fusion | flops 8594128896 | bytes 16777216 | tf_op jit(solution)/shard_map/dot_general | solution.py:521
  (135 shorter events, 59.7 us)
Async XLA Ops:
  16.1 15.8 %collective-permute-start.4 = (bf16[128,2048]{1,0:T(8,128)(2,1)}, bf16[128,2048]{1,0:T(8,128)(2,1)S(1)}, u32[]{:S(2)}, u32[]{:S(2)}) collective-permute-start(bf16[128,2048]{1,0:T(8,128)(2,1)} %dynamic-slice_bitcast_fusion), channel_id=1, source_target_pairs={{0,1},{1,0},{2,3},{3,2},{4,5},{5,4},{6,7},{7,6},{8,9},{9,8},{10,11... | collective-permute-start | bytes 1572872 | tf_op jit(solution)/shard_map/ppermute | solution.py:104
  27.4 13.1 %collective-permute-start.20 = (bf16[2,1024,128]{2,1,0:T(8,128)(2,1)S(1)}, bf16[2,1024,128]{2,1,0:T(8,128)(2,1)S(1)}, u32[]{:S(2)}, u32[]{:S(2)}) collective-permute-start(bf16[2,1024,128]{2,1,0:T(8,128)(2,1)S(1)} %get-tuple-element.31), channel_id=1, source_target_pairs={{0,8},{8,0},{16,24},{24,16},{1,9},{9,1},{17,25},{25,17},{2,10},{10... | collective-permute-start | bytes 1572872 | tf_op jit(solution)/shard_map/ppermute | solution.py:104
  30.6 24.4 %collective-permute-start.22 = (bf16[2,1024,128]{2,1,0:T(8,128)(2,1)}, bf16[2,1024,128]{2,1,0:T(8,128)(2,1)S(1)}, u32[]{:S(2)}, u32[]{:S(2)}) collective-permute-start(bf16[2,1024,128]{2,1,0:T(8,128)(2,1)} %get-tuple-element.33), channel_id=1, source_target_pairs={{0,16},{8,24},{16,0},{24,8},{1,17},{9,25},{17,1},{25,9},{2,18},{10... | collective-permute-start | bytes 1572872 | tf_op jit(solution)/shard_map/ppermute | solution.py:104
  33.5 43.9 %collective-permute-start.6 = (bf16[256,2048]{1,0:T(8,128)(2,1)}, bf16[256,2048]{1,0:T(8,128)(2,1)}, u32[]{:S(2)}, u32[]{:S(2)}) collective-permute-start(bf16[256,2048]{1,0:T(8,128)(2,1)} %get-tuple-element.43), channel_id=1, source_target_pairs={{2,0},{4,2},{6,4},{3,1},{5,3},{7,5},{10,8},{12,10},{14,12},{11,9},... | collective-permute-start | bytes 3145736 | tf_op jit(solution)/shard_map/ppermute | solution.py:113
  34.8 42.6 %collective-permute-start.5 = (bf16[256,2048]{1,0:T(8,128)(2,1)}, bf16[256,2048]{1,0:T(8,128)(2,1)}, u32[]{:S(2)}, u32[]{:S(2)}) collective-permute-start(bf16[256,2048]{1,0:T(8,128)(2,1)} %get-tuple-element.43), channel_id=1, source_target_pairs={{0,2},{2,4},{4,6},{1,3},{3,5},{5,7},{8,10},{10,12},{12,14},{9,11},... | collective-permute-start | bytes 3145736 | tf_op jit(solution)/shard_map/ppermute | solution.py:113
  41.3 15.6 %collective-permute-start.21 = (bf16[1,1024,128]{2,1,0:T(8,128)(2,1)S(1)}, bf16[1,1024,128]{2,1,0:T(8,128)(2,1)S(1)}, u32[]{:S(2)}, u32[]{:S(2)}) collective-permute-start(bf16[1,1024,128]{2,1,0:T(8,128)(2,1)S(1)} %add_convert_fusion.1), channel_id=1, source_target_pairs={{0,16},{8,24},{16,0},{24,8},{1,17},{9,25},{17,1},{25,9},{2,18},{10... | collective-permute-start | bytes 786440 | tf_op jit(solution)/shard_map/ppermute | solution.py:104
  53.8 23.5 %collective-permute-start.7 = (bf16[2,1024,128]{2,1,0:T(8,128)(2,1)}, bf16[2,1024,128]{2,1,0:T(8,128)(2,1)S(1)}, u32[]{:S(2)}, u32[]{:S(2)}) collective-permute-start(bf16[2,1024,128]{2,1,0:T(8,128)(2,1)} %get-tuple-element.21), channel_id=1, source_target_pairs={{0,8},{8,0},{16,24},{24,16},{1,9},{9,1},{17,25},{25,17},{2,10},{10... | collective-permute-start | bytes 1572872 | tf_op jit(solution)/shard_map/ppermute | solution.py:104
  55.0 22.4 %collective-permute-start.8 = (bf16[2,1024,128]{2,1,0:T(8,128)(2,1)}, bf16[2,1024,128]{2,1,0:T(8,128)(2,1)}, u32[]{:S(2)}, u32[]{:S(2)}) collective-permute-start(bf16[2,1024,128]{2,1,0:T(8,128)(2,1)} %get-tuple-element.22), channel_id=1, source_target_pairs={{0,16},{8,24},{16,0},{24,8},{1,17},{9,25},{17,1},{25,9},{2,18},{10... | collective-permute-start | bytes 1572872 | tf_op jit(solution)/shard_map/ppermute | solution.py:104
  56.9 14.8 %collective-permute-start.23 = (bf16[1,1024,128]{2,1,0:T(8,128)(2,1)}, bf16[1,1024,128]{2,1,0:T(8,128)(2,1)}, u32[]{:S(2)}, u32[]{:S(2)}) collective-permute-start(bf16[1,1024,128]{2,1,0:T(8,128)(2,1)} %add_convert_fusion), channel_id=1, source_target_pairs={{0,8},{8,0},{16,24},{24,16},{1,9},{9,1},{17,25},{25,17},{2,10},{10... | collective-permute-start | bytes 786440 | tf_op jit(solution)/shard_map/ppermute | solution.py:104
  71.7 18.2 %collective-permute-start.13 = (bf16[128,2,256]{2,0,1:T(8,128)(2,1)S(1)}, bf16[128,2,256]{2,0,1:T(8,128)(2,1)S(1)}, u32[]{:S(2)}, u32[]{:S(2)}) collective-permute-start(bf16[128,2,256]{2,0,1:T(8,128)(2,1)S(1)} %bitcast.170), channel_id=1, source_target_pairs={{0,1},{1,0},{2,3},{3,2},{4,5},{5,4},{6,7},{7,6},{8,9},{9,8},{10,11... | collective-permute-start | bytes 393224 | tf_op jit(solution)/shard_map/ppermute | solution.py:104
  88.6 14.1 %collective-permute-start.11 = (bf16[2,256,256]{2,1,0:T(8,128)(2,1)S(1)}, bf16[2,256,256]{2,1,0:T(8,128)(2,1)S(1)}, u32[]{:S(2)}, u32[]{:S(2)}) collective-permute-start(bf16[2,256,256]{2,1,0:T(8,128)(2,1)S(1)} %get-tuple-element.28), channel_id=1, source_target_pairs={{0,2},{2,0},{4,6},{6,4},{1,3},{3,1},{5,7},{7,5},{8,10},{10,8},{12,... | collective-permute-start | bytes 786440 | tf_op jit(solution)/shard_map/ppermute | solution.py:104
  102.7 11.8 %collective-permute-start.12 = (bf16[1,256,256]{2,1,0:T(8,128)(2,1)S(1)}, bf16[1,256,256]{2,1,0:T(8,128)(2,1)S(1)}, u32[]{:S(2)}, u32[]{:S(2)}) collective-permute-start(bf16[1,256,256]{2,1,0:T(8,128)(2,1)S(1)} %fusion.20), channel_id=1, source_target_pairs={{0,4},{2,6},{4,0},{6,2},{1,5},{3,7},{5,1},{7,3},{8,12},{10,14},{12... | collective-permute-start | bytes 393224 | tf_op jit(solution)/shard_map/ppermute | solution.py:104
  103.7 58.1 %collective-permute-start.35 = (bf16[256,2048]{1,0:T(8,128)(2,1)}, bf16[256,2048]{1,0:T(8,128)(2,1)S(1)}, u32[]{:S(2)}, u32[]{:S(2)}) collective-permute-start(bf16[256,2048]{1,0:T(8,128)(2,1)} %collective-permute-done.6), channel_id=1, source_target_pairs={{2,0},{4,2},{3,1},{5,3},{10,8},{12,10},{11,9},{13,11},{18,16},{20,... | collective-permute-start | bytes 3145736 | tf_op jit(solution)/shard_map/ppermute | solution.py:113
  105.2 61.5 %collective-permute-start.33 = (bf16[256,2048]{1,0:T(8,128)(2,1)}, bf16[256,2048]{1,0:T(8,128)(2,1)S(1)}, u32[]{:S(2)}, u32[]{:S(2)}) collective-permute-start(bf16[256,2048]{1,0:T(8,128)(2,1)} %collective-permute-done.5), channel_id=1, source_target_pairs={{2,4},{4,6},{3,5},{5,7},{10,12},{12,14},{11,13},{13,15},{18,20},{2... | collective-permute-start | bytes 3145736 | tf_op jit(solution)/shard_map/ppermute | solution.py:113
  114.2 32.0 %collective-permute-start.29 = (bf16[1024,256]{1,0:T(8,128)(2,1)S(1)}, bf16[1024,256]{1,0:T(8,128)(2,1)S(1)}, u32[]{:S(2)}, u32[]{:S(2)}) collective-permute-start(bf16[1024,256]{1,0:T(8,128)(2,1)S(1)} %bitcast.141), channel_id=1, source_target_pairs={{0,16},{8,24},{16,0},{24,8},{1,17},{9,25},{17,1},{25,9},{2,18},{10... | collective-permute-start | bytes 1572872 | tf_op jit(solution)/shard_map/ppermute | solution.py:104
  114.7 24.6 %collective-permute-start.14 = (bf16[1,256,256]{2,1,0:T(8,128)(2,1)S(1)}, bf16[1,256,256]{2,1,0:T(8,128)(2,1)S(1)}, u32[]{:S(2)}, u32[]{:S(2)}) collective-permute-start(bf16[1,256,256]{2,1,0:T(8,128)(2,1)S(1)} %fusion.6), channel_id=1, source_target_pairs={{0,4},{2,6},{4,0},{6,2},{1,5},{3,7},{5,1},{7,3},{8,12},{10,14},{12... | collective-permute-start | bytes 393224 | tf_op jit(solution)/shard_map/ppermute | solution.py:104
  140.3 14.1 %collective-permute-start.28 = (bf16[1024,256]{1,0:T(8,128)(2,1)S(1)}, bf16[1024,256]{1,0:T(8,128)(2,1)S(1)}, u32[]{:S(2)}, u32[]{:S(2)}) collective-permute-start(bf16[1024,256]{1,0:T(8,128)(2,1)S(1)} %bitcast.142), channel_id=1, source_target_pairs={{0,8},{8,0},{16,24},{24,16},{1,9},{9,1},{17,25},{25,17},{2,10},{10... | collective-permute-start | bytes 1572872 | tf_op jit(solution)/shard_map/ppermute | solution.py:104
  145.9 16.1 %collective-permute-start.17 = (bf16[1024,256]{1,0:T(8,128)(2,1)S(1)}, bf16[1024,256]{1,0:T(8,128)(2,1)S(1)}, u32[]{:S(2)}, u32[]{:S(2)}) collective-permute-start(bf16[1024,256]{1,0:T(8,128)(2,1)S(1)} %bitcast.145), channel_id=1, source_target_pairs={{0,16},{8,24},{16,0},{24,8},{1,17},{9,25},{17,1},{25,9},{2,18},{10... | collective-permute-start | bytes 1572872 | tf_op jit(solution)/shard_map/ppermute | solution.py:104
  146.2 19.3 %collective-permute-start.16 = (bf16[1024,256]{1,0:T(8,128)(2,1)S(1)}, bf16[1024,256]{1,0:T(8,128)(2,1)S(1)}, u32[]{:S(2)}, u32[]{:S(2)}) collective-permute-start(bf16[1024,256]{1,0:T(8,128)(2,1)S(1)} %bitcast.146), channel_id=1, source_target_pairs={{0,8},{8,0},{16,24},{24,16},{1,9},{9,1},{17,25},{25,17},{2,10},{10... | collective-permute-start | bytes 1572872 | tf_op jit(solution)/shard_map/ppermute | solution.py:104
  154.3 16.9 %collective-permute-start.30 = (bf16[1024,128]{1,0:T(8,128)(2,1)S(1)}, bf16[1024,128]{1,0:T(8,128)(2,1)S(1)}, u32[]{:S(2)}, u32[]{:S(2)}) collective-permute-start(bf16[1024,128]{1,0:T(8,128)(2,1)S(1)} %slice.113), channel_id=1, source_target_pairs={{0,8},{8,0},{16,24},{24,16},{1,9},{9,1},{17,25},{25,17},{2,10},{10... | collective-permute-start | bytes 786440 | tf_op jit(solution)/shard_map/ppermute | solution.py:104
  162.0 43.2 %collective-permute-start.36 = (bf16[256,2048]{1,0:T(8,128)(2,1)S(1)}, bf16[256,2048]{1,0:T(8,128)(2,1)S(1)}, u32[]{:S(2)}, u32[]{:S(2)}) collective-permute-start(bf16[256,2048]{1,0:T(8,128)(2,1)S(1)} %collective-permute-done.35), channel_id=1, source_target_pairs={{2,0},{3,1},{10,8},{11,9},{18,16},{19,17},{26,24},{27,25}} | collective-permute-start | bytes 3145736 | tf_op jit(solution)/shard_map/ppermute | solution.py:113
  165.6 11.2 %collective-permute-start.18 = (bf16[1024,128]{1,0:T(8,128)(2,1)S(1)}, bf16[1024,128]{1,0:T(8,128)(2,1)S(1)}, u32[]{:S(2)}, u32[]{:S(2)}) collective-permute-start(bf16[1024,128]{1,0:T(8,128)(2,1)S(1)} %slice.105), channel_id=1, source_target_pairs={{0,8},{8,0},{16,24},{24,16},{1,9},{9,1},{17,25},{25,17},{2,10},{10... | collective-permute-start | bytes 786440 | tf_op jit(solution)/shard_map/ppermute | solution.py:104
  171.2 35.5 %collective-permute-start.34 = (bf16[256,2048]{1,0:T(8,128)(2,1)S(1)}, bf16[256,2048]{1,0:T(8,128)(2,1)S(1)}, u32[]{:S(2)}, u32[]{:S(2)}) collective-permute-start(bf16[256,2048]{1,0:T(8,128)(2,1)S(1)} %collective-permute-done.33), channel_id=1, source_target_pairs={{4,6},{5,7},{12,14},{13,15},{20,22},{21,23},{28,30},{29,31}} | collective-permute-start | bytes 3145736 | tf_op jit(solution)/shard_map/ppermute | solution.py:113
  184.6 24.4 %collective-permute-start.32 = (f32[2,128,1024]{2,1,0:T(8,128)S(1)}, f32[2,128,1024]{2,1,0:T(8,128)S(1)}, u32[]{:S(2)}, u32[]{:S(2)}) collective-permute-start(f32[2,128,1024]{2,1,0:T(8,128)S(1)} %add_add_fusion.own_ref), channel_id=1, source_target_pairs={{0,1},{1,0},{2,3},{3,2},{4,5},{5,4},{6,7},{7,6},{8,9},{9,8},{10,11... | collective-permute-start | bytes 3145736 | tf_op jit(solution)/shard_map/ppermute | solution.py:104
  (23 other events, 225.3 us)

commit v3 on v2

--- a/solution.py
+++ b/solution.py
@@ -123,8 +123,8 @@
 
 def cost(rows, depth, columns):
     return pl.CostEstimate(
-        flops=2 * rows * depth * columns,
-        bytes_accessed=2 * (rows * depth + depth * columns + rows * columns),
+        flops=rows * depth * columns // 2,
+        bytes_accessed=(rows * depth + depth * columns + rows * columns) // 2,
         transcendentals=0,
     )
 
@@ -133,102 +133,88 @@
     return pl.BlockSpec(shape, lambda i, s: (0,) * len(shape))
 
 
-def forward_kernel(groups, blocks, scalar_ref, message_ref, weight_ref, *refs):
-    outs, (codes, id_map, pre) = refs[:4], refs[4:]
+def gather_kernel(scalar_ref, source_ref, out_ref):
+    out_ref[...] = source_ref[...].reshape(out_ref.shape)
+
+
+def gather_columns(source, columns, width):
+    rows = source.shape[-2]
+    lead = (1,) * (source.ndim - 2)
+    count = columns.shape[0]
+    return pl.pallas_call(
+        gather_kernel,
+        out_shape=jax.ShapeDtypeStruct((rows, count * width), source.dtype),
+        grid_spec=pltpu.PrefetchScalarGridSpec(
+            num_scalar_prefetch=1,
+            grid=(count,),
+            in_specs=[pl.BlockSpec(lead + (rows, width), lambda i, s: (0,) * len(lead) + (0, s[i]))],
+            out_specs=pl.BlockSpec((rows, width), lambda i, s: (0, i)),
+        ),
+        compiler_params=params(),
+        cost_estimate=cost(rows, 1, count * width),
+        name="gather_columns",
+    )(columns.astype(jnp.int32), source)
+
+
+def codes_kernel(groups, blocks, scalar_ref, message_ref, codes, id_map, pre):
     tok = message_ref.shape[2]
     pad = message_ref.shape[1] - 2 * tok
-    half = outs[0].shape[2]
-    step = pl.program_id(0)
-
-    @pl.when(step == 0)
-    def _():
-        first = scalar_ref[0].astype(jnp.float32)
-        rows = [message_ref[g, 2 * tok:2 * tok + pad, :].astype(jnp.float32) for g in range(groups)]
-        fill = tok - groups * pad
-        if fill:
-            rows.append(jnp.zeros((fill, tok), jnp.float32))
-        table = jnp.concatenate(rows, axis=0).T - first
+    first = scalar_ref[0].astype(jnp.float32)
+    rows = [message_ref[g, 2 * tok:2 * tok + pad, :].astype(jnp.float32) for g in range(groups)]
+    fill = tok - groups * pad
+    if fill:
+        rows.append(jnp.zeros((fill, tok), jnp.float32))
+    table = jnp.concatenate(rows, axis=0).T - first
+    for g in range(groups):
+        pre[g] = jnp.maximum(message_ref[g, 0:2 * tok, :], jnp.zeros((), jnp.bfloat16))
+        for j in range(2):
+            at = g * pad + j
+            wide = jnp.broadcast_to(table[:, at:at + 1], (tok, tok))
+            id_map[g, j * tok:(j + 1) * tok, :] = wide.astype(jnp.bfloat16)
+
+    def block_step(b, carry):
+        block = b.astype(jnp.float32).astype(jnp.bfloat16)
+        at = pl.multiple_of(b * tok, tok)
         for g in range(groups):
-            pre[g] = jnp.maximum(message_ref[g, 0:2 * tok, :], jnp.zeros((), jnp.bfloat16))
-            for j in range(2):
-                at = g * pad + j
-                wide = jnp.broadcast_to(table[:, at:at + 1], (tok, tok))
-                id_map[g, j * tok:(j + 1) * tok, :] = wide.astype(jnp.bfloat16)
-
-        def block_step(b, carry):
-            block = b.astype(jnp.float32).astype(jnp.bfloat16)
-            at = pl.multiple_of(b * tok, tok)
-            for g in range(groups):
-                value = jnp.where(id_map[g, tok:2 * tok, :] == block, pre[g, tok:2 * tok, :], jnp.zeros((), jnp.bfloat16))
-                value = jnp.where(id_map[g, 0:tok, :] == block, pre[g, 0:tok, :], value)
-                codes[g * tok:(g + 1) * tok, pl.ds(at, tok)] = value
-            return carry
-
-        lax.fori_loop(0, blocks, block_step, 0)
-
-    step_rows = 4 * tok if codes.shape[0] % (4 * tok) == 0 else tok
-    stores = {0: (0, 2), 1: (0, 3), 2: (1, 2), 3: (1, 3)}
-
-    def row_step(i, carry):
-        at = pl.multiple_of(i * step_rows, step_rows)
-        rows = pl.ds(at, step_rows)
-        value = jnp.dot(codes[rows, :], weight_ref[0], preferred_element_type=jnp.float32).astype(jnp.bfloat16)
-        for n, (to_a, to_b) in {0: (0, 2), 1: (0, 3), 2: (1, 2), 3: (1, 3)}.items():
-
-            @pl.when(step == n)
-            def _(to_a=to_a, to_b=to_b):
-                outs[to_a][0, rows, :] = value[:, :half]
-                outs[to_b][0, rows, :] = value[:, half:]
-
+            value = jnp.where(id_map[g, tok:2 * tok, :] == block, pre[g, tok:2 * tok, :], jnp.zeros((), jnp.bfloat16))
+            value = jnp.where(id_map[g, 0:tok, :] == block, pre[g, 0:tok, :], value)
+            codes[g * tok:(g + 1) * tok, pl.ds(at, tok)] = value
         return carry
 
-    lax.fori_loop(0, codes.shape[0] // step_rows, row_step, 0)
-
-
-def forward(message, decoder, first, columns, width):
+    lax.fori_loop(0, blocks, block_step, 0)
+
+
+def spread_codes(message, first, lat_rows):
     groups, _, tok = message.shape
-    lat_rows = decoder.shape[1]
     rows = groups * tok
-    scalars = jnp.concatenate([first[None], columns]).astype(jnp.int32)
-    part = jax.ShapeDtypeStruct((2, rows, width // 2), jnp.bfloat16)
-    block = (1, rows, width // 2)
     return pl.pallas_call(
-        functools.partial(forward_kernel, groups, lat_rows // tok),
-        out_shape=[part] * 4,
+        functools.partial(codes_kernel, groups, lat_rows // tok),
+        out_shape=jax.ShapeDtypeStruct((rows, lat_rows), jnp.bfloat16),
         grid_spec=pltpu.PrefetchScalarGridSpec(
             num_scalar_prefetch=1,
-            grid=(4,),
-            in_specs=[
-                resident(message.shape),
-                pl.BlockSpec((1, lat_rows, width), lambda i, s: (0, 0, s[i + 1])),
-            ],
-            out_specs=[
-                pl.BlockSpec(block, lambda i, s: (jnp.where(i < 1, 1, 0), 0, 0)),
-                pl.BlockSpec(block, lambda i, s: (jnp.where(i < 3, 1, 0), 0, 0)),
-                pl.BlockSpec(block, lambda i, s: (jnp.where(i < 2, 1, 0), 0, 0)),
-                pl.BlockSpec(block, lambda i, s: (jnp.where(i < 3, 1, 0), 0, 0)),
-            ],
+            grid=(1,),
+            in_specs=[resident(message.shape)],
+            out_specs=resident((rows, lat_rows)),
             scratch_shapes=[
-                pltpu.VMEM((rows, lat_rows), jnp.bfloat16),
                 pltpu.VMEM((groups, 2 * tok, tok), jnp.bfloat16),
                 pltpu.VMEM((groups, 2 * tok, tok), jnp.bfloat16),
             ],
         ),
         compiler_params=params(),
-        cost_estimate=cost(rows, lat_rows, 4 * width),
-        name="forward",
-    )(scalars, message, decoder)
+        cost_estimate=cost(rows, 1, lat_rows),
+        name="spread_codes",
+    )(first[None].astype(jnp.int32), message)
 
 
 def layer_sum_kernel(got_a, kept_a, far_a, got_b, kept_b, far_b, sent_ref, held_ref):
-    half = got_a.shape[2]
+    half = far_a.shape[1]
     rows = sent_ref.shape[1]
     for side, (got, kept, far) in enumerate(((got_a, kept_a, far_a), (got_b, kept_b, far_b))):
         lanes = slice(side * half, (side + 1) * half)
         for n in range(2 * sent_ref.shape[0]):
             at = slice(n * rows, (n + 1) * rows)
-            total = got[0, at, :].astype(jnp.float32) + kept[0, at, :].astype(jnp.float32)
-            total = total + far[0, at, :].astype(jnp.float32)
+            total = got[at, :half].astype(jnp.float32) + kept[at, :half].astype(jnp.float32)
+            total = total + far[at, :].astype(jnp.float32)
             if n % 2:
                 sent_ref[n // 2, :, lanes] = total.astype(jnp.bfloat16)
             else:
@@ -236,15 +222,13 @@
 
 
 def layer_sum(terms_a, terms_b, blocks):
-    _, rows, half = terms_a[0].shape
+    rows, half = terms_a[2].shape
     cut = (blocks // 2, rows // blocks, 2 * half)
     return pl.pallas_call(
         layer_sum_kernel,
         out_shape=[jax.ShapeDtypeStruct(cut, jnp.bfloat16), jax.ShapeDtypeStruct(cut, jnp.float32)],
         grid=(1,),
-        in_specs=[
-            pl.BlockSpec((1, rows, half), lambda i: (0, 0, 0)) for _ in range(6)
-        ],
+        in_specs=[pl.BlockSpec((rows, half), lambda i: (0, 0)) for _ in range(6)],
         out_specs=[pl.BlockSpec(cut, lambda i: (0, 0, 0))] * 2,
         compiler_params=params(),
         cost_estimate=cost(rows, 4, half),
@@ -442,36 +426,54 @@
         up.append(hop(up[-1], "latent", 1, step - 1))
         down.append(hop(down[-1], "latent", -1, step - 1))
 
-    next_hops()
+    def places(pair, names, offset, fine=1, sub=0):
+        return [(offset + pair * lay_count + (lay_here ^ r)) * fine + sub for r in names]
+
+    def weight_places(pair, names):
+        return jnp.stack(places(pair, names, dp_here * (half // width)))
+
+    wanted = [((1, 3), 0), ((2, 3), 1), ((0, 2), 0), ((0, 1), 1)]
+    at = [
+        c for p in range(PAIRS) for names, n in wanted for c in places(p, names, dp_here * (half // width), 2, n)
+    ]
+    weights = gather_columns(decoder, jnp.stack(at), side)
+    goal_at = [which * (half // width) + p * lay_count + lay_here for which in (dp_here, 1 - dp_here) for p in range(PAIRS)]
+    goals = gather_columns(target, jnp.stack(goal_at), width)
+    span = PAIRS * width
+    goals = jnp.concatenate([goals[:, :span], flip(goals[:, span:], "dp", 1)])
+
     message = jnp.stack([message, flip(message, "dp", 1)], axis=1)
     message = message.reshape(lat_count * dp_count, own.shape[0], block_size)
-
-    goal = target.reshape(tok_count, dp_count, PAIRS, lay_count, width)
-
-    def goal_of(which):
-        cut = lax.dynamic_index_in_dim(goal, which, 1, False)
-        return lax.dynamic_index_in_dim(cut, lay_here, 2, False)
-
-    goals = jnp.concatenate([goal_of(dp_here), flip(goal_of(1 - dp_here), "dp", 1)])
-
-    def places(pair, names, offset):
-        return jnp.stack([offset + pair * lay_count + (lay_here ^ r) for r in names])
-
-    def weight_places(pair, names):
-        return places(pair, names, dp_here * (half // width))
-
-    parts = [forward(message, decoder, first, weight_places(p, (3, 1, 2, 0)), width) for p in range(PAIRS)]
-    got = [(flip(parts[p][0], "layer", 1), flip(parts[p][2], "layer", 2)) for p in range(PAIRS)]
-    up[1], down[1], got[0] = lax.optimization_barrier((up[1], down[1], got[0]))
+    message, acts_now, weights = lax.optimization_barrier((message, acts, weights))
+    up, down = [acts_now], [acts_now]
+    next_hops()
+
+    codes = spread_codes(message, first, lat_rows)
+
+    def rows_for(spread, pair, n):
+        cols = weights[:, (4 * pair + n) * width:(4 * pair + n + 1) * width]
+        return jnp.dot(spread, cols, preferred_element_type=f32).astype(bf16)
+
+    parts, got = [], []
+    for p in range(PAIRS):
+        if p == 1:
+            codes, up[1], down[1] = lax.optimization_barrier((codes, up[1], down[1]))
+            if lat_count > 2:
+                next_hops()
+        sent = rows_for(codes, p, 0), rows_for(codes, p, 1)
+        got.append((flip(sent[0], "layer", 1), flip(sent[1], "layer", 2)))
+        parts.append((rows_for(codes, p, 2), rows_for(codes, p, 3)))
 
     def add(one, two):
-        return (one.astype(f32) + two.astype(f32)).astype(bf16)
+        return (one[:, side:].astype(f32) + two[:, side:].astype(f32)).astype(bf16)
 
     lat_bits = [1 << i for i in range(lat_count.bit_length() - 1)]
     own_errors = []
     for p in range(PAIRS):
-        kept = parts[p][1], parts[p][3]
-        far = [flip(add(got[p][n][1:], kept[n][1:]), "layer", 2 - n) for n in range(2)]
+        kept = parts[p]
+        far = [flip(add(got[p][n], kept[n]), "layer", 2 - n) for n in range(2)]
+        if p == 0 and len(up) > 2:
+            up[2], down[2], far[0] = lax.optimization_barrier((up[2], down[2], far[0]))
         sent, held = layer_sum((got[p][0], kept[0], far[0]), (got[p][1], kept[1], far[1]), lat_count)
         near = flip(sent, "latent", 1)
         terms = [held, near]
@@ -480,22 +482,25 @@
             out = sum(c[:, 1].astype(f32) for c in cut).astype(bf16)
             terms = [c[:, 0] for c in cut] + [flip(out, "latent", bit)]
         total = sum(t[0].astype(f32) for t in terms)
-        own_errors.append(((total - goals[:, p].astype(f32)) / tok_count).astype(bf16))
-
-    if lat_count > 2:
-        up[1], down[1], own_errors[-1] = lax.optimization_barrier((up[1], down[1], own_errors[-1]))
-    while len(up) < lat_count:
-        next_hops()
-
-    pieces = []
+        own_errors.append(((total - goals[:, p * width:(p + 1) * width].astype(f32)) / tok_count).astype(bf16))
+
+    gathered = []
     for p in range(PAIRS):
         rows = own_errors[p][None]
         for bit in lat_bits[:0:-1]:
             rows = jnp.stack([rows, flip(rows, "latent", bit)], axis=1).reshape((-1,) + rows.shape[1:])
-        rows = jnp.stack([rows, flip(rows, "latent", 1)], axis=1).reshape(tokens, width)
+        gathered.append(jnp.stack([rows, flip(rows, "latent", 1)], axis=1).reshape(tokens, width))
+    if len(up) < lat_count:
+        up[-1], down[-1], gathered[-1] = lax.optimization_barrier((up[-1], down[-1], gathered[-1]))
+    while len(up) < lat_count:
+        next_hops()
+
+    pieces = []
+    for rows in gathered:
         one, two = flip(rows, "layer", 1), flip(rows, "layer", 2)
+        one, two = lax.optimization_barrier((one, two))
         three = (flip(two[:, :side], "layer", 1), flip(one[:, side:], "layer", 2))
-        pieces.append([(rows,), (one,), (two,), three])
+        pieces.append([(rows,), (one,), (two,), lax.optimization_barrier(three)])
 
     cut = message.reshape(tokens // tok_count, own.shape[0], block_size)
     pre_lanes = cut[:, :active_count * tok_count].reshape(-1, active_count, tok_count, block_size)
@@ -512,7 +517,9 @@
         for names in ((0, 1, 2, 3),) if p < PAIRS - 1 else ((0, 1, 2), (3,)):
             here = [pieces[p][r] for r in names]
             grads.append(code_grad(here, ids, decoder, first, weight_places(p, names), block_size))
-            dec = decoder_part(here, ids_wide, code_lanes, first, places(p, names, 0), lat_rows, half, dec)
+            dec = decoder_part(here, ids_wide, code_lanes, first, jnp.stack(places(p, names, 0)), lat_rows, half, dec)
+            if p + 1 < PAIRS:
+                pieces[p + 1][3], grads[-1], dec = lax.optimization_barrier((pieces[p + 1][3], grads[-1], dec))
     grad = sum(grads)
     pre_grad = pre_grad_spread(grad, flip(grad, "dp", 1), ids_wide, pre_lanes, first, lat_rows, tok_count)
     along = [acts] + [down[k] + up[lat_count - k] for k in range(1, lat_count)]

time: 223 us -> 227 us (1.018)
  waiting for transfers between devices: 81 us -> 48.7 us
  starting transfers between devices: 41.1 us -> 70.3 us
  matrix products: 10.8 us -> 20.9 us
  Pallas kernels: 62 us -> 55.5 us
  local copies, waits for them, and re-layouts: 14.2 us -> 18.3 us
    ppermute x31, waiting for transfers between devices: 81 us -> 46.4 us  [flip(): return lax.ppermute(value, axis, [(i, i ^ bit) for i in range(count)])]
    ppermute x31, starting transfers between devices: 30.3 us -> 58.7 us  [flip(): return lax.ppermute(value, axis, [(i, i ^ bit) for i in range(count)])]
    dot_general x0 -> x8, matrix products: none -> 10.1 us  [rows_for(): return jnp.dot(spread, cols, preferred_element_type=f32).astype(bf16)]
    pallas_call x2 -> x3, Pallas kernels: 22.4 us -> 14.2 us  [the longest x2 11.6 us: gather_columns(): pl.pallas_call(gather_kernel, out_shape=jax.ShapeDtypeStruct((rows, count...]
    unnamed x27 -> x31, local copies, waits for them, and re-layouts: 6.75 us -> 11.5 us
    reshape x1 -> x0, local copies, waits for them, and re-layouts: 2.63 us -> none  [dense_plan(): goal = target.reshape(tok_count, dp_count, PAIRS, lay_count, width)]
  transfers between devices with their start and end apart: 37 -> 37, of which waited for: 16 -> 14; matrix products, arithmetic and copies ran while one was open for 9% -> 13% of each run, Pallas kernels for 28% -> 24%
where the time goes in v3:
time: 227 us; the launch traced here: 225 us
  starting transfers between devices  70.3 us (31%)
  Pallas kernels  55.5 us (24%)
  waiting for transfers between devices  48.7 us (21%)
  matrix products  20.9 us (9%)
  local copies, waits for them, and re-layouts  18.3 us (8%)
  other arithmetic  10.5 us (5%)
    ppermute x31, starting transfers between devices, flip(): return lax.ppermute(value, axis, [(i, i ^ bit) for i in range(count)])  58.7 us
    ppermute x31, waiting for transfers between devices, flip(): return lax.ppermute(value, axis, [(i, i ^ bit) for i in range(count)])  46.4 us
    pallas_call x3, Pallas kernels, decoder_part(): pl.pallas_call(functools.partial(decoder_kernel, size, [len(p) for p in p...  19.6 us
    pallas_call x3, Pallas kernels, code_grad(): pl.pallas_call(functools.partial(code_grad_kernel, size, [len(p) for p in...  18.1 us
    pallas_call x2, Pallas kernels, gather_columns(): pl.pallas_call(gather_kernel, out_shape=jax.ShapeDtypeStruct((rows, count...  11.6 us
    ppermute x6, starting transfers between devices, hop(): return lax.ppermute(value, axis, pairs)  11.6 us
    unnamed x31, local copies, waits for them, and re-layouts  11.5 us
    dot_general x1, matrix products, dense_plan(): jnp.dot(pre_grad, jnp.concatenate(along), preferred_element_type=f32)  10.8 us
  transfers between devices with their start and end apart: 37, of which 14 were waited for; matrix products, arithmetic and copies ran while one was open for 13% of the time, Pallas kernels for 24%

profile of v3, /device:TPU:1, one launch (start us, length us, event | category | flops | bytes accessed | tf_op | source)
XLA Modules:
  0.0 225.3 jit_solution(16409156059311674281)
XLA Ops:
  2.2 3.2 %collective-permute-start.1 = (bf16[272,128]{1,0:T(8,128)(2,1)S(1)}, bf16[272,128]{1,0:T(8,128)(2,1)S(1)}, u32[]{:S(2)}, u32[]{:S(2)}) collective-permute-start(bf16[272,128]{1,0:T(8,128)(2,1)S(1)} %get-tuple-element.75), channel_id=1, source_target_pairs={{0,4},{2,6},{4,0},{6,2},{1,5},{3,7},{5,1},{7,3},{8,12},{10,14},{12... | collective-permute-start | bytes 208904 | tf_op jit(solution)/shard_map/ppermute | solution.py:104
  9.1 2.6 %collective-permute-done.2 = bf16[272,128]{1,0:T(8,128)(2,1)S(1)} collective-permute-done((bf16[272,128]{1,0:T(8,128)(2,1)S(1)}, bf16[272,128]{1,0:T(8,128)(2,1)S(1)}, u32[]{:S(2)}, u32[]{:S(2)}) %collective-permute-start.2) | collective-permute-done | bytes 69664 | tf_op jit(solution)/shard_map/ppermute | solution.py:104
  14.3 10.9 %gather_columns.2 = bf16[2048,2048]{1,0:T(8,128)(2,1)S(1)} custom-call(s32[16]{0:T(128)S(1)} %stack.198.scalar_ref, bf16[1,2048,4096]{2,1,0:T(8,128)(2,1)} %refs_0_.5), custom_call_target="tpu_custom_call" | custom-call | flops 2097152 | bytes 2099200 | tf_op jit(solution)/shard_map/gather_columns/pallas_call | solution.py:144
  28.8 5.0 %collective-permute-start.5 = (bf16[256,2048]{1,0:T(8,128)(2,1)S(1)}, bf16[256,2048]{1,0:T(8,128)(2,1)}, u32[]{:S(2)}, u32[]{:S(2)}) collective-permute-start(bf16[256,2048]{1,0:T(8,128)(2,1)S(1)} %get-tuple-element.31), channel_id=1, source_target_pairs={{0,2},{2,4},{4,6},{1,3},{3,5},{5,7},{8,10},{10,12},{12,14},{9,11},... | collective-permute-start | bytes 3145736 | tf_op jit(solution)/shard_map/ppermute | solution.py:113
  33.8 2.6 %spread_codes.1 = bf16[1024,2048]{1,0:T(8,128)(2,1)S(1)} custom-call(s32[1]{0:T(128)} %bitcast.scalar_ref, bf16[8,272,128]{2,1,0:T(8,128)(2,1)S(1)} %bitcast.147), custom_call_target="tpu_custom_call" | custom-call | flops 1048576 | bytes 1050112 | tf_op jit(solution)/shard_map/spread_codes/pallas_call | solution.py:190
  44.0 7.9 %collective-permute-done.9.got_a = bf16[1024,256]{1,0:T(8,128)(2,1)S(1)} collective-permute-done((bf16[1024,256]{1,0:T(8,128)(2,1)S(1)}, bf16[1024,256]{1,0:T(8,128)(2,1)S(1)}, u32[]{:S(2)}, u32[]{:S(2)}) %collective-permute-start.9) | collective-permute-done | bytes 524320 | tf_op jit(solution)/shard_map/ppermute | solution.py:104
  65.8 4.1 %collective-permute-done.11.got_a = bf16[1024,256]{1,0:T(8,128)(2,1)S(1)} collective-permute-done((bf16[1024,256]{1,0:T(8,128)(2,1)S(1)}, bf16[1024,256]{1,0:T(8,128)(2,1)S(1)}, u32[]{:S(2)}, u32[]{:S(2)}) %collective-permute-start.11) | collective-permute-done | bytes 524320 | tf_op jit(solution)/shard_map/ppermute | solution.py:104
  75.3 8.8 %collective-permute-done.12.far_a = bf16[1024,128]{1,0:T(8,128)(2,1)S(1)} collective-permute-done((bf16[1024,128]{1,0:T(8,128)(2,1)S(1)}, bf16[1024,128]{1,0:T(8,128)(2,1)S(1)}, u32[]{:S(2)}, u32[]{:S(2)}) %collective-permute-start.12) | collective-permute-done | bytes 262176 | tf_op jit(solution)/shard_map/ppermute | solution.py:104
  96.1 2.5 %collective-permute-start.17 = (bf16[128,512]{1,0:T(8,128)(2,1)S(1)}, bf16[128,512]{1,0:T(8,128)(2,1)S(1)}, u32[]{:S(2)}, u32[]{:S(2)}) collective-permute-start(bf16[128,512]{1,0:T(8,128)(2,1)S(1)} %get-tuple-element.72), channel_id=1, source_target_pairs={{0,1},{1,0},{2,3},{3,2},{4,5},{5,4},{6,7},{7,6},{8,9},{9,8},{10,11... | collective-permute-start | bytes 393224 | tf_op jit(solution)/shard_map/ppermute | solution.py:104
  101.0 3.2 %collective-permute-done.26 = bf16[2,256,256]{2,1,0:T(8,128)(2,1)S(1)} collective-permute-done((bf16[2,256,256]{2,1,0:T(8,128)(2,1)S(1)}, bf16[2,256,256]{2,1,0:T(8,128)(2,1)S(1)}, u32[]{:S(2)}, u32[]{:S(2)}) %collective-permute-start.26) | collective-permute-done | bytes 262176 | tf_op jit(solution)/shard_map/ppermute | solution.py:104
  105.2 6.6 %collective-permute-done.27 = bf16[1,256,256]{2,1,0:T(8,128)(2,1)S(1)} collective-permute-done((bf16[1,256,256]{2,1,0:T(8,128)(2,1)S(1)}, bf16[1,256,256]{2,1,0:T(8,128)(2,1)S(1)}, u32[]{:S(2)}, u32[]{:S(2)}) %collective-permute-start.27) | collective-permute-done | bytes 131104 | tf_op jit(solution)/shard_map/ppermute | solution.py:104
  116.8 5.6 %collective-permute-start.29 = (bf16[2,256,256]{2,1,0:T(8,128)(2,1)S(1)}, bf16[2,256,256]{2,1,0:T(8,128)(2,1)S(1)}, u32[]{:S(2)}, u32[]{:S(2)}) collective-permute-start(bf16[2,256,256]{2,1,0:T(8,128)(2,1)S(1)} %get-tuple-element.67), channel_id=1, source_target_pairs={{0,2},{2,0},{4,6},{6,4},{1,3},{3,1},{5,7},{7,5},{8,10},{10,8},{12,... | collective-permute-start | bytes 786440 | tf_op jit(solution)/shard_map/ppermute | solution.py:104
  124.1 3.6 %collective-permute-done.29 = bf16[2,256,256]{2,1,0:T(8,128)(2,1)S(1)} collective-permute-done((bf16[2,256,256]{2,1,0:T(8,128)(2,1)S(1)}, bf16[2,256,256]{2,1,0:T(8,128)(2,1)S(1)}, u32[]{:S(2)}, u32[]{:S(2)}) %collective-permute-start.29) | collective-permute-done | bytes 262176 | tf_op jit(solution)/shard_map/ppermute | solution.py:104
  128.4 7.6 %collective-permute-start.30 = (bf16[1024,256]{1,0:T(8,128)(2,1)S(1)}, bf16[1024,256]{1,0:T(8,128)(2,1)}, u32[]{:S(2)}, u32[]{:S(2)}) collective-permute-start(bf16[1024,256]{1,0:T(8,128)(2,1)S(1)} %bitcast.155), channel_id=1, source_target_pairs={{0,8},{8,0},{16,24},{24,16},{1,9},{9,1},{17,25},{25,17},{2,10},{10... | collective-permute-start | bytes 1572872 | tf_op jit(solution)/shard_map/ppermute | solution.py:104
  136.3 5.4 %collective-permute-start.20 = (bf16[1024,256]{1,0:T(8,128)(2,1)S(1)}, bf16[1024,256]{1,0:T(8,128)(2,1)S(1)}, u32[]{:S(2)}, u32[]{:S(2)}) collective-permute-start(bf16[1024,256]{1,0:T(8,128)(2,1)S(1)} %bitcast.151), channel_id=1, source_target_pairs={{0,8},{8,0},{16,24},{24,16},{1,9},{9,1},{17,25},{25,17},{2,10},{10... | collective-permute-start | bytes 1572872 | tf_op jit(solution)/shard_map/ppermute | solution.py:104
  150.3 5.3 %collective-permute-done.20.refs_2_.refs_4_ = bf16[1024,256]{1,0:T(8,128)(2,1)S(1)} collective-permute-done((bf16[1024,256]{1,0:T(8,128)(2,1)S(1)}, bf16[1024,256]{1,0:T(8,128)(2,1)S(1)}, u32[]{:S(2)}, u32[]{:S(2)}) %collective-permute-start.20) | collective-permute-done | bytes 524320 | tf_op jit(solution)/shard_map/ppermute | solution.py:104
  158.8 6.3 %code_grad.4 = f32[2,128,1024]{2,1,0:T(8,128)S(1)} custom-call(s32[4]{0:T(128)S(1)} %get-tuple-element.79.scalar_ref, f32[2,1024]{1,0:T(2,128)S(1)} %get-tuple-element.62.ids_ref, bf16[1,2048,4096]{2,1,0:T(8,128)(2,1)} %refs_0_.5, bf16[1,2048,4096]{2,1,0:T(8,128)(2,1)} %refs_0_.5, bf16[1,2048,4096]{2,1,0:T(8,128)(2,1)} %refs_0_.5, ...), custom_call_target="tpu_custom_call" | custom-call | flops 805306368 | bytes 2228224 | tf_op jit(solution)/shard_map/code_grad/pallas_call | solution.py:289
  166.8 7.7 %code_grad.3 = f32[2,128,1024]{2,1,0:T(8,128)S(1)} custom-call(s32[5]{0:T(128)S(1)} %concatenate.36.scalar_ref, f32[2,1024]{1,0:T(2,128)S(1)} %get-tuple-element.62.ids_ref, bf16[1,2048,4096]{2,1,0:T(8,128)(2,1)} %refs_0_.5, bf16[1,2048,4096]{2,1,0:T(8,128)(2,1)} %refs_0_.5, bf16[1,2048,4096]{2,1,0:T(8,128)(2,1)} %refs_0_.5, bf16[1,2048,4096]{2,1,0:T(8,128)(2,1)} %refs_0_.5, ...), custom_call_target="tpu_custom_call" | custom-call | flops 1073741824 | bytes 2621440 | tf_op jit(solution)/shard_map/code_grad/pallas_call | solution.py:289
  174.6 9.3 %decoder_part.3.refs_0_ = bf16[2048,2048]{1,0:T(8,128)(2,1)} custom-call(s32[5]{0:T(128)S(1)} %concatenate.37.scalar_ref, bf16[2,16,1024]{2,1,0:T(8,128)(2,1)S(1)} %broadcast_in_dim.31.ids_ref, bf16[2,128,1024]{2,1,0:T(8,128)(2,1)S(1)} %broadcast_maximum_fusion.codes_ref, bf16[1024,256]{1,0:T(8,128)(2,1)S(1)} %bitcast.157, ...), custom_call_target="tpu_custom_call" | custom-call | flops 1073741824 | bytes 2621440 | tf_op jit(solution)/shard_map/decoder_part/pallas_call | solution.py:338
  183.8 4.2 %code_grad.5 = f32[2,128,1024]{2,1,0:T(8,128)S(1)} custom-call(s32[2]{0:T(128)S(1)} %get-tuple-element.77.scalar_ref, f32[2,1024]{1,0:T(2,128)S(1)} %get-tuple-element.62.ids_ref, bf16[1,2048,4096]{2,1,0:T(8,128)(2,1)} %refs_0_.5, bf16[1024,128]{1,0:T(8,128)(2,1)S(1)} %collective-permute-done.22.refs_1_, bf16[1024,128]{1,0:T(8,128)(2,1)S(1)} %collective-permute-done.23.refs_2_), custom_call_target="tpu_custom_call" | custom-call | flops 268435456 | bytes 1441792 | tf_op jit(solution)/shard_map/code_grad/pallas_call | solution.py:289
  188.3 9.6 %collective-permute-start.34 = (f32[2,128,1024]{2,1,0:T(8,128)S(1)}, f32[2,128,1024]{2,1,0:T(8,128)S(1)}, u32[]{:S(2)}, u32[]{:S(2)}) collective-permute-start(f32[2,128,1024]{2,1,0:T(8,128)S(1)} %add_add_fusion.own_ref), channel_id=1, source_target_pairs={{0,1},{1,0},{2,3},{3,2},{4,5},{5,4},{6,7},{7,6},{8,9},{9,8},{10,11... | collective-permute-start | bytes 3145736 | tf_op jit(solution)/shard_map/ppermute | solution.py:104
  197.9 6.7 %decoder_part.4.refs_0_ = bf16[2048,2048]{1,0:T(8,128)(2,1)} custom-call(s32[4]{0:T(128)S(1)} %get-tuple-element.78.scalar_ref, bf16[2,16,1024]{2,1,0:T(8,128)(2,1)S(1)} %broadcast_in_dim.31.ids_ref, bf16[2,128,1024]{2,1,0:T(8,128)(2,1)S(1)} %broadcast_maximum_fusion.codes_ref, ...), custom_call_target="tpu_custom_call", output_to_operand_aliasing={{}: (3, {})} | custom-call | flops 805306368 | bytes 2228224 | tf_op jit(solution)/shard_map/decoder_part/pallas_call | solution.py:338
  204.6 3.7 %decoder_part.5 = bf16[2048,2048]{1,0:T(8,128)(2,1)} custom-call(s32[2]{0:T(128)S(1)} %get-tuple-element.76.scalar_ref, bf16[2,16,1024]{2,1,0:T(8,128)(2,1)S(1)} %broadcast_in_dim.31.ids_ref, bf16[2,128,1024]{2,1,0:T(8,128)(2,1)S(1)} %broadcast_maximum_fusion.codes_ref, bf16[2048,2048]{1,0:T(8,128)(2,1)} %decoder_part.4.refs_0_, ...), custom_call_target="tpu_custom_call", output_to_operand_aliasing={{}: (3, {})} | custom-call | flops 268435456 | bytes 1441792 | tf_op jit(solution)/shard_map/decoder_part/pallas_call | solution.py:338
  214.5 10.8 %convert_bitcast_fusion = bf16[1,2048,2048]{2,1,0:T(8,128)(2,1)} fusion(bf16[2048,1024]{1,0:T(8,128)(2,1)S(1)} %pre_grad_spread.1, bf16[1024,2048]{1,0:T(8,128)(2,1)S(1)} %bitcast_dynamic-update-slice_fusion), kind=kOutput, calls=%fused_computation | convolution fusion | flops 8594128896 | bytes 16777216 | tf_op jit(solution)/shard_map/dot_general | solution.py:528
  (145 shorter events, 81.0 us)
Async XLA Ops:
  7.8 18.4 %collective-permute-start.4 = (bf16[128,2048]{1,0:T(8,128)(2,1)S(1)}, bf16[128,2048]{1,0:T(8,128)(2,1)S(1)}, u32[]{:S(2)}, u32[]{:S(2)}) collective-permute-start(bf16[128,2048]{1,0:T(8,128)(2,1)S(1)} %dynamic-slice_bitcast_fusion), channel_id=1, source_target_pairs={{0,1},{1,0},{2,3},{3,2},{4,5},{5,4},{6,7},{7,6},{8,9},{9,8},{10,11... | collective-permute-start | bytes 1572872 | tf_op jit(solution)/shard_map/ppermute | solution.py:104
  11.8 14.3 %collective-permute-start.3 = (bf16[4,272,128]{2,1,0:T(8,128)(2,1)S(1)}, bf16[4,272,128]{2,1,0:T(8,128)(2,1)S(1)}, u32[]{:S(2)}, u32[]{:S(2)}) collective-permute-start(bf16[4,272,128]{2,1,0:T(8,128)(2,1)S(1)} %get-tuple-element.65), channel_id=1, source_target_pairs={{0,1},{1,0},{2,3},{3,2},{4,5},{5,4},{6,7},{7,6},{8,9},{9,8},{10,11... | collective-permute-start | bytes 835592 | tf_op jit(solution)/shard_map/ppermute | solution.py:104
  27.5 26.7 %collective-permute-start.6 = (bf16[256,2048]{1,0:T(8,128)(2,1)S(1)}, bf16[256,2048]{1,0:T(8,128)(2,1)}, u32[]{:S(2)}, u32[]{:S(2)}) collective-permute-start(bf16[256,2048]{1,0:T(8,128)(2,1)S(1)} %get-tuple-element.31), channel_id=1, source_target_pairs={{2,0},{4,2},{6,4},{3,1},{5,3},{7,5},{10,8},{12,10},{14,12},{11,9},... | collective-permute-start | bytes 3145736 | tf_op jit(solution)/shard_map/ppermute | solution.py:113
  28.8 26.2 %collective-permute-start.5 = (bf16[256,2048]{1,0:T(8,128)(2,1)S(1)}, bf16[256,2048]{1,0:T(8,128)(2,1)}, u32[]{:S(2)}, u32[]{:S(2)}) collective-permute-start(bf16[256,2048]{1,0:T(8,128)(2,1)S(1)} %get-tuple-element.31), channel_id=1, source_target_pairs={{0,2},{2,4},{4,6},{1,3},{3,5},{5,7},{8,10},{10,12},{12,14},{9,11},... | collective-permute-start | bytes 3145736 | tf_op jit(solution)/shard_map/ppermute | solution.py:113
  38.9 13.0 %collective-permute-start.9 = (bf16[1024,256]{1,0:T(8,128)(2,1)S(1)}, bf16[1024,256]{1,0:T(8,128)(2,1)S(1)}, u32[]{:S(2)}, u32[]{:S(2)}) collective-permute-start(bf16[1024,256]{1,0:T(8,128)(2,1)S(1)} %convolution_convert_fusion.7), channel_id=1, source_target_pairs={{0,8},{8,0},{16,24},{24,16},{1,9},{9,1},{17,25},{25,17},{2,10},{10... | collective-permute-start | bytes 1572872 | tf_op jit(solution)/shard_map/ppermute | solution.py:104
  41.5 32.8 %collective-permute-start.24 = (bf16[1024,256]{1,0:T(8,128)(2,1)S(1)}, bf16[1024,256]{1,0:T(8,128)(2,1)S(1)}, u32[]{:S(2)}, u32[]{:S(2)}) collective-permute-start(bf16[1024,256]{1,0:T(8,128)(2,1)S(1)} %convolution_convert_fusion.1), channel_id=1, source_target_pairs={{0,16},{8,24},{16,0},{24,8},{1,17},{9,25},{17,1},{25,9},{2,18},{10... | collective-permute-start | bytes 1572872 | tf_op jit(solution)/shard_map/ppermute | solution.py:104
  57.5 12.3 %collective-permute-start.11 = (bf16[1024,256]{1,0:T(8,128)(2,1)S(1)}, bf16[1024,256]{1,0:T(8,128)(2,1)S(1)}, u32[]{:S(2)}, u32[]{:S(2)}) collective-permute-start(bf16[1024,256]{1,0:T(8,128)(2,1)S(1)} %convolution_convert_fusion.5), channel_id=1, source_target_pairs={{0,8},{8,0},{16,24},{24,16},{1,9},{9,1},{17,25},{25,17},{2,10},{10... | collective-permute-start | bytes 1572872 | tf_op jit(solution)/shard_map/ppermute | solution.py:104
  60.1 12.0 %collective-permute-start.13 = (bf16[1024,256]{1,0:T(8,128)(2,1)S(1)}, bf16[1024,256]{1,0:T(8,128)(2,1)S(1)}, u32[]{:S(2)}, u32[]{:S(2)}) collective-permute-start(bf16[1024,256]{1,0:T(8,128)(2,1)S(1)} %convolution_convert_fusion.3), channel_id=1, source_target_pairs={{0,16},{8,24},{16,0},{24,8},{1,17},{9,25},{17,1},{25,9},{2,18},{10... | collective-permute-start | bytes 1572872 | tf_op jit(solution)/shard_map/ppermute | solution.py:104
  61.4 33.3 %collective-permute-start.7 = (bf16[256,2048]{1,0:T(8,128)(2,1)}, bf16[256,2048]{1,0:T(8,128)(2,1)}, u32[]{:S(2)}, u32[]{:S(2)}) collective-permute-start(bf16[256,2048]{1,0:T(8,128)(2,1)} %collective-permute-done.5), channel_id=1, source_target_pairs={{2,4},{4,6},{3,5},{5,7},{10,12},{12,14},{11,13},{13,15},{18,20},{2... | collective-permute-start | bytes 3145736 | tf_op jit(solution)/shard_map/ppermute | solution.py:113
  63.0 31.6 %collective-permute-start.8 = (bf16[256,2048]{1,0:T(8,128)(2,1)}, bf16[256,2048]{1,0:T(8,128)(2,1)}, u32[]{:S(2)}, u32[]{:S(2)}) collective-permute-start(bf16[256,2048]{1,0:T(8,128)(2,1)} %collective-permute-done.6), channel_id=1, source_target_pairs={{2,0},{4,2},{3,1},{5,3},{10,8},{12,10},{11,9},{13,11},{18,16},{20,... | collective-permute-start | bytes 3145736 | tf_op jit(solution)/shard_map/ppermute | solution.py:113
  69.8 24.8 %collective-permute-start.10 = (bf16[1024,128]{1,0:T(8,128)(2,1)}, bf16[1024,128]{1,0:T(8,128)(2,1)S(1)}, u32[]{:S(2)}, u32[]{:S(2)}) collective-permute-start(bf16[1024,128]{1,0:T(8,128)(2,1)} %add_convert_fusion.3), channel_id=1, source_target_pairs={{0,16},{8,24},{16,0},{24,8},{1,17},{9,25},{17,1},{25,9},{2,18},{10... | collective-permute-start | bytes 786440 | tf_op jit(solution)/shard_map/ppermute | solution.py:104
  72.1 12.0 %collective-permute-start.12 = (bf16[1024,128]{1,0:T(8,128)(2,1)S(1)}, bf16[1024,128]{1,0:T(8,128)(2,1)S(1)}, u32[]{:S(2)}, u32[]{:S(2)}) collective-permute-start(bf16[1024,128]{1,0:T(8,128)(2,1)S(1)} %add_convert_fusion.2), channel_id=1, source_target_pairs={{0,16},{8,24},{16,0},{24,8},{1,17},{9,25},{17,1},{25,9},{2,18},{10... | collective-permute-start | bytes 786440 | tf_op jit(solution)/shard_map/ppermute | solution.py:104
  122.4 13.6 %collective-permute-start.19 = (bf16[2,256,256]{2,1,0:T(8,128)(2,1)S(1)}, bf16[2,256,256]{2,1,0:T(8,128)(2,1)S(1)}, u32[]{:S(2)}, u32[]{:S(2)}) collective-permute-start(bf16[2,256,256]{2,1,0:T(8,128)(2,1)S(1)} %get-tuple-element.71), channel_id=1, source_target_pairs={{0,2},{2,0},{4,6},{6,4},{1,3},{3,1},{5,7},{7,5},{8,10},{10,8},{12,... | collective-permute-start | bytes 786440 | tf_op jit(solution)/shard_map/ppermute | solution.py:104
  127.8 20.7 %collective-permute-start.31 = (bf16[1024,256]{1,0:T(8,128)(2,1)S(1)}, bf16[1024,256]{1,0:T(8,128)(2,1)S(1)}, u32[]{:S(2)}, u32[]{:S(2)}) collective-permute-start(bf16[1024,256]{1,0:T(8,128)(2,1)S(1)} %bitcast.154), channel_id=1, source_target_pairs={{0,16},{8,24},{16,0},{24,8},{1,17},{9,25},{17,1},{25,9},{2,18},{10... | collective-permute-start | bytes 1572872 | tf_op jit(solution)/shard_map/ppermute | solution.py:104
  128.4 20.1 %collective-permute-start.30 = (bf16[1024,256]{1,0:T(8,128)(2,1)S(1)}, bf16[1024,256]{1,0:T(8,128)(2,1)}, u32[]{:S(2)}, u32[]{:S(2)}) collective-permute-start(bf16[1024,256]{1,0:T(8,128)(2,1)S(1)} %bitcast.155), channel_id=1, source_target_pairs={{0,8},{8,0},{16,24},{24,16},{1,9},{9,1},{17,25},{25,17},{2,10},{10... | collective-permute-start | bytes 1572872 | tf_op jit(solution)/shard_map/ppermute | solution.py:104
  136.1 14.2 %collective-permute-start.21 = (bf16[1024,256]{1,0:T(8,128)(2,1)S(1)}, bf16[1024,256]{1,0:T(8,128)(2,1)S(1)}, u32[]{:S(2)}, u32[]{:S(2)}) collective-permute-start(bf16[1024,256]{1,0:T(8,128)(2,1)S(1)} %bitcast.150), channel_id=1, source_target_pairs={{0,16},{8,24},{16,0},{24,8},{1,17},{9,25},{17,1},{25,9},{2,18},{10... | collective-permute-start | bytes 1572872 | tf_op jit(solution)/shard_map/ppermute | solution.py:104
  136.3 19.3 %collective-permute-start.20 = (bf16[1024,256]{1,0:T(8,128)(2,1)S(1)}, bf16[1024,256]{1,0:T(8,128)(2,1)S(1)}, u32[]{:S(2)}, u32[]{:S(2)}) collective-permute-start(bf16[1024,256]{1,0:T(8,128)(2,1)S(1)} %bitcast.151), channel_id=1, source_target_pairs={{0,8},{8,0},{16,24},{24,16},{1,9},{9,1},{17,25},{25,17},{2,10},{10... | collective-permute-start | bytes 1572872 | tf_op jit(solution)/shard_map/ppermute | solution.py:104
  147.8 60.5 %collective-permute-start.35 = (bf16[256,2048]{1,0:T(8,128)(2,1)}, bf16[256,2048]{1,0:T(8,128)(2,1)S(1)}, u32[]{:S(2)}, u32[]{:S(2)}) collective-permute-start(bf16[256,2048]{1,0:T(8,128)(2,1)} %collective-permute-done.7), channel_id=1, source_target_pairs={{4,6},{5,7},{12,14},{13,15},{20,22},{21,23},{28,30},{29,31}} | collective-permute-start | bytes 3145736 | tf_op jit(solution)/shard_map/ppermute | solution.py:113
  149.5 15.6 %collective-permute-start.32 = (bf16[1024,128]{1,0:T(8,128)(2,1)S(1)}, bf16[1024,128]{1,0:T(8,128)(2,1)S(1)}, u32[]{:S(2)}, u32[]{:S(2)}) collective-permute-start(bf16[1024,128]{1,0:T(8,128)(2,1)S(1)} %slice.135), channel_id=1, source_target_pairs={{0,8},{8,0},{16,24},{24,16},{1,9},{9,1},{17,25},{25,17},{2,10},{10... | collective-permute-start | bytes 786440 | tf_op jit(solution)/shard_map/ppermute | solution.py:104
  149.6 17.0 %collective-permute-start.33 = (bf16[1024,128]{1,0:T(8,128)(2,1)S(1)}, bf16[1024,128]{1,0:T(8,128)(2,1)S(1)}, u32[]{:S(2)}, u32[]{:S(2)}) collective-permute-start(bf16[1024,128]{1,0:T(8,128)(2,1)S(1)} %slice.136), channel_id=1, source_target_pairs={{0,16},{8,24},{16,0},{24,8},{1,17},{9,25},{17,1},{25,9},{2,18},{10... | collective-permute-start | bytes 786440 | tf_op jit(solution)/shard_map/ppermute | solution.py:104
  155.6 11.0 %collective-permute-start.23 = (bf16[1024,128]{1,0:T(8,128)(2,1)S(1)}, bf16[1024,128]{1,0:T(8,128)(2,1)S(1)}, u32[]{:S(2)}, u32[]{:S(2)}) collective-permute-start(bf16[1024,128]{1,0:T(8,128)(2,1)S(1)} %slice.125), channel_id=1, source_target_pairs={{0,16},{8,24},{16,0},{24,8},{1,17},{9,25},{17,1},{25,9},{2,18},{10... | collective-permute-start | bytes 786440 | tf_op jit(solution)/shard_map/ppermute | solution.py:104
  155.8 11.1 %collective-permute-start.22 = (bf16[1024,128]{1,0:T(8,128)(2,1)S(1)}, bf16[1024,128]{1,0:T(8,128)(2,1)S(1)}, u32[]{:S(2)}, u32[]{:S(2)}) collective-permute-start(bf16[1024,128]{1,0:T(8,128)(2,1)S(1)} %slice.124), channel_id=1, source_target_pairs={{0,8},{8,0},{16,24},{24,16},{1,9},{9,1},{17,25},{25,17},{2,10},{10... | collective-permute-start | bytes 786440 | tf_op jit(solution)/shard_map/ppermute | solution.py:104
  165.1 44.6 %collective-permute-start.36 = (bf16[256,2048]{1,0:T(8,128)(2,1)}, bf16[256,2048]{1,0:T(8,128)(2,1)S(1)}, u32[]{:S(2)}, u32[]{:S(2)}) collective-permute-start(bf16[256,2048]{1,0:T(8,128)(2,1)} %collective-permute-done.8), channel_id=1, source_target_pairs={{2,0},{3,1},{10,8},{11,9},{18,16},{19,17},{26,24},{27,25}} | collective-permute-start | bytes 3145736 | tf_op jit(solution)/shard_map/ppermute | solution.py:113
  188.3 25.2 %collective-permute-start.34 = (f32[2,128,1024]{2,1,0:T(8,128)S(1)}, f32[2,128,1024]{2,1,0:T(8,128)S(1)}, u32[]{:S(2)}, u32[]{:S(2)}) collective-permute-start(f32[2,128,1024]{2,1,0:T(8,128)S(1)} %add_add_fusion.own_ref), channel_id=1, source_target_pairs={{0,1},{1,0},{2,3},{3,2},{4,5},{5,4},{6,7},{7,6},{8,9},{9,8},{10,11... | collective-permute-start | bytes 3145736 | tf_op jit(solution)/shard_map/ppermute | solution.py:104
  (26 other events, 147.8 us)

commit v4 on v3

--- a/solution.py
+++ b/solution.py
@@ -7,7 +7,6 @@
 from jax.experimental.pallas import tpu as pltpu
 from jax.sharding import PartitionSpec as P
 
-PAIRS = 2
 VMEM_BYTES = 40 * 1024 * 1024
 
 
@@ -111,10 +110,6 @@
     else:
         pairs = [(i, i - 1) for i in range(1, count - least)]
     return lax.ppermute(value, axis, pairs)
-
-
-def after(value, *others):
-    return lax.optimization_barrier((value,) + others)[0]
 
 
 def params():
@@ -206,30 +201,30 @@
     )(first[None].astype(jnp.int32), message)
 
 
-def layer_sum_kernel(got_a, kept_a, far_a, got_b, kept_b, far_b, sent_ref, held_ref):
+def layer_sum_kernel(got_a, kept_a, far_a, got_b, kept_b, far_b, own_ref, *sent_refs):
     half = far_a.shape[1]
-    rows = sent_ref.shape[1]
+    rows = own_ref.shape[0]
     for side, (got, kept, far) in enumerate(((got_a, kept_a, far_a), (got_b, kept_b, far_b))):
         lanes = slice(side * half, (side + 1) * half)
-        for n in range(2 * sent_ref.shape[0]):
+        for n in range(1 + len(sent_refs)):
             at = slice(n * rows, (n + 1) * rows)
             total = got[at, :half].astype(jnp.float32) + kept[at, :half].astype(jnp.float32)
             total = total + far[at, :].astype(jnp.float32)
-            if n % 2:
-                sent_ref[n // 2, :, lanes] = total.astype(jnp.bfloat16)
+            if n:
+                sent_refs[n - 1][:, lanes] = total.astype(jnp.bfloat16)
             else:
-                held_ref[n // 2, :, lanes] = total
+                own_ref[:, lanes] = total
 
 
 def layer_sum(terms_a, terms_b, blocks):
     rows, half = terms_a[2].shape
-    cut = (blocks // 2, rows // blocks, 2 * half)
+    cut = (rows // blocks, 2 * half)
     return pl.pallas_call(
         layer_sum_kernel,
-        out_shape=[jax.ShapeDtypeStruct(cut, jnp.bfloat16), jax.ShapeDtypeStruct(cut, jnp.float32)],
+        out_shape=[jax.ShapeDtypeStruct(cut, jnp.float32)] + [jax.ShapeDtypeStruct(cut, jnp.bfloat16)] * (blocks - 1),
         grid=(1,),
         in_specs=[pl.BlockSpec((rows, half), lambda i: (0, 0)) for _ in range(6)],
-        out_specs=[pl.BlockSpec(cut, lambda i: (0, 0, 0))] * 2,
+        out_specs=[pl.BlockSpec(cut, lambda i: (0, 0))] * blocks,
         compiler_params=params(),
         cost_estimate=cost(rows, 4, half),
         name="layer_sum",
@@ -403,22 +398,32 @@
     half = model_width // dp_count
     group = dp_count * tok_count
     tokens = lat_count * group
-    width = half // (PAIRS * lay_count)
+    width = half // lay_count
     side = width // 2
     f32, bf16 = jnp.float32, jnp.bfloat16
     first = lat_here * local_blocks
 
     def columns(rows, which):
         return lax.dynamic_slice_in_dim(rows, which * half, half, axis=1)
+
+    def places(names, offset, fine=1, sub=0):
+        return [(offset + (lay_here ^ r)) * fine + sub for r in names]
+
+    def weight_places(names):
+        return jnp.stack(places(names, dp_here * lay_count))
 
     pre_rows = jnp.swapaxes(pre_codes[0], 0, 1).reshape(active_count * tok_count, block_size)
     id_rows = jnp.pad(block_ids[0].T, ((0, 16 - active_count), (0, 0))).astype(bf16)
     own = jnp.concatenate([pre_rows, id_rows], axis=0)
     message = jnp.stack([own] + [flip(own, "latent", r) for r in range(1, lat_count)])
 
+    at = places((1, 3), dp_here * lay_count, 2, 0) + places((2, 3), dp_here * lay_count, 2, 1)
+    send_weights = gather_columns(decoder, jnp.stack(at), side)
+
     acts = jnp.concatenate(
         [columns(activations[0], dp_here), flip(columns(activations[0], 1 - dp_here), "dp", 1)]
     )
+    message, acts, send_weights = lax.optimization_barrier((message, acts, send_weights))
     up, down = [acts], [acts]
 
     def next_hops():
@@ -426,81 +431,42 @@
         up.append(hop(up[-1], "latent", 1, step - 1))
         down.append(hop(down[-1], "latent", -1, step - 1))
 
-    def places(pair, names, offset, fine=1, sub=0):
-        return [(offset + pair * lay_count + (lay_here ^ r)) * fine + sub for r in names]
-
-    def weight_places(pair, names):
-        return jnp.stack(places(pair, names, dp_here * (half // width)))
-
-    wanted = [((1, 3), 0), ((2, 3), 1), ((0, 2), 0), ((0, 1), 1)]
-    at = [
-        c for p in range(PAIRS) for names, n in wanted for c in places(p, names, dp_here * (half // width), 2, n)
-    ]
-    weights = gather_columns(decoder, jnp.stack(at), side)
-    goal_at = [which * (half // width) + p * lay_count + lay_here for which in (dp_here, 1 - dp_here) for p in range(PAIRS)]
-    goals = gather_columns(target, jnp.stack(goal_at), width)
-    span = PAIRS * width
-    goals = jnp.concatenate([goals[:, :span], flip(goals[:, span:], "dp", 1)])
-
     message = jnp.stack([message, flip(message, "dp", 1)], axis=1)
     message = message.reshape(lat_count * dp_count, own.shape[0], block_size)
-    message, acts_now, weights = lax.optimization_barrier((message, acts, weights))
-    up, down = [acts_now], [acts_now]
     next_hops()
 
+    at = places((0, 2), dp_here * lay_count, 2, 0) + places((0, 1), dp_here * lay_count, 2, 1)
+    keep_weights = gather_columns(decoder, jnp.stack(at), side)
+    goals = gather_columns(target, jnp.stack([which * lay_count + lay_here for which in (dp_here, 1 - dp_here)]), width)
+    goals = jnp.concatenate([goals[:, :width], flip(goals[:, width:], "dp", 1)])
+
     codes = spread_codes(message, first, lat_rows)
 
-    def rows_for(spread, pair, n):
-        cols = weights[:, (4 * pair + n) * width:(4 * pair + n + 1) * width]
-        return jnp.dot(spread, cols, preferred_element_type=f32).astype(bf16)
-
-    parts, got = [], []
-    for p in range(PAIRS):
-        if p == 1:
-            codes, up[1], down[1] = lax.optimization_barrier((codes, up[1], down[1]))
-            if lat_count > 2:
-                next_hops()
-        sent = rows_for(codes, p, 0), rows_for(codes, p, 1)
-        got.append((flip(sent[0], "layer", 1), flip(sent[1], "layer", 2)))
-        parts.append((rows_for(codes, p, 2), rows_for(codes, p, 3)))
+    def rows_for(spread, weights, n):
+        return jnp.dot(spread, weights[:, n * width:(n + 1) * width], preferred_element_type=f32).astype(bf16)
+
+    got = flip(rows_for(codes, send_weights, 0), "layer", 1), flip(rows_for(codes, send_weights, 1), "layer", 2)
+    keep_codes = codes
+    if lat_count > 2:
+        keep_codes, up[1], down[1] = lax.optimization_barrier((codes, up[1], down[1]))
+        next_hops()
+    kept = rows_for(keep_codes, keep_weights, 0), rows_for(keep_codes, keep_weights, 1)
 
     def add(one, two):
         return (one[:, side:].astype(f32) + two[:, side:].astype(f32)).astype(bf16)
 
-    lat_bits = [1 << i for i in range(lat_count.bit_length() - 1)]
-    own_errors = []
-    for p in range(PAIRS):
-        kept = parts[p]
-        far = [flip(add(got[p][n], kept[n]), "layer", 2 - n) for n in range(2)]
-        if p == 0 and len(up) > 2:
-            up[2], down[2], far[0] = lax.optimization_barrier((up[2], down[2], far[0]))
-        sent, held = layer_sum((got[p][0], kept[0], far[0]), (got[p][1], kept[1], far[1]), lat_count)
-        near = flip(sent, "latent", 1)
-        terms = [held, near]
-        for bit in lat_bits[1:]:
-            cut = [t.reshape((-1, 2) + t.shape[1:]) for t in terms]
-            out = sum(c[:, 1].astype(f32) for c in cut).astype(bf16)
-            terms = [c[:, 0] for c in cut] + [flip(out, "latent", bit)]
-        total = sum(t[0].astype(f32) for t in terms)
-        own_errors.append(((total - goals[:, p * width:(p + 1) * width].astype(f32)) / tok_count).astype(bf16))
-
-    gathered = []
-    for p in range(PAIRS):
-        rows = own_errors[p][None]
-        for bit in lat_bits[:0:-1]:
-            rows = jnp.stack([rows, flip(rows, "latent", bit)], axis=1).reshape((-1,) + rows.shape[1:])
-        gathered.append(jnp.stack([rows, flip(rows, "latent", 1)], axis=1).reshape(tokens, width))
-    if len(up) < lat_count:
-        up[-1], down[-1], gathered[-1] = lax.optimization_barrier((up[-1], down[-1], gathered[-1]))
+    far = [flip(add(got[n], kept[n]), "layer", 2 - n) for n in range(2)]
+    far, goals, up[-1], down[-1] = lax.optimization_barrier((far, goals, up[-1], down[-1]))
+
+    total, *sent = layer_sum((got[0], kept[0], far[0]), (got[1], kept[1], far[1]), lat_count)
+    for r in range(1, lat_count):
+        total = total + flip(sent[r - 1], "latent", r).astype(f32)
+    errors = ((total - goals.astype(f32)) / tok_count).astype(bf16)
+    rows = jnp.concatenate([errors] + [flip(errors, "latent", r) for r in range(1, lat_count)])
+    rows, up[-1], down[-1] = lax.optimization_barrier((rows, up[-1], down[-1]))
     while len(up) < lat_count:
         next_hops()
-
-    pieces = []
-    for rows in gathered:
-        one, two = flip(rows, "layer", 1), flip(rows, "layer", 2)
-        one, two = lax.optimization_barrier((one, two))
-        three = (flip(two[:, :side], "layer", 1), flip(one[:, side:], "layer", 2))
-        pieces.append([(rows,), (one,), (two,), lax.optimization_barrier(three)])
+    one, two = flip(rows, "layer", 1), flip(rows, "layer", 2)
 
     cut = message.reshape(tokens // tok_count, own.shape[0], block_size)
     pre_lanes = cut[:, :active_count * tok_count].reshape(-1, active_count, tok_count, block_size)
@@ -511,21 +477,27 @@
     ids_wide = jnp.broadcast_to(ids[:, None, :], (active_count, 16, tokens))
     ids = ids.astype(f32)
 
-    grads = []
-    dec = None
-    for p in range(PAIRS):
-        for names in ((0, 1, 2, 3),) if p < PAIRS - 1 else ((0, 1, 2), (3,)):
-            here = [pieces[p][r] for r in names]
-            grads.append(code_grad(here, ids, decoder, first, weight_places(p, names), block_size))
-            dec = decoder_part(here, ids_wide, code_lanes, first, jnp.stack(places(p, names, 0)), lat_rows, half, dec)
-            if p + 1 < PAIRS:
-                pieces[p + 1][3], grads[-1], dec = lax.optimization_barrier((pieces[p + 1][3], grads[-1], dec))
-    grad = sum(grads)
-    pre_grad = pre_grad_spread(grad, flip(grad, "dp", 1), ids_wide, pre_lanes, first, lat_rows, tok_count)
+    def grads_of(here, names, dec):
+        grad = code_grad(here, ids, decoder, first, weight_places(names), block_size)
+        where = jnp.stack(places(names, 0))
+        return grad, decoder_part(here, ids_wide, code_lanes, first, where, lat_rows, half, dec)
+
+    grad, dec = grads_of([(rows,)], (0,), None)
+    one, two, grad, dec, up[-1], down[-1] = lax.optimization_barrier((one, two, grad, dec, up[-1], down[-1]))
+    three = flip(two[:, :side], "layer", 1), flip(one[:, side:], "layer", 2)
     along = [acts] + [down[k] + up[lat_count - k] for k in range(1, lat_count)]
     along = jnp.stack(along)
-    along = [lax.dynamic_index_in_dim(along, lax.rem((lat_here ^ r) - lat_here + lat_count, lat_count), 0, False) for r in range(lat_count)]
-    enc = jnp.dot(pre_grad, jnp.concatenate(along), preferred_element_type=f32).astype(bf16)
+    along = [
+        lax.dynamic_index_in_dim(along, lax.rem((lat_here ^ r) - lat_here + lat_count, lat_count), 0, False)
+        for r in range(lat_count)
+    ]
+    along = jnp.concatenate(along)
+    more, dec = grads_of([(one,), (two,)], (1, 2), dec)
+    three, more, dec, along = lax.optimization_barrier((three, more, dec, along))
+    last, dec = grads_of([three], (3,), dec)
+    grad = grad + more + last
+    pre_grad = pre_grad_spread(grad, flip(grad, "dp", 1), ids_wide, pre_lanes, first, lat_rows, tok_count)
+    enc = jnp.dot(pre_grad, along, preferred_element_type=f32).astype(bf16)
     return dec[None], enc[None]
 
 
@@ -548,7 +520,7 @@
         and lat_count & (lat_count - 1) == 0
         and tok_count == block_size
         and lat_count * dp_count * 16 <= tok_count
-        and model_width % (dp_count * 2 * PAIRS * lay_count * 128) == 0
+        and model_width % (dp_count * 2 * lay_count * 128) == 0
         and all_blocks <= 256
     )
     plan = dense_plan if dense else slot_plan

time: 227 us -> 196 us (0.86)
  starting transfers between devices: 70.3 us -> 47.5 us
  waiting for transfers between devices: 48.7 us -> 67.8 us
  local copies, waits for them, and re-layouts: 18.3 us -> 5.32 us
  Pallas kernels: 55.5 us -> 48.3 us
  other arithmetic: 10.5 us -> 4.74 us
    ppermute x6, waiting for transfers between devices: 2.27 us -> 28.6 us  [hop(): return lax.ppermute(value, axis, pairs)]
    ppermute x31 -> x21, starting transfers between devices: 58.7 us -> 37.5 us  [flip(): return lax.ppermute(value, axis, [(i, i ^ bit) for i in range(count)])]
    unnamed x31 -> x23, local copies, waits for them, and re-layouts: 11.5 us -> 2.9 us
    ppermute x31 -> x21, waiting for transfers between devices: 46.4 us -> 39.2 us  [flip(): return lax.ppermute(value, axis, [(i, i ^ bit) for i in range(count)])]
    another operation x5 -> x4, other arithmetic: 6.27 us -> 0.87 us  [dense_plan(): along = jnp.stack(along)]
    pallas_call x2 -> x3, Pallas kernels: 11.6 us -> 8.39 us  [gather_columns(): pl.pallas_call(gather_kernel, out_shape=jax.ShapeDtypeStruct((rows, count...]
    pallas_call x2 -> x1, Pallas kernels: 2.64 us -> 0.37 us  [layer_sum(): pl.pallas_call(layer_sum_kernel, out_shape=[jax.ShapeDtypeStruct(cut, jnp...]
    dot_general x9 -> x5, matrix products: 20.9 us -> 20.2 us  [the longest x1 10.9 us: dense_plan(): enc = jnp.dot(pre_grad, along, preferred_element_type=f32).astype(bf16)]
  transfers between devices with their start and end apart: 37 -> 27, of which waited for: 14 -> 11; matrix products, arithmetic and copies ran while one was open for 13% -> 7% of each run, Pallas kernels for 24% -> 21%
where the time goes in v4:
time: 196 us; the launch traced here: 195 us
  waiting for transfers between devices  67.8 us (35%)
  Pallas kernels  48.3 us (25%)
  starting transfers between devices  47.5 us (24%)
  matrix products  20.2 us (10%)
  local copies, waits for them, and re-layouts  5.32 us (3%)
  other arithmetic  4.74 us (2%)
    ppermute x21, waiting for transfers between devices, flip(): return lax.ppermute(value, axis, [(i, i ^ bit) for i in range(count)])  39.2 us
    ppermute x21, starting transfers between devices, flip(): return lax.ppermute(value, axis, [(i, i ^ bit) for i in range(count)])  37.5 us
    ppermute x6, waiting for transfers between devices, hop(): return lax.ppermute(value, axis, pairs)  28.6 us
    pallas_call x3, Pallas kernels, code_grad(): pl.pallas_call(functools.partial(code_grad_kernel, size, [len(p) for p in...  18.1 us
    pallas_call x3, Pallas kernels, decoder_part(): pl.pallas_call(functools.partial(decoder_kernel, size, [len(p) for p in p...  17.9 us
    dot_general x1, matrix products, dense_plan(): enc = jnp.dot(pre_grad, along, preferred_element_type=f32).astype(bf16)  10.9 us
    ppermute x6, starting transfers between devices, hop(): return lax.ppermute(value, axis, pairs)  10 us
    dot_general x4, matrix products, rows_for(): jnp.dot(spread, weights[:, n * width:(n + 1) * width], preferred_element_...  9.3 us
  transfers between devices with their start and end apart: 27, of which 11 were waited for; matrix products, arithmetic and copies ran while one was open for 7% of the time, Pallas kernels for 21%

profile of v4, /device:TPU:1, one launch (start us, length us, event | category | flops | bytes accessed | tf_op | source)
XLA Modules:
  0.0 195.0 jit_solution(5538335792626126854)
XLA Ops:
  3.6 3.8 %collective-permute-start.1 = (bf16[272,128]{1,0:T(8,128)(2,1)S(1)}, bf16[272,128]{1,0:T(8,128)(2,1)S(1)}, u32[]{:S(2)}, u32[]{:S(2)}) collective-permute-start(bf16[272,128]{1,0:T(8,128)(2,1)S(1)} %get-tuple-element.70), channel_id=1, source_target_pairs={{0,4},{2,6},{4,0},{6,2},{1,5},{3,7},{5,1},{7,3},{8,12},{10,14},{12... | collective-permute-start | bytes 208904 | tf_op jit(solution)/shard_map/ppermute | solution.py:103
  8.8 3.9 %gather_columns.3 = bf16[2048,1024]{1,0:T(8,128)(2,1)S(1)} custom-call(s32[4]{0:T(128)S(1)} %pad_add_fusion.1.scalar_ref, bf16[1,2048,4096]{2,1,0:T(8,128)(2,1)} %refs_0_.5), custom_call_target="tpu_custom_call" | custom-call | flops 1048576 | bytes 1050112 | tf_op jit(solution)/shard_map/gather_columns/pallas_call | solution.py:139
  15.7 3.9 %gather_columns.4 = bf16[2048,1024]{1,0:T(8,128)(2,1)S(1)} custom-call(s32[4]{0:T(128)S(1)} %pad_add_fusion.2.scalar_ref, bf16[1,2048,4096]{2,1,0:T(8,128)(2,1)} %refs_0_.5), custom_call_target="tpu_custom_call" | custom-call | flops 1048576 | bytes 1050112 | tf_op jit(solution)/shard_map/gather_columns/pallas_call | solution.py:139
  21.1 4.1 %collective-permute-start.6 = (bf16[256,2048]{1,0:T(8,128)(2,1)S(1)}, bf16[256,2048]{1,0:T(8,128)(2,1)S(1)}, u32[]{:S(2)}, u32[]{:S(2)}) collective-permute-start(bf16[256,2048]{1,0:T(8,128)(2,1)S(1)} %pad_maximum_fusion.2), channel_id=1, source_target_pairs={{0,2},{2,4},{4,6},{1,3},{3,5},{5,7},{8,10},{10,12},{12,14},{9,11},... | collective-permute-start | bytes 3145736 | tf_op jit(solution)/shard_map/ppermute | solution.py:112
  25.3 2.6 %spread_codes.1 = bf16[1024,2048]{1,0:T(8,128)(2,1)S(1)} custom-call(s32[1]{0:T(128)} %bitcast.scalar_ref, bf16[8,272,128]{2,1,0:T(8,128)(2,1)S(1)} %bitcast.71), custom_call_target="tpu_custom_call" | custom-call | flops 1048576 | bytes 1050112 | tf_op jit(solution)/shard_map/spread_codes/pallas_call | solution.py:185
  35.3 11.2 %collective-permute-done.7 = bf16[256,2048]{1,0:T(8,128)(2,1)S(1)} collective-permute-done((bf16[256,2048]{1,0:T(8,128)(2,1)S(1)}, bf16[256,2048]{1,0:T(8,128)(2,1)S(1)}, u32[]{:S(2)}, u32[]{:S(2)}) %collective-permute-start.7) | collective-permute-done | bytes 1048608 | tf_op jit(solution)/shard_map/ppermute | solution.py:112
  51.9 2.3 %fusion.14.kept_a = bf16[1024,512]{1,0:T(8,128)(2,1)S(1)} fusion(bf16[1024,2048]{1,0:T(8,128)(2,1)S(1)} %spread_codes.1, bf16[2048,1024]{1,0:T(8,128)(2,1)S(1)} %gather_columns.4), kind=kOutput, calls=%fused_computation.13 | convolution fusion | flops 2148007936 | bytes 7340032 | tf_op jit(solution)/shard_map/dot_general | solution.py:446
  59.0 3.1 %collective-permute-start.11 = (bf16[128,512]{1,0:T(8,128)(2,1)S(1)}, bf16[128,512]{1,0:T(8,128)(2,1)S(1)}, u32[]{:S(2)}, u32[]{:S(2)}) collective-permute-start(bf16[128,512]{1,0:T(8,128)(2,1)S(1)} %get-tuple-element.68), channel_id=1, source_target_pairs={{0,1},{1,0},{2,3},{3,2},{4,5},{5,4},{6,7},{7,6},{8,9},{9,8},{10,11... | collective-permute-start | bytes 393224 | tf_op jit(solution)/shard_map/ppermute | solution.py:103
  63.1 6.0 %collective-permute-done.8.far_a = bf16[1024,256]{1,0:T(8,128)(2,1)S(1)} collective-permute-done((bf16[1024,256]{1,0:T(8,128)(2,1)S(1)}, bf16[1024,256]{1,0:T(8,128)(2,1)S(1)}, u32[]{:S(2)}, u32[]{:S(2)}) %collective-permute-start.8) | collective-permute-done | bytes 524320 | tf_op jit(solution)/shard_map/ppermute | solution.py:103
  69.1 7.8 %collective-permute-done.13 = bf16[256,2048]{1,0:T(8,128)(2,1)S(1)} collective-permute-done((bf16[256,2048]{1,0:T(8,128)(2,1)S(1)}, bf16[256,2048]{1,0:T(8,128)(2,1)S(1)}, u32[]{:S(2)}, u32[]{:S(2)}) %collective-permute-start.13) | collective-permute-done | bytes 1048608 | tf_op jit(solution)/shard_map/ppermute | solution.py:112
  78.5 2.4 %collective-permute-start.16 = (bf16[256,512]{1,0:T(8,128)(2,1)S(1)}, bf16[256,512]{1,0:T(8,128)(2,1)S(1)}, u32[]{:S(2)}, u32[]{:S(2)}) collective-permute-start(bf16[256,512]{1,0:T(8,128)(2,1)S(1)} %get-tuple-element.42), channel_id=1, source_target_pairs={{0,6},{2,4},{4,2},{6,0},{1,7},{3,5},{5,3},{7,1},{8,14},{10,12},{12... | collective-permute-start | bytes 786440 | tf_op jit(solution)/shard_map/ppermute | solution.py:103
  80.9 4.7 %collective-permute-done.14 = bf16[256,512]{1,0:T(8,128)(2,1)S(1)} collective-permute-done((bf16[256,512]{1,0:T(8,128)(2,1)S(1)}, bf16[256,512]{1,0:T(8,128)(2,1)S(1)}, u32[]{:S(2)}, u32[]{:S(2)}) %collective-permute-start.14) | collective-permute-done | bytes 262176 | tf_op jit(solution)/shard_map/ppermute | solution.py:103
  85.6 11.4 %collective-permute-done.15 = bf16[256,512]{1,0:T(8,128)(2,1)S(1)} collective-permute-done((bf16[256,512]{1,0:T(8,128)(2,1)S(1)}, bf16[256,512]{1,0:T(8,128)(2,1)S(1)}, u32[]{:S(2)}, u32[]{:S(2)}) %collective-permute-start.15) | collective-permute-done | bytes 262176 | tf_op jit(solution)/shard_map/ppermute | solution.py:103
  97.5 9.7 %collective-permute-start.18 = (bf16[256,512]{1,0:T(8,128)(2,1)S(1)}, bf16[256,512]{1,0:T(8,128)(2,1)S(1)}, u32[]{:S(2)}, u32[]{:S(2)}) collective-permute-start(bf16[256,512]{1,0:T(8,128)(2,1)S(1)} %multiply_convert_fusion), channel_id=1, source_target_pairs={{0,4},{2,6},{4,0},{6,2},{1,5},{3,7},{5,1},{7,3},{8,12},{10,14},{12... | collective-permute-start | bytes 786440 | tf_op jit(solution)/shard_map/ppermute | solution.py:103
  108.0 14.0 %collective-permute-done.18 = bf16[256,512]{1,0:T(8,128)(2,1)S(1)} collective-permute-done((bf16[256,512]{1,0:T(8,128)(2,1)S(1)}, bf16[256,512]{1,0:T(8,128)(2,1)S(1)}, u32[]{:S(2)}, u32[]{:S(2)}) %collective-permute-start.18) | collective-permute-done | bytes 262176 | tf_op jit(solution)/shard_map/ppermute | solution.py:103
  127.9 5.3 %code_grad.3 = f32[2,128,1024]{2,1,0:T(8,128)S(1)} custom-call(s32[2]{0:T(128)S(1)} %get-tuple-element.71.scalar_ref, f32[2,1024]{1,0:T(2,128)S(1)} %get-tuple-element.65.ids_ref, bf16[1,2048,4096]{2,1,0:T(8,128)(2,1)} %refs_0_.5, bf16[1024,512]{1,0:T(8,128)(2,1)S(1)} %pad_maximum_fusion.3.refs_1_.refs_0_), custom_call_target="tpu_custom_call" | custom-call | flops 536870912 | bytes 1835008 | tf_op jit(solution)/shard_map/code_grad/pallas_call | solution.py:284
  133.3 5.1 %decoder_part.3.refs_0_ = bf16[2048,2048]{1,0:T(8,128)(2,1)} custom-call(s32[2]{0:T(128)S(1)} %get-tuple-element.72.scalar_ref, bf16[2,16,1024]{2,1,0:T(8,128)(2,1)S(1)} %broadcast_in_dim.12.ids_ref, bf16[2,128,1024]{2,1,0:T(8,128)(2,1)S(1)} %broadcast_maximum_fusion.codes_ref, bf16[1024,512]{1,0:T(8,128)(2,1)S(1)} %pad_maximum_fusion.3.refs_1_.refs_0_), custom_call_target="tpu_custom_call" | custom-call | flops 536870912 | bytes 1835008 | tf_op jit(solution)/shard_map/decoder_part/pallas_call | solution.py:333
  138.5 8.7 %collective-permute-done.23 = bf16[256,2048]{1,0:T(8,128)(2,1)S(1)} collective-permute-done((bf16[256,2048]{1,0:T(8,128)(2,1)}, bf16[256,2048]{1,0:T(8,128)(2,1)S(1)}, u32[]{:S(2)}, u32[]{:S(2)}) %collective-permute-start.23) | collective-permute-done | bytes 1048608 | tf_op jit(solution)/shard_map/ppermute | solution.py:112
  149.1 7.5 %code_grad.4 = f32[2,128,1024]{2,1,0:T(8,128)S(1)} custom-call(s32[3]{0:T(128)S(1)} %get-tuple-element.73.scalar_ref, f32[2,1024]{1,0:T(2,128)S(1)} %get-tuple-element.65.ids_ref, bf16[1,2048,4096]{2,1,0:T(8,128)(2,1)} %refs_0_.5, bf16[1,2048,4096]{2,1,0:T(8,128)(2,1)} %refs_0_.5, bf16[1024,512]{1,0:T(8,128)(2,1)S(1)} %collective-permute-done.20.refs_2_.refs_1_, ...), custom_call_target="tpu_custom_call" | custom-call | flops 1073741824 | bytes 2621440 | tf_op jit(solution)/shard_map/code_grad/pallas_call | solution.py:284
  156.5 7.8 %decoder_part.4.refs_0_ = bf16[2048,2048]{1,0:T(8,128)(2,1)} custom-call(s32[3]{0:T(128)S(1)} %get-tuple-element.74.scalar_ref, bf16[2,16,1024]{2,1,0:T(8,128)(2,1)S(1)} %broadcast_in_dim.12.ids_ref, bf16[2,128,1024]{2,1,0:T(8,128)(2,1)S(1)} %broadcast_maximum_fusion.codes_ref, ...), custom_call_target="tpu_custom_call", output_to_operand_aliasing={{}: (3, {})} | custom-call | flops 1073741824 | bytes 2621440 | tf_op jit(solution)/shard_map/decoder_part/pallas_call | solution.py:333
  165.0 5.3 %code_grad.5 = f32[2,128,1024]{2,1,0:T(8,128)S(1)} custom-call(s32[2]{0:T(128)S(1)} %pad_add_fusion.8.scalar_ref, f32[2,1024]{1,0:T(2,128)S(1)} %get-tuple-element.65.ids_ref, bf16[1,2048,4096]{2,1,0:T(8,128)(2,1)} %refs_0_.5, bf16[1024,256]{1,0:T(8,128)(2,1)S(1)} %collective-permute-done.24.refs_1_, bf16[1024,256]{1,0:T(8,128)(2,1)S(1)} %collective-permute-done.25.refs_2_), custom_call_target="tpu_custom_call" | custom-call | flops 536870912 | bytes 1835008 | tf_op jit(solution)/shard_map/code_grad/pallas_call | solution.py:284
  170.6 7.5 %collective-permute-start.26 = (f32[2,128,1024]{2,1,0:T(8,128)S(1)}, f32[2,128,1024]{2,1,0:T(8,128)S(1)}, u32[]{:S(2)}, u32[]{:S(2)}) collective-permute-start(f32[2,128,1024]{2,1,0:T(8,128)S(1)} %add_add_fusion.own_ref), channel_id=1, source_target_pairs={{0,1},{1,0},{2,3},{3,2},{4,5},{5,4},{6,7},{7,6},{8,9},{9,8},{10,11... | collective-permute-start | bytes 3145736 | tf_op jit(solution)/shard_map/ppermute | solution.py:103
  178.1 5.1 %decoder_part.5 = bf16[2048,2048]{1,0:T(8,128)(2,1)} custom-call(s32[2]{0:T(128)S(1)} %pad_add_fusion.scalar_ref, bf16[2,16,1024]{2,1,0:T(8,128)(2,1)S(1)} %broadcast_in_dim.12.ids_ref, bf16[2,128,1024]{2,1,0:T(8,128)(2,1)S(1)} %broadcast_maximum_fusion.codes_ref, bf16[2048,2048]{1,0:T(8,128)(2,1)} %decoder_part.4.refs_0_, ...), custom_call_target="tpu_custom_call", output_to_operand_aliasing={{}: (3, {})} | custom-call | flops 536870912 | bytes 1835008 | tf_op jit(solution)/shard_map/decoder_part/pallas_call | solution.py:333
  184.1 10.9 %convert_bitcast_fusion = bf16[1,2048,2048]{2,1,0:T(8,128)(2,1)} fusion(bf16[2048,1024]{1,0:T(8,128)(2,1)S(1)} %pre_grad_spread.1, bf16[1024,2048]{1,0:T(8,128)(2,1)S(1)} %pad_maximum_fusion.1), kind=kOutput, calls=%fused_computation | convolution fusion | flops 8594128896 | bytes 16777216 | tf_op jit(solution)/shard_map/dot_general | solution.py:500
  (105 shorter events, 39.9 us)
Async XLA Ops:
  1.9 12.8 %collective-permute-start.3 = (bf16[128,2048]{1,0:T(8,128)(2,1)S(1)}, bf16[128,2048]{1,0:T(8,128)(2,1)S(1)}, u32[]{:S(2)}, u32[]{:S(2)}) collective-permute-start(bf16[128,2048]{1,0:T(8,128)(2,1)S(1)} %get-tuple-element.64), channel_id=1, source_target_pairs={{0,1},{1,0},{2,3},{3,2},{4,5},{5,4},{6,7},{7,6},{8,9},{9,8},{10,11... | collective-permute-start | bytes 1572872 | tf_op jit(solution)/shard_map/ppermute | solution.py:103
  3.6 11.1 %collective-permute-start.1 = (bf16[272,128]{1,0:T(8,128)(2,1)S(1)}, bf16[272,128]{1,0:T(8,128)(2,1)S(1)}, u32[]{:S(2)}, u32[]{:S(2)}) collective-permute-start(bf16[272,128]{1,0:T(8,128)(2,1)S(1)} %get-tuple-element.70), channel_id=1, source_target_pairs={{0,4},{2,6},{4,0},{6,2},{1,5},{3,7},{5,1},{7,3},{8,12},{10,14},{12... | collective-permute-start | bytes 208904 | tf_op jit(solution)/shard_map/ppermute | solution.py:103
  14.9 10.3 %collective-permute-start.4 = (bf16[4,272,128]{2,1,0:T(8,128)(2,1)S(1)}, bf16[4,272,128]{2,1,0:T(8,128)(2,1)S(1)}, u32[]{:S(2)}, u32[]{:S(2)}) collective-permute-start(bf16[4,272,128]{2,1,0:T(8,128)(2,1)S(1)} %pad_maximum_fusion.5), channel_id=1, source_target_pairs={{0,1},{1,0},{2,3},{3,2},{4,5},{5,4},{6,7},{7,6},{8,9},{9,8},{10,11... | collective-permute-start | bytes 835592 | tf_op jit(solution)/shard_map/ppermute | solution.py:103
  19.6 26.9 %collective-permute-start.7 = (bf16[256,2048]{1,0:T(8,128)(2,1)S(1)}, bf16[256,2048]{1,0:T(8,128)(2,1)S(1)}, u32[]{:S(2)}, u32[]{:S(2)}) collective-permute-start(bf16[256,2048]{1,0:T(8,128)(2,1)S(1)} %pad_maximum_fusion.2), channel_id=1, source_target_pairs={{2,0},{4,2},{6,4},{3,1},{5,3},{7,5},{10,8},{12,10},{14,12},{11,9},... | collective-permute-start | bytes 3145736 | tf_op jit(solution)/shard_map/ppermute | solution.py:112
  21.1 26.2 %collective-permute-start.6 = (bf16[256,2048]{1,0:T(8,128)(2,1)S(1)}, bf16[256,2048]{1,0:T(8,128)(2,1)S(1)}, u32[]{:S(2)}, u32[]{:S(2)}) collective-permute-start(bf16[256,2048]{1,0:T(8,128)(2,1)S(1)} %pad_maximum_fusion.2), channel_id=1, source_target_pairs={{0,2},{2,4},{4,6},{1,3},{3,5},{5,7},{8,10},{10,12},{12,14},{9,11},... | collective-permute-start | bytes 3145736 | tf_op jit(solution)/shard_map/ppermute | solution.py:112
  30.3 24.2 %collective-permute-start.5 = (bf16[1024,512]{1,0:T(8,128)(2,1)S(1)}, bf16[1024,512]{1,0:T(8,128)(2,1)S(1)}, u32[]{:S(2)}, u32[]{:S(2)}) collective-permute-start(bf16[1024,512]{1,0:T(8,128)(2,1)S(1)} %fusion.8), channel_id=1, source_target_pairs={{0,8},{8,0},{16,24},{24,16},{1,9},{9,1},{17,25},{25,17},{2,10},{10... | collective-permute-start | bytes 3145736 | tf_op jit(solution)/shard_map/ppermute | solution.py:103
  34.0 23.9 %collective-permute-start.9 = (bf16[1024,512]{1,0:T(8,128)(2,1)S(1)}, bf16[1024,512]{1,0:T(8,128)(2,1)S(1)}, u32[]{:S(2)}, u32[]{:S(2)}) collective-permute-start(bf16[1024,512]{1,0:T(8,128)(2,1)S(1)} %fusion.11), channel_id=1, source_target_pairs={{0,16},{8,24},{16,0},{24,8},{1,17},{9,25},{17,1},{25,9},{2,18},{10... | collective-permute-start | bytes 3145736 | tf_op jit(solution)/shard_map/ppermute | solution.py:103
  47.4 21.7 %collective-permute-start.12 = (bf16[256,2048]{1,0:T(8,128)(2,1)S(1)}, bf16[256,2048]{1,0:T(8,128)(2,1)S(1)}, u32[]{:S(2)}, u32[]{:S(2)}) collective-permute-start(bf16[256,2048]{1,0:T(8,128)(2,1)S(1)} %collective-permute-done.6), channel_id=1, source_target_pairs={{2,4},{4,6},{3,5},{5,7},{10,12},{12,14},{11,13},{13,15},{18,20},{2... | collective-permute-start | bytes 3145736 | tf_op jit(solution)/shard_map/ppermute | solution.py:112
  48.1 28.8 %collective-permute-start.13 = (bf16[256,2048]{1,0:T(8,128)(2,1)S(1)}, bf16[256,2048]{1,0:T(8,128)(2,1)S(1)}, u32[]{:S(2)}, u32[]{:S(2)}) collective-permute-start(bf16[256,2048]{1,0:T(8,128)(2,1)S(1)} %collective-permute-done.7), channel_id=1, source_target_pairs={{2,0},{4,2},{3,1},{5,3},{10,8},{12,10},{11,9},{13,11},{18,16},{20,... | collective-permute-start | bytes 3145736 | tf_op jit(solution)/shard_map/ppermute | solution.py:112
  54.6 14.5 %collective-permute-start.8 = (bf16[1024,256]{1,0:T(8,128)(2,1)S(1)}, bf16[1024,256]{1,0:T(8,128)(2,1)S(1)}, u32[]{:S(2)}, u32[]{:S(2)}) collective-permute-start(bf16[1024,256]{1,0:T(8,128)(2,1)S(1)} %add_convert_fusion.1), channel_id=1, source_target_pairs={{0,16},{8,24},{16,0},{24,8},{1,17},{9,25},{17,1},{25,9},{2,18},{10... | collective-permute-start | bytes 1572872 | tf_op jit(solution)/shard_map/ppermute | solution.py:103
  58.0 11.1 %collective-permute-start.10 = (bf16[1024,256]{1,0:T(8,128)(2,1)S(1)}, bf16[1024,256]{1,0:T(8,128)(2,1)S(1)}, u32[]{:S(2)}, u32[]{:S(2)}) collective-permute-start(bf16[1024,256]{1,0:T(8,128)(2,1)S(1)} %add_convert_fusion), channel_id=1, source_target_pairs={{0,8},{8,0},{16,24},{24,16},{1,9},{9,1},{17,25},{25,17},{2,10},{10... | collective-permute-start | bytes 1572872 | tf_op jit(solution)/shard_map/ppermute | solution.py:103
  77.2 8.4 %collective-permute-start.14 = (bf16[256,512]{1,0:T(8,128)(2,1)S(1)}, bf16[256,512]{1,0:T(8,128)(2,1)S(1)}, u32[]{:S(2)}, u32[]{:S(2)}) collective-permute-start(bf16[256,512]{1,0:T(8,128)(2,1)S(1)} %get-tuple-element.40), channel_id=1, source_target_pairs={{0,2},{2,0},{4,6},{6,4},{1,3},{3,1},{5,7},{7,5},{8,10},{10,8},{12,... | collective-permute-start | bytes 786440 | tf_op jit(solution)/shard_map/ppermute | solution.py:103
  78.5 18.6 %collective-permute-start.15 = (bf16[256,512]{1,0:T(8,128)(2,1)S(1)}, bf16[256,512]{1,0:T(8,128)(2,1)S(1)}, u32[]{:S(2)}, u32[]{:S(2)}) collective-permute-start(bf16[256,512]{1,0:T(8,128)(2,1)S(1)} %get-tuple-element.41), channel_id=1, source_target_pairs={{0,4},{2,6},{4,0},{6,2},{1,5},{3,7},{5,1},{7,3},{8,12},{10,14},{12... | collective-permute-start | bytes 786440 | tf_op jit(solution)/shard_map/ppermute | solution.py:103
  78.5 18.6 %collective-permute-start.16 = (bf16[256,512]{1,0:T(8,128)(2,1)S(1)}, bf16[256,512]{1,0:T(8,128)(2,1)S(1)}, u32[]{:S(2)}, u32[]{:S(2)}) collective-permute-start(bf16[256,512]{1,0:T(8,128)(2,1)S(1)} %get-tuple-element.42), channel_id=1, source_target_pairs={{0,6},{2,4},{4,2},{6,0},{1,7},{3,5},{5,3},{7,1},{8,14},{10,12},{12... | collective-permute-start | bytes 786440 | tf_op jit(solution)/shard_map/ppermute | solution.py:103
  97.2 10.8 %collective-permute-start.19 = (bf16[256,512]{1,0:T(8,128)(2,1)S(1)}, bf16[256,512]{1,0:T(8,128)(2,1)S(1)}, u32[]{:S(2)}, u32[]{:S(2)}) collective-permute-start(bf16[256,512]{1,0:T(8,128)(2,1)S(1)} %multiply_convert_fusion), channel_id=1, source_target_pairs={{0,6},{2,4},{4,2},{6,0},{1,7},{3,5},{5,3},{7,1},{8,14},{10,12},{12... | collective-permute-start | bytes 786440 | tf_op jit(solution)/shard_map/ppermute | solution.py:103
  97.5 24.5 %collective-permute-start.18 = (bf16[256,512]{1,0:T(8,128)(2,1)S(1)}, bf16[256,512]{1,0:T(8,128)(2,1)S(1)}, u32[]{:S(2)}, u32[]{:S(2)}) collective-permute-start(bf16[256,512]{1,0:T(8,128)(2,1)S(1)} %multiply_convert_fusion), channel_id=1, source_target_pairs={{0,4},{2,6},{4,0},{6,2},{1,5},{3,7},{5,1},{7,3},{8,12},{10,14},{12... | collective-permute-start | bytes 786440 | tf_op jit(solution)/shard_map/ppermute | solution.py:103
  107.2 14.9 %collective-permute-start.17 = (bf16[256,512]{1,0:T(8,128)(2,1)S(1)}, bf16[256,512]{1,0:T(8,128)(2,1)}, u32[]{:S(2)}, u32[]{:S(2)}) collective-permute-start(bf16[256,512]{1,0:T(8,128)(2,1)S(1)} %multiply_convert_fusion), channel_id=1, source_target_pairs={{0,2},{2,0},{4,6},{6,4},{1,3},{3,1},{5,7},{7,5},{8,10},{10,8},{12,... | collective-permute-start | bytes 786440 | tf_op jit(solution)/shard_map/ppermute | solution.py:103
  123.1 24.1 %collective-permute-start.21 = (bf16[1024,512]{1,0:T(8,128)(2,1)S(1)}, bf16[1024,512]{1,0:T(8,128)(2,1)S(1)}, u32[]{:S(2)}, u32[]{:S(2)}) collective-permute-start(bf16[1024,512]{1,0:T(8,128)(2,1)S(1)} %pad_maximum_fusion.3.refs_1_.refs_0_), channel_id=1, source_target_pairs={{0,16},{8,24},{16,0},{24,8},{1,17},{9,25},{17,1},{25,9},{2,18},{10... | collective-permute-start | bytes 3145736 | tf_op jit(solution)/shard_map/ppermute | solution.py:103
  124.4 22.8 %collective-permute-start.20 = (bf16[1024,512]{1,0:T(8,128)(2,1)S(1)}, bf16[1024,512]{1,0:T(8,128)(2,1)S(1)}, u32[]{:S(2)}, u32[]{:S(2)}) collective-permute-start(bf16[1024,512]{1,0:T(8,128)(2,1)S(1)} %pad_maximum_fusion.3.refs_1_.refs_0_), channel_id=1, source_target_pairs={{0,8},{8,0},{16,24},{24,16},{1,9},{9,1},{17,25},{25,17},{2,10},{10... | collective-permute-start | bytes 3145736 | tf_op jit(solution)/shard_map/ppermute | solution.py:103
  125.6 12.9 %collective-permute-start.22 = (bf16[256,2048]{1,0:T(8,128)(2,1)}, bf16[256,2048]{1,0:T(8,128)(2,1)S(1)}, u32[]{:S(2)}, u32[]{:S(2)}) collective-permute-start(bf16[256,2048]{1,0:T(8,128)(2,1)} %copy-done.7), channel_id=1, source_target_pairs={{4,6},{5,7},{12,14},{13,15},{20,22},{21,23},{28,30},{29,31}} | collective-permute-start | bytes 3145736 | tf_op jit(solution)/shard_map/ppermute | solution.py:112
  126.3 20.9 %collective-permute-start.23 = (bf16[256,2048]{1,0:T(8,128)(2,1)}, bf16[256,2048]{1,0:T(8,128)(2,1)S(1)}, u32[]{:S(2)}, u32[]{:S(2)}) collective-permute-start(bf16[256,2048]{1,0:T(8,128)(2,1)} %copy-done.9), channel_id=1, source_target_pairs={{2,0},{3,1},{10,8},{11,9},{18,16},{19,17},{26,24},{27,25}} | collective-permute-start | bytes 3145736 | tf_op jit(solution)/shard_map/ppermute | solution.py:112
  147.5 17.4 %collective-permute-start.25 = (bf16[1024,256]{1,0:T(8,128)(2,1)S(1)}, bf16[1024,256]{1,0:T(8,128)(2,1)S(1)}, u32[]{:S(2)}, u32[]{:S(2)}) collective-permute-start(bf16[1024,256]{1,0:T(8,128)(2,1)S(1)} %slice.56), channel_id=1, source_target_pairs={{0,16},{8,24},{16,0},{24,8},{1,17},{9,25},{17,1},{25,9},{2,18},{10... | collective-permute-start | bytes 1572872 | tf_op jit(solution)/shard_map/ppermute | solution.py:103
  147.8 17.1 %collective-permute-start.24 = (bf16[1024,256]{1,0:T(8,128)(2,1)S(1)}, bf16[1024,256]{1,0:T(8,128)(2,1)S(1)}, u32[]{:S(2)}, u32[]{:S(2)}) collective-permute-start(bf16[1024,256]{1,0:T(8,128)(2,1)S(1)} %slice.55), channel_id=1, source_target_pairs={{0,8},{8,0},{16,24},{24,16},{1,9},{9,1},{17,25},{25,17},{2,10},{10... | collective-permute-start | bytes 1572872 | tf_op jit(solution)/shard_map/ppermute | solution.py:103
  170.6 12.6 %collective-permute-start.26 = (f32[2,128,1024]{2,1,0:T(8,128)S(1)}, f32[2,128,1024]{2,1,0:T(8,128)S(1)}, u32[]{:S(2)}, u32[]{:S(2)}) collective-permute-start(f32[2,128,1024]{2,1,0:T(8,128)S(1)} %add_add_fusion.own_ref), channel_id=1, source_target_pairs={{0,1},{1,0},{2,3},{3,2},{4,5},{5,4},{6,7},{7,6},{8,9},{9,8},{10,11... | collective-permute-start | bytes 3145736 | tf_op jit(solution)/shard_map/ppermute | solution.py:103
  (14 other events, 145.6 us)

commit v5 on v4

--- a/solution.py
+++ b/solution.py
@@ -231,155 +231,221 @@
     )(*terms_a, *terms_b)
 
 
-def spread_into(target, ids_ref, rows_refs, first, size):
-    low = ids_ref.shape[1]
-
-    def build(b, carry):
-        at = pl.multiple_of(b * size, size)
-        block = (first + b).astype(jnp.float32).astype(jnp.bfloat16)
-        here = [ids_ref[j] == block for j in range(2)]
-        for n in range(size // low):
-            rows = slice(n * low, (n + 1) * low)
-            value = jnp.where(here[1], rows_refs[1][rows, :], jnp.zeros((), jnp.bfloat16))
-            target[pl.ds(at + n * low, low), :] = jnp.where(here[0], rows_refs[0][rows, :], value)
-        return carry
-
-    lax.fori_loop(0, target.shape[0] // size, build, 0)
-
-
-def lanes_of(refs):
-    return refs[0][...] if len(refs) == 1 else jnp.concatenate([r[...] for r in refs], axis=1)
-
-
-def code_grad_kernel(size, shape, scalar_ref, ids_ref, *refs):
-    grad_ref = refs[-1]
-    weights, pieces = refs[:len(shape)], refs[len(shape):-1]
-
-    @pl.when(pl.program_id(0) == 0)
+def slots_kernel(groups, blocks, cap, scalar_ref, message_ref, hot_ref, pre_ref, code_ref):
+    tok = message_ref.shape[2]
+    pad = message_ref.shape[1] - 2 * tok
+    f32, bf16 = jnp.float32, jnp.bfloat16
+    first = scalar_ref[0].astype(f32)
+    rows = [message_ref[g, 2 * tok:2 * tok + pad, :].astype(f32) for g in range(groups)]
+    fill = tok - groups * pad
+    table = jnp.concatenate(rows + ([jnp.zeros((fill, tok), f32)] if fill else []), axis=0).T
+    earlier = lax.broadcasted_iota(jnp.int32, (tok, tok), 0) < lax.broadcasted_iota(jnp.int32, (tok, tok), 1)
+    per = 2 * cap
+    for z in range(groups // 2):
+        pre = 0.0
+        hot = []
+        for core in range(2):
+            g = 2 * z + core
+            lanes = [rows[g][j:j + 1] for j in range(2)]
+            down = [table[:, g * pad + j:g * pad + j + 1] for j in range(2)]
+            same = [jnp.where((down[j] == lanes[j]) & earlier, 1.0, 0.0) for j in range(2)]
+            cross = jnp.where(down[0] == lanes[1], 1.0, 0.0)
+            rank = [jnp.sum(same[0], axis=0, keepdims=True), jnp.sum(same[1] + cross, axis=0, keepdims=True)]
+            here = []
+            for j in range(2):
+                block = lanes[j] - first
+                slot = block * per + (core * cap + rank[j])
+                slot = jnp.where((block >= 0) & (block < blocks), slot, -1.0)
+                number = lax.broadcasted_iota(jnp.int32, (blocks * per, tok), 0).astype(f32)
+                here.append(jnp.where(number == slot, 1.0, 0.0).astype(bf16))
+                pre = pre + jnp.dot(
+                    here[j], message_ref[g, j * tok:(j + 1) * tok, :], preferred_element_type=f32
+                )
+            hot.append(here[0] + here[1])
+        hot_ref[z] = jnp.concatenate(hot, axis=1)
+        for b in range(blocks):
+            pre_ref[b, z * per:(z + 1) * per, :] = pre[b * per:(b + 1) * per].astype(bf16)
+    for b in range(blocks):
+        code_ref[b] = jnp.maximum(pre_ref[b].astype(f32), 0.0).T.astype(bf16)
+
+
+def make_slots(message, first, lat_rows, cap):
+    groups, _, tok = message.shape
+    blocks = lat_rows // tok
+    per = 2 * cap
+    shards = groups // 2
+    shapes = [(shards, blocks * per, 2 * tok), (blocks, shards * per, tok), (blocks, tok, shards * per)]
+    return pl.pallas_call(
+        functools.partial(slots_kernel, groups, blocks, cap),
+        out_shape=[jax.ShapeDtypeStruct(shape, jnp.bfloat16) for shape in shapes],
+        grid_spec=pltpu.PrefetchScalarGridSpec(
+            num_scalar_prefetch=1,
+            grid=(1,),
+            in_specs=[resident(message.shape)],
+            out_specs=[resident(shape) for shape in shapes],
+        ),
+        compiler_params=params(),
+        cost_estimate=cost(groups * tok, 2 * tok, tok),
+        name="make_slots",
+    )(first[None].astype(jnp.int32), message)
+
+
+def into_slots(hot, rows, out, z):
+    per = out.shape[1] // hot.shape[0]
+    value = jnp.dot(hot[z], rows, preferred_element_type=jnp.float32).astype(jnp.bfloat16)
+    for b in range(out.shape[0]):
+        out[b, z * per:(z + 1) * per, :] = value[b * per:(b + 1) * per]
+
+
+def lanes_of(refs, rows):
+    parts = [r[rows, :] for r in refs]
+    return parts[0] if len(parts) == 1 else jnp.concatenate(parts, axis=1)
+
+
+def piece_grad_kernel(layout, scalar_ref, hot_ref, weight_ref, *refs):
+    parts, (slots_ref, grad_ref) = refs[:-2], refs[-2:]
+    blocks, _, size = grad_ref.shape
+    group = hot_ref.shape[2]
+    step = pl.program_id(0)
+
+    @pl.when(step == 0)
     def _():
         grad_ref[...] = jnp.zeros_like(grad_ref)
 
-    weight = jnp.concatenate([w[0] for w in weights], axis=1)
-    grad = lax.dot_general(
-        weight, lanes_of(pieces), (((1,), (1,)), ((), ())), preferred_element_type=jnp.float32
-    )
-    several = weight.shape[0] // size
-    add0, add1 = 0.0, 0.0
-    for n in range(several):
-        block = (scalar_ref[0] + pl.program_id(0) * several + n).astype(jnp.float32)
-        part = grad[n * size:(n + 1) * size]
-        add0 = jnp.where(ids_ref[0:1] == block, part, add0)
-        add1 = jnp.where(ids_ref[1:2] == block, part, add1)
-    grad_ref[0] += add0
-    grad_ref[1] += add1
-
-
-def code_grad(pieces, ids, decoder, first, columns, size):
+    at = 0
+    for i, piece in enumerate(layout):
+        z = 0
+        for lanes in piece:
+            here = parts[at:at + lanes]
+            at += lanes
+            for n in range(here[0].shape[0] // group):
+
+                @pl.when(step == i)
+                def _(z=z, n=n, here=here):
+                    into_slots(hot_ref, lanes_of(here, slice(n * group, (n + 1) * group)), slots_ref.at[0], z)
+
+                z += 1
+    for b in range(blocks):
+        grad_ref[b] += lax.dot_general(
+            slots_ref[0, b],
+            weight_ref[0, b * size:(b + 1) * size, :],
+            (((1,), (1,)), ((), ())),
+            preferred_element_type=jnp.float32,
+        )
+
+
+def piece_grad(pieces, hot, decoder, columns, size):
     lat_rows = decoder.shape[1]
-    tokens = pieces[0][0].shape[0]
-    width = sum(p.shape[1] for p in pieces[0])
-    scalars = jnp.concatenate([first[None], columns]).astype(jnp.int32)
-    flat = [p for piece in pieces for p in piece]
-    several = 4 * size if lat_rows % (4 * size) == 0 else size
-    return pl.pallas_call(
-        functools.partial(code_grad_kernel, size, [len(p) for p in pieces]),
-        out_shape=jax.ShapeDtypeStruct((2, size, tokens), jnp.float32),
+    blocks = lat_rows // size
+    slots = hot.shape[0] * hot.shape[1] // blocks
+    width = sum(p.shape[1] for p in pieces[0][0])
+    flat = [p for piece in pieces for row in piece for p in row]
+    return pl.pallas_call(
+        functools.partial(piece_grad_kernel, [[len(row) for row in piece] for piece in pieces]),
+        out_shape=[
+            jax.ShapeDtypeStruct((len(pieces), blocks, slots, width), jnp.bfloat16),
+            jax.ShapeDtypeStruct((blocks, slots, size), jnp.float32),
+        ],
         grid_spec=pltpu.PrefetchScalarGridSpec(
             num_scalar_prefetch=1,
-            grid=(lat_rows // several,),
-            in_specs=[resident(ids.shape)]
-            + [pl.BlockSpec((1, several, width), lambda i, s, n=n: (0, i, s[n + 1])) for n in range(len(pieces))]
+            grid=(len(pieces),),
+            in_specs=[resident(hot.shape), pl.BlockSpec((1, lat_rows, width), lambda i, s: (0, 0, s[i]))]
             + [resident(p.shape) for p in flat],
-            out_specs=resident((2, size, tokens)),
+            out_specs=[
+                pl.BlockSpec((1, blocks, slots, width), lambda i, s: (i, 0, 0, 0)),
+                resident((blocks, slots, size)),
+            ],
         ),
         compiler_params=params(),
-        cost_estimate=cost(lat_rows, len(pieces) * width, tokens),
-        name="code_grad",
-    )(scalars, ids, *[decoder] * len(pieces), *flat)
-
-
-def decoder_kernel(size, shape, skip, scalar_ref, ids_ref, codes_ref, *refs):
-    refs = refs[skip:]
-    pieces, (out_ref, now, codes) = refs[:-3], refs[-3:]
-    at = 0
-    for i, count in enumerate(shape):
-
-        @pl.when(pl.program_id(0) == i)
-        def _(at=at, count=count):
-            now[...] = lanes_of(pieces[at:at + count])
-
-        at += count
-
-    @pl.when(pl.program_id(0) == 0)
-    def _():
-        spread_into(codes, ids_ref, [codes_ref.at[0], codes_ref.at[1]], scalar_ref[0], size)
-
-    several = 8 * size if codes.shape[0] % (8 * size) == 0 else size
-
-    def step(i, carry):
-        rows = pl.ds(pl.multiple_of(i * several, several), several)
-        out_ref[rows, :] = jnp.dot(codes[rows, :], now[...], preferred_element_type=jnp.float32).astype(jnp.bfloat16)
-        return carry
-
-    lax.fori_loop(0, codes.shape[0] // several, step, 0)
-
-
-def decoder_part(pieces, ids, code_lanes, first, columns, lat_rows, half, held):
-    _, size, tokens = code_lanes.shape
-    width = sum(p.shape[1] for p in pieces[0])
-    scalars = jnp.concatenate([first[None], columns]).astype(jnp.int32)
-    flat = [p for piece in pieces for p in piece]
+        cost_estimate=cost(lat_rows, 256, len(pieces) * width),
+        name="piece_grad",
+    )(columns.astype(jnp.int32), hot, decoder, *flat)
+
+
+def decoder_kernel(skip, scalar_ref, code_ref, slots_ref, *refs):
+    out_ref = refs[skip]
+    size = code_ref.shape[1]
+    for b in range(code_ref.shape[0]):
+        out_ref[b * size:(b + 1) * size, :] = jnp.dot(
+            code_ref[b], slots_ref[0, b], preferred_element_type=jnp.float32
+        ).astype(jnp.bfloat16)
+
+
+def decoder_part(slots, codes, columns, half, held):
+    count, blocks, _, width = slots.shape
+    lat_rows = blocks * codes.shape[1]
     onto = [] if held is None else [held]
     return pl.pallas_call(
-        functools.partial(decoder_kernel, size, [len(p) for p in pieces], len(onto)),
+        functools.partial(decoder_kernel, len(onto)),
         out_shape=jax.ShapeDtypeStruct((lat_rows, half), jnp.bfloat16),
         grid_spec=pltpu.PrefetchScalarGridSpec(
             num_scalar_prefetch=1,
-            grid=(len(pieces),),
-            in_specs=[resident(ids.shape), resident(code_lanes.shape)]
-            + [pl.BlockSpec(memory_space=pl.ANY) for _ in onto]
-            + [resident(p.shape) for p in flat],
-            out_specs=pl.BlockSpec((lat_rows, width), lambda i, s: (0, s[i + 1])),
-            scratch_shapes=[
-                pltpu.VMEM((tokens, width), jnp.bfloat16),
-                pltpu.VMEM((lat_rows, tokens), jnp.bfloat16),
-            ],
+            grid=(count,),
+            in_specs=[resident(codes.shape), pl.BlockSpec((1,) + slots.shape[1:], lambda i, s: (i, 0, 0, 0))]
+            + [pl.BlockSpec(memory_space=pl.ANY) for _ in onto],
+            out_specs=pl.BlockSpec((lat_rows, width), lambda i, s: (0, s[i])),
         ),
         compiler_params=params(),
         input_output_aliases={3: 0} if onto else {},
-        cost_estimate=cost(lat_rows, tokens, len(pieces) * width),
+        cost_estimate=cost(lat_rows, 256, count * width),
         name="decoder_part",
-    )(scalars, ids, code_lanes, *onto, *flat)
-
-
-def pre_grad_kernel(size, tok, scalar_ref, ids_ref, pre_ref, own_ref, theirs_ref, out_ref, rows):
-    for j in range(2):
-        for at in range(0, pre_ref.shape[2], 2 * tok):
+    )(columns.astype(jnp.int32), codes, slots, *onto)
+
+
+def act_slots_kernel(hot_ref, *refs):
+    out_ref = refs[-1]
+    for z, act in enumerate(refs[:-1]):
+        into_slots(hot_ref, act[...], out_ref, z)
+
+
+def act_slots(acts, hot, blocks):
+    group, half = acts[0].shape
+    slots = hot.shape[0] * hot.shape[1] // blocks
+    tile = half // 4
+    return pl.pallas_call(
+        act_slots_kernel,
+        out_shape=jax.ShapeDtypeStruct((blocks, slots, half), jnp.bfloat16),
+        grid=(4,),
+        in_specs=[pl.BlockSpec(hot.shape, lambda i: (0, 0, 0))]
+        + [pl.BlockSpec((group, tile), lambda i: (0, i)) for _ in acts],
+        out_specs=pl.BlockSpec((blocks, slots, tile), lambda i: (0, 0, i)),
+        compiler_params=params(),
+        cost_estimate=cost(blocks * slots, group, half),
+        name="act_slots",
+    )(hot, *acts)
+
+
+def encoder_kernel(cap, shared, pre_ref, own_ref, theirs_ref, act_ref, out_ref):
+    size = pre_ref.shape[2]
+    for n in range(shared):
+        parts = []
+        for at in range(0, own_ref.shape[1], 2 * cap):
             for core in range(2):
-                here = slice(at + core * tok, at + (core + 1) * tok)
-                there = slice(at + (1 - core) * tok, at + (2 - core) * tok)
-                total = own_ref[j, :, here] + theirs_ref[j, :, there]
-                rows[j, :, here] = jnp.where(pre_ref[j, :, here].astype(jnp.float32) > 0, total, 0.0).astype(jnp.bfloat16)
-    spread_into(out_ref, ids_ref, [rows.at[0], rows.at[1]], scalar_ref[0], size)
-
-
-def pre_grad_spread(own, theirs, ids, pre_lanes, first, lat_rows, tok):
-    _, size, tokens = pre_lanes.shape
-    scalars = first[None].astype(jnp.int32)
-    return pl.pallas_call(
-        functools.partial(pre_grad_kernel, size, tok),
-        out_shape=jax.ShapeDtypeStruct((lat_rows, tokens), jnp.bfloat16),
-        grid_spec=pltpu.PrefetchScalarGridSpec(
-            num_scalar_prefetch=1,
-            grid=(1,),
-            in_specs=[resident(ids.shape)] + [resident(pre_lanes.shape)] * 3,
-            out_specs=resident((lat_rows, tokens)),
-            scratch_shapes=[pltpu.VMEM((2, size, tokens), jnp.bfloat16)],
-        ),
-        compiler_params=params(),
-        cost_estimate=cost(lat_rows, 2, tokens),
-        name="pre_grad_spread",
-    )(scalars, ids, pre_lanes, own, theirs)
+                here = slice(at + core * cap, at + (core + 1) * cap)
+                there = slice(at + (1 - core) * cap, at + (2 - core) * cap)
+                parts.append(own_ref[n, here, :] + theirs_ref[n, there, :])
+        total = jnp.concatenate(parts, axis=0)
+        grad = jnp.where(pre_ref[n].astype(jnp.float32) > 0, total, 0.0).T.astype(jnp.bfloat16)
+        out_ref[n * size:(n + 1) * size, :] = jnp.dot(
+            grad, act_ref[n], preferred_element_type=jnp.float32
+        ).astype(jnp.bfloat16)
+
+
+def encoder_part(pre, own, theirs, acts, cap):
+    blocks, slots, size = pre.shape
+    half = acts.shape[2]
+    shared = 2 if blocks % 2 == 0 else 1
+    block = pl.BlockSpec((shared, slots, size), lambda i: (i, 0, 0))
+    return pl.pallas_call(
+        functools.partial(encoder_kernel, cap, shared),
+        out_shape=jax.ShapeDtypeStruct((blocks * size, half), jnp.bfloat16),
+        grid=(blocks // shared,),
+        in_specs=[block, block, block, pl.BlockSpec((shared, slots, half), lambda i: (i, 0, 0))],
+        out_specs=pl.BlockSpec((shared * size, half), lambda i: (i, 0)),
+        compiler_params=params(),
+        cost_estimate=cost(blocks * size, 256, half),
+        name="encoder_part",
+    )(pre, own, theirs, acts)
 
 
 def dense_plan(pre_codes, block_ids, activations, target, decoder):
@@ -402,6 +468,7 @@
     side = width // 2
     f32, bf16 = jnp.float32, jnp.bfloat16
     first = lat_here * local_blocks
+    capacity = 2 * tok_count * active_count // (local_blocks * lat_count)
 
     def columns(rows, which):
         return lax.dynamic_slice_in_dim(rows, which * half, half, axis=1)
@@ -435,12 +502,12 @@
     message = message.reshape(lat_count * dp_count, own.shape[0], block_size)
     next_hops()
 
+    codes = spread_codes(message, first, lat_rows)
     at = places((0, 2), dp_here * lay_count, 2, 0) + places((0, 1), dp_here * lay_count, 2, 1)
-    keep_weights = gather_columns(decoder, jnp.stack(at), side)
+    at, codes, target = lax.optimization_barrier((jnp.stack(at), codes, target))
+    keep_weights = gather_columns(decoder, at, side)
     goals = gather_columns(target, jnp.stack([which * lay_count + lay_here for which in (dp_here, 1 - dp_here)]), width)
     goals = jnp.concatenate([goals[:, :width], flip(goals[:, width:], "dp", 1)])
-
-    codes = spread_codes(message, first, lat_rows)
 
     def rows_for(spread, weights, n):
         return jnp.dot(spread, weights[:, n * width:(n + 1) * width], preferred_element_type=f32).astype(bf16)
@@ -462,42 +529,39 @@
     for r in range(1, lat_count):
         total = total + flip(sent[r - 1], "latent", r).astype(f32)
     errors = ((total - goals.astype(f32)) / tok_count).astype(bf16)
-    rows = jnp.concatenate([errors] + [flip(errors, "latent", r) for r in range(1, lat_count)])
-    rows, up[-1], down[-1] = lax.optimization_barrier((rows, up[-1], down[-1]))
+    blocks_of = [errors] + [flip(errors, "latent", r) for r in range(1, lat_count)]
+    near = jnp.concatenate(blocks_of[:lat_count // 2])
+    one_near, two_near = flip(near, "layer", 1), flip(near, "layer", 2)
+    one_near, two_near, far_blocks, up[-1], down[-1] = lax.optimization_barrier(
+        (one_near, two_near, blocks_of[lat_count // 2:], up[-1], down[-1])
+    )
     while len(up) < lat_count:
         next_hops()
-    one, two = flip(rows, "layer", 1), flip(rows, "layer", 2)
-
-    cut = message.reshape(tokens // tok_count, own.shape[0], block_size)
-    pre_lanes = cut[:, :active_count * tok_count].reshape(-1, active_count, tok_count, block_size)
-    pre_lanes = jnp.transpose(pre_lanes, (1, 3, 0, 2)).reshape(active_count, block_size, tokens)
-    code_lanes = jnp.maximum(pre_lanes, jnp.zeros((), bf16))
-    ids = cut[:, active_count * tok_count:active_count * tok_count + active_count]
-    ids = jnp.swapaxes(ids, 0, 1).reshape(active_count, tokens)
-    ids_wide = jnp.broadcast_to(ids[:, None, :], (active_count, 16, tokens))
-    ids = ids.astype(f32)
+    distant = jnp.concatenate(far_blocks)
+    one_far, two_far = flip(distant, "layer", 1), flip(distant, "layer", 2)
+    three_near = flip(two_near[:, :side], "layer", 1), flip(one_near[:, side:], "layer", 2)
+
+    hot, pre_slots, code_slots = make_slots(message, first, lat_rows, capacity)
 
     def grads_of(here, names, dec):
-        grad = code_grad(here, ids, decoder, first, weight_places(names), block_size)
-        where = jnp.stack(places(names, 0))
-        return grad, decoder_part(here, ids_wide, code_lanes, first, where, lat_rows, half, dec)
-
-    grad, dec = grads_of([(rows,)], (0,), None)
-    one, two, grad, dec, up[-1], down[-1] = lax.optimization_barrier((one, two, grad, dec, up[-1], down[-1]))
-    three = flip(two[:, :side], "layer", 1), flip(one[:, side:], "layer", 2)
+        slots, grad = piece_grad(here, hot, decoder, weight_places(names), block_size)
+        return grad, decoder_part(slots, code_slots, jnp.stack(places(names, 0)), half, dec)
+
+    grad, dec = grads_of([[(near,), (distant,)]], (0,), None)
+    one_far, two_far, three_near, grad, dec = lax.optimization_barrier((one_far, two_far, three_near, grad, dec))
+    three_far = flip(two_far[:, :side], "layer", 1), flip(one_far[:, side:], "layer", 2)
     along = [acts] + [down[k] + up[lat_count - k] for k in range(1, lat_count)]
     along = jnp.stack(along)
     along = [
         lax.dynamic_index_in_dim(along, lax.rem((lat_here ^ r) - lat_here + lat_count, lat_count), 0, False)
         for r in range(lat_count)
     ]
-    along = jnp.concatenate(along)
-    more, dec = grads_of([(one,), (two,)], (1, 2), dec)
-    three, more, dec, along = lax.optimization_barrier((three, more, dec, along))
-    last, dec = grads_of([three], (3,), dec)
+    along = act_slots(along, hot, local_blocks)
+    more, dec = grads_of([[(one_near,), (one_far,)], [(two_near,), (two_far,)]], (1, 2), dec)
+    three_far, more, dec = lax.optimization_barrier((three_far, more, dec))
+    last, dec = grads_of([[three_near, three_far]], (3,), dec)
     grad = grad + more + last
-    pre_grad = pre_grad_spread(grad, flip(grad, "dp", 1), ids_wide, pre_lanes, first, lat_rows, tok_count)
-    enc = jnp.dot(pre_grad, along, preferred_element_type=f32).astype(bf16)
+    enc = encoder_part(pre_slots, grad, flip(grad, "dp", 1), along, capacity)
     return dec[None], enc[None]
 
 
@@ -522,6 +586,7 @@
         and lat_count * dp_count * 16 <= tok_count
         and model_width % (dp_count * 2 * lay_count * 128) == 0
         and all_blocks <= 256
+        and 2 * tok_count * active_count == 8 * all_blocks
     )
     plan = dense_plan if dense else slot_plan
     return plan(pre_codes, block_ids, activations, target, decoder)

time: 196 us -> 189 us (0.964); the launches traced: 195 us -> 186 us
  matrix products: 20.2 us -> 9.3 us
  Pallas kernels: 48.3 us -> 39 us
  waiting for transfers between devices: 67.8 us -> 76.2 us
  local copies, waits for them, and re-layouts: 5.32 us -> 9.48 us
  starting transfers between devices: 47.5 us -> 45.4 us
    ppermute x21 -> x25, waiting for transfers between devices: 39.2 us -> 58.6 us  [flip(): return lax.ppermute(value, axis, [(i, i ^ bit) for i in range(count)])]
    ppermute x6, waiting for transfers between devices: 28.6 us -> 17.6 us  [hop(): return lax.ppermute(value, axis, pairs)]
    dot_general x1 -> x0, matrix products: 10.9 us -> none  [dense_plan(): enc = jnp.dot(pre_grad, along, preferred_element_type=f32).astype(bf16)]
    pallas_call x7 -> x9, Pallas kernels: 36.9 us -> 27.6 us  [the longest x3 10.7 us: piece_grad(): pl.pallas_call(functools.partial(piece_grad_kernel, [[len(row) for row in...]
    ppermute x21 -> x25, starting transfers between devices: 37.5 us -> 33.6 us  [flip(): return lax.ppermute(value, axis, [(i, i ^ bit) for i in range(count)])]
    slice x3 -> x4, local copies, waits for them, and re-layouts: 0.11 us -> 3.41 us  [the longest x1 0.97 us: dense_plan(): two_far[:, :side]]
    another operation x4, other arithmetic: 0.87 us -> 3.35 us  [dense_plan(): along = jnp.stack(along)]
  transfers between devices with their start and end apart: 27 -> 31, of which waited for: 11 -> 14; matrix products, arithmetic and copies ran while one was open for 7% -> 10% of each run, Pallas kernels for 21% -> 17%
where the time goes in v5:
time: 189 us; the launch traced here: 186 us
  waiting for transfers between devices  76.2 us (40%)
  starting transfers between devices  45.4 us (24%)
  Pallas kernels  39 us (21%)
  local copies, waits for them, and re-layouts  9.48 us (5%)
  matrix products  9.3 us (5%)
  other arithmetic  5.22 us (3%)
    ppermute x25, waiting for transfers between devices, flip(): return lax.ppermute(value, axis, [(i, i ^ bit) for i in range(count)])  58.6 us
    ppermute x25, starting transfers between devices, flip(): return lax.ppermute(value, axis, [(i, i ^ bit) for i in range(count)])  33.6 us
    ppermute x6, waiting for transfers between devices, hop(): return lax.ppermute(value, axis, pairs)  17.6 us
    ppermute x6, starting transfers between devices, hop(): return lax.ppermute(value, axis, pairs)  11.8 us
    pallas_call x3, Pallas kernels, piece_grad(): pl.pallas_call(functools.partial(piece_grad_kernel, [[len(row) for row in...  10.7 us
    dot_general x4, matrix products, rows_for(): jnp.dot(spread, weights[:, n * width:(n + 1) * width], preferred_element_...  9.3 us
    pallas_call x3, Pallas kernels, gather_columns(): pl.pallas_call(gather_kernel, out_shape=jax.ShapeDtypeStruct((rows, count...  8.39 us
    pallas_call x3, Pallas kernels, decoder_part(): pl.pallas_call(functools.partial(decoder_kernel, len(onto)), out_shape=ja...  7.28 us
  transfers between devices with their start and end apart: 31, of which 14 were waited for; matrix products, arithmetic and copies ran while one was open for 10% of the time, Pallas kernels for 17%

profile of v5, /device:TPU:1, one launch (start us, length us, event | category | flops | bytes accessed | tf_op | source)
XLA Modules:
  0.0 185.6 jit_solution(9506411794232821165)
XLA Ops:
  3.6 3.8 %collective-permute-start.1 = (bf16[272,128]{1,0:T(8,128)(2,1)S(1)}, bf16[272,128]{1,0:T(8,128)(2,1)S(1)}, u32[]{:S(2)}, u32[]{:S(2)}) collective-permute-start(bf16[272,128]{1,0:T(8,128)(2,1)S(1)} %get-tuple-element.96), channel_id=1, source_target_pairs={{0,4},{2,6},{4,0},{6,2},{1,5},{3,7},{5,1},{7,3},{8,12},{10,14},{12... | collective-permute-start | bytes 208904 | tf_op jit(solution)/shard_map/ppermute | solution.py:103
  8.8 3.9 %gather_columns.3 = bf16[2048,1024]{1,0:T(8,128)(2,1)S(1)} custom-call(s32[4]{0:T(128)S(1)} %pad_add_fusion.scalar_ref, bf16[1,2048,4096]{2,1,0:T(8,128)(2,1)} %weight_ref.5), custom_call_target="tpu_custom_call" | custom-call | flops 1048576 | bytes 1050112 | tf_op jit(solution)/shard_map/gather_columns/pallas_call | solution.py:139
  17.2 4.1 %collective-permute-start.6 = (bf16[256,2048]{1,0:T(8,128)(2,1)S(1)}, bf16[256,2048]{1,0:T(8,128)(2,1)S(1)}, u32[]{:S(2)}, u32[]{:S(2)}) collective-permute-start(bf16[256,2048]{1,0:T(8,128)(2,1)S(1)} %pad_maximum_fusion.1.refs_0_), channel_id=1, source_target_pairs={{0,2},{2,4},{4,6},{1,3},{3,5},{5,7},{8,10},{10,12},{12,14},{9,11},... | collective-permute-start | bytes 3145736 | tf_op jit(solution)/shard_map/ppermute | solution.py:112
  21.4 2.6 %spread_codes.1 = bf16[1024,2048]{1,0:T(8,128)(2,1)S(1)} custom-call(s32[1]{0:T(128)} %bitcast.1.scalar_ref, bf16[8,272,128]{2,1,0:T(8,128)(2,1)S(1)} %bitcast.59), custom_call_target="tpu_custom_call" | custom-call | flops 1048576 | bytes 1050112 | tf_op jit(solution)/shard_map/spread_codes/pallas_call | solution.py:185
  31.4 3.9 %gather_columns.4 = bf16[2048,1024]{1,0:T(8,128)(2,1)S(1)} custom-call(s32[4]{0:T(128)S(1)} %pad_add_fusion.1.scalar_ref, bf16[1,2048,4096]{2,1,0:T(8,128)(2,1)} %weight_ref.5), custom_call_target="tpu_custom_call" | custom-call | flops 1048576 | bytes 1050112 | tf_op jit(solution)/shard_map/gather_columns/pallas_call | solution.py:139
  35.2 7.3 %collective-permute-done.7 = bf16[256,2048]{1,0:T(8,128)(2,1)S(1)} collective-permute-done((bf16[256,2048]{1,0:T(8,128)(2,1)S(1)}, bf16[256,2048]{1,0:T(8,128)(2,1)S(1)}, u32[]{:S(2)}, u32[]{:S(2)}) %collective-permute-start.7) | collective-permute-done | bytes 1048608 | tf_op jit(solution)/shard_map/ppermute | solution.py:112
  51.2 2.7 %collective-permute-done.9.got_b = bf16[1024,512]{1,0:T(8,128)(2,1)S(1)} collective-permute-done((bf16[1024,512]{1,0:T(8,128)(2,1)S(1)}, bf16[1024,512]{1,0:T(8,128)(2,1)S(1)}, u32[]{:S(2)}, u32[]{:S(2)}) %collective-permute-start.9) | collective-permute-done | bytes 1048608 | tf_op jit(solution)/shard_map/ppermute | solution.py:103
  56.7 2.4 %collective-permute-start.11 = (bf16[128,512]{1,0:T(8,128)(2,1)S(1)}, bf16[128,512]{1,0:T(8,128)(2,1)S(1)}, u32[]{:S(2)}, u32[]{:S(2)}) collective-permute-start(bf16[128,512]{1,0:T(8,128)(2,1)S(1)} %get-tuple-element.94), channel_id=1, source_target_pairs={{0,1},{1,0},{2,3},{3,2},{4,5},{5,4},{6,7},{7,6},{8,9},{9,8},{10,11... | collective-permute-start | bytes 393224 | tf_op jit(solution)/shard_map/ppermute | solution.py:103
  60.1 5.7 %collective-permute-done.10.far_b = bf16[1024,256]{1,0:T(8,128)(2,1)S(1)} collective-permute-done((bf16[1024,256]{1,0:T(8,128)(2,1)S(1)}, bf16[1024,256]{1,0:T(8,128)(2,1)S(1)}, u32[]{:S(2)}, u32[]{:S(2)}) %collective-permute-start.10) | collective-permute-done | bytes 524320 | tf_op jit(solution)/shard_map/ppermute | solution.py:103
  65.9 8.0 %collective-permute-done.13 = bf16[256,2048]{1,0:T(8,128)(2,1)S(1)} collective-permute-done((bf16[256,2048]{1,0:T(8,128)(2,1)S(1)}, bf16[256,2048]{1,0:T(8,128)(2,1)S(1)}, u32[]{:S(2)}, u32[]{:S(2)}) %collective-permute-start.13) | collective-permute-done | bytes 1048608 | tf_op jit(solution)/shard_map/ppermute | solution.py:112
  77.8 4.7 %collective-permute-done.14 = bf16[256,512]{1,0:T(8,128)(2,1)S(1)} collective-permute-done((bf16[256,512]{1,0:T(8,128)(2,1)S(1)}, bf16[256,512]{1,0:T(8,128)(2,1)S(1)}, u32[]{:S(2)}, u32[]{:S(2)}) %collective-permute-start.14) | collective-permute-done | bytes 262176 | tf_op jit(solution)/shard_map/ppermute | solution.py:103
  82.6 11.4 %collective-permute-done.15 = bf16[256,512]{1,0:T(8,128)(2,1)S(1)} collective-permute-done((bf16[256,512]{1,0:T(8,128)(2,1)S(1)}, bf16[256,512]{1,0:T(8,128)(2,1)S(1)}, u32[]{:S(2)}, u32[]{:S(2)}) %collective-permute-start.15) | collective-permute-done | bytes 262176 | tf_op jit(solution)/shard_map/ppermute | solution.py:103
  94.2 6.0 %collective-permute-start.17 = (bf16[256,512]{1,0:T(8,128)(2,1)S(1)}, bf16[256,512]{1,0:T(8,128)(2,1)S(1)}, u32[]{:S(2)}, u32[]{:S(2)}) collective-permute-start(bf16[256,512]{1,0:T(8,128)(2,1)S(1)} %multiply_convert_fusion), channel_id=1, source_target_pairs={{0,2},{2,0},{4,6},{6,4},{1,3},{3,1},{5,7},{7,5},{8,10},{10,8},{12,... | collective-permute-start | bytes 786440 | tf_op jit(solution)/shard_map/ppermute | solution.py:103
  100.2 4.3 %collective-permute-done.17 = bf16[256,512]{1,0:T(8,128)(2,1)S(1)} collective-permute-done((bf16[256,512]{1,0:T(8,128)(2,1)S(1)}, bf16[256,512]{1,0:T(8,128)(2,1)S(1)}, u32[]{:S(2)}, u32[]{:S(2)}) %collective-permute-start.17) | collective-permute-done | bytes 262176 | tf_op jit(solution)/shard_map/ppermute | solution.py:103
  109.5 4.8 %collective-permute-done.21 = bf16[256,512]{1,0:T(8,128)(2,1)S(1)} collective-permute-done((bf16[256,512]{1,0:T(8,128)(2,1)S(1)}, bf16[256,512]{1,0:T(8,128)(2,1)S(1)}, u32[]{:S(2)}, u32[]{:S(2)}) %collective-permute-start.21) | collective-permute-done | bytes 262176 | tf_op jit(solution)/shard_map/ppermute | solution.py:103
  114.2 17.9 %collective-permute-done.20 = bf16[256,512]{1,0:T(8,128)(2,1)S(1)} collective-permute-done((bf16[256,512]{1,0:T(8,128)(2,1)S(1)}, bf16[256,512]{1,0:T(8,128)(2,1)S(1)}, u32[]{:S(2)}, u32[]{:S(2)}) %collective-permute-start.20) | collective-permute-done | bytes 262176 | tf_op jit(solution)/shard_map/ppermute | solution.py:103
  140.6 2.9 %piece_grad.3 = (bf16[1,16,64,512]{3,2,1,0:T(8,128)(2,1)S(1)}, f32[16,64,128]{2,1,0:T(8,128)S(1)}) custom-call(s32[1]{0:T(128)} %bitcast.25.scalar_ref, bf16[4,256,256]{2,1,0:T(8,128)(2,1)S(1)} %get-tuple-element.47.hot_ref, bf16[1,2048,4096]{2,1,0:T(8,128)(2,1)} %weight_ref.5, bf16[512,512]{1,0:T(8,128)(2,1)S(1)} %pad_maximum_fusion.3.refs_0_, ...), custom_call_target="tpu_custom_call" | custom-call | flops 134217728 | bytes 851968 | tf_op jit(solution)/shard_map/piece_grad/pallas_call | solution.py:343
  145.5 5.9 %collective-permute-done.25.refs_1_ = bf16[512,256]{1,0:T(8,128)(2,1)S(1)} collective-permute-done((bf16[512,256]{1,0:T(8,128)(2,1)}, bf16[512,256]{1,0:T(8,128)(2,1)S(1)}, u32[]{:S(2)}, u32[]{:S(2)}) %collective-permute-start.25) | collective-permute-done | bytes 262176 | tf_op jit(solution)/shard_map/ppermute | solution.py:103
  156.8 5.0 %piece_grad.4 = (bf16[2,16,64,512]{3,2,1,0:T(8,128)(2,1)S(1)}, f32[16,64,128]{2,1,0:T(8,128)S(1)}) custom-call(s32[2]{0:T(128)S(1)} %get-tuple-element.98.scalar_ref, bf16[4,256,256]{2,1,0:T(8,128)(2,1)S(1)} %get-tuple-element.47.hot_ref, bf16[1,2048,4096]{2,1,0:T(8,128)(2,1)} %weight_ref.5, bf16[512,512]{1,0:T(8,128)(2,1)S(1)} %collective-permute-done.18.refs_0_, ...), custom_call_target="tpu_custom_call" | custom-call | flops 268435456 | bytes 1441792 | tf_op jit(solution)/shard_map/piece_grad/pallas_call | solution.py:343
  161.9 3.3 %decoder_part.4.refs_0_ = bf16[2048,2048]{1,0:T(8,128)(2,1)} custom-call(s32[2]{0:T(128)S(1)} %pad_add_fusion.4.scalar_ref, bf16[16,128,64]{2,1,0:T(8,128)(2,1)S(1)} %get-tuple-element.46.code_ref, bf16[2,16,64,512]{3,2,1,0:T(8,128)(2,1)S(1)} %get-tuple-element.76.slots_ref, bf16[2048,2048]{1,0:T(8,128)(2,1)} %decoder_part.3.refs_0_), custom_call_target="tpu_custom_call", output_to_operand_aliasing={{}: (3, {})} | custom-call | flops 268435456 | bytes 1441792 | tf_op jit(solution)/shard_map/decoder_part/pallas_call | solution.py:378
  165.2 2.8 %piece_grad.5 = (bf16[1,16,64,512]{3,2,1,0:T(8,128)(2,1)S(1)}, f32[16,64,128]{2,1,0:T(8,128)S(1)}) custom-call(s32[1]{0:T(128)} %bitcast.20.scalar_ref, bf16[4,256,256]{2,1,0:T(8,128)(2,1)S(1)} %get-tuple-element.47.hot_ref, bf16[1,2048,4096]{2,1,0:T(8,128)(2,1)} %weight_ref.5, bf16[512,256]{1,0:T(8,128)(2,1)} %collective-permute-done.24.refs_0_, ...), custom_call_target="tpu_custom_call" | custom-call | flops 134217728 | bytes 851968 | tf_op jit(solution)/shard_map/piece_grad/pallas_call | solution.py:343
  168.0 2.9 %collective-permute-start.28 = (f32[16,64,128]{2,1,0:T(8,128)S(1)}, f32[16,64,128]{2,1,0:T(8,128)S(1)}, u32[]{:S(2)}, u32[]{:S(2)}) collective-permute-start(f32[16,64,128]{2,1,0:T(8,128)S(1)} %add_add_fusion.own_ref), channel_id=1, source_target_pairs={{0,1},{1,0},{2,3},{3,2},{4,5},{5,4},{6,7},{7,6},{8,9},{9,8},{10,11... | collective-permute-start | bytes 1572872 | tf_op jit(solution)/shard_map/ppermute | solution.py:103
  176.8 2.4 %act_slots.1.act_ref = bf16[16,64,2048]{2,1,0:T(8,128)(2,1)S(1)} custom-call(bf16[4,256,256]{2,1,0:T(8,128)(2,1)S(1)} %get-tuple-element.47.hot_ref, bf16[256,2048]{1,0:T(8,128)(2,1)S(1)} %pad_maximum_fusion.1.refs_0_, bf16[256,2048]{1,0:T(8,128)(2,1)S(1)} %get-tuple-element.90.refs_1_, bf16[256,2048]{1,0:T(8,128)(2,1)S(1)} %get-tuple-element.89.refs_2_, ...), custom_call_target="tpu_custom_call" | custom-call | flops 268435456 | bytes 1441792 | tf_op jit(solution)/shard_map/act_slots/pallas_call | solution.py:405
  179.2 6.3 %encoder_part.1 = bf16[2048,2048]{1,0:T(8,128)(2,1)} custom-call(bf16[16,64,128]{2,1,0:T(8,128)(2,1)S(1)} %get-tuple-element.82.pre_ref, f32[16,64,128]{2,1,0:T(8,128)S(1)} %add_add_fusion.own_ref, f32[16,64,128]{2,1,0:T(8,128)S(1)} %collective-permute-done.28.theirs_ref, bf16[16,64,2048]{2,1,0:T(8,128)(2,1)S(1)} %act_slots.1.act_ref), custom_call_target="tpu_custom_call" | custom-call | flops 536870912 | bytes 2621440 | tf_op jit(solution)/shard_map/encoder_part/pallas_call | solution.py:439
  (104 shorter events, 59.6 us)
Async XLA Ops:
  1.9 12.8 %collective-permute-start.3 = (bf16[128,2048]{1,0:T(8,128)(2,1)S(1)}, bf16[128,2048]{1,0:T(8,128)(2,1)S(1)}, u32[]{:S(2)}, u32[]{:S(2)}) collective-permute-start(bf16[128,2048]{1,0:T(8,128)(2,1)S(1)} %get-tuple-element.92), channel_id=1, source_target_pairs={{0,1},{1,0},{2,3},{3,2},{4,5},{5,4},{6,7},{7,6},{8,9},{9,8},{10,11... | collective-permute-start | bytes 1572872 | tf_op jit(solution)/shard_map/ppermute | solution.py:103
  3.6 11.1 %collective-permute-start.1 = (bf16[272,128]{1,0:T(8,128)(2,1)S(1)}, bf16[272,128]{1,0:T(8,128)(2,1)S(1)}, u32[]{:S(2)}, u32[]{:S(2)}) collective-permute-start(bf16[272,128]{1,0:T(8,128)(2,1)S(1)} %get-tuple-element.96), channel_id=1, source_target_pairs={{0,4},{2,6},{4,0},{6,2},{1,5},{3,7},{5,1},{7,3},{8,12},{10,14},{12... | collective-permute-start | bytes 208904 | tf_op jit(solution)/shard_map/ppermute | solution.py:103
  15.7 26.9 %collective-permute-start.7 = (bf16[256,2048]{1,0:T(8,128)(2,1)S(1)}, bf16[256,2048]{1,0:T(8,128)(2,1)S(1)}, u32[]{:S(2)}, u32[]{:S(2)}) collective-permute-start(bf16[256,2048]{1,0:T(8,128)(2,1)S(1)} %pad_maximum_fusion.1.refs_0_), channel_id=1, source_target_pairs={{2,0},{4,2},{6,4},{3,1},{5,3},{7,5},{10,8},{12,10},{14,12},{11,9},... | collective-permute-start | bytes 3145736 | tf_op jit(solution)/shard_map/ppermute | solution.py:112
  17.2 26.2 %collective-permute-start.6 = (bf16[256,2048]{1,0:T(8,128)(2,1)S(1)}, bf16[256,2048]{1,0:T(8,128)(2,1)S(1)}, u32[]{:S(2)}, u32[]{:S(2)}) collective-permute-start(bf16[256,2048]{1,0:T(8,128)(2,1)S(1)} %pad_maximum_fusion.1.refs_0_), channel_id=1, source_target_pairs={{0,2},{2,4},{4,6},{1,3},{3,5},{5,7},{8,10},{10,12},{12,14},{9,11},... | collective-permute-start | bytes 3145736 | tf_op jit(solution)/shard_map/ppermute | solution.py:112
  26.4 27.9 %collective-permute-start.5 = (bf16[1024,512]{1,0:T(8,128)(2,1)S(1)}, bf16[1024,512]{1,0:T(8,128)(2,1)S(1)}, u32[]{:S(2)}, u32[]{:S(2)}) collective-permute-start(bf16[1024,512]{1,0:T(8,128)(2,1)S(1)} %fusion.8), channel_id=1, source_target_pairs={{0,8},{8,0},{16,24},{24,16},{1,9},{9,1},{17,25},{25,17},{2,10},{10... | collective-permute-start | bytes 3145736 | tf_op jit(solution)/shard_map/ppermute | solution.py:103
  30.1 23.9 %collective-permute-start.9 = (bf16[1024,512]{1,0:T(8,128)(2,1)S(1)}, bf16[1024,512]{1,0:T(8,128)(2,1)S(1)}, u32[]{:S(2)}, u32[]{:S(2)}) collective-permute-start(bf16[1024,512]{1,0:T(8,128)(2,1)S(1)} %fusion.11), channel_id=1, source_target_pairs={{0,16},{8,24},{16,0},{24,8},{1,17},{9,25},{17,1},{25,9},{2,18},{10... | collective-permute-start | bytes 3145736 | tf_op jit(solution)/shard_map/ppermute | solution.py:103
  43.4 22.5 %collective-permute-start.12 = (bf16[256,2048]{1,0:T(8,128)(2,1)S(1)}, bf16[256,2048]{1,0:T(8,128)(2,1)}, u32[]{:S(2)}, u32[]{:S(2)}) collective-permute-start(bf16[256,2048]{1,0:T(8,128)(2,1)S(1)} %collective-permute-done.6), channel_id=1, source_target_pairs={{2,4},{4,6},{3,5},{5,7},{10,12},{12,14},{11,13},{13,15},{18,20},{2... | collective-permute-start | bytes 3145736 | tf_op jit(solution)/shard_map/ppermute | solution.py:112
  45.1 28.8 %collective-permute-start.13 = (bf16[256,2048]{1,0:T(8,128)(2,1)S(1)}, bf16[256,2048]{1,0:T(8,128)(2,1)S(1)}, u32[]{:S(2)}, u32[]{:S(2)}) collective-permute-start(bf16[256,2048]{1,0:T(8,128)(2,1)S(1)} %collective-permute-done.7), channel_id=1, source_target_pairs={{2,0},{4,2},{3,1},{5,3},{10,8},{12,10},{11,9},{13,11},{18,16},{20,... | collective-permute-start | bytes 3145736 | tf_op jit(solution)/shard_map/ppermute | solution.py:112
  54.1 11.7 %collective-permute-start.10 = (bf16[1024,256]{1,0:T(8,128)(2,1)S(1)}, bf16[1024,256]{1,0:T(8,128)(2,1)S(1)}, u32[]{:S(2)}, u32[]{:S(2)}) collective-permute-start(bf16[1024,256]{1,0:T(8,128)(2,1)S(1)} %add_convert_fusion), channel_id=1, source_target_pairs={{0,8},{8,0},{16,24},{24,16},{1,9},{9,1},{17,25},{25,17},{2,10},{10... | collective-permute-start | bytes 1572872 | tf_op jit(solution)/shard_map/ppermute | solution.py:103
  54.5 11.4 %collective-permute-start.8 = (bf16[1024,256]{1,0:T(8,128)(2,1)S(1)}, bf16[1024,256]{1,0:T(8,128)(2,1)S(1)}, u32[]{:S(2)}, u32[]{:S(2)}) collective-permute-start(bf16[1024,256]{1,0:T(8,128)(2,1)S(1)} %add_convert_fusion.1), channel_id=1, source_target_pairs={{0,16},{8,24},{16,0},{24,8},{1,17},{9,25},{17,1},{25,9},{2,18},{10... | collective-permute-start | bytes 1572872 | tf_op jit(solution)/shard_map/ppermute | solution.py:103
  75.4 18.6 %collective-permute-start.15 = (bf16[256,512]{1,0:T(8,128)(2,1)S(1)}, bf16[256,512]{1,0:T(8,128)(2,1)S(1)}, u32[]{:S(2)}, u32[]{:S(2)}) collective-permute-start(bf16[256,512]{1,0:T(8,128)(2,1)S(1)} %get-tuple-element.60), channel_id=1, source_target_pairs={{0,4},{2,6},{4,0},{6,2},{1,5},{3,7},{5,1},{7,3},{8,12},{10,14},{12... | collective-permute-start | bytes 786440 | tf_op jit(solution)/shard_map/ppermute | solution.py:103
  75.4 18.6 %collective-permute-start.16 = (bf16[256,512]{1,0:T(8,128)(2,1)S(1)}, bf16[256,512]{1,0:T(8,128)(2,1)S(1)}, u32[]{:S(2)}, u32[]{:S(2)}) collective-permute-start(bf16[256,512]{1,0:T(8,128)(2,1)S(1)} %get-tuple-element.61), channel_id=1, source_target_pairs={{0,6},{2,4},{4,2},{6,0},{1,7},{3,5},{5,3},{7,1},{8,14},{10,12},{12... | collective-permute-start | bytes 786440 | tf_op jit(solution)/shard_map/ppermute | solution.py:103
  94.2 10.3 %collective-permute-start.17 = (bf16[256,512]{1,0:T(8,128)(2,1)S(1)}, bf16[256,512]{1,0:T(8,128)(2,1)S(1)}, u32[]{:S(2)}, u32[]{:S(2)}) collective-permute-start(bf16[256,512]{1,0:T(8,128)(2,1)S(1)} %multiply_convert_fusion), channel_id=1, source_target_pairs={{0,2},{2,0},{4,6},{6,4},{1,3},{3,1},{5,7},{7,5},{8,10},{10,8},{12,... | collective-permute-start | bytes 786440 | tf_op jit(solution)/shard_map/ppermute | solution.py:103
  104.6 27.5 %collective-permute-start.19 = (bf16[512,512]{1,0:T(8,128)(2,1)S(1)}, bf16[512,512]{1,0:T(8,128)(2,1)S(1)}, u32[]{:S(2)}, u32[]{:S(2)}) collective-permute-start(bf16[512,512]{1,0:T(8,128)(2,1)S(1)} %pad_maximum_fusion.3.refs_0_), channel_id=1, source_target_pairs={{0,16},{8,24},{16,0},{24,8},{1,17},{9,25},{17,1},{25,9},{2,18},{10... | collective-permute-start | bytes 1572872 | tf_op jit(solution)/shard_map/ppermute | solution.py:103
  105.9 26.2 %collective-permute-start.18 = (bf16[512,512]{1,0:T(8,128)(2,1)S(1)}, bf16[512,512]{1,0:T(8,128)(2,1)S(1)}, u32[]{:S(2)}, u32[]{:S(2)}) collective-permute-start(bf16[512,512]{1,0:T(8,128)(2,1)S(1)} %pad_maximum_fusion.3.refs_0_), channel_id=1, source_target_pairs={{0,8},{8,0},{16,24},{24,16},{1,9},{9,1},{17,25},{25,17},{2,10},{10... | collective-permute-start | bytes 1572872 | tf_op jit(solution)/shard_map/ppermute | solution.py:103
  107.2 24.9 %collective-permute-start.20 = (bf16[256,512]{1,0:T(8,128)(2,1)S(1)}, bf16[256,512]{1,0:T(8,128)(2,1)S(1)}, u32[]{:S(2)}, u32[]{:S(2)}) collective-permute-start(bf16[256,512]{1,0:T(8,128)(2,1)S(1)} %multiply_convert_fusion), channel_id=1, source_target_pairs={{0,4},{2,6},{4,0},{6,2},{1,5},{3,7},{5,1},{7,3},{8,12},{10,14},{12... | collective-permute-start | bytes 786440 | tf_op jit(solution)/shard_map/ppermute | solution.py:103
  133.6 19.4 %collective-permute-start.23 = (bf16[512,512]{1,0:T(8,128)(2,1)}, bf16[512,512]{1,0:T(8,128)(2,1)}, u32[]{:S(2)}, u32[]{:S(2)}) collective-permute-start(bf16[512,512]{1,0:T(8,128)(2,1)} %constant_dynamic-update-slice_fusion.refs_1_), channel_id=1, source_target_pairs={{0,16},{8,24},{16,0},{24,8},{1,17},{9,25},{17,1},{25,9},{2,18},{10... | collective-permute-start | bytes 1572872 | tf_op jit(solution)/shard_map/ppermute | solution.py:103
  133.8 19.2 %collective-permute-start.22 = (bf16[512,512]{1,0:T(8,128)(2,1)}, bf16[512,512]{1,0:T(8,128)(2,1)}, u32[]{:S(2)}, u32[]{:S(2)}) collective-permute-start(bf16[512,512]{1,0:T(8,128)(2,1)} %constant_dynamic-update-slice_fusion.refs_1_), channel_id=1, source_target_pairs={{0,8},{8,0},{16,24},{24,16},{1,9},{9,1},{17,25},{25,17},{2,10},{10... | collective-permute-start | bytes 1572872 | tf_op jit(solution)/shard_map/ppermute | solution.py:103
  134.8 16.7 %collective-permute-start.25 = (bf16[512,256]{1,0:T(8,128)(2,1)}, bf16[512,256]{1,0:T(8,128)(2,1)S(1)}, u32[]{:S(2)}, u32[]{:S(2)}) collective-permute-start(bf16[512,256]{1,0:T(8,128)(2,1)} %slice.54), channel_id=1, source_target_pairs={{0,16},{8,24},{16,0},{24,8},{1,17},{9,25},{17,1},{25,9},{2,18},{10... | collective-permute-start | bytes 786440 | tf_op jit(solution)/shard_map/ppermute | solution.py:103
  136.8 16.2 %collective-permute-start.24 = (bf16[512,256]{1,0:T(8,128)(2,1)}, bf16[512,256]{1,0:T(8,128)(2,1)}, u32[]{:S(2)}, u32[]{:S(2)}) collective-permute-start(bf16[512,256]{1,0:T(8,128)(2,1)} %slice.53), channel_id=1, source_target_pairs={{0,8},{8,0},{16,24},{24,16},{1,9},{9,1},{17,25},{25,17},{2,10},{10... | collective-permute-start | bytes 786440 | tf_op jit(solution)/shard_map/ppermute | solution.py:103
  138.0 35.0 %collective-permute-start.29 = (bf16[256,2048]{1,0:T(8,128)(2,1)}, bf16[256,2048]{1,0:T(8,128)(2,1)}, u32[]{:S(2)}, u32[]{:S(2)}) collective-permute-start(bf16[256,2048]{1,0:T(8,128)(2,1)} %collective-permute-done.12), channel_id=1, source_target_pairs={{4,6},{5,7},{12,14},{13,15},{20,22},{21,23},{28,30},{29,31}} | collective-permute-start | bytes 3145736 | tf_op jit(solution)/shard_map/ppermute | solution.py:112
  151.5 24.3 %collective-permute-start.30 = (bf16[256,2048]{1,0:T(8,128)(2,1)S(1)}, bf16[256,2048]{1,0:T(8,128)(2,1)S(1)}, u32[]{:S(2)}, u32[]{:S(2)}) collective-permute-start(bf16[256,2048]{1,0:T(8,128)(2,1)S(1)} %copy-done.8), channel_id=1, source_target_pairs={{2,0},{3,1},{10,8},{11,9},{18,16},{19,17},{26,24},{27,25}} | collective-permute-start | bytes 3145736 | tf_op jit(solution)/shard_map/ppermute | solution.py:112
  155.0 10.2 %collective-permute-start.27 = (bf16[512,256]{1,0:T(8,128)(2,1)S(1)}, bf16[512,256]{1,0:T(8,128)(2,1)S(1)}, u32[]{:S(2)}, u32[]{:S(2)}) collective-permute-start(bf16[512,256]{1,0:T(8,128)(2,1)S(1)} %slice.56), channel_id=1, source_target_pairs={{0,16},{8,24},{16,0},{24,8},{1,17},{9,25},{17,1},{25,9},{2,18},{10... | collective-permute-start | bytes 786440 | tf_op jit(solution)/shard_map/ppermute | solution.py:103
  168.0 11.2 %collective-permute-start.28 = (f32[16,64,128]{2,1,0:T(8,128)S(1)}, f32[16,64,128]{2,1,0:T(8,128)S(1)}, u32[]{:S(2)}, u32[]{:S(2)}) collective-permute-start(f32[16,64,128]{2,1,0:T(8,128)S(1)} %add_add_fusion.own_ref), channel_id=1, source_target_pairs={{0,1},{1,0},{2,3},{3,2},{4,5},{5,4},{6,7},{7,6},{8,9},{9,8},{10,11... | collective-permute-start | bytes 1572872 | tf_op jit(solution)/shard_map/ppermute | solution.py:103
  (16 other events, 151.5 us)

commit v6 on v5

--- a/solution.py
+++ b/solution.py
@@ -392,27 +392,54 @@
     )(columns.astype(jnp.int32), codes, slots, *onto)
 
 
-def act_slots_kernel(hot_ref, *refs):
+def act_slots_kernel(counts, skip, scalar_ref, hot_ref, *refs):
+    refs = refs[skip:]
     out_ref = refs[-1]
-    for z, act in enumerate(refs[:-1]):
-        into_slots(hot_ref, act[...], out_ref, z)
-
-
-def act_slots(acts, hot, blocks):
-    group, half = acts[0].shape
-    slots = hot.shape[0] * hot.shape[1] // blocks
+    per = out_ref.shape[2]
+    at = 0
+    for i, layout in enumerate(counts):
+        mine = refs[at:at + sum(layout)]
+        at += sum(layout)
+
+        @pl.when(pl.program_id(1) == i)
+        def _(i=i, layout=layout, mine=mine):
+            rows = []
+            n = 0
+            for count in layout:
+                part = mine[n][...]
+                for more in mine[n + 1:n + count]:
+                    part = part + more[...]
+                rows.append(part)
+                n += count
+            rows = rows[0] if len(rows) == 1 else jnp.concatenate(rows, axis=0)
+            value = jnp.dot(hot_ref[scalar_ref[i]], rows, preferred_element_type=jnp.float32).astype(jnp.bfloat16)
+            for b in range(out_ref.shape[1]):
+                out_ref[0, b] = value[b * per:(b + 1) * per]
+
+
+def act_slots(blocks_of, places, hot, count, held):
+    group, half = hot.shape[2], blocks_of[0][0][0].shape[1]
+    shards, per = hot.shape[0], hot.shape[1] // count
     tile = half // 4
-    return pl.pallas_call(
-        act_slots_kernel,
-        out_shape=jax.ShapeDtypeStruct((blocks, slots, half), jnp.bfloat16),
-        grid=(4,),
-        in_specs=[pl.BlockSpec(hot.shape, lambda i: (0, 0, 0))]
-        + [pl.BlockSpec((group, tile), lambda i: (0, i)) for _ in acts],
-        out_specs=pl.BlockSpec((blocks, slots, tile), lambda i: (0, 0, i)),
-        compiler_params=params(),
-        cost_estimate=cost(blocks * slots, group, half),
+    onto = [] if held is None else [held]
+    flat = [part for parts in blocks_of for row in parts for part in row]
+    out = pl.BlockSpec((1, count, per, tile), lambda i, j, s: (s[j], 0, 0, i))
+    return pl.pallas_call(
+        functools.partial(act_slots_kernel, [[len(row) for row in parts] for parts in blocks_of], len(onto)),
+        out_shape=jax.ShapeDtypeStruct((shards, count, per, half), jnp.bfloat16),
+        grid_spec=pltpu.PrefetchScalarGridSpec(
+            num_scalar_prefetch=1,
+            grid=(4, len(blocks_of)),
+            in_specs=[pl.BlockSpec(hot.shape, lambda i, j, s: (0, 0, 0))]
+            + [pl.BlockSpec(memory_space=pl.ANY) for _ in onto]
+            + [pl.BlockSpec((part.shape[0], tile), lambda i, j, s: (0, i)) for part in flat],
+            out_specs=out,
+        ),
+        compiler_params=params(),
+        cost_estimate=cost(count * per, group, half),
         name="act_slots",
-    )(hot, *acts)
+        input_output_aliases={2: 0} if onto else {},
+    )(jnp.stack(places).astype(jnp.int32), hot, *onto, *flat)
 
 
 def encoder_kernel(cap, shared, pre_ref, own_ref, theirs_ref, act_ref, out_ref):
@@ -426,21 +453,22 @@
                 parts.append(own_ref[n, here, :] + theirs_ref[n, there, :])
         total = jnp.concatenate(parts, axis=0)
         grad = jnp.where(pre_ref[n].astype(jnp.float32) > 0, total, 0.0).T.astype(jnp.bfloat16)
+        act = jnp.concatenate([act_ref[z, n] for z in range(act_ref.shape[0])], axis=0)
         out_ref[n * size:(n + 1) * size, :] = jnp.dot(
-            grad, act_ref[n], preferred_element_type=jnp.float32
+            grad, act, preferred_element_type=jnp.float32
         ).astype(jnp.bfloat16)
 
 
 def encoder_part(pre, own, theirs, acts, cap):
     blocks, slots, size = pre.shape
-    half = acts.shape[2]
+    half = acts.shape[3]
     shared = 2 if blocks % 2 == 0 else 1
     block = pl.BlockSpec((shared, slots, size), lambda i: (i, 0, 0))
     return pl.pallas_call(
         functools.partial(encoder_kernel, cap, shared),
         out_shape=jax.ShapeDtypeStruct((blocks * size, half), jnp.bfloat16),
         grid=(blocks // shared,),
-        in_specs=[block, block, block, pl.BlockSpec((shared, slots, half), lambda i: (i, 0, 0))],
+        in_specs=[block, block, block, pl.BlockSpec((acts.shape[0], shared) + acts.shape[2:], lambda i: (0, i, 0, 0))],
         out_specs=pl.BlockSpec((shared * size, half), lambda i: (i, 0)),
         compiler_params=params(),
         cost_estimate=cost(blocks * size, 256, half),
@@ -487,10 +515,10 @@
     at = places((1, 3), dp_here * lay_count, 2, 0) + places((2, 3), dp_here * lay_count, 2, 1)
     send_weights = gather_columns(decoder, jnp.stack(at), side)
 
-    acts = jnp.concatenate(
-        [columns(activations[0], dp_here), flip(columns(activations[0], 1 - dp_here), "dp", 1)]
-    )
-    message, acts, send_weights = lax.optimization_barrier((message, acts, send_weights))
+    own, inputs = lax.optimization_barrier((own, activations[0]))
+    acts = jnp.concatenate([columns(inputs, dp_here), flip(columns(inputs, 1 - dp_here), "dp", 1)])
+    corner = send_weights[:16, :128]
+    message, corner, acts = lax.optimization_barrier((message, corner, acts))
     up, down = [acts], [acts]
 
     def next_hops():
@@ -509,37 +537,51 @@
     goals = gather_columns(target, jnp.stack([which * lay_count + lay_here for which in (dp_here, 1 - dp_here)]), width)
     goals = jnp.concatenate([goals[:, :width], flip(goals[:, width:], "dp", 1)])
 
+    codes = spread_codes(message, first, lat_rows)
+    at = places((0, 2), dp_here * lay_count, 2, 0) + places((0, 1), dp_here * lay_count, 2, 1)
+    at, codes, target = lax.optimization_barrier((jnp.stack(at), codes, target))
+    keep_weights = gather_columns(decoder, at, side)
+    goals = gather_columns(target, jnp.stack([which * lay_count + lay_here for which in (dp_here, 1 - dp_here)]), width)
+    goals = jnp.concatenate([goals[:, :width], flip(goals[:, width:], "dp", 1)])
+
     def rows_for(spread, weights, n):
         return jnp.dot(spread, weights[:, n * width:(n + 1) * width], preferred_element_type=f32).astype(bf16)
 
     got = flip(rows_for(codes, send_weights, 0), "layer", 1), flip(rows_for(codes, send_weights, 1), "layer", 2)
-    keep_codes = codes
+    keep_codes, up[1], down[1] = lax.optimization_barrier((codes, up[1], down[1]))
+    early = group * 11 // 16
+    ups, downs = ([up[1][:early], up[1][early:]], [down[1][:early], down[1][early:]])
+    ups, downs = [[part] for part in ups], [[part] for part in downs]
+
+    def next_hop(part):
+        step = len(ups[part])
+        ups[part].append(hop(ups[part][-1], "latent", 1, step))
+        downs[part].append(hop(downs[part][-1], "latent", -1, step))
+
     if lat_count > 2:
-        keep_codes, up[1], down[1] = lax.optimization_barrier((codes, up[1], down[1]))
-        next_hops()
+        next_hop(0)
     kept = rows_for(keep_codes, keep_weights, 0), rows_for(keep_codes, keep_weights, 1)
 
     def add(one, two):
         return (one[:, side:].astype(f32) + two[:, side:].astype(f32)).astype(bf16)
 
     far = [flip(add(got[n], kept[n]), "layer", 2 - n) for n in range(2)]
-    far, goals, up[-1], down[-1] = lax.optimization_barrier((far, goals, up[-1], down[-1]))
+    far, goals, ups[0][-1], downs[0][-1] = lax.optimization_barrier((far, goals, ups[0][-1], downs[0][-1]))
 
     total, *sent = layer_sum((got[0], kept[0], far[0]), (got[1], kept[1], far[1]), lat_count)
     for r in range(1, lat_count):
         total = total + flip(sent[r - 1], "latent", r).astype(f32)
     errors = ((total - goals.astype(f32)) / tok_count).astype(bf16)
-    blocks_of = [errors] + [flip(errors, "latent", r) for r in range(1, lat_count)]
-    near = jnp.concatenate(blocks_of[:lat_count // 2])
-    one_near, two_near = flip(near, "layer", 1), flip(near, "layer", 2)
-    one_near, two_near, far_blocks, up[-1], down[-1] = lax.optimization_barrier(
-        (one_near, two_near, blocks_of[lat_count // 2:], up[-1], down[-1])
-    )
-    while len(up) < lat_count:
-        next_hops()
-    distant = jnp.concatenate(far_blocks)
+    others = [flip(errors, "latent", r) for r in range(1, lat_count)]
+    one_near, two_near = flip(errors, "layer", 1), flip(errors, "layer", 2)
+    one_near, two_near, others, ups, downs = lax.optimization_barrier((one_near, two_near, others, ups, downs))
+    distant = jnp.concatenate(others)
     one_far, two_far = flip(distant, "layer", 1), flip(distant, "layer", 2)
     three_near = flip(two_near[:, :side], "layer", 1), flip(one_near[:, side:], "layer", 2)
+    while len(ups[0]) < lat_count - 1:
+        next_hop(0)
+    while len(ups[1]) < lat_count - 2:
+        next_hop(1)
 
     hot, pre_slots, code_slots = make_slots(message, first, lat_rows, capacity)
 
@@ -547,21 +589,30 @@
         slots, grad = piece_grad(here, hot, decoder, weight_places(names), block_size)
         return grad, decoder_part(slots, code_slots, jnp.stack(places(names, 0)), half, dec)
 
-    grad, dec = grads_of([[(near,), (distant,)]], (0,), None)
-    one_far, two_far, three_near, grad, dec = lax.optimization_barrier((one_far, two_far, three_near, grad, dec))
+    grad, dec = grads_of([[(errors,), (distant,)]], (0,), None)
+    one_far, two_far, three_near, grad, dec, ups, downs = lax.optimization_barrier(
+        (one_far, two_far, three_near, grad, dec, ups, downs)
+    )
+    while len(ups[1]) < lat_count - 1:
+        next_hop(1)
     three_far = flip(two_far[:, :side], "layer", 1), flip(one_far[:, side:], "layer", 2)
-    along = [acts] + [down[k] + up[lat_count - k] for k in range(1, lat_count)]
-    along = jnp.stack(along)
-    along = [
-        lax.dynamic_index_in_dim(along, lax.rem((lat_here ^ r) - lat_here + lat_count, lat_count), 0, False)
-        for r in range(lat_count)
-    ]
-    along = act_slots(along, hot, local_blocks)
     more, dec = grads_of([[(one_near,), (one_far,)], [(two_near,), (two_far,)]], (1, 2), dec)
     three_far, more, dec = lax.optimization_barrier((three_far, more, dec))
     last, dec = grads_of([[three_near, three_far]], (3,), dec)
     grad = grad + more + last
-    enc = encoder_part(pre_slots, grad, flip(grad, "dp", 1), along, capacity)
+
+    shards = [lax.rem(lat_here + k, lat_count) ^ lat_here for k in range(lat_count)]
+    along = [[(acts,)]] + [
+        [(downs[n][k - 1], ups[n][lat_count - k - 1]) for n in range(2)] for k in range(1, lat_count)
+    ]
+    middle = [k for k in range(lat_count) if k == 0 or 2 * k == lat_count]
+    others = [k for k in range(lat_count) if k not in middle]
+    slotted = None
+    for names in (middle, others):
+        if names:
+            here = [along[k] for k in names]
+            slotted = act_slots(here, [shards[k] for k in names], hot, local_blocks, slotted)
+    enc = encoder_part(pre_slots, grad, flip(grad, "dp", 1), slotted, capacity)
     return dec[None], enc[None]
 
 

time: 189 us -> 202 us (1.069)
  Pallas kernels: 39 us -> 49.5 us
  starting transfers between devices: 45.4 us -> 54.8 us
  local copies, waits for them, and re-layouts: 9.48 us -> 5.84 us
  other arithmetic: 5.22 us -> 2.8 us
    ppermute x6 -> x10, waiting for transfers between devices: 17.6 us -> 42.3 us  [hop(): return lax.ppermute(value, axis, pairs)]
    ppermute x25, waiting for transfers between devices: 58.6 us -> 34.3 us  [flip(): return lax.ppermute(value, axis, [(i, i ^ bit) for i in range(count)])]
    pallas_call x1 -> x2, Pallas kernels: 2.4 us -> 11.7 us  [act_slots(): pl.pallas_call(functools.partial(act_slots_kernel, [[len(row) for row in...]
    ppermute x25, starting transfers between devices: 33.6 us -> 41.8 us  [flip(): return lax.ppermute(value, axis, [(i, i ^ bit) for i in range(count)])]
    another operation x4 -> x3, other arithmetic: 3.35 us -> 0.23 us  [the longest x2 0.15 us: act_slots(): jnp.stack(places).astype(jnp.int32)]
    ppermute x6 -> x10, starting transfers between devices: 11.8 us -> 13 us  [hop(): return lax.ppermute(value, axis, pairs)]
    unnamed x20 -> x37, local copies, waits for them, and re-layouts: 3.63 us -> 4.25 us
  transfers between devices with their start and end apart: 31 -> 35, of which waited for: 14 -> 16; matrix products, arithmetic and copies ran while one was open for 10% -> 5% of each run, Pallas kernels for 17% -> 19%
where the time goes in v6:
time: 202 us; the launch traced here: 200 us
  waiting for transfers between devices  76.6 us (38%)
  starting transfers between devices  54.8 us (27%)
  Pallas kernels  49.5 us (25%)
  matrix products  9.34 us (5%)
  local copies, waits for them, and re-layouts  5.84 us (3%)
  other arithmetic  2.8 us (1%)
    ppermute x10, waiting for transfers between devices, hop(): return lax.ppermute(value, axis, pairs)  42.3 us
    ppermute x25, starting transfers between devices, flip(): return lax.ppermute(value, axis, [(i, i ^ bit) for i in range(count)])  41.8 us
    ppermute x25, waiting for transfers between devices, flip(): return lax.ppermute(value, axis, [(i, i ^ bit) for i in range(count)])  34.3 us
    ppermute x10, starting transfers between devices, hop(): return lax.ppermute(value, axis, pairs)  13 us
    pallas_call x2, Pallas kernels, act_slots(): pl.pallas_call(functools.partial(act_slots_kernel, [[len(row) for row in...  11.7 us
    pallas_call x3, Pallas kernels, piece_grad(): pl.pallas_call(functools.partial(piece_grad_kernel, [[len(row) for row in...  10.4 us
    dot_general x4, matrix products, rows_for(): jnp.dot(spread, weights[:, n * width:(n + 1) * width], preferred_element_...  9.34 us
    pallas_call x3, Pallas kernels, gather_columns(): pl.pallas_call(gather_kernel, out_shape=jax.ShapeDtypeStruct((rows, count...  8.39 us
  transfers between devices with their start and end apart: 35, of which 16 were waited for; matrix products, arithmetic and copies ran while one was open for 5% of the time, Pallas kernels for 19%

profile of v6, /device:TPU:1, one launch (start us, length us, event | category | flops | bytes accessed | tf_op | source)
XLA Modules:
  0.0 200.1 jit_solution(2519579604294840248)
XLA Ops:
  3.6 4.8 %collective-permute-start.2 = (bf16[272,128]{1,0:T(8,128)(2,1)S(1)}, bf16[272,128]{1,0:T(8,128)(2,1)S(1)}, u32[]{:S(2)}, u32[]{:S(2)}) collective-permute-start(bf16[272,128]{1,0:T(8,128)(2,1)S(1)} %get-tuple-element.125), channel_id=1, source_target_pairs={{0,6},{2,4},{4,2},{6,0},{1,7},{3,5},{5,3},{7,1},{8,14},{10,12},{12... | collective-permute-start | bytes 208904 | tf_op jit(solution)/shard_map/ppermute | solution.py:103
  10.9 2.5 %collective-permute-done = bf16[272,128]{1,0:T(8,128)(2,1)S(1)} collective-permute-done((bf16[272,128]{1,0:T(8,128)(2,1)S(1)}, bf16[272,128]{1,0:T(8,128)(2,1)S(1)}, u32[]{:S(2)}, u32[]{:S(2)}) %collective-permute-start) | collective-permute-done | bytes 69664 | tf_op jit(solution)/shard_map/ppermute | solution.py:103
  15.7 3.9 %gather_columns.3 = bf16[2048,1024]{1,0:T(8,128)(2,1)S(1)} custom-call(s32[4]{0:T(128)S(1)} %pad_add_fusion.1.scalar_ref, bf16[1,2048,4096]{2,1,0:T(8,128)(2,1)} %weight_ref.5), custom_call_target="tpu_custom_call" | custom-call | flops 1048576 | bytes 1050112 | tf_op jit(solution)/shard_map/gather_columns/pallas_call | solution.py:139
  23.3 2.6 %spread_codes.1 = bf16[1024,2048]{1,0:T(8,128)(2,1)S(1)} custom-call(s32[1]{0:T(128)} %bitcast.1.scalar_ref, bf16[8,272,128]{2,1,0:T(8,128)(2,1)S(1)} %bitcast.46), custom_call_target="tpu_custom_call" | custom-call | flops 1048576 | bytes 1050112 | tf_op jit(solution)/shard_map/spread_codes/pallas_call | solution.py:185
  33.2 3.9 %gather_columns.4 = bf16[2048,1024]{1,0:T(8,128)(2,1)S(1)} custom-call(s32[4]{0:T(128)S(1)} %pad_add_fusion.scalar_ref, bf16[1,2048,4096]{2,1,0:T(8,128)(2,1)} %weight_ref.5), custom_call_target="tpu_custom_call" | custom-call | flops 1048576 | bytes 1050112 | tf_op jit(solution)/shard_map/gather_columns/pallas_call | solution.py:139
  37.0 7.3 %collective-permute-done.6 = bf16[256,2048]{1,0:T(8,128)(2,1)S(1)} collective-permute-done((bf16[256,2048]{1,0:T(8,128)(2,1)S(1)}, bf16[256,2048]{1,0:T(8,128)(2,1)S(1)}, u32[]{:S(2)}, u32[]{:S(2)}) %collective-permute-start.6) | collective-permute-done | bytes 1048608 | tf_op jit(solution)/shard_map/ppermute | solution.py:112
  44.4 3.9 %collective-permute-done.7 = bf16[256,2048]{1,0:T(8,128)(2,1)S(1)} collective-permute-done((bf16[256,2048]{1,0:T(8,128)(2,1)S(1)}, bf16[256,2048]{1,0:T(8,128)(2,1)S(1)}, u32[]{:S(2)}, u32[]{:S(2)}) %collective-permute-start.7) | collective-permute-done | bytes 1048608 | tf_op jit(solution)/shard_map/ppermute | solution.py:112
  61.7 7.0 %collective-permute-done.13.refs_1_ = bf16[176,2048]{1,0:T(8,128)(2,1)S(1)} collective-permute-done((bf16[176,2048]{1,0:T(8,128)(2,1)S(1)}, bf16[176,2048]{1,0:T(8,128)(2,1)S(1)}, u32[]{:S(2)}, u32[]{:S(2)}) %collective-permute-start.13) | collective-permute-done | bytes 720928 | tf_op jit(solution)/shard_map/ppermute | solution.py:112
  69.2 3.2 %collective-permute-start.14 = (bf16[256,512]{1,0:T(8,128)(2,1)S(1)}, bf16[256,512]{1,0:T(8,128)(2,1)S(1)}, u32[]{:S(2)}, u32[]{:S(2)}) collective-permute-start(bf16[256,512]{1,0:T(8,128)(2,1)S(1)} %get-tuple-element.76), channel_id=1, source_target_pairs={{0,2},{2,0},{4,6},{6,4},{1,3},{3,1},{5,7},{7,5},{8,10},{10,8},{12,... | collective-permute-start | bytes 786440 | tf_op jit(solution)/shard_map/ppermute | solution.py:103
  74.6 4.8 %collective-permute-done.14 = bf16[256,512]{1,0:T(8,128)(2,1)S(1)} collective-permute-done((bf16[256,512]{1,0:T(8,128)(2,1)S(1)}, bf16[256,512]{1,0:T(8,128)(2,1)S(1)}, u32[]{:S(2)}, u32[]{:S(2)}) %collective-permute-start.14) | collective-permute-done | bytes 262176 | tf_op jit(solution)/shard_map/ppermute | solution.py:103
  81.0 7.9 %collective-permute-done.16 = bf16[256,512]{1,0:T(8,128)(2,1)S(1)} collective-permute-done((bf16[256,512]{1,0:T(8,128)(2,1)S(1)}, bf16[256,512]{1,0:T(8,128)(2,1)S(1)}, u32[]{:S(2)}, u32[]{:S(2)}) %collective-permute-start.16) | collective-permute-done | bytes 262176 | tf_op jit(solution)/shard_map/ppermute | solution.py:103
  90.7 7.3 %collective-permute-start.19 = (bf16[256,512]{1,0:T(8,128)(2,1)S(1)}, bf16[256,512]{1,0:T(8,128)(2,1)S(1)}, u32[]{:S(2)}, u32[]{:S(2)}) collective-permute-start(bf16[256,512]{1,0:T(8,128)(2,1)S(1)} %multiply_convert_fusion.refs_0_), channel_id=1, source_target_pairs={{0,2},{2,0},{4,6},{6,4},{1,3},{3,1},{5,7},{7,5},{8,10},{10,8},{12,... | collective-permute-start | bytes 786440 | tf_op jit(solution)/shard_map/ppermute | solution.py:103
  100.3 4.7 %collective-permute-done.19 = bf16[256,512]{1,0:T(8,128)(2,1)S(1)} collective-permute-done((bf16[256,512]{1,0:T(8,128)(2,1)S(1)}, bf16[256,512]{1,0:T(8,128)(2,1)S(1)}, u32[]{:S(2)}, u32[]{:S(2)}) %collective-permute-start.19) | collective-permute-done | bytes 262176 | tf_op jit(solution)/shard_map/ppermute | solution.py:103
  105.6 8.6 %collective-permute-done.21 = bf16[256,512]{1,0:T(8,128)(2,1)S(1)} collective-permute-done((bf16[256,512]{1,0:T(8,128)(2,1)S(1)}, bf16[256,512]{1,0:T(8,128)(2,1)S(1)}, u32[]{:S(2)}, u32[]{:S(2)}) %collective-permute-start.21) | collective-permute-done | bytes 262176 | tf_op jit(solution)/shard_map/ppermute | solution.py:103
  123.4 2.8 %piece_grad.3 = (bf16[1,16,64,512]{3,2,1,0:T(8,128)(2,1)S(1)}, f32[16,64,128]{2,1,0:T(8,128)S(1)}) custom-call(s32[1]{0:T(128)} %bitcast.24.scalar_ref, bf16[4,256,256]{2,1,0:T(8,128)(2,1)S(1)} %get-tuple-element.64.hot_ref, bf16[1,2048,4096]{2,1,0:T(8,128)(2,1)} %weight_ref.5, bf16[256,512]{1,0:T(8,128)(2,1)S(1)} %multiply_convert_fusion.refs_0_, ...), custom_call_target="tpu_custom_call" | custom-call | flops 134217728 | bytes 851968 | tf_op jit(solution)/shard_map/piece_grad/pallas_call | solution.py:343
  128.2 16.8 %collective-permute-done.29.refs_3_ = bf16[80,2048]{1,0:T(8,128)(2,1)} collective-permute-done((bf16[80,2048]{1,0:T(8,128)(2,1)S(1)}, bf16[80,2048]{1,0:T(8,128)(2,1)}, u32[]{:S(2)}, u32[]{:S(2)}) %collective-permute-start.29) | collective-permute-done | bytes 327712 | tf_op jit(solution)/shard_map/ppermute | solution.py:112
  146.9 4.8 %piece_grad.4 = (bf16[2,16,64,512]{3,2,1,0:T(8,128)(2,1)S(1)}, f32[16,64,128]{2,1,0:T(8,128)S(1)}) custom-call(s32[2]{0:T(128)S(1)} %pad_add_fusion.3.scalar_ref, bf16[4,256,256]{2,1,0:T(8,128)(2,1)S(1)} %get-tuple-element.64.hot_ref, bf16[1,2048,4096]{2,1,0:T(8,128)(2,1)} %weight_ref.5, bf16[256,512]{1,0:T(8,128)(2,1)S(1)} %collective-permute-done.17.refs_0_, ...), custom_call_target="tpu_custom_call" | custom-call | flops 268435456 | bytes 1441792 | tf_op jit(solution)/shard_map/piece_grad/pallas_call | solution.py:343
  151.7 3.3 %decoder_part.4.refs_0_ = bf16[2048,2048]{1,0:T(8,128)(2,1)} custom-call(s32[2]{0:T(128)S(1)} %pad_add_fusion.4.scalar_ref, bf16[16,128,64]{2,1,0:T(8,128)(2,1)S(1)} %get-tuple-element.63.code_ref, bf16[2,16,64,512]{3,2,1,0:T(8,128)(2,1)S(1)} %get-tuple-element.100.slots_ref, bf16[2048,2048]{1,0:T(8,128)(2,1)} %decoder_part.3.refs_0_), custom_call_target="tpu_custom_call", output_to_operand_aliasing={{}: (3, {})} | custom-call | flops 268435456 | bytes 1441792 | tf_op jit(solution)/shard_map/decoder_part/pallas_call | solution.py:378
  155.0 2.8 %piece_grad.5 = (bf16[1,16,64,512]{3,2,1,0:T(8,128)(2,1)S(1)}, f32[16,64,128]{2,1,0:T(8,128)S(1)}) custom-call(s32[1]{0:T(128)} %bitcast.15.scalar_ref, bf16[4,256,256]{2,1,0:T(8,128)(2,1)S(1)} %get-tuple-element.64.hot_ref, bf16[1,2048,4096]{2,1,0:T(8,128)(2,1)} %weight_ref.5, bf16[256,256]{1,0:T(8,128)(2,1)S(1)} %collective-permute-done.24.refs_0_, ...), custom_call_target="tpu_custom_call" | custom-call | flops 134217728 | bytes 851968 | tf_op jit(solution)/shard_map/piece_grad/pallas_call | solution.py:343
  159.6 6.4 %collective-permute-start.32 = (f32[16,64,128]{2,1,0:T(8,128)}, f32[16,64,128]{2,1,0:T(8,128)}, u32[]{:S(2)}, u32[]{:S(2)}) collective-permute-start(f32[16,64,128]{2,1,0:T(8,128)} %add_add_fusion.own_ref), channel_id=1, source_target_pairs={{0,1},{1,0},{2,3},{3,2},{4,5},{5,4},{6,7},{7,6},{8,9},{9,8},{10,11... | collective-permute-start | bytes 1572872 | tf_op jit(solution)/shard_map/ppermute | solution.py:103
  171.2 5.8 %act_slots.2.refs_0_ = bf16[4,16,16,2048]{3,2,1,0:T(8,128)(2,1)S(1)} custom-call(s32[2]{0:T(128)S(1)} %pad_add_fusion.6.scalar_ref, bf16[4,256,256]{2,1,0:T(8,128)(2,1)S(1)} %get-tuple-element.64.hot_ref, bf16[256,2048]{1,0:T(8,128)(2,1)S(1)} %pad_maximum_fusion.refs_0_, bf16[176,2048]{1,0:T(8,128)(2,1)S(1)} %copy-done.14, bf16[176,2048]{1,0:T(8,128)(2,1)S(1)} %copy-done.12, ...), custom_call_target="tpu_custom_call" | custom-call | flops 67108864 | bytes 557056 | tf_op jit(solution)/shard_map/act_slots/pallas_call | solution.py:427
  177.1 7.3 %collective-permute-done.34.refs_7_ = bf16[80,2048]{1,0:T(8,128)(2,1)} collective-permute-done((bf16[80,2048]{1,0:T(8,128)(2,1)}, bf16[80,2048]{1,0:T(8,128)(2,1)}, u32[]{:S(2)}, u32[]{:S(2)}) %collective-permute-start.34) | collective-permute-done | bytes 327712 | tf_op jit(solution)/shard_map/ppermute | solution.py:112
  184.4 5.9 %act_slots.3.act_ref = bf16[4,16,16,2048]{3,2,1,0:T(8,128)(2,1)S(1)} custom-call(s32[2]{0:T(128)S(1)} %pad_add_fusion.5.scalar_ref, bf16[4,256,256]{2,1,0:T(8,128)(2,1)S(1)} %get-tuple-element.64.hot_ref, bf16[4,16,16,2048]{3,2,1,0:T(8,128)(2,1)S(1)} %act_slots.2.refs_0_, bf16[176,2048]{1,0:T(8,128)(2,1)S(1)} %slice.66.refs_1_, ...), custom_call_target="tpu_custom_call", output_to_operand_aliasing={{}: (2, {})} | custom-call | flops 67108864 | bytes 557056 | tf_op jit(solution)/shard_map/act_slots/pallas_call | solution.py:427
  192.3 7.8 %encoder_part.1 = bf16[2048,2048]{1,0:T(8,128)(2,1)} custom-call(bf16[16,64,128]{2,1,0:T(8,128)(2,1)S(1)} %copy-done.16, f32[16,64,128]{2,1,0:T(8,128)} %add_add_fusion.own_ref, f32[16,64,128]{2,1,0:T(8,128)} %collective-permute-done.32.theirs_ref, bf16[4,16,16,2048]{3,2,1,0:T(8,128)(2,1)S(1)} %act_slots.3.act_ref), custom_call_target="tpu_custom_call" | custom-call | flops 536870912 | bytes 2621440 | tf_op jit(solution)/shard_map/encoder_part/pallas_call | solution.py:467
  (131 shorter events, 63.1 us)
Async XLA Ops:
  3.5 9.9 %collective-permute-start.3 = (bf16[128,2048]{1,0:T(8,128)(2,1)S(1)}, bf16[128,2048]{1,0:T(8,128)(2,1)S(1)}, u32[]{:S(2)}, u32[]{:S(2)}) collective-permute-start(bf16[128,2048]{1,0:T(8,128)(2,1)S(1)} %get-tuple-element.121), channel_id=1, source_target_pairs={{0,1},{1,0},{2,3},{3,2},{4,5},{5,4},{6,7},{7,6},{8,9},{9,8},{10,11... | collective-permute-start | bytes 1572872 | tf_op jit(solution)/shard_map/ppermute | solution.py:103
  19.7 24.7 %collective-permute-start.6 = (bf16[256,2048]{1,0:T(8,128)(2,1)S(1)}, bf16[256,2048]{1,0:T(8,128)(2,1)S(1)}, u32[]{:S(2)}, u32[]{:S(2)}) collective-permute-start(bf16[256,2048]{1,0:T(8,128)(2,1)S(1)} %pad_maximum_fusion.refs_0_), channel_id=1, source_target_pairs={{0,2},{2,4},{4,6},{1,3},{3,5},{5,7},{8,10},{10,12},{12,14},{9,11},... | collective-permute-start | bytes 3145736 | tf_op jit(solution)/shard_map/ppermute | solution.py:112
  21.9 26.3 %collective-permute-start.7 = (bf16[256,2048]{1,0:T(8,128)(2,1)S(1)}, bf16[256,2048]{1,0:T(8,128)(2,1)S(1)}, u32[]{:S(2)}, u32[]{:S(2)}) collective-permute-start(bf16[256,2048]{1,0:T(8,128)(2,1)S(1)} %pad_maximum_fusion.refs_0_), channel_id=1, source_target_pairs={{2,0},{4,2},{6,4},{3,1},{5,3},{7,5},{10,8},{12,10},{14,12},{11,9},... | collective-permute-start | bytes 3145736 | tf_op jit(solution)/shard_map/ppermute | solution.py:112
  28.3 27.0 %collective-permute-start.9 = (bf16[1024,512]{1,0:T(8,128)(2,1)S(1)}, bf16[1024,512]{1,0:T(8,128)(2,1)S(1)}, u32[]{:S(2)}, u32[]{:S(2)}) collective-permute-start(bf16[1024,512]{1,0:T(8,128)(2,1)S(1)} %fusion.14), channel_id=1, source_target_pairs={{0,16},{8,24},{16,0},{24,8},{1,17},{9,25},{17,1},{25,9},{2,18},{10... | collective-permute-start | bytes 3145736 | tf_op jit(solution)/shard_map/ppermute | solution.py:103
  31.9 24.8 %collective-permute-start.5 = (bf16[1024,512]{1,0:T(8,128)(2,1)S(1)}, bf16[1024,512]{1,0:T(8,128)(2,1)S(1)}, u32[]{:S(2)}, u32[]{:S(2)}) collective-permute-start(bf16[1024,512]{1,0:T(8,128)(2,1)S(1)} %fusion.8), channel_id=1, source_target_pairs={{0,8},{8,0},{16,24},{24,16},{1,9},{9,1},{17,25},{25,17},{2,10},{10... | collective-permute-start | bytes 3145736 | tf_op jit(solution)/shard_map/ppermute | solution.py:103
  48.3 13.4 %collective-permute-start.12 = (bf16[176,2048]{1,0:T(8,128)(2,1)S(1)}, bf16[176,2048]{1,0:T(8,128)(2,1)S(1)}, u32[]{:S(2)}, u32[]{:S(2)}) collective-permute-start(bf16[176,2048]{1,0:T(8,128)(2,1)S(1)} %slice.65.refs_6_), channel_id=1, source_target_pairs={{2,4},{4,6},{3,5},{5,7},{10,12},{12,14},{11,13},{13,15},{18,20},{2... | collective-permute-start | bytes 2162696 | tf_op jit(solution)/shard_map/ppermute | solution.py:112
  49.0 19.7 %collective-permute-start.13 = (bf16[176,2048]{1,0:T(8,128)(2,1)S(1)}, bf16[176,2048]{1,0:T(8,128)(2,1)S(1)}, u32[]{:S(2)}, u32[]{:S(2)}) collective-permute-start(bf16[176,2048]{1,0:T(8,128)(2,1)S(1)} %slice.66.refs_1_), channel_id=1, source_target_pairs={{2,0},{4,2},{3,1},{5,3},{10,8},{12,10},{11,9},{13,11},{18,16},{20,... | collective-permute-start | bytes 2162696 | tf_op jit(solution)/shard_map/ppermute | solution.py:112
  55.4 13.4 %collective-permute-start.10 = (bf16[1024,256]{1,0:T(8,128)(2,1)S(1)}, bf16[1024,256]{1,0:T(8,128)(2,1)S(1)}, u32[]{:S(2)}, u32[]{:S(2)}) collective-permute-start(bf16[1024,256]{1,0:T(8,128)(2,1)S(1)} %add_convert_fusion), channel_id=1, source_target_pairs={{0,8},{8,0},{16,24},{24,16},{1,9},{9,1},{17,25},{25,17},{2,10},{10... | collective-permute-start | bytes 1572872 | tf_op jit(solution)/shard_map/ppermute | solution.py:103
  56.8 12.1 %collective-permute-start.8 = (bf16[1024,256]{1,0:T(8,128)(2,1)S(1)}, bf16[1024,256]{1,0:T(8,128)(2,1)S(1)}, u32[]{:S(2)}, u32[]{:S(2)}) collective-permute-start(bf16[1024,256]{1,0:T(8,128)(2,1)S(1)} %add_convert_fusion.1), channel_id=1, source_target_pairs={{0,16},{8,24},{16,0},{24,8},{1,17},{9,25},{17,1},{25,9},{2,18},{10... | collective-permute-start | bytes 1572872 | tf_op jit(solution)/shard_map/ppermute | solution.py:103
  69.2 10.1 %collective-permute-start.14 = (bf16[256,512]{1,0:T(8,128)(2,1)S(1)}, bf16[256,512]{1,0:T(8,128)(2,1)S(1)}, u32[]{:S(2)}, u32[]{:S(2)}) collective-permute-start(bf16[256,512]{1,0:T(8,128)(2,1)S(1)} %get-tuple-element.76), channel_id=1, source_target_pairs={{0,2},{2,0},{4,6},{6,4},{1,3},{3,1},{5,7},{7,5},{8,10},{10,8},{12,... | collective-permute-start | bytes 786440 | tf_op jit(solution)/shard_map/ppermute | solution.py:103
  73.4 15.5 %collective-permute-start.16 = (bf16[256,512]{1,0:T(8,128)(2,1)S(1)}, bf16[256,512]{1,0:T(8,128)(2,1)S(1)}, u32[]{:S(2)}, u32[]{:S(2)}) collective-permute-start(bf16[256,512]{1,0:T(8,128)(2,1)S(1)} %get-tuple-element.78), channel_id=1, source_target_pairs={{0,6},{2,4},{4,2},{6,0},{1,7},{3,5},{5,3},{7,1},{8,14},{10,12},{12... | collective-permute-start | bytes 786440 | tf_op jit(solution)/shard_map/ppermute | solution.py:103
  89.1 11.2 %collective-permute-start.17 = (bf16[256,512]{1,0:T(8,128)(2,1)S(1)}, bf16[256,512]{1,0:T(8,128)(2,1)S(1)}, u32[]{:S(2)}, u32[]{:S(2)}) collective-permute-start(bf16[256,512]{1,0:T(8,128)(2,1)S(1)} %multiply_convert_fusion.refs_0_), channel_id=1, source_target_pairs={{0,8},{8,0},{16,24},{24,16},{1,9},{9,1},{17,25},{25,17},{2,10},{10... | collective-permute-start | bytes 786440 | tf_op jit(solution)/shard_map/ppermute | solution.py:103
  89.4 10.9 %collective-permute-start.18 = (bf16[256,512]{1,0:T(8,128)(2,1)S(1)}, bf16[256,512]{1,0:T(8,128)(2,1)S(1)}, u32[]{:S(2)}, u32[]{:S(2)}) collective-permute-start(bf16[256,512]{1,0:T(8,128)(2,1)S(1)} %multiply_convert_fusion.refs_0_), channel_id=1, source_target_pairs={{0,16},{8,24},{16,0},{24,8},{1,17},{9,25},{17,1},{25,9},{2,18},{10... | collective-permute-start | bytes 786440 | tf_op jit(solution)/shard_map/ppermute | solution.py:103
  90.7 14.4 %collective-permute-start.19 = (bf16[256,512]{1,0:T(8,128)(2,1)S(1)}, bf16[256,512]{1,0:T(8,128)(2,1)S(1)}, u32[]{:S(2)}, u32[]{:S(2)}) collective-permute-start(bf16[256,512]{1,0:T(8,128)(2,1)S(1)} %multiply_convert_fusion.refs_0_), channel_id=1, source_target_pairs={{0,2},{2,0},{4,6},{6,4},{1,3},{3,1},{5,7},{7,5},{8,10},{10,8},{12,... | collective-permute-start | bytes 786440 | tf_op jit(solution)/shard_map/ppermute | solution.py:103
  99.0 15.1 %collective-permute-start.21 = (bf16[256,512]{1,0:T(8,128)(2,1)S(1)}, bf16[256,512]{1,0:T(8,128)(2,1)S(1)}, u32[]{:S(2)}, u32[]{:S(2)}) collective-permute-start(bf16[256,512]{1,0:T(8,128)(2,1)S(1)} %multiply_convert_fusion.refs_0_), channel_id=1, source_target_pairs={{0,6},{2,4},{4,2},{6,0},{1,7},{3,5},{5,3},{7,1},{8,14},{10,12},{12... | collective-permute-start | bytes 786440 | tf_op jit(solution)/shard_map/ppermute | solution.py:103
  115.9 29.2 %collective-permute-start.22 = (bf16[768,512]{1,0:T(8,128)(2,1)S(1)}, bf16[768,512]{1,0:T(8,128)(2,1)S(1)}, u32[]{:S(2)}, u32[]{:S(2)}) collective-permute-start(bf16[768,512]{1,0:T(8,128)(2,1)S(1)} %constant_dynamic-update-slice_fusion.refs_1_), channel_id=1, source_target_pairs={{0,8},{8,0},{16,24},{24,16},{1,9},{9,1},{17,25},{25,17},{2,10},{10... | collective-permute-start | bytes 2359304 | tf_op jit(solution)/shard_map/ppermute | solution.py:103
  116.2 28.9 %collective-permute-start.23 = (bf16[768,512]{1,0:T(8,128)(2,1)S(1)}, bf16[768,512]{1,0:T(8,128)(2,1)S(1)}, u32[]{:S(2)}, u32[]{:S(2)}) collective-permute-start(bf16[768,512]{1,0:T(8,128)(2,1)S(1)} %constant_dynamic-update-slice_fusion.refs_1_), channel_id=1, source_target_pairs={{0,16},{8,24},{16,0},{24,8},{1,17},{9,25},{17,1},{25,9},{2,18},{10... | collective-permute-start | bytes 2359304 | tf_op jit(solution)/shard_map/ppermute | solution.py:103
  117.4 27.7 %collective-permute-start.26 = (bf16[176,2048]{1,0:T(8,128)(2,1)S(1)}, bf16[176,2048]{1,0:T(8,128)(2,1)S(1)}, u32[]{:S(2)}, u32[]{:S(2)}) collective-permute-start(bf16[176,2048]{1,0:T(8,128)(2,1)S(1)} %collective-permute-done.12.refs_2_), channel_id=1, source_target_pairs={{4,6},{5,7},{12,14},{13,15},{20,22},{21,23},{28,30},{29,31}} | collective-permute-start | bytes 2162696 | tf_op jit(solution)/shard_map/ppermute | solution.py:112
  118.4 26.7 %collective-permute-start.28 = (bf16[176,2048]{1,0:T(8,128)(2,1)S(1)}, bf16[176,2048]{1,0:T(8,128)(2,1)S(1)}, u32[]{:S(2)}, u32[]{:S(2)}) collective-permute-start(bf16[176,2048]{1,0:T(8,128)(2,1)S(1)} %collective-permute-done.13.refs_1_), channel_id=1, source_target_pairs={{2,0},{3,1},{10,8},{11,9},{18,16},{19,17},{26,24},{27,25}} | collective-permute-start | bytes 2162696 | tf_op jit(solution)/shard_map/ppermute | solution.py:112
  121.1 24.0 %collective-permute-start.29 = (bf16[80,2048]{1,0:T(8,128)(2,1)S(1)}, bf16[80,2048]{1,0:T(8,128)(2,1)}, u32[]{:S(2)}, u32[]{:S(2)}) collective-permute-start(bf16[80,2048]{1,0:T(8,128)(2,1)S(1)} %slice.68.refs_3_), channel_id=1, source_target_pairs={{2,0},{4,2},{3,1},{5,3},{10,8},{12,10},{11,9},{13,11},{18,16},{20,... | collective-permute-start | bytes 983048 | tf_op jit(solution)/shard_map/ppermute | solution.py:112
  145.1 9.9 %collective-permute-start.30 = (bf16[768,256]{1,0:T(8,128)(2,1)S(1)}, bf16[768,256]{1,0:T(8,128)(2,1)S(1)}, u32[]{:S(2)}, u32[]{:S(2)}) collective-permute-start(bf16[768,256]{1,0:T(8,128)(2,1)S(1)} %slice.71), channel_id=1, source_target_pairs={{0,8},{8,0},{16,24},{24,16},{1,9},{9,1},{17,25},{25,17},{2,10},{10... | collective-permute-start | bytes 1179656 | tf_op jit(solution)/shard_map/ppermute | solution.py:103
  159.6 32.7 %collective-permute-start.32 = (f32[16,64,128]{2,1,0:T(8,128)}, f32[16,64,128]{2,1,0:T(8,128)}, u32[]{:S(2)}, u32[]{:S(2)}) collective-permute-start(f32[16,64,128]{2,1,0:T(8,128)} %add_add_fusion.own_ref), channel_id=1, source_target_pairs={{0,1},{1,0},{2,3},{3,2},{4,5},{5,4},{6,7},{7,6},{8,9},{9,8},{10,11... | collective-permute-start | bytes 1572872 | tf_op jit(solution)/shard_map/ppermute | solution.py:103
  166.0 11.1 %collective-permute-start.33 = (bf16[80,2048]{1,0:T(8,128)(2,1)}, bf16[80,2048]{1,0:T(8,128)(2,1)}, u32[]{:S(2)}, u32[]{:S(2)}) collective-permute-start(bf16[80,2048]{1,0:T(8,128)(2,1)} %collective-permute-done.27.refs_4_), channel_id=1, source_target_pairs={{4,6},{5,7},{12,14},{13,15},{20,22},{21,23},{28,30},{29,31}} | collective-permute-start | bytes 983048 | tf_op jit(solution)/shard_map/ppermute | solution.py:112
  167.4 17.0 %collective-permute-start.34 = (bf16[80,2048]{1,0:T(8,128)(2,1)}, bf16[80,2048]{1,0:T(8,128)(2,1)}, u32[]{:S(2)}, u32[]{:S(2)}) collective-permute-start(bf16[80,2048]{1,0:T(8,128)(2,1)} %collective-permute-done.29.refs_3_), channel_id=1, source_target_pairs={{2,0},{3,1},{10,8},{11,9},{18,16},{19,17},{26,24},{27,25}} | collective-permute-start | bytes 983048 | tf_op jit(solution)/shard_map/ppermute | solution.py:112
  (28 other events, 319.3 us)

commit v7 on v5

--- a/solution.py
+++ b/solution.py
@@ -392,27 +392,42 @@
     )(columns.astype(jnp.int32), codes, slots, *onto)
 
 
-def act_slots_kernel(hot_ref, *refs):
+def act_slots_kernel(layouts, scalar_ref, hot_ref, *refs):
     out_ref = refs[-1]
-    for z, act in enumerate(refs[:-1]):
-        into_slots(hot_ref, act[...], out_ref, z)
-
-
-def act_slots(acts, hot, blocks):
-    group, half = acts[0].shape
-    slots = hot.shape[0] * hot.shape[1] // blocks
+    per = out_ref.shape[1] // hot_ref.shape[0]
+    at = 0
+    for i, layout in enumerate(layouts):
+        z = scalar_ref[i]
+        total = None
+        for count in layout:
+            rows = [ref[...] for ref in refs[at:at + count]]
+            rows = rows[0] if count == 1 else jnp.concatenate(rows, axis=0)
+            total = rows if total is None else total + rows
+            at += count
+        value = jnp.dot(hot_ref[z], total, preferred_element_type=jnp.float32).astype(jnp.bfloat16)
+        to = pl.ds(pl.multiple_of(z * per, per), per)
+        for b in range(out_ref.shape[0]):
+            out_ref[b, to, :] = value[b * per:(b + 1) * per]
+
+
+def act_slots(terms_of, places, hot, count):
+    half = terms_of[0][0][0].shape[1]
+    slots = hot.shape[0] * hot.shape[1] // count
     tile = half // 4
-    return pl.pallas_call(
-        act_slots_kernel,
-        out_shape=jax.ShapeDtypeStruct((blocks, slots, half), jnp.bfloat16),
-        grid=(4,),
-        in_specs=[pl.BlockSpec(hot.shape, lambda i: (0, 0, 0))]
-        + [pl.BlockSpec((group, tile), lambda i: (0, i)) for _ in acts],
-        out_specs=pl.BlockSpec((blocks, slots, tile), lambda i: (0, 0, i)),
-        compiler_params=params(),
-        cost_estimate=cost(blocks * slots, group, half),
+    flat = [part for terms in terms_of for term in terms for part in term]
+    return pl.pallas_call(
+        functools.partial(act_slots_kernel, [[len(term) for term in terms] for terms in terms_of]),
+        out_shape=jax.ShapeDtypeStruct((count, slots, half), jnp.bfloat16),
+        grid_spec=pltpu.PrefetchScalarGridSpec(
+            num_scalar_prefetch=1,
+            grid=(4,),
+            in_specs=[resident(hot.shape)] + [pl.BlockSpec((part.shape[0], tile), lambda i, s: (0, i)) for part in flat],
+            out_specs=pl.BlockSpec((count, slots, tile), lambda i, s: (0, 0, i)),
+        ),
+        compiler_params=params(),
+        cost_estimate=cost(count * slots, 256, half),
         name="act_slots",
-    )(hot, *acts)
+    )(jnp.stack(places).astype(jnp.int32), hot, *flat)
 
 
 def encoder_kernel(cap, shared, pre_ref, own_ref, theirs_ref, act_ref, out_ref):
@@ -482,15 +497,17 @@
     pre_rows = jnp.swapaxes(pre_codes[0], 0, 1).reshape(active_count * tok_count, block_size)
     id_rows = jnp.pad(block_ids[0].T, ((0, 16 - active_count), (0, 0))).astype(bf16)
     own = jnp.concatenate([pre_rows, id_rows], axis=0)
-    message = jnp.stack([own] + [flip(own, "latent", r) for r in range(1, lat_count)])
-
     at = places((1, 3), dp_here * lay_count, 2, 0) + places((2, 3), dp_here * lay_count, 2, 1)
     send_weights = gather_columns(decoder, jnp.stack(at), side)
 
-    acts = jnp.concatenate(
-        [columns(activations[0], dp_here), flip(columns(activations[0], 1 - dp_here), "dp", 1)]
-    )
-    message, acts, send_weights = lax.optimization_barrier((message, acts, send_weights))
+    corner = send_weights[:16, :128]
+    later, corner = lax.optimization_barrier((own, corner))
+    message = [own, flip(later, "latent", 1)] + [flip(own, "latent", r) for r in range(2, lat_count)]
+    message = jnp.stack(message)
+
+    own, inputs = lax.optimization_barrier((own, activations[0]))
+    acts = jnp.concatenate([columns(inputs, dp_here), flip(columns(inputs, 1 - dp_here), "dp", 1)])
+    message, acts = lax.optimization_barrier((message, acts))
     up, down = [acts], [acts]
 
     def next_hops():
@@ -509,13 +526,19 @@
     goals = gather_columns(target, jnp.stack([which * lay_count + lay_here for which in (dp_here, 1 - dp_here)]), width)
     goals = jnp.concatenate([goals[:, :width], flip(goals[:, width:], "dp", 1)])
 
+    codes = spread_codes(message, first, lat_rows)
+    at = places((0, 2), dp_here * lay_count, 2, 0) + places((0, 1), dp_here * lay_count, 2, 1)
+    at, codes, target = lax.optimization_barrier((jnp.stack(at), codes, target))
+    keep_weights = gather_columns(decoder, at, side)
+    goals = gather_columns(target, jnp.stack([which * lay_count + lay_here for which in (dp_here, 1 - dp_here)]), width)
+    goals = jnp.concatenate([goals[:, :width], flip(goals[:, width:], "dp", 1)])
+
     def rows_for(spread, weights, n):
         return jnp.dot(spread, weights[:, n * width:(n + 1) * width], preferred_element_type=f32).astype(bf16)
 
     got = flip(rows_for(codes, send_weights, 0), "layer", 1), flip(rows_for(codes, send_weights, 1), "layer", 2)
-    keep_codes = codes
+    keep_codes, up[1], down[1] = lax.optimization_barrier((codes, up[1], down[1]))
     if lat_count > 2:
-        keep_codes, up[1], down[1] = lax.optimization_barrier((codes, up[1], down[1]))
         next_hops()
     kept = rows_for(keep_codes, keep_weights, 0), rows_for(keep_codes, keep_weights, 1)
 
@@ -529,17 +552,21 @@
     for r in range(1, lat_count):
         total = total + flip(sent[r - 1], "latent", r).astype(f32)
     errors = ((total - goals.astype(f32)) / tok_count).astype(bf16)
-    blocks_of = [errors] + [flip(errors, "latent", r) for r in range(1, lat_count)]
-    near = jnp.concatenate(blocks_of[:lat_count // 2])
-    one_near, two_near = flip(near, "layer", 1), flip(near, "layer", 2)
-    one_near, two_near, far_blocks, up[-1], down[-1] = lax.optimization_barrier(
-        (one_near, two_near, blocks_of[lat_count // 2:], up[-1], down[-1])
-    )
-    while len(up) < lat_count:
-        next_hops()
-    distant = jnp.concatenate(far_blocks)
+    others = [flip(errors, "latent", r) for r in range(1, lat_count)]
+    one_near, two_near = flip(errors, "layer", 1), flip(errors, "layer", 2)
+    one_near, two_near, others, up[-1], down[-1] = lax.optimization_barrier(
+        (one_near, two_near, others, up[-1], down[-1])
+    )
+    distant = jnp.concatenate(others)
     one_far, two_far = flip(distant, "layer", 1), flip(distant, "layer", 2)
     three_near = flip(two_near[:, :side], "layer", 1), flip(one_near[:, side:], "layer", 2)
+    while len(up) < lat_count - 1:
+        next_hops()
+    early = group * 11 // 16
+    ends = []
+    if len(up) < lat_count:
+        for rows in (slice(0, early), slice(early, group)):
+            ends.append([hop(up[-1][rows], "latent", 1, len(up) - 1), hop(down[-1][rows], "latent", -1, len(up) - 1)])
 
     hot, pre_slots, code_slots = make_slots(message, first, lat_rows, capacity)
 
@@ -547,21 +574,24 @@
         slots, grad = piece_grad(here, hot, decoder, weight_places(names), block_size)
         return grad, decoder_part(slots, code_slots, jnp.stack(places(names, 0)), half, dec)
 
-    grad, dec = grads_of([[(near,), (distant,)]], (0,), None)
-    one_far, two_far, three_near, grad, dec = lax.optimization_barrier((one_far, two_far, three_near, grad, dec))
+    grad, dec = grads_of([[(errors,), (distant,)]], (0,), None)
+    one_far, two_far, three_near, grad, dec, ends[:1] = lax.optimization_barrier(
+        (one_far, two_far, three_near, grad, dec, ends[:1])
+    )
     three_far = flip(two_far[:, :side], "layer", 1), flip(one_far[:, side:], "layer", 2)
-    along = [acts] + [down[k] + up[lat_count - k] for k in range(1, lat_count)]
-    along = jnp.stack(along)
-    along = [
-        lax.dynamic_index_in_dim(along, lax.rem((lat_here ^ r) - lat_here + lat_count, lat_count), 0, False)
-        for r in range(lat_count)
-    ]
-    along = act_slots(along, hot, local_blocks)
     more, dec = grads_of([[(one_near,), (one_far,)], [(two_near,), (two_far,)]], (1, 2), dec)
-    three_far, more, dec = lax.optimization_barrier((three_far, more, dec))
+    three_far, more, dec, ends = lax.optimization_barrier((three_far, more, dec, ends))
     last, dec = grads_of([[three_near, three_far]], (3,), dec)
     grad = grad + more + last
-    enc = encoder_part(pre_slots, grad, flip(grad, "dp", 1), along, capacity)
+
+    ups, downs = [[part] for part in up], [[part] for part in down]
+    if ends:
+        ups.append([part[0] for part in ends])
+        downs.append([part[1] for part in ends])
+    terms_of = [[[acts]]] + [[downs[k], ups[lat_count - k]] for k in range(1, lat_count)]
+    shards = [lax.rem(lat_here + k, lat_count) ^ lat_here for k in range(lat_count)]
+    slotted = act_slots(terms_of, shards, hot, local_blocks)
+    enc = encoder_part(pre_slots, grad, flip(grad, "dp", 1), slotted, capacity)
     return dec[None], enc[None]
 
 

time: 189 us -> 191 us (1.011)
  waiting for transfers between devices: 76.2 us -> 85 us
  local copies, waits for them, and re-layouts: 9.48 us -> 6.48 us
  starting transfers between devices: 45.4 us -> 42.4 us
  other arithmetic: 5.22 us -> 2.76 us
  Pallas kernels: 39 us -> 41.1 us
    ppermute x25, waiting for transfers between devices: 58.6 us -> 63.7 us  [flip(): return lax.ppermute(value, axis, [(i, i ^ bit) for i in range(count)])]
    ppermute x6 -> x8, waiting for transfers between devices: 17.6 us -> 21.3 us  [hop(): return lax.ppermute(value, axis, pairs)]
    another operation x6 -> x4, other arithmetic: 3.4 us -> 0.2 us  [the longest x1 0.08 us: weight_places(): return jnp.stack(places(names, dp_here * lay_count))]
    ppermute x6 -> x8, starting transfers between devices: 11.8 us -> 10.5 us  [hop(): return lax.ppermute(value, axis, pairs)]
    unnamed x20 -> x37, local copies, waits for them, and re-layouts: 3.63 us -> 4.88 us
  transfers between devices with their start and end apart: 31 -> 33, of which waited for: 14 -> 16; matrix products, arithmetic and copies ran while one was open for 10% -> 6% of each run, Pallas kernels for 17% -> 16%
where the time goes in v7:
time: 191 us; the launch traced here: 188 us
  waiting for transfers between devices  85 us (45%)
  starting transfers between devices  42.4 us (22%)
  Pallas kernels  41.1 us (22%)
  matrix products  9.34 us (5%)
  local copies, waits for them, and re-layouts  6.48 us (3%)
  other arithmetic  2.76 us (1%)
    ppermute x25, waiting for transfers between devices, flip(): return lax.ppermute(value, axis, [(i, i ^ bit) for i in range(count)])  63.7 us
    ppermute x25, starting transfers between devices, flip(): return lax.ppermute(value, axis, [(i, i ^ bit) for i in range(count)])  31.9 us
    ppermute x8, waiting for transfers between devices, hop(): return lax.ppermute(value, axis, pairs)  21.3 us
    ppermute x8, starting transfers between devices, hop(): return lax.ppermute(value, axis, pairs)  10.5 us
    pallas_call x3, Pallas kernels, piece_grad(): pl.pallas_call(functools.partial(piece_grad_kernel, [[len(row) for row in...  10.4 us
    dot_general x4, matrix products, rows_for(): jnp.dot(spread, weights[:, n * width:(n + 1) * width], preferred_element_...  9.34 us
    pallas_call x3, Pallas kernels, gather_columns(): pl.pallas_call(gather_kernel, out_shape=jax.ShapeDtypeStruct((rows, count...  8.39 us
    pallas_call x1, Pallas kernels, encoder_part(): pl.pallas_call(functools.partial(encoder_kernel, cap, shared), out_shape=...  7.84 us
  transfers between devices with their start and end apart: 33, of which 16 were waited for; matrix products, arithmetic and copies ran while one was open for 6% of the time, Pallas kernels for 16%

profile of v7, /device:TPU:1, one launch (start us, length us, event | category | flops | bytes accessed | tf_op | source)
XLA Modules:
  0.0 188.2 jit_solution(17194825948741578236)
XLA Ops:
  3.6 4.8 %collective-permute-start.2 = (bf16[272,128]{1,0:T(8,128)(2,1)S(1)}, bf16[272,128]{1,0:T(8,128)(2,1)S(1)}, u32[]{:S(2)}, u32[]{:S(2)}) collective-permute-start(bf16[272,128]{1,0:T(8,128)(2,1)S(1)} %get-tuple-element.109), channel_id=1, source_target_pairs={{0,6},{2,4},{4,2},{6,0},{1,7},{3,5},{5,3},{7,1},{8,14},{10,12},{12... | collective-permute-start | bytes 208904 | tf_op jit(solution)/shard_map/ppermute | solution.py:103
  10.9 3.4 %collective-permute-done.1 = bf16[272,128]{1,0:T(8,128)(2,1)S(1)} collective-permute-done((bf16[272,128]{1,0:T(8,128)(2,1)S(1)}, bf16[272,128]{1,0:T(8,128)(2,1)S(1)}, u32[]{:S(2)}, u32[]{:S(2)}) %collective-permute-start.1) | collective-permute-done | bytes 69664 | tf_op jit(solution)/shard_map/ppermute | solution.py:103
  15.4 3.9 %gather_columns.3 = bf16[2048,1024]{1,0:T(8,128)(2,1)S(1)} custom-call(s32[4]{0:T(128)S(1)} %pad_add_fusion.1.scalar_ref, bf16[1,2048,4096]{2,1,0:T(8,128)(2,1)} %weight_ref.5), custom_call_target="tpu_custom_call" | custom-call | flops 1048576 | bytes 1050112 | tf_op jit(solution)/shard_map/gather_columns/pallas_call | solution.py:139
  19.4 2.8 %collective-permute-start.6 = (bf16[256,2048]{1,0:T(8,128)(2,1)S(1)}, bf16[256,2048]{1,0:T(8,128)(2,1)S(1)}, u32[]{:S(2)}, u32[]{:S(2)}) collective-permute-start(bf16[256,2048]{1,0:T(8,128)(2,1)S(1)} %pad_maximum_fusion.refs_0_), channel_id=1, source_target_pairs={{0,2},{2,4},{4,6},{1,3},{3,5},{5,7},{8,10},{10,12},{12,14},{9,11},... | collective-permute-start | bytes 3145736 | tf_op jit(solution)/shard_map/ppermute | solution.py:112
  23.6 2.6 %spread_codes.1 = bf16[1024,2048]{1,0:T(8,128)(2,1)S(1)} custom-call(s32[1]{0:T(128)} %bitcast.1.scalar_ref, bf16[8,272,128]{2,1,0:T(8,128)(2,1)S(1)} %bitcast.46), custom_call_target="tpu_custom_call" | custom-call | flops 1048576 | bytes 1050112 | tf_op jit(solution)/shard_map/spread_codes/pallas_call | solution.py:185
  33.5 3.9 %gather_columns.4 = bf16[2048,1024]{1,0:T(8,128)(2,1)S(1)} custom-call(s32[4]{0:T(128)S(1)} %pad_add_fusion.scalar_ref, bf16[1,2048,4096]{2,1,0:T(8,128)(2,1)} %weight_ref.5), custom_call_target="tpu_custom_call" | custom-call | flops 1048576 | bytes 1050112 | tf_op jit(solution)/shard_map/gather_columns/pallas_call | solution.py:139
  37.4 7.3 %collective-permute-done.6.refs_8_ = bf16[256,2048]{1,0:T(8,128)(2,1)S(1)} collective-permute-done((bf16[256,2048]{1,0:T(8,128)(2,1)S(1)}, bf16[256,2048]{1,0:T(8,128)(2,1)S(1)}, u32[]{:S(2)}, u32[]{:S(2)}) %collective-permute-start.6) | collective-permute-done | bytes 1048608 | tf_op jit(solution)/shard_map/ppermute | solution.py:112
  44.7 3.9 %collective-permute-done.7.refs_1_ = bf16[256,2048]{1,0:T(8,128)(2,1)S(1)} collective-permute-done((bf16[256,2048]{1,0:T(8,128)(2,1)S(1)}, bf16[256,2048]{1,0:T(8,128)(2,1)S(1)}, u32[]{:S(2)}, u32[]{:S(2)}) %collective-permute-start.7) | collective-permute-done | bytes 1048608 | tf_op jit(solution)/shard_map/ppermute | solution.py:112
  61.9 6.0 %collective-permute-done.8.far_a = bf16[1024,256]{1,0:T(8,128)(2,1)S(1)} collective-permute-done((bf16[1024,256]{1,0:T(8,128)(2,1)S(1)}, bf16[1024,256]{1,0:T(8,128)(2,1)S(1)}, u32[]{:S(2)}, u32[]{:S(2)}) %collective-permute-start.8) | collective-permute-done | bytes 524320 | tf_op jit(solution)/shard_map/ppermute | solution.py:103
  69.1 7.1 %collective-permute-done.13.refs_4_ = bf16[256,2048]{1,0:T(8,128)(2,1)S(1)} collective-permute-done((bf16[256,2048]{1,0:T(8,128)(2,1)S(1)}, bf16[256,2048]{1,0:T(8,128)(2,1)S(1)}, u32[]{:S(2)}, u32[]{:S(2)}) %collective-permute-start.13) | collective-permute-done | bytes 1048608 | tf_op jit(solution)/shard_map/ppermute | solution.py:112
  76.8 2.3 %collective-permute-start.15 = (bf16[256,512]{1,0:T(8,128)(2,1)S(1)}, bf16[256,512]{1,0:T(8,128)(2,1)S(1)}, u32[]{:S(2)}, u32[]{:S(2)}) collective-permute-start(bf16[256,512]{1,0:T(8,128)(2,1)S(1)} %get-tuple-element.69), channel_id=1, source_target_pairs={{0,4},{2,6},{4,0},{6,2},{1,5},{3,7},{5,1},{7,3},{8,12},{10,14},{12... | collective-permute-start | bytes 786440 | tf_op jit(solution)/shard_map/ppermute | solution.py:103
  80.3 4.1 %collective-permute-done.16 = bf16[256,512]{1,0:T(8,128)(2,1)S(1)} collective-permute-done((bf16[256,512]{1,0:T(8,128)(2,1)S(1)}, bf16[256,512]{1,0:T(8,128)(2,1)S(1)}, u32[]{:S(2)}, u32[]{:S(2)}) %collective-permute-start.16) | collective-permute-done | bytes 262176 | tf_op jit(solution)/shard_map/ppermute | solution.py:103
  84.4 17.4 %collective-permute-done.15 = bf16[256,512]{1,0:T(8,128)(2,1)S(1)} collective-permute-done((bf16[256,512]{1,0:T(8,128)(2,1)S(1)}, bf16[256,512]{1,0:T(8,128)(2,1)S(1)}, u32[]{:S(2)}, u32[]{:S(2)}) %collective-permute-start.15) | collective-permute-done | bytes 262176 | tf_op jit(solution)/shard_map/ppermute | solution.py:103
  109.3 6.6 %collective-permute-done.19 = bf16[256,512]{1,0:T(8,128)(2,1)S(1)} collective-permute-done((bf16[256,512]{1,0:T(8,128)(2,1)S(1)}, bf16[256,512]{1,0:T(8,128)(2,1)S(1)}, u32[]{:S(2)}, u32[]{:S(2)}) %collective-permute-start.19) | collective-permute-done | bytes 262176 | tf_op jit(solution)/shard_map/ppermute | solution.py:103
  115.9 7.3 %collective-permute-done.21 = bf16[256,512]{1,0:T(8,128)(2,1)S(1)} collective-permute-done((bf16[256,512]{1,0:T(8,128)(2,1)S(1)}, bf16[256,512]{1,0:T(8,128)(2,1)S(1)}, u32[]{:S(2)}, u32[]{:S(2)}) %collective-permute-start.21) | collective-permute-done | bytes 262176 | tf_op jit(solution)/shard_map/ppermute | solution.py:103
  127.3 13.2 %collective-permute-done.24.refs_0_ = bf16[256,256]{1,0:T(8,128)(2,1)S(1)} collective-permute-done((bf16[256,256]{1,0:T(8,128)(2,1)S(1)}, bf16[256,256]{1,0:T(8,128)(2,1)S(1)}, u32[]{:S(2)}, u32[]{:S(2)}) %collective-permute-start.24) | collective-permute-done | bytes 131104 | tf_op jit(solution)/shard_map/ppermute | solution.py:103
  142.4 2.7 %piece_grad.3 = (bf16[1,16,64,512]{3,2,1,0:T(8,128)(2,1)S(1)}, f32[16,64,128]{2,1,0:T(8,128)S(1)}) custom-call(s32[1]{0:T(128)} %bitcast.24.scalar_ref, bf16[4,256,256]{2,1,0:T(8,128)(2,1)S(1)} %get-tuple-element.56.hot_ref, bf16[1,2048,4096]{2,1,0:T(8,128)(2,1)} %weight_ref.5, bf16[256,512]{1,0:T(8,128)(2,1)S(1)} %multiply_convert_fusion.refs_0_, ...), custom_call_target="tpu_custom_call" | custom-call | flops 134217728 | bytes 851968 | tf_op jit(solution)/shard_map/piece_grad/pallas_call | solution.py:343
  151.3 4.8 %piece_grad.4 = (bf16[2,16,64,512]{3,2,1,0:T(8,128)(2,1)S(1)}, f32[16,64,128]{2,1,0:T(8,128)S(1)}) custom-call(s32[2]{0:T(128)S(1)} %pad_add_fusion.3.scalar_ref, bf16[4,256,256]{2,1,0:T(8,128)(2,1)S(1)} %get-tuple-element.56.hot_ref, bf16[1,2048,4096]{2,1,0:T(8,128)(2,1)} %weight_ref.5, bf16[256,512]{1,0:T(8,128)(2,1)S(1)} %collective-permute-done.17.refs_0_, ...), custom_call_target="tpu_custom_call" | custom-call | flops 268435456 | bytes 1441792 | tf_op jit(solution)/shard_map/piece_grad/pallas_call | solution.py:343
  156.1 3.3 %decoder_part.4.refs_0_ = bf16[2048,2048]{1,0:T(8,128)(2,1)} custom-call(s32[2]{0:T(128)S(1)} %pad_add_fusion.4.scalar_ref, bf16[16,128,64]{2,1,0:T(8,128)(2,1)S(1)} %get-tuple-element.55.code_ref, bf16[2,16,64,512]{3,2,1,0:T(8,128)(2,1)S(1)} %get-tuple-element.88.slots_ref, bf16[2048,2048]{1,0:T(8,128)(2,1)} %decoder_part.3.refs_0_), custom_call_target="tpu_custom_call", output_to_operand_aliasing={{}: (3, {})} | custom-call | flops 268435456 | bytes 1441792 | tf_op jit(solution)/shard_map/decoder_part/pallas_call | solution.py:378
  159.4 3.0 %collective-permute-done.31.refs_7_ = bf16[80,2048]{1,0:T(8,128)(2,1)S(1)} collective-permute-done((bf16[80,2048]{1,0:T(8,128)(2,1)S(1)}, bf16[80,2048]{1,0:T(8,128)(2,1)S(1)}, u32[]{:S(2)}, u32[]{:S(2)}) %collective-permute-start.31) | collective-permute-done | bytes 327712 | tf_op jit(solution)/shard_map/ppermute | solution.py:112
  162.3 2.9 %piece_grad.5 = (bf16[1,16,64,512]{3,2,1,0:T(8,128)(2,1)S(1)}, f32[16,64,128]{2,1,0:T(8,128)S(1)}) custom-call(s32[1]{0:T(128)} %bitcast.15.scalar_ref, bf16[4,256,256]{2,1,0:T(8,128)(2,1)S(1)} %get-tuple-element.56.hot_ref, bf16[1,2048,4096]{2,1,0:T(8,128)(2,1)} %weight_ref.5, bf16[256,256]{1,0:T(8,128)(2,1)S(1)} %collective-permute-done.24.refs_0_, ...), custom_call_target="tpu_custom_call" | custom-call | flops 134217728 | bytes 851968 | tf_op jit(solution)/shard_map/piece_grad/pallas_call | solution.py:343
  167.1 5.5 %collective-permute-start.32 = (f32[16,64,128]{2,1,0:T(8,128)}, f32[16,64,128]{2,1,0:T(8,128)}, u32[]{:S(2)}, u32[]{:S(2)}) collective-permute-start(f32[16,64,128]{2,1,0:T(8,128)} %add_add_fusion.own_ref), channel_id=1, source_target_pairs={{0,1},{1,0},{2,3},{3,2},{4,5},{5,4},{6,7},{7,6},{8,9},{9,8},{10,11... | collective-permute-start | bytes 1572872 | tf_op jit(solution)/shard_map/ppermute | solution.py:103
  177.1 3.3 %act_slots.1.act_ref = bf16[16,64,2048]{2,1,0:T(8,128)(2,1)S(1)} custom-call(s32[4]{0:T(128)S(1)} %pad_add_fusion.5.scalar_ref, bf16[4,256,256]{2,1,0:T(8,128)(2,1)S(1)} %get-tuple-element.56.hot_ref, bf16[256,2048]{1,0:T(8,128)(2,1)S(1)} %pad_maximum_fusion.refs_0_, bf16[256,2048]{1,0:T(8,128)(2,1)S(1)} %copy-done.5, bf16[176,2048]{1,0:T(8,128)(2,1)S(1)} %copy-done.10, ...), custom_call_target="tpu_custom_call" | custom-call | flops 268435456 | bytes 1441792 | tf_op jit(solution)/shard_map/act_slots/pallas_call | solution.py:418
  180.4 7.8 %encoder_part.1 = bf16[2048,2048]{1,0:T(8,128)(2,1)} custom-call(bf16[16,64,128]{2,1,0:T(8,128)(2,1)S(1)} %copy-done.16, f32[16,64,128]{2,1,0:T(8,128)} %add_add_fusion.own_ref, f32[16,64,128]{2,1,0:T(8,128)} %collective-permute-done.32.theirs_ref, bf16[16,64,2048]{2,1,0:T(8,128)(2,1)S(1)} %act_slots.1.act_ref), custom_call_target="tpu_custom_call" | custom-call | flops 536870912 | bytes 2621440 | tf_op jit(solution)/shard_map/encoder_part/pallas_call | solution.py:454
  (125 shorter events, 57.3 us)
Async XLA Ops:
  3.5 10.9 %collective-permute-start.3 = (bf16[128,2048]{1,0:T(8,128)(2,1)S(1)}, bf16[128,2048]{1,0:T(8,128)(2,1)S(1)}, u32[]{:S(2)}, u32[]{:S(2)}) collective-permute-start(bf16[128,2048]{1,0:T(8,128)(2,1)S(1)} %get-tuple-element.105), channel_id=1, source_target_pairs={{0,1},{1,0},{2,3},{3,2},{4,5},{5,4},{6,7},{7,6},{8,9},{9,8},{10,11... | collective-permute-start | bytes 1572872 | tf_op jit(solution)/shard_map/ppermute | solution.py:103
  19.4 25.3 %collective-permute-start.6 = (bf16[256,2048]{1,0:T(8,128)(2,1)S(1)}, bf16[256,2048]{1,0:T(8,128)(2,1)S(1)}, u32[]{:S(2)}, u32[]{:S(2)}) collective-permute-start(bf16[256,2048]{1,0:T(8,128)(2,1)S(1)} %pad_maximum_fusion.refs_0_), channel_id=1, source_target_pairs={{0,2},{2,4},{4,6},{1,3},{3,5},{5,7},{8,10},{10,12},{12,14},{9,11},... | collective-permute-start | bytes 3145736 | tf_op jit(solution)/shard_map/ppermute | solution.py:112
  22.2 26.3 %collective-permute-start.7 = (bf16[256,2048]{1,0:T(8,128)(2,1)S(1)}, bf16[256,2048]{1,0:T(8,128)(2,1)S(1)}, u32[]{:S(2)}, u32[]{:S(2)}) collective-permute-start(bf16[256,2048]{1,0:T(8,128)(2,1)S(1)} %pad_maximum_fusion.refs_0_), channel_id=1, source_target_pairs={{2,0},{4,2},{6,4},{3,1},{5,3},{7,5},{10,8},{12,10},{14,12},{11,9},... | collective-permute-start | bytes 3145736 | tf_op jit(solution)/shard_map/ppermute | solution.py:112
  28.6 26.9 %collective-permute-start.5 = (bf16[1024,512]{1,0:T(8,128)(2,1)S(1)}, bf16[1024,512]{1,0:T(8,128)(2,1)S(1)}, u32[]{:S(2)}, u32[]{:S(2)}) collective-permute-start(bf16[1024,512]{1,0:T(8,128)(2,1)S(1)} %fusion.8), channel_id=1, source_target_pairs={{0,8},{8,0},{16,24},{24,16},{1,9},{9,1},{17,25},{25,17},{2,10},{10... | collective-permute-start | bytes 3145736 | tf_op jit(solution)/shard_map/ppermute | solution.py:103
  32.2 24.7 %collective-permute-start.9 = (bf16[1024,512]{1,0:T(8,128)(2,1)S(1)}, bf16[1024,512]{1,0:T(8,128)(2,1)S(1)}, u32[]{:S(2)}, u32[]{:S(2)}) collective-permute-start(bf16[1024,512]{1,0:T(8,128)(2,1)S(1)} %fusion.14), channel_id=1, source_target_pairs={{0,16},{8,24},{16,0},{24,8},{1,17},{9,25},{17,1},{25,9},{2,18},{10... | collective-permute-start | bytes 3145736 | tf_op jit(solution)/shard_map/ppermute | solution.py:103
  48.5 20.6 %collective-permute-start.12 = (bf16[256,2048]{1,0:T(8,128)(2,1)S(1)}, bf16[256,2048]{1,0:T(8,128)(2,1)S(1)}, u32[]{:S(2)}, u32[]{:S(2)}) collective-permute-start(bf16[256,2048]{1,0:T(8,128)(2,1)S(1)} %collective-permute-done.6.refs_8_), channel_id=1, source_target_pairs={{2,4},{4,6},{3,5},{5,7},{10,12},{12,14},{11,13},{13,15},{18,20},{2... | collective-permute-start | bytes 3145736 | tf_op jit(solution)/shard_map/ppermute | solution.py:112
  49.3 27.0 %collective-permute-start.13 = (bf16[256,2048]{1,0:T(8,128)(2,1)S(1)}, bf16[256,2048]{1,0:T(8,128)(2,1)S(1)}, u32[]{:S(2)}, u32[]{:S(2)}) collective-permute-start(bf16[256,2048]{1,0:T(8,128)(2,1)S(1)} %collective-permute-done.7.refs_1_), channel_id=1, source_target_pairs={{2,0},{4,2},{3,1},{5,3},{10,8},{12,10},{11,9},{13,11},{18,16},{20,... | collective-permute-start | bytes 3145736 | tf_op jit(solution)/shard_map/ppermute | solution.py:112
  55.6 12.3 %collective-permute-start.8 = (bf16[1024,256]{1,0:T(8,128)(2,1)S(1)}, bf16[1024,256]{1,0:T(8,128)(2,1)S(1)}, u32[]{:S(2)}, u32[]{:S(2)}) collective-permute-start(bf16[1024,256]{1,0:T(8,128)(2,1)S(1)} %add_convert_fusion.1), channel_id=1, source_target_pairs={{0,16},{8,24},{16,0},{24,8},{1,17},{9,25},{17,1},{25,9},{2,18},{10... | collective-permute-start | bytes 1572872 | tf_op jit(solution)/shard_map/ppermute | solution.py:103
  57.1 12.1 %collective-permute-start.10 = (bf16[1024,256]{1,0:T(8,128)(2,1)S(1)}, bf16[1024,256]{1,0:T(8,128)(2,1)S(1)}, u32[]{:S(2)}, u32[]{:S(2)}) collective-permute-start(bf16[1024,256]{1,0:T(8,128)(2,1)S(1)} %add_convert_fusion), channel_id=1, source_target_pairs={{0,8},{8,0},{16,24},{24,16},{1,9},{9,1},{17,25},{25,17},{2,10},{10... | collective-permute-start | bytes 1572872 | tf_op jit(solution)/shard_map/ppermute | solution.py:103
  76.8 25.0 %collective-permute-start.15 = (bf16[256,512]{1,0:T(8,128)(2,1)S(1)}, bf16[256,512]{1,0:T(8,128)(2,1)S(1)}, u32[]{:S(2)}, u32[]{:S(2)}) collective-permute-start(bf16[256,512]{1,0:T(8,128)(2,1)S(1)} %get-tuple-element.69), channel_id=1, source_target_pairs={{0,4},{2,6},{4,0},{6,2},{1,5},{3,7},{5,1},{7,3},{8,12},{10,14},{12... | collective-permute-start | bytes 786440 | tf_op jit(solution)/shard_map/ppermute | solution.py:103
  79.1 22.6 %collective-permute-start.14 = (bf16[256,512]{1,0:T(8,128)(2,1)S(1)}, bf16[256,512]{1,0:T(8,128)(2,1)S(1)}, u32[]{:S(2)}, u32[]{:S(2)}) collective-permute-start(bf16[256,512]{1,0:T(8,128)(2,1)S(1)} %get-tuple-element.68), channel_id=1, source_target_pairs={{0,2},{2,0},{4,6},{6,4},{1,3},{3,1},{5,7},{7,5},{8,10},{10,8},{12,... | collective-permute-start | bytes 786440 | tf_op jit(solution)/shard_map/ppermute | solution.py:103
  104.5 11.4 %collective-permute-start.19 = (bf16[256,512]{1,0:T(8,128)(2,1)S(1)}, bf16[256,512]{1,0:T(8,128)(2,1)S(1)}, u32[]{:S(2)}, u32[]{:S(2)}) collective-permute-start(bf16[256,512]{1,0:T(8,128)(2,1)S(1)} %multiply_convert_fusion.refs_0_), channel_id=1, source_target_pairs={{0,2},{2,0},{4,6},{6,4},{1,3},{3,1},{5,7},{7,5},{8,10},{10,8},{12,... | collective-permute-start | bytes 786440 | tf_op jit(solution)/shard_map/ppermute | solution.py:103
  104.5 11.4 %collective-permute-start.20 = (bf16[256,512]{1,0:T(8,128)(2,1)S(1)}, bf16[256,512]{1,0:T(8,128)(2,1)S(1)}, u32[]{:S(2)}, u32[]{:S(2)}) collective-permute-start(bf16[256,512]{1,0:T(8,128)(2,1)S(1)} %multiply_convert_fusion.refs_0_), channel_id=1, source_target_pairs={{0,4},{2,6},{4,0},{6,2},{1,5},{3,7},{5,1},{7,3},{8,12},{10,14},{12... | collective-permute-start | bytes 786440 | tf_op jit(solution)/shard_map/ppermute | solution.py:103
  106.6 16.6 %collective-permute-start.21 = (bf16[256,512]{1,0:T(8,128)(2,1)S(1)}, bf16[256,512]{1,0:T(8,128)(2,1)S(1)}, u32[]{:S(2)}, u32[]{:S(2)}) collective-permute-start(bf16[256,512]{1,0:T(8,128)(2,1)S(1)} %multiply_convert_fusion.refs_0_), channel_id=1, source_target_pairs={{0,6},{2,4},{4,2},{6,0},{1,7},{3,5},{5,3},{7,1},{8,14},{10,12},{12... | collective-permute-start | bytes 786440 | tf_op jit(solution)/shard_map/ppermute | solution.py:103
  123.3 23.9 %collective-permute-start.22 = (bf16[768,512]{1,0:T(8,128)(2,1)S(1)}, bf16[768,512]{1,0:T(8,128)(2,1)S(1)}, u32[]{:S(2)}, u32[]{:S(2)}) collective-permute-start(bf16[768,512]{1,0:T(8,128)(2,1)S(1)} %constant_dynamic-update-slice_fusion.refs_1_), channel_id=1, source_target_pairs={{0,8},{8,0},{16,24},{24,16},{1,9},{9,1},{17,25},{25,17},{2,10},{10... | collective-permute-start | bytes 2359304 | tf_op jit(solution)/shard_map/ppermute | solution.py:103
  123.6 23.6 %collective-permute-start.23 = (bf16[768,512]{1,0:T(8,128)(2,1)S(1)}, bf16[768,512]{1,0:T(8,128)(2,1)S(1)}, u32[]{:S(2)}, u32[]{:S(2)}) collective-permute-start(bf16[768,512]{1,0:T(8,128)(2,1)S(1)} %constant_dynamic-update-slice_fusion.refs_1_), channel_id=1, source_target_pairs={{0,16},{8,24},{16,0},{24,8},{1,17},{9,25},{17,1},{25,9},{2,18},{10... | collective-permute-start | bytes 2359304 | tf_op jit(solution)/shard_map/ppermute | solution.py:103
  123.9 23.3 %collective-permute-start.26 = (bf16[176,2048]{1,0:T(8,128)(2,1)S(1)}, bf16[176,2048]{1,0:T(8,128)(2,1)S(1)}, u32[]{:S(2)}, u32[]{:S(2)}) collective-permute-start(bf16[176,2048]{1,0:T(8,128)(2,1)S(1)} %slice.67), channel_id=1, source_target_pairs={{4,6},{5,7},{12,14},{13,15},{20,22},{21,23},{28,30},{29,31}} | collective-permute-start | bytes 2162696 | tf_op jit(solution)/shard_map/ppermute | solution.py:112
  124.7 22.5 %collective-permute-start.27 = (bf16[176,2048]{1,0:T(8,128)(2,1)S(1)}, bf16[176,2048]{1,0:T(8,128)(2,1)S(1)}, u32[]{:S(2)}, u32[]{:S(2)}) collective-permute-start(bf16[176,2048]{1,0:T(8,128)(2,1)S(1)} %slice.68), channel_id=1, source_target_pairs={{2,0},{3,1},{10,8},{11,9},{18,16},{19,17},{26,24},{27,25}} | collective-permute-start | bytes 2162696 | tf_op jit(solution)/shard_map/ppermute | solution.py:112
  126.0 14.5 %collective-permute-start.24 = (bf16[256,256]{1,0:T(8,128)(2,1)S(1)}, bf16[256,256]{1,0:T(8,128)(2,1)S(1)}, u32[]{:S(2)}, u32[]{:S(2)}) collective-permute-start(bf16[256,256]{1,0:T(8,128)(2,1)S(1)} %slice.65), channel_id=1, source_target_pairs={{0,8},{8,0},{16,24},{24,16},{1,9},{9,1},{17,25},{25,17},{2,10},{10... | collective-permute-start | bytes 393224 | tf_op jit(solution)/shard_map/ppermute | solution.py:103
  147.2 15.1 %collective-permute-start.28 = (bf16[768,256]{1,0:T(8,128)(2,1)S(1)}, bf16[768,256]{1,0:T(8,128)(2,1)S(1)}, u32[]{:S(2)}, u32[]{:S(2)}) collective-permute-start(bf16[768,256]{1,0:T(8,128)(2,1)S(1)} %slice.69), channel_id=1, source_target_pairs={{0,8},{8,0},{16,24},{24,16},{1,9},{9,1},{17,25},{25,17},{2,10},{10... | collective-permute-start | bytes 1179656 | tf_op jit(solution)/shard_map/ppermute | solution.py:103
  147.6 14.8 %collective-permute-start.29 = (bf16[768,256]{1,0:T(8,128)(2,1)S(1)}, bf16[768,256]{1,0:T(8,128)(2,1)S(1)}, u32[]{:S(2)}, u32[]{:S(2)}) collective-permute-start(bf16[768,256]{1,0:T(8,128)(2,1)S(1)} %slice.70), channel_id=1, source_target_pairs={{0,16},{8,24},{16,0},{24,8},{1,17},{9,25},{17,1},{25,9},{2,18},{10... | collective-permute-start | bytes 1179656 | tf_op jit(solution)/shard_map/ppermute | solution.py:103
  148.9 10.4 %collective-permute-start.30 = (bf16[80,2048]{1,0:T(8,128)(2,1)S(1)}, bf16[80,2048]{1,0:T(8,128)(2,1)S(1)}, u32[]{:S(2)}, u32[]{:S(2)}) collective-permute-start(bf16[80,2048]{1,0:T(8,128)(2,1)S(1)} %slice.71), channel_id=1, source_target_pairs={{4,6},{5,7},{12,14},{13,15},{20,22},{21,23},{28,30},{29,31}} | collective-permute-start | bytes 983048 | tf_op jit(solution)/shard_map/ppermute | solution.py:112
  149.6 12.7 %collective-permute-start.31 = (bf16[80,2048]{1,0:T(8,128)(2,1)S(1)}, bf16[80,2048]{1,0:T(8,128)(2,1)S(1)}, u32[]{:S(2)}, u32[]{:S(2)}) collective-permute-start(bf16[80,2048]{1,0:T(8,128)(2,1)S(1)} %slice.72), channel_id=1, source_target_pairs={{2,0},{3,1},{10,8},{11,9},{18,16},{19,17},{26,24},{27,25}} | collective-permute-start | bytes 983048 | tf_op jit(solution)/shard_map/ppermute | solution.py:112
  167.1 13.2 %collective-permute-start.32 = (f32[16,64,128]{2,1,0:T(8,128)}, f32[16,64,128]{2,1,0:T(8,128)}, u32[]{:S(2)}, u32[]{:S(2)}) collective-permute-start(f32[16,64,128]{2,1,0:T(8,128)} %add_add_fusion.own_ref), channel_id=1, source_target_pairs={{0,1},{1,0},{2,3},{3,2},{4,5},{5,4},{6,7},{7,6},{8,9},{9,8},{10,11... | collective-permute-start | bytes 1572872 | tf_op jit(solution)/shard_map/ppermute | solution.py:103
  (26 other events, 186.1 us)

commit v8 on v7

--- a/solution.py
+++ b/solution.py
@@ -116,12 +116,8 @@
     return pltpu.CompilerParams(vmem_limit_bytes=VMEM_BYTES)
 
 
-def cost(rows, depth, columns):
-    return pl.CostEstimate(
-        flops=rows * depth * columns // 2,
-        bytes_accessed=(rows * depth + depth * columns + rows * columns) // 2,
-        transcendentals=0,
-    )
+def cost(microseconds):
+    return pl.CostEstimate(flops=int(microseconds * 1.1e9), bytes_accessed=1, transcendentals=0)
 
 
 def resident(shape):
@@ -146,7 +142,7 @@
             out_specs=pl.BlockSpec((rows, width), lambda i, s: (0, i)),
         ),
         compiler_params=params(),
-        cost_estimate=cost(rows, 1, count * width),
+        cost_estimate=cost(0.9 * count),
         name="gather_columns",
     )(columns.astype(jnp.int32), source)
 
@@ -196,7 +192,7 @@
             ],
         ),
         compiler_params=params(),
-        cost_estimate=cost(rows, 1, lat_rows),
+        cost_estimate=cost(2.5),
         name="spread_codes",
     )(first[None].astype(jnp.int32), message)
 
@@ -226,9 +222,29 @@
         in_specs=[pl.BlockSpec((rows, half), lambda i: (0, 0)) for _ in range(6)],
         out_specs=[pl.BlockSpec(cut, lambda i: (0, 0))] * blocks,
         compiler_params=params(),
-        cost_estimate=cost(rows, 4, half),
+        cost_estimate=cost(0.5),
         name="layer_sum",
     )(*terms_a, *terms_b)
+
+
+def join_kernel(*refs):
+    out_ref = refs[-1]
+    for i in range(out_ref.shape[0]):
+        out_ref[i] = refs[i][...]
+
+
+def join(parts, waited):
+    shape = (len(parts),) + parts[0].shape
+    vmem = pl.BlockSpec(memory_space=pltpu.VMEM)
+    return pl.pallas_call(
+        join_kernel,
+        out_shape=jax.ShapeDtypeStruct(shape, parts[0].dtype),
+        in_specs=[vmem] * len(parts) + [pl.BlockSpec(memory_space=pl.ANY)],
+        out_specs=vmem,
+        compiler_params=params(),
+        cost_estimate=cost(0.3),
+        name="join",
+    )(*parts, waited)
 
 
 def slots_kernel(groups, blocks, cap, scalar_ref, message_ref, hot_ref, pre_ref, code_ref):
@@ -285,7 +301,7 @@
             out_specs=[resident(shape) for shape in shapes],
         ),
         compiler_params=params(),
-        cost_estimate=cost(groups * tok, 2 * tok, tok),
+        cost_estimate=cost(1),
         name="make_slots",
     )(first[None].astype(jnp.int32), message)
 
@@ -302,15 +318,15 @@
     return parts[0] if len(parts) == 1 else jnp.concatenate(parts, axis=1)
 
 
-def piece_grad_kernel(layout, scalar_ref, hot_ref, weight_ref, *refs):
-    parts, (slots_ref, grad_ref) = refs[:-2], refs[-2:]
+def piece_grad_kernel(layout, onto, scalar_ref, hot_ref, weight_ref, *refs):
+    parts, (slots_ref, grad_ref) = refs[onto:-2], refs[-2:]
     blocks, _, size = grad_ref.shape
     group = hot_ref.shape[2]
     step = pl.program_id(0)
 
     @pl.when(step == 0)
     def _():
-        grad_ref[...] = jnp.zeros_like(grad_ref)
+        grad_ref[...] = refs[0][...] if onto else jnp.zeros_like(grad_ref)
 
     at = 0
     for i, piece in enumerate(layout):
@@ -334,14 +350,15 @@
         )
 
 
-def piece_grad(pieces, hot, decoder, columns, size):
+def piece_grad(pieces, hot, decoder, columns, size, held):
     lat_rows = decoder.shape[1]
     blocks = lat_rows // size
     slots = hot.shape[0] * hot.shape[1] // blocks
     width = sum(p.shape[1] for p in pieces[0][0])
     flat = [p for piece in pieces for row in piece for p in row]
-    return pl.pallas_call(
-        functools.partial(piece_grad_kernel, [[len(row) for row in piece] for piece in pieces]),
+    onto = [] if held is None else [held]
+    return pl.pallas_call(
+        functools.partial(piece_grad_kernel, [[len(row) for row in piece] for piece in pieces], len(onto)),
         out_shape=[
             jax.ShapeDtypeStruct((len(pieces), blocks, slots, width), jnp.bfloat16),
             jax.ShapeDtypeStruct((blocks, slots, size), jnp.float32),
@@ -350,16 +367,16 @@
             num_scalar_prefetch=1,
             grid=(len(pieces),),
             in_specs=[resident(hot.shape), pl.BlockSpec((1, lat_rows, width), lambda i, s: (0, 0, s[i]))]
-            + [resident(p.shape) for p in flat],
+            + [resident(p.shape) for p in onto + flat],
             out_specs=[
                 pl.BlockSpec((1, blocks, slots, width), lambda i, s: (i, 0, 0, 0)),
                 resident((blocks, slots, size)),
             ],
         ),
         compiler_params=params(),
-        cost_estimate=cost(lat_rows, 256, len(pieces) * width),
+        cost_estimate=cost(0.8 + 2 * len(pieces)),
         name="piece_grad",
-    )(columns.astype(jnp.int32), hot, decoder, *flat)
+    )(columns.astype(jnp.int32), hot, decoder, *onto, *flat)
 
 
 def decoder_kernel(skip, scalar_ref, code_ref, slots_ref, *refs):
@@ -387,7 +404,7 @@
         ),
         compiler_params=params(),
         input_output_aliases={3: 0} if onto else {},
-        cost_estimate=cost(lat_rows, 256, count * width),
+        cost_estimate=cost(0.7 + 1.3 * count),
         name="decoder_part",
     )(columns.astype(jnp.int32), codes, slots, *onto)
 
@@ -425,7 +442,7 @@
             out_specs=pl.BlockSpec((count, slots, tile), lambda i, s: (0, 0, i)),
         ),
         compiler_params=params(),
-        cost_estimate=cost(count * slots, 256, half),
+        cost_estimate=cost(3.3),
         name="act_slots",
     )(jnp.stack(places).astype(jnp.int32), hot, *flat)
 
@@ -458,7 +475,7 @@
         in_specs=[block, block, block, pl.BlockSpec((shared, slots, half), lambda i: (i, 0, 0))],
         out_specs=pl.BlockSpec((shared * size, half), lambda i: (i, 0)),
         compiler_params=params(),
-        cost_estimate=cost(blocks * size, 256, half),
+        cost_estimate=cost(6.5),
         name="encoder_part",
     )(pre, own, theirs, acts)
 
@@ -500,14 +517,11 @@
     at = places((1, 3), dp_here * lay_count, 2, 0) + places((2, 3), dp_here * lay_count, 2, 1)
     send_weights = gather_columns(decoder, jnp.stack(at), side)
 
-    corner = send_weights[:16, :128]
-    later, corner = lax.optimization_barrier((own, corner))
-    message = [own, flip(later, "latent", 1)] + [flip(own, "latent", r) for r in range(2, lat_count)]
-    message = jnp.stack(message)
+    message = [own] + [flip(own, "latent", r) for r in range(1, lat_count)]
 
     own, inputs = lax.optimization_barrier((own, activations[0]))
     acts = jnp.concatenate([columns(inputs, dp_here), flip(columns(inputs, 1 - dp_here), "dp", 1)])
-    message, acts = lax.optimization_barrier((message, acts))
+    message, acts = lax.optimization_barrier((join(message, send_weights), acts))
     up, down = [acts], [acts]
 
     def next_hops():
@@ -554,12 +568,13 @@
     errors = ((total - goals.astype(f32)) / tok_count).astype(bf16)
     others = [flip(errors, "latent", r) for r in range(1, lat_count)]
     one_near, two_near = flip(errors, "layer", 1), flip(errors, "layer", 2)
-    one_near, two_near, others, up[-1], down[-1] = lax.optimization_barrier(
-        (one_near, two_near, others, up[-1], down[-1])
-    )
+    made = make_slots(message, first, lat_rows, capacity)
+    one_near, two_near, others, up[-1], down[-1], made = lax.optimization_barrier(
+        (one_near, two_near, others, up[-1], down[-1], made)
+    )
+    hot, pre_slots, code_slots = made
     distant = jnp.concatenate(others)
     one_far, two_far = flip(distant, "layer", 1), flip(distant, "layer", 2)
-    three_near = flip(two_near[:, :side], "layer", 1), flip(one_near[:, side:], "layer", 2)
     while len(up) < lat_count - 1:
         next_hops()
     early = group * 11 // 16
@@ -568,21 +583,15 @@
         for rows in (slice(0, early), slice(early, group)):
             ends.append([hop(up[-1][rows], "latent", 1, len(up) - 1), hop(down[-1][rows], "latent", -1, len(up) - 1)])
 
-    hot, pre_slots, code_slots = make_slots(message, first, lat_rows, capacity)
-
-    def grads_of(here, names, dec):
-        slots, grad = piece_grad(here, hot, decoder, weight_places(names), block_size)
+    def grads_of(here, names, grad, dec):
+        slots, grad = piece_grad(here, hot, decoder, weight_places(names), block_size, grad)
         return grad, decoder_part(slots, code_slots, jnp.stack(places(names, 0)), half, dec)
 
-    grad, dec = grads_of([[(errors,), (distant,)]], (0,), None)
-    one_far, two_far, three_near, grad, dec, ends[:1] = lax.optimization_barrier(
-        (one_far, two_far, three_near, grad, dec, ends[:1])
-    )
-    three_far = flip(two_far[:, :side], "layer", 1), flip(one_far[:, side:], "layer", 2)
-    more, dec = grads_of([[(one_near,), (one_far,)], [(two_near,), (two_far,)]], (1, 2), dec)
-    three_far, more, dec, ends = lax.optimization_barrier((three_far, more, dec, ends))
-    last, dec = grads_of([[three_near, three_far]], (3,), dec)
-    grad = grad + more + last
+    grad, dec = grads_of([[(errors,), (distant,)]], (0,), None, None)
+    one_far, two_far, grad, dec, ends[:1] = lax.optimization_barrier((one_far, two_far, grad, dec, ends[:1]))
+    three_a = flip(jnp.concatenate([two_near[:, :side], two_far[:, :side]]), "layer", 1)
+    three_b = flip(jnp.concatenate([one_near[:, side:], one_far[:, side:]]), "layer", 2)
+    grad, dec = grads_of([[(one_near,), (one_far,)], [(two_near,), (two_far,)]], (1, 2), grad, dec)
 
     ups, downs = [[part] for part in up], [[part] for part in down]
     if ends:
@@ -591,6 +600,8 @@
     terms_of = [[[acts]]] + [[downs[k], ups[lat_count - k]] for k in range(1, lat_count)]
     shards = [lax.rem(lat_here + k, lat_count) ^ lat_here for k in range(lat_count)]
     slotted = act_slots(terms_of, shards, hot, local_blocks)
+    three_a, three_b, grad, dec, slotted = lax.optimization_barrier((three_a, three_b, grad, dec, slotted))
+    grad, dec = grads_of([[(three_a, three_b)]], (3,), grad, dec)
     enc = encoder_part(pre_slots, grad, flip(grad, "dp", 1), slotted, capacity)
     return dec[None], enc[None]
 

time: 191 us -> 180 us (0.942); the launches traced: 188 us -> 179 us
  waiting for transfers between devices: 85 us -> 54.7 us
  starting transfers between devices: 42.4 us -> 56.1 us
  local copies, waits for them, and re-layouts: 6.48 us -> 15.1 us
    ppermute x25 -> x23, waiting for transfers between devices: 63.7 us -> 39 us  [flip(): return lax.ppermute(value, axis, [(i, i ^ bit) for i in range(count)])]
    ppermute x25 -> x23, starting transfers between devices: 31.9 us -> 42.7 us  [flip(): return lax.ppermute(value, axis, [(i, i ^ bit) for i in range(count)])]
    ppermute x8, waiting for transfers between devices: 21.3 us -> 15.7 us  [hop(): return lax.ppermute(value, axis, pairs)]
    slice x2, local copies, waits for them, and re-layouts: 0.09 us -> 3.07 us  [dense_plan(): down[-1][rows]]
    slice x2, local copies, waits for them, and re-layouts: 0.07 us -> 3.03 us  [dense_plan(): up[-1][rows]]
    ppermute x8, starting transfers between devices: 10.5 us -> 13.4 us  [hop(): return lax.ppermute(value, axis, pairs)]
    unnamed x37 -> x42, local copies, waits for them, and re-layouts: 4.88 us -> 5.75 us
  transfers between devices with their start and end apart: 33 -> 31, of which waited for: 16 -> 11; matrix products, arithmetic and copies ran while one was open for 6% -> 9% of each run, Pallas kernels for 16% -> 18%
where the time goes in v8:
time: 180 us; the launch traced here: 179 us
  starting transfers between devices  56.1 us (31%)
  waiting for transfers between devices  54.7 us (30%)
  Pallas kernels  40.9 us (23%)
  local copies, waits for them, and re-layouts  15.1 us (8%)
  matrix products  9.3 us (5%)
  other arithmetic  1.83 us (1%)
    ppermute x23, starting transfers between devices, flip(): return lax.ppermute(value, axis, [(i, i ^ bit) for i in range(count)])  42.7 us
    ppermute x23, waiting for transfers between devices, flip(): return lax.ppermute(value, axis, [(i, i ^ bit) for i in range(count)])  39 us
    ppermute x8, waiting for transfers between devices, hop(): return lax.ppermute(value, axis, pairs)  15.7 us
    ppermute x8, starting transfers between devices, hop(): return lax.ppermute(value, axis, pairs)  13.4 us
    pallas_call x3, Pallas kernels, piece_grad(): pl.pallas_call(functools.partial(piece_grad_kernel, [[len(row) for row in...  10.3 us
    dot_general x4, matrix products, rows_for(): jnp.dot(spread, weights[:, n * width:(n + 1) * width], preferred_element_...  9.3 us
    pallas_call x3, Pallas kernels, gather_columns(): pl.pallas_call(gather_kernel, out_shape=jax.ShapeDtypeStruct((rows, count...  8.39 us
    pallas_call x3, Pallas kernels, decoder_part(): pl.pallas_call(functools.partial(decoder_kernel, len(onto)), out_shape=ja...  7.29 us
  transfers between devices with their start and end apart: 31, of which 11 were waited for; matrix products, arithmetic and copies ran while one was open for 9% of the time, Pallas kernels for 18%

profile of v8, /device:TPU:1, one launch (start us, length us, event | category | flops | bytes accessed | tf_op | source)
XLA Modules:
  0.0 179.2 jit_solution(5630509387917892304)
XLA Ops:
  3.6 4.8 %collective-permute-start.2 = (bf16[272,128]{1,0:T(8,128)(2,1)S(1)}, bf16[272,128]{1,0:T(8,128)(2,1)S(1)}, u32[]{:S(2)}, u32[]{:S(2)}) collective-permute-start(bf16[272,128]{1,0:T(8,128)(2,1)S(1)} %fusion.21.refs_0_), channel_id=1, source_target_pairs={{0,6},{2,4},{4,2},{6,0},{1,7},{3,5},{5,3},{7,1},{8,14},{10,12},{12... | collective-permute-start | bytes 208904 | tf_op jit(solution)/shard_map/ppermute | solution.py:103
  8.8 3.9 %gather_columns.3.refs_4_ = bf16[2048,1024]{1,0:T(8,128)(2,1)S(1)} custom-call(s32[4]{0:T(128)S(1)} %pad_add_fusion.1.scalar_ref, bf16[1,2048,4096]{2,1,0:T(8,128)(2,1)} %weight_ref.5), custom_call_target="tpu_custom_call" | custom-call | flops 3960000000 | bytes 1 | tf_op jit(solution)/shard_map/gather_columns/pallas_call | solution.py:135
  18.8 4.1 %collective-permute-start.6 = (bf16[256,2048]{1,0:T(8,128)(2,1)S(1)}, bf16[256,2048]{1,0:T(8,128)(2,1)S(1)}, u32[]{:S(2)}, u32[]{:S(2)}) collective-permute-start(bf16[256,2048]{1,0:T(8,128)(2,1)S(1)} %pad_maximum_fusion.refs_0_), channel_id=1, source_target_pairs={{0,2},{2,4},{4,6},{1,3},{3,5},{5,7},{8,10},{10,12},{12,14},{9,11},... | collective-permute-start | bytes 3145736 | tf_op jit(solution)/shard_map/ppermute | solution.py:112
  23.0 2.6 %spread_codes.1 = bf16[1024,2048]{1,0:T(8,128)(2,1)S(1)} custom-call(s32[1]{0:T(128)} %bitcast.5.scalar_ref, bf16[8,272,128]{2,1,0:T(8,128)(2,1)S(1)} %bitcast.41), custom_call_target="tpu_custom_call" | custom-call | flops 2750000128 | bytes 1 | tf_op jit(solution)/shard_map/spread_codes/pallas_call | solution.py:181
  25.6 2.3 %fusion.8 = bf16[1024,512]{1,0:T(8,128)(2,1)S(1)} fusion(bf16[1024,2048]{1,0:T(8,128)(2,1)S(1)} %spread_codes.1, bf16[2048,1024]{1,0:T(8,128)(2,1)S(1)} %copy-done.1), kind=kOutput, calls=%fused_computation.8 | convolution fusion | flops 2148007936 | bytes 7340032 | tf_op jit(solution)/shard_map/dot_general | solution.py:551
  32.9 3.9 %gather_columns.4 = bf16[2048,1024]{1,0:T(8,128)(2,1)S(1)} custom-call(s32[4]{0:T(128)S(1)} %pad_add_fusion.scalar_ref, bf16[1,2048,4096]{2,1,0:T(8,128)(2,1)} %weight_ref.5), custom_call_target="tpu_custom_call" | custom-call | flops 3960000000 | bytes 1 | tf_op jit(solution)/shard_map/gather_columns/pallas_call | solution.py:135
  36.7 7.4 %collective-permute-done.7.refs_1_ = bf16[256,2048]{1,0:T(8,128)(2,1)S(1)} collective-permute-done((bf16[256,2048]{1,0:T(8,128)(2,1)S(1)}, bf16[256,2048]{1,0:T(8,128)(2,1)S(1)}, u32[]{:S(2)}, u32[]{:S(2)}) %collective-permute-start.7) | collective-permute-done | bytes 1048608 | tf_op jit(solution)/shard_map/ppermute | solution.py:112
  48.1 2.3 %fusion.17.kept_b = bf16[1024,512]{1,0:T(8,128)(2,1)S(1)} fusion(bf16[1024,2048]{1,0:T(8,128)(2,1)S(1)} %spread_codes.1, bf16[2048,1024]{1,0:T(8,128)(2,1)S(1)} %gather_columns.4), kind=kOutput, calls=%fused_computation.11 | convolution fusion | flops 2148007936 | bytes 7340032 | tf_op jit(solution)/shard_map/dot_general | solution.py:551
  52.8 2.6 %collective-permute-done.9.got_b = bf16[1024,512]{1,0:T(8,128)(2,1)S(1)} collective-permute-done((bf16[1024,512]{1,0:T(8,128)(2,1)S(1)}, bf16[1024,512]{1,0:T(8,128)(2,1)S(1)}, u32[]{:S(2)}, u32[]{:S(2)}) %collective-permute-start.9) | collective-permute-done | bytes 1048608 | tf_op jit(solution)/shard_map/ppermute | solution.py:103
  58.1 2.4 %collective-permute-start.11 = (bf16[128,512]{1,0:T(8,128)(2,1)S(1)}, bf16[128,512]{1,0:T(8,128)(2,1)S(1)}, u32[]{:S(2)}, u32[]{:S(2)}) collective-permute-start(bf16[128,512]{1,0:T(8,128)(2,1)S(1)} %get-tuple-element.103), channel_id=1, source_target_pairs={{0,1},{1,0},{2,3},{3,2},{4,5},{5,4},{6,7},{7,6},{8,9},{9,8},{10,11... | collective-permute-start | bytes 393224 | tf_op jit(solution)/shard_map/ppermute | solution.py:103
  61.5 5.9 %collective-permute-done.10.far_b = bf16[1024,256]{1,0:T(8,128)(2,1)S(1)} collective-permute-done((bf16[1024,256]{1,0:T(8,128)(2,1)S(1)}, bf16[1024,256]{1,0:T(8,128)(2,1)S(1)}, u32[]{:S(2)}, u32[]{:S(2)}) %collective-permute-start.10) | collective-permute-done | bytes 524320 | tf_op jit(solution)/shard_map/ppermute | solution.py:103
  67.6 7.4 %collective-permute-done.13.refs_4_ = bf16[256,2048]{1,0:T(8,128)(2,1)} collective-permute-done((bf16[256,2048]{1,0:T(8,128)(2,1)S(1)}, bf16[256,2048]{1,0:T(8,128)(2,1)}, u32[]{:S(2)}, u32[]{:S(2)}) %collective-permute-start.13) | collective-permute-done | bytes 1048608 | tf_op jit(solution)/shard_map/ppermute | solution.py:112
  76.6 2.4 %collective-permute-start.16 = (bf16[256,512]{1,0:T(8,128)(2,1)S(1)}, bf16[256,512]{1,0:T(8,128)(2,1)S(1)}, u32[]{:S(2)}, u32[]{:S(2)}) collective-permute-start(bf16[256,512]{1,0:T(8,128)(2,1)S(1)} %get-tuple-element.66), channel_id=1, source_target_pairs={{0,6},{2,4},{4,2},{6,0},{1,7},{3,5},{5,3},{7,1},{8,14},{10,12},{12... | collective-permute-start | bytes 786440 | tf_op jit(solution)/shard_map/ppermute | solution.py:103
  79.0 4.3 %collective-permute-done.14 = bf16[256,512]{1,0:T(8,128)(2,1)S(1)} collective-permute-done((bf16[256,512]{1,0:T(8,128)(2,1)S(1)}, bf16[256,512]{1,0:T(8,128)(2,1)S(1)}, u32[]{:S(2)}, u32[]{:S(2)}) %collective-permute-start.14) | collective-permute-done | bytes 262176 | tf_op jit(solution)/shard_map/ppermute | solution.py:103
  83.3 12.0 %collective-permute-done.15 = bf16[256,512]{1,0:T(8,128)(2,1)S(1)} collective-permute-done((bf16[256,512]{1,0:T(8,128)(2,1)S(1)}, bf16[256,512]{1,0:T(8,128)(2,1)S(1)}, u32[]{:S(2)}, u32[]{:S(2)}) %collective-permute-start.15) | collective-permute-done | bytes 262176 | tf_op jit(solution)/shard_map/ppermute | solution.py:103
  95.5 9.9 %collective-permute-start.20 = (bf16[256,512]{1,0:T(8,128)(2,1)S(1)}, bf16[256,512]{1,0:T(8,128)(2,1)S(1)}, u32[]{:S(2)}, u32[]{:S(2)}) collective-permute-start(bf16[256,512]{1,0:T(8,128)(2,1)S(1)} %multiply_convert_fusion.refs_0_), channel_id=1, source_target_pairs={{0,4},{2,6},{4,0},{6,2},{1,5},{3,7},{5,1},{7,3},{8,12},{10,14},{12... | collective-permute-start | bytes 786440 | tf_op jit(solution)/shard_map/ppermute | solution.py:103
  108.9 11.3 %collective-permute-done.20 = bf16[256,512]{1,0:T(8,128)(2,1)S(1)} collective-permute-done((bf16[256,512]{1,0:T(8,128)(2,1)S(1)}, bf16[256,512]{1,0:T(8,128)(2,1)S(1)}, u32[]{:S(2)}, u32[]{:S(2)}) %collective-permute-start.20) | collective-permute-done | bytes 262176 | tf_op jit(solution)/shard_map/ppermute | solution.py:103
  137.9 2.7 %piece_grad.3 = (bf16[1,16,64,512]{3,2,1,0:T(8,128)(2,1)S(1)}, f32[16,64,128]{2,1,0:T(8,128)S(1)}) custom-call(s32[1]{0:T(128)} %bitcast.19.scalar_ref, bf16[4,256,256]{2,1,0:T(8,128)(2,1)S(1)} %get-tuple-element.74.hot_ref, bf16[1,2048,4096]{2,1,0:T(8,128)(2,1)} %weight_ref.5, bf16[256,512]{1,0:T(8,128)(2,1)S(1)} %copy-done.3, ...), custom_call_target="tpu_custom_call" | custom-call | flops 3080000000 | bytes 1 | tf_op jit(solution)/shard_map/piece_grad/pallas_call | solution.py:360
  144.4 4.8 %piece_grad.4 = (bf16[2,16,64,512]{3,2,1,0:T(8,128)(2,1)S(1)}, f32[16,64,128]{2,1,0:T(8,128)S(1)}) custom-call(s32[2]{0:T(128)S(1)} %pad_add_fusion.3.scalar_ref, bf16[4,256,256]{2,1,0:T(8,128)(2,1)S(1)} %get-tuple-element.74.hot_ref, bf16[1,2048,4096]{2,1,0:T(8,128)(2,1)} %weight_ref.5, f32[16,64,128]{2,1,0:T(8,128)S(1)} %get-tuple-element.86.refs_0_, ...), custom_call_target="tpu_custom_call" | custom-call | flops 5280000000 | bytes 1 | tf_op jit(solution)/shard_map/piece_grad/pallas_call | solution.py:360
  149.2 3.3 %decoder_part.4.refs_0_ = bf16[2048,2048]{1,0:T(8,128)(2,1)} custom-call(s32[2]{0:T(128)S(1)} %pad_add_fusion.4.scalar_ref, bf16[16,128,64]{2,1,0:T(8,128)(2,1)S(1)} %get-tuple-element.73.code_ref, bf16[2,16,64,512]{3,2,1,0:T(8,128)(2,1)S(1)} %get-tuple-element.88.slots_ref, bf16[2048,2048]{1,0:T(8,128)(2,1)} %decoder_part.3.refs_0_), custom_call_target="tpu_custom_call", output_to_operand_aliasing={{}: (3, {})} | custom-call | flops 3630000128 | bytes 1 | tf_op jit(solution)/shard_map/decoder_part/pallas_call | solution.py:395
  152.5 4.7 %act_slots.1.act_ref = bf16[16,64,2048]{2,1,0:T(8,128)(2,1)S(1)} custom-call(s32[4]{0:T(128)S(1)} %pad_add_fusion.5.scalar_ref, bf16[4,256,256]{2,1,0:T(8,128)(2,1)S(1)} %get-tuple-element.74.hot_ref, bf16[256,2048]{1,0:T(8,128)(2,1)S(1)} %copy-done.5, bf16[256,2048]{1,0:T(8,128)(2,1)S(1)} %copy-done.12, bf16[176,2048]{1,0:T(8,128)(2,1)} %collective-permute-done.24.refs_2_, ...), custom_call_target="tpu_custom_call" | custom-call | flops 3630000128 | bytes 1 | tf_op jit(solution)/shard_map/act_slots/pallas_call | solution.py:435
  157.3 2.8 %piece_grad.5 = (bf16[1,16,64,512]{3,2,1,0:T(8,128)(2,1)S(1)}, f32[16,64,128]{2,1,0:T(8,128)S(1)}) custom-call(s32[1]{0:T(128)} %bitcast.21.scalar_ref, bf16[4,256,256]{2,1,0:T(8,128)(2,1)S(1)} %get-tuple-element.74.hot_ref, bf16[1,2048,4096]{2,1,0:T(8,128)(2,1)} %weight_ref.5, f32[16,64,128]{2,1,0:T(8,128)S(1)} %get-tuple-element.92.refs_0_, ...), custom_call_target="tpu_custom_call" | custom-call | flops 3080000000 | bytes 1 | tf_op jit(solution)/shard_map/piece_grad/pallas_call | solution.py:360
  160.1 10.9 %collective-permute-start.30 = (f32[16,64,128]{2,1,0:T(8,128)S(1)}, f32[16,64,128]{2,1,0:T(8,128)S(1)}, u32[]{:S(2)}, u32[]{:S(2)}) collective-permute-start(f32[16,64,128]{2,1,0:T(8,128)S(1)} %get-tuple-element.98.own_ref), channel_id=1, source_target_pairs={{0,1},{1,0},{2,3},{3,2},{4,5},{5,4},{6,7},{7,6},{8,9},{9,8},{10,11... | collective-permute-start | bytes 1572872 | tf_op jit(solution)/shard_map/ppermute | solution.py:103
  172.9 6.3 %encoder_part.1 = bf16[2048,2048]{1,0:T(8,128)(2,1)} custom-call(bf16[16,64,128]{2,1,0:T(8,128)(2,1)S(1)} %copy-done.16, f32[16,64,128]{2,1,0:T(8,128)S(1)} %get-tuple-element.98.own_ref, f32[16,64,128]{2,1,0:T(8,128)S(1)} %collective-permute-done.30.theirs_ref, bf16[16,64,2048]{2,1,0:T(8,128)(2,1)S(1)} %act_slots.1.act_ref), custom_call_target="tpu_custom_call" | custom-call | flops 7150000128 | bytes 1 | tf_op jit(solution)/shard_map/encoder_part/pallas_call | solution.py:471
  (130 shorter events, 53.2 us)
Async XLA Ops:
  3.5 12.9 %collective-permute-start.3 = (bf16[128,2048]{1,0:T(8,128)(2,1)S(1)}, bf16[128,2048]{1,0:T(8,128)(2,1)S(1)}, u32[]{:S(2)}, u32[]{:S(2)}) collective-permute-start(bf16[128,2048]{1,0:T(8,128)(2,1)S(1)} %get-tuple-element.101), channel_id=1, source_target_pairs={{0,1},{1,0},{2,3},{3,2},{4,5},{5,4},{6,7},{7,6},{8,9},{9,8},{10,11... | collective-permute-start | bytes 1572872 | tf_op jit(solution)/shard_map/ppermute | solution.py:103
  17.5 26.6 %collective-permute-start.7 = (bf16[256,2048]{1,0:T(8,128)(2,1)S(1)}, bf16[256,2048]{1,0:T(8,128)(2,1)S(1)}, u32[]{:S(2)}, u32[]{:S(2)}) collective-permute-start(bf16[256,2048]{1,0:T(8,128)(2,1)S(1)} %pad_maximum_fusion.refs_0_), channel_id=1, source_target_pairs={{2,0},{4,2},{6,4},{3,1},{5,3},{7,5},{10,8},{12,10},{14,12},{11,9},... | collective-permute-start | bytes 3145736 | tf_op jit(solution)/shard_map/ppermute | solution.py:112
  18.8 26.2 %collective-permute-start.6 = (bf16[256,2048]{1,0:T(8,128)(2,1)S(1)}, bf16[256,2048]{1,0:T(8,128)(2,1)S(1)}, u32[]{:S(2)}, u32[]{:S(2)}) collective-permute-start(bf16[256,2048]{1,0:T(8,128)(2,1)S(1)} %pad_maximum_fusion.refs_0_), channel_id=1, source_target_pairs={{0,2},{2,4},{4,6},{1,3},{3,5},{5,7},{8,10},{10,12},{12,14},{9,11},... | collective-permute-start | bytes 3145736 | tf_op jit(solution)/shard_map/ppermute | solution.py:112
  28.0 27.9 %collective-permute-start.5 = (bf16[1024,512]{1,0:T(8,128)(2,1)S(1)}, bf16[1024,512]{1,0:T(8,128)(2,1)S(1)}, u32[]{:S(2)}, u32[]{:S(2)}) collective-permute-start(bf16[1024,512]{1,0:T(8,128)(2,1)S(1)} %fusion.8), channel_id=1, source_target_pairs={{0,8},{8,0},{16,24},{24,16},{1,9},{9,1},{17,25},{25,17},{2,10},{10... | collective-permute-start | bytes 3145736 | tf_op jit(solution)/shard_map/ppermute | solution.py:103
  31.6 23.9 %collective-permute-start.9 = (bf16[1024,512]{1,0:T(8,128)(2,1)S(1)}, bf16[1024,512]{1,0:T(8,128)(2,1)S(1)}, u32[]{:S(2)}, u32[]{:S(2)}) collective-permute-start(bf16[1024,512]{1,0:T(8,128)(2,1)S(1)} %fusion.14), channel_id=1, source_target_pairs={{0,16},{8,24},{16,0},{24,8},{1,17},{9,25},{17,1},{25,9},{2,18},{10... | collective-permute-start | bytes 3145736 | tf_op jit(solution)/shard_map/ppermute | solution.py:103
  45.0 22.6 %collective-permute-start.12 = (bf16[256,2048]{1,0:T(8,128)(2,1)S(1)}, bf16[256,2048]{1,0:T(8,128)(2,1)}, u32[]{:S(2)}, u32[]{:S(2)}) collective-permute-start(bf16[256,2048]{1,0:T(8,128)(2,1)S(1)} %collective-permute-done.6.refs_8_), channel_id=1, source_target_pairs={{2,4},{4,6},{3,5},{5,7},{10,12},{12,14},{11,13},{13,15},{18,20},{2... | collective-permute-start | bytes 3145736 | tf_op jit(solution)/shard_map/ppermute | solution.py:112
  46.7 28.3 %collective-permute-start.13 = (bf16[256,2048]{1,0:T(8,128)(2,1)S(1)}, bf16[256,2048]{1,0:T(8,128)(2,1)}, u32[]{:S(2)}, u32[]{:S(2)}) collective-permute-start(bf16[256,2048]{1,0:T(8,128)(2,1)S(1)} %collective-permute-done.7.refs_1_), channel_id=1, source_target_pairs={{2,0},{4,2},{3,1},{5,3},{10,8},{12,10},{11,9},{13,11},{18,16},{20,... | collective-permute-start | bytes 3145736 | tf_op jit(solution)/shard_map/ppermute | solution.py:112
  55.6 11.8 %collective-permute-start.10 = (bf16[1024,256]{1,0:T(8,128)(2,1)S(1)}, bf16[1024,256]{1,0:T(8,128)(2,1)S(1)}, u32[]{:S(2)}, u32[]{:S(2)}) collective-permute-start(bf16[1024,256]{1,0:T(8,128)(2,1)S(1)} %add_convert_fusion), channel_id=1, source_target_pairs={{0,8},{8,0},{16,24},{24,16},{1,9},{9,1},{17,25},{25,17},{2,10},{10... | collective-permute-start | bytes 1572872 | tf_op jit(solution)/shard_map/ppermute | solution.py:103
  56.0 11.5 %collective-permute-start.8 = (bf16[1024,256]{1,0:T(8,128)(2,1)S(1)}, bf16[1024,256]{1,0:T(8,128)(2,1)S(1)}, u32[]{:S(2)}, u32[]{:S(2)}) collective-permute-start(bf16[1024,256]{1,0:T(8,128)(2,1)S(1)} %add_convert_fusion.1), channel_id=1, source_target_pairs={{0,16},{8,24},{16,0},{24,8},{1,17},{9,25},{17,1},{25,9},{2,18},{10... | collective-permute-start | bytes 1572872 | tf_op jit(solution)/shard_map/ppermute | solution.py:103
  76.6 18.6 %collective-permute-start.15 = (bf16[256,512]{1,0:T(8,128)(2,1)S(1)}, bf16[256,512]{1,0:T(8,128)(2,1)S(1)}, u32[]{:S(2)}, u32[]{:S(2)}) collective-permute-start(bf16[256,512]{1,0:T(8,128)(2,1)S(1)} %get-tuple-element.65), channel_id=1, source_target_pairs={{0,4},{2,6},{4,0},{6,2},{1,5},{3,7},{5,1},{7,3},{8,12},{10,14},{12... | collective-permute-start | bytes 786440 | tf_op jit(solution)/shard_map/ppermute | solution.py:103
  76.6 18.6 %collective-permute-start.16 = (bf16[256,512]{1,0:T(8,128)(2,1)S(1)}, bf16[256,512]{1,0:T(8,128)(2,1)S(1)}, u32[]{:S(2)}, u32[]{:S(2)}) collective-permute-start(bf16[256,512]{1,0:T(8,128)(2,1)S(1)} %get-tuple-element.66), channel_id=1, source_target_pairs={{0,6},{2,4},{4,2},{6,0},{1,7},{3,5},{5,3},{7,1},{8,14},{10,12},{12... | collective-permute-start | bytes 786440 | tf_op jit(solution)/shard_map/ppermute | solution.py:103
  95.5 13.4 %collective-permute-start.21 = (bf16[256,512]{1,0:T(8,128)(2,1)S(1)}, bf16[256,512]{1,0:T(8,128)(2,1)S(1)}, u32[]{:S(2)}, u32[]{:S(2)}) collective-permute-start(bf16[256,512]{1,0:T(8,128)(2,1)S(1)} %multiply_convert_fusion.refs_0_), channel_id=1, source_target_pairs={{0,6},{2,4},{4,2},{6,0},{1,7},{3,5},{5,3},{7,1},{8,14},{10,12},{12... | collective-permute-start | bytes 786440 | tf_op jit(solution)/shard_map/ppermute | solution.py:103
  95.5 24.6 %collective-permute-start.20 = (bf16[256,512]{1,0:T(8,128)(2,1)S(1)}, bf16[256,512]{1,0:T(8,128)(2,1)S(1)}, u32[]{:S(2)}, u32[]{:S(2)}) collective-permute-start(bf16[256,512]{1,0:T(8,128)(2,1)S(1)} %multiply_convert_fusion.refs_0_), channel_id=1, source_target_pairs={{0,4},{2,6},{4,0},{6,2},{1,5},{3,7},{5,1},{7,3},{8,12},{10,14},{12... | collective-permute-start | bytes 786440 | tf_op jit(solution)/shard_map/ppermute | solution.py:103
  105.4 14.8 %collective-permute-start.19 = (bf16[256,512]{1,0:T(8,128)(2,1)S(1)}, bf16[256,512]{1,0:T(8,128)(2,1)S(1)}, u32[]{:S(2)}, u32[]{:S(2)}) collective-permute-start(bf16[256,512]{1,0:T(8,128)(2,1)S(1)} %multiply_convert_fusion.refs_0_), channel_id=1, source_target_pairs={{0,2},{2,0},{4,6},{6,4},{1,3},{3,1},{5,7},{7,5},{8,10},{10,8},{12,... | collective-permute-start | bytes 786440 | tf_op jit(solution)/shard_map/ppermute | solution.py:103
  105.4 14.8 %collective-permute-start.18 = (bf16[256,512]{1,0:T(8,128)(2,1)S(1)}, bf16[256,512]{1,0:T(8,128)(2,1)S(1)}, u32[]{:S(2)}, u32[]{:S(2)}) collective-permute-start(bf16[256,512]{1,0:T(8,128)(2,1)S(1)} %multiply_convert_fusion.refs_0_), channel_id=1, source_target_pairs={{0,16},{8,24},{16,0},{24,8},{1,17},{9,25},{17,1},{25,9},{2,18},{10... | collective-permute-start | bytes 786440 | tf_op jit(solution)/shard_map/ppermute | solution.py:103
  106.7 13.6 %collective-permute-start.17 = (bf16[256,512]{1,0:T(8,128)(2,1)S(1)}, bf16[256,512]{1,0:T(8,128)(2,1)S(1)}, u32[]{:S(2)}, u32[]{:S(2)}) collective-permute-start(bf16[256,512]{1,0:T(8,128)(2,1)S(1)} %multiply_convert_fusion.refs_0_), channel_id=1, source_target_pairs={{0,8},{8,0},{16,24},{24,16},{1,9},{9,1},{17,25},{25,17},{2,10},{10... | collective-permute-start | bytes 786440 | tf_op jit(solution)/shard_map/ppermute | solution.py:103
  124.0 19.6 %collective-permute-start.23 = (bf16[768,512]{1,0:T(8,128)(2,1)S(1)}, bf16[768,512]{1,0:T(8,128)(2,1)S(1)}, u32[]{:S(2)}, u32[]{:S(2)}) collective-permute-start(bf16[768,512]{1,0:T(8,128)(2,1)S(1)} %constant_dynamic-update-slice_fusion.refs_1_), channel_id=1, source_target_pairs={{0,16},{8,24},{16,0},{24,8},{1,17},{9,25},{17,1},{25,9},{2,18},{10... | collective-permute-start | bytes 2359304 | tf_op jit(solution)/shard_map/ppermute | solution.py:103
  125.3 18.3 %collective-permute-start.22 = (bf16[768,512]{1,0:T(8,128)(2,1)S(1)}, bf16[768,512]{1,0:T(8,128)(2,1)S(1)}, u32[]{:S(2)}, u32[]{:S(2)}) collective-permute-start(bf16[768,512]{1,0:T(8,128)(2,1)S(1)} %constant_dynamic-update-slice_fusion.refs_1_), channel_id=1, source_target_pairs={{0,8},{8,0},{16,24},{24,16},{1,9},{9,1},{17,25},{25,17},{2,10},{10... | collective-permute-start | bytes 2359304 | tf_op jit(solution)/shard_map/ppermute | solution.py:103
  128.6 14.0 %collective-permute-start.25 = (bf16[176,2048]{1,0:T(8,128)(2,1)}, bf16[176,2048]{1,0:T(8,128)(2,1)}, u32[]{:S(2)}, u32[]{:S(2)}) collective-permute-start(bf16[176,2048]{1,0:T(8,128)(2,1)} %slice.66), channel_id=1, source_target_pairs={{2,0},{3,1},{10,8},{11,9},{18,16},{19,17},{26,24},{27,25}} | collective-permute-start | bytes 2162696 | tf_op jit(solution)/shard_map/ppermute | solution.py:112
  132.0 11.6 %collective-permute-start.24 = (bf16[176,2048]{1,0:T(8,128)(2,1)}, bf16[176,2048]{1,0:T(8,128)(2,1)}, u32[]{:S(2)}, u32[]{:S(2)}) collective-permute-start(bf16[176,2048]{1,0:T(8,128)(2,1)} %slice.65), channel_id=1, source_target_pairs={{4,6},{5,7},{12,14},{13,15},{20,22},{21,23},{28,30},{29,31}} | collective-permute-start | bytes 2162696 | tf_op jit(solution)/shard_map/ppermute | solution.py:112
  135.6 16.9 %collective-permute-start.29 = (bf16[80,2048]{1,0:T(8,128)(2,1)S(1)}, bf16[80,2048]{1,0:T(8,128)(2,1)S(1)}, u32[]{:S(2)}, u32[]{:S(2)}) collective-permute-start(bf16[80,2048]{1,0:T(8,128)(2,1)S(1)} %slice.71), channel_id=1, source_target_pairs={{2,0},{3,1},{10,8},{11,9},{18,16},{19,17},{26,24},{27,25}} | collective-permute-start | bytes 983048 | tf_op jit(solution)/shard_map/ppermute | solution.py:112
  143.7 13.5 %collective-permute-start.27 = (bf16[1024,256]{1,0:T(8,128)(2,1)S(1)}, bf16[1024,256]{1,0:T(8,128)(2,1)S(1)}, u32[]{:S(2)}, u32[]{:S(2)}) collective-permute-start(bf16[1024,256]{1,0:T(8,128)(2,1)S(1)} %pad_maximum_fusion.3), channel_id=1, source_target_pairs={{0,16},{8,24},{16,0},{24,8},{1,17},{9,25},{17,1},{25,9},{2,18},{10... | collective-permute-start | bytes 1572872 | tf_op jit(solution)/shard_map/ppermute | solution.py:103
  144.1 13.2 %collective-permute-start.26 = (bf16[1024,256]{1,0:T(8,128)(2,1)S(1)}, bf16[1024,256]{1,0:T(8,128)(2,1)S(1)}, u32[]{:S(2)}, u32[]{:S(2)}) collective-permute-start(bf16[1024,256]{1,0:T(8,128)(2,1)S(1)} %pad_maximum_fusion.2), channel_id=1, source_target_pairs={{0,8},{8,0},{16,24},{24,16},{1,9},{9,1},{17,25},{25,17},{2,10},{10... | collective-permute-start | bytes 1572872 | tf_op jit(solution)/shard_map/ppermute | solution.py:103
  160.1 12.9 %collective-permute-start.30 = (f32[16,64,128]{2,1,0:T(8,128)S(1)}, f32[16,64,128]{2,1,0:T(8,128)S(1)}, u32[]{:S(2)}, u32[]{:S(2)}) collective-permute-start(f32[16,64,128]{2,1,0:T(8,128)S(1)} %get-tuple-element.98.own_ref), channel_id=1, source_target_pairs={{0,1},{1,0},{2,3},{3,2},{4,5},{5,4},{6,7},{7,6},{8,9},{9,8},{10,11... | collective-permute-start | bytes 1572872 | tf_op jit(solution)/shard_map/ppermute | solution.py:103
  (29 other events, 171.3 us)

commit v9 on v8

--- a/solution.py
+++ b/solution.py
@@ -124,8 +124,9 @@
     return pl.BlockSpec(shape, lambda i, s: (0,) * len(shape))
 
 
-def gather_kernel(scalar_ref, source_ref, out_ref):
+def gather_kernel(scalar_ref, source_ref, out_ref, token_ref):
     out_ref[...] = source_ref[...].reshape(out_ref.shape)
+    token_ref[...] = jnp.zeros_like(token_ref)
 
 
 def gather_columns(source, columns, width):
@@ -134,12 +135,15 @@
     count = columns.shape[0]
     return pl.pallas_call(
         gather_kernel,
-        out_shape=jax.ShapeDtypeStruct((rows, count * width), source.dtype),
+        out_shape=[
+            jax.ShapeDtypeStruct((rows, count * width), source.dtype),
+            jax.ShapeDtypeStruct((8, 128), jnp.float32),
+        ],
         grid_spec=pltpu.PrefetchScalarGridSpec(
             num_scalar_prefetch=1,
             grid=(count,),
             in_specs=[pl.BlockSpec(lead + (rows, width), lambda i, s: (0,) * len(lead) + (0, s[i]))],
-            out_specs=pl.BlockSpec((rows, width), lambda i, s: (0, i)),
+            out_specs=[pl.BlockSpec((rows, width), lambda i, s: (0, i)), resident((8, 128))],
         ),
         compiler_params=params(),
         cost_estimate=cost(0.9 * count),
@@ -227,24 +231,25 @@
     )(*terms_a, *terms_b)
 
 
-def join_kernel(*refs):
+def join_kernel(count, *refs):
     out_ref = refs[-1]
-    for i in range(out_ref.shape[0]):
-        out_ref[i] = refs[i][...]
-
-
-def join(parts, waited):
-    shape = (len(parts),) + parts[0].shape
+    rows = out_ref.shape[0] // count
+    for i in range(count):
+        out_ref[i * rows:(i + 1) * rows] = refs[i][...]
+
+
+def join(parts, *waited):
+    shape = (len(parts) * parts[0].shape[0],) + parts[0].shape[1:]
     vmem = pl.BlockSpec(memory_space=pltpu.VMEM)
     return pl.pallas_call(
-        join_kernel,
+        functools.partial(join_kernel, len(parts)),
         out_shape=jax.ShapeDtypeStruct(shape, parts[0].dtype),
-        in_specs=[vmem] * len(parts) + [pl.BlockSpec(memory_space=pl.ANY)],
+        in_specs=[vmem] * (len(parts) + len(waited)),
         out_specs=vmem,
         compiler_params=params(),
-        cost_estimate=cost(0.3),
+        cost_estimate=cost(0.4),
         name="join",
-    )(*parts, waited)
+    )(*parts, *waited)
 
 
 def slots_kernel(groups, blocks, cap, scalar_ref, message_ref, hot_ref, pre_ref, code_ref):
@@ -515,52 +520,60 @@
     id_rows = jnp.pad(block_ids[0].T, ((0, 16 - active_count), (0, 0))).astype(bf16)
     own = jnp.concatenate([pre_rows, id_rows], axis=0)
     at = places((1, 3), dp_here * lay_count, 2, 0) + places((2, 3), dp_here * lay_count, 2, 1)
-    send_weights = gather_columns(decoder, jnp.stack(at), side)
+    send_weights, token = gather_columns(decoder, jnp.stack(at), side)
 
     message = [own] + [flip(own, "latent", r) for r in range(1, lat_count)]
 
     own, inputs = lax.optimization_barrier((own, activations[0]))
-    acts = jnp.concatenate([columns(inputs, dp_here), flip(columns(inputs, 1 - dp_here), "dp", 1)])
-    message, acts = lax.optimization_barrier((join(message, send_weights), acts))
-    up, down = [acts], [acts]
-
-    def next_hops():
-        step = len(up)
-        up.append(hop(up[-1], "latent", 1, step - 1))
-        down.append(hop(down[-1], "latent", -1, step - 1))
-
+    ups = [[columns(inputs, dp_here)]]
+    downs = [[ups[0][0]]]
+    ups.append([flip(columns(inputs, 1 - dp_here), "dp", 1)])
+    downs.append([ups[1][0]])
+
+    def next_hop(part):
+        step = len(ups[part])
+        ups[part].append(hop(ups[part][-1], "latent", 1, step - 1))
+        downs[part].append(hop(downs[part][-1], "latent", -1, step - 1))
+
+    next_hop(0)
+    message = join(message, token)
+    message, ups, downs = lax.optimization_barrier((message, ups, downs))
+    message = message.reshape((lat_count,) + own.shape)
     message = jnp.stack([message, flip(message, "dp", 1)], axis=1)
     message = message.reshape(lat_count * dp_count, own.shape[0], block_size)
-    next_hops()
+    next_hop(1)
+    for part in range(2):
+        if lat_count > 2:
+            next_hop(part)
 
     codes = spread_codes(message, first, lat_rows)
     at = places((0, 2), dp_here * lay_count, 2, 0) + places((0, 1), dp_here * lay_count, 2, 1)
     at, codes, target = lax.optimization_barrier((jnp.stack(at), codes, target))
-    keep_weights = gather_columns(decoder, at, side)
-    goals = gather_columns(target, jnp.stack([which * lay_count + lay_here for which in (dp_here, 1 - dp_here)]), width)
+    keep_weights, _ = gather_columns(decoder, at, side)
+    goals, _ = gather_columns(target, jnp.stack([which * lay_count + lay_here for which in (dp_here, 1 - dp_here)]), width)
     goals = jnp.concatenate([goals[:, :width], flip(goals[:, width:], "dp", 1)])
 
     codes = spread_codes(message, first, lat_rows)
     at = places((0, 2), dp_here * lay_count, 2, 0) + places((0, 1), dp_here * lay_count, 2, 1)
     at, codes, target = lax.optimization_barrier((jnp.stack(at), codes, target))
-    keep_weights = gather_columns(decoder, at, side)
-    goals = gather_columns(target, jnp.stack([which * lay_count + lay_here for which in (dp_here, 1 - dp_here)]), width)
+    keep_weights, _ = gather_columns(decoder, at, side)
+    goals, _ = gather_columns(target, jnp.stack([which * lay_count + lay_here for which in (dp_here, 1 - dp_here)]), width)
     goals = jnp.concatenate([goals[:, :width], flip(goals[:, width:], "dp", 1)])
 
     def rows_for(spread, weights, n):
         return jnp.dot(spread, weights[:, n * width:(n + 1) * width], preferred_element_type=f32).astype(bf16)
 
     got = flip(rows_for(codes, send_weights, 0), "layer", 1), flip(rows_for(codes, send_weights, 1), "layer", 2)
-    keep_codes, up[1], down[1] = lax.optimization_barrier((codes, up[1], down[1]))
-    if lat_count > 2:
-        next_hops()
+    keep_codes, ups, downs = lax.optimization_barrier((codes, ups, downs))
+    for step in range(3, lat_count):
+        next_hop(0)
     kept = rows_for(keep_codes, keep_weights, 0), rows_for(keep_codes, keep_weights, 1)
 
     def add(one, two):
         return (one[:, side:].astype(f32) + two[:, side:].astype(f32)).astype(bf16)
 
     far = [flip(add(got[n], kept[n]), "layer", 2 - n) for n in range(2)]
-    far, goals, up[-1], down[-1] = lax.optimization_barrier((far, goals, up[-1], down[-1]))
+    far, goals, ups, downs = lax.optimization_barrier((far, goals, ups, downs))
 
     total, *sent = layer_sum((got[0], kept[0], far[0]), (got[1], kept[1], far[1]), lat_count)
     for r in range(1, lat_count):
@@ -569,35 +582,28 @@
     others = [flip(errors, "latent", r) for r in range(1, lat_count)]
     one_near, two_near = flip(errors, "layer", 1), flip(errors, "layer", 2)
     made = make_slots(message, first, lat_rows, capacity)
-    one_near, two_near, others, up[-1], down[-1], made = lax.optimization_barrier(
-        (one_near, two_near, others, up[-1], down[-1], made)
+    one_near, two_near, others, ups, downs, made = lax.optimization_barrier(
+        (one_near, two_near, others, ups, downs, made)
     )
     hot, pre_slots, code_slots = made
-    distant = jnp.concatenate(others)
+    distant = join(others)
     one_far, two_far = flip(distant, "layer", 1), flip(distant, "layer", 2)
-    while len(up) < lat_count - 1:
-        next_hops()
-    early = group * 11 // 16
-    ends = []
-    if len(up) < lat_count:
-        for rows in (slice(0, early), slice(early, group)):
-            ends.append([hop(up[-1][rows], "latent", 1, len(up) - 1), hop(down[-1][rows], "latent", -1, len(up) - 1)])
+    for step in range(3, lat_count):
+        next_hop(1)
 
     def grads_of(here, names, grad, dec):
         slots, grad = piece_grad(here, hot, decoder, weight_places(names), block_size, grad)
         return grad, decoder_part(slots, code_slots, jnp.stack(places(names, 0)), half, dec)
 
     grad, dec = grads_of([[(errors,), (distant,)]], (0,), None, None)
-    one_far, two_far, grad, dec, ends[:1] = lax.optimization_barrier((one_far, two_far, grad, dec, ends[:1]))
+    one_far, two_far, grad, dec, ups, downs = lax.optimization_barrier((one_far, two_far, grad, dec, ups, downs))
     three_a = flip(jnp.concatenate([two_near[:, :side], two_far[:, :side]]), "layer", 1)
     three_b = flip(jnp.concatenate([one_near[:, side:], one_far[:, side:]]), "layer", 2)
     grad, dec = grads_of([[(one_near,), (one_far,)], [(two_near,), (two_far,)]], (1, 2), grad, dec)
 
-    ups, downs = [[part] for part in up], [[part] for part in down]
-    if ends:
-        ups.append([part[0] for part in ends])
-        downs.append([part[1] for part in ends])
-    terms_of = [[[acts]]] + [[downs[k], ups[lat_count - k]] for k in range(1, lat_count)]
+    terms_of = [[[ups[0][0], ups[1][0]]]]
+    for k in range(1, lat_count):
+        terms_of.append([[downs[part][k] for part in range(2)], [ups[part][lat_count - k] for part in range(2)]])
     shards = [lax.rem(lat_here + k, lat_count) ^ lat_here for k in range(lat_count)]
     slotted = act_slots(terms_of, shards, hot, local_blocks)
     three_a, three_b, grad, dec, slotted = lax.optimization_barrier((three_a, three_b, grad, dec, slotted))

time: 180 us -> 198 us (1.10)
  waiting for transfers between devices: 54.7 us -> 77 us
  local copies, waits for them, and re-layouts: 15.1 us -> 4.3 us
  starting transfers between devices: 56.1 us -> 61.5 us
    ppermute x8 -> x12, waiting for transfers between devices: 15.7 us -> 29 us  [hop(): return lax.ppermute(value, axis, pairs)]
    ppermute x23, waiting for transfers between devices: 39 us -> 48.1 us  [flip(): return lax.ppermute(value, axis, [(i, i ^ bit) for i in range(count)])]
    ppermute x8 -> x12, starting transfers between devices: 13.4 us -> 20.7 us  [hop(): return lax.ppermute(value, axis, pairs)]
    slice x4 -> x0, local copies, waits for them, and re-layouts: 6.1 us -> none  [the longest x2 3.07 us: dense_plan(): down[-1][rows]]
    unnamed x42 -> x46, local copies, waits for them, and re-layouts: 5.75 us -> 2.11 us
    pallas_call x4 -> x5, Pallas kernels: 8.41 us -> 10.9 us  [the longest x3 9.53 us: gather_columns(): pl.pallas_call(gather_kernel, out_shape=[jax.ShapeDtypeStruct((rows, coun...]
  transfers between devices with their start and end apart: 31 -> 35, of which waited for: 11 -> 14; matrix products, arithmetic and copies ran while one was open for 9% -> 6% of each run, Pallas kernels for 18% -> 16%
where the time goes in v9:
time: 198 us; the launch traced here: 197 us
  waiting for transfers between devices  77 us (39%)
  starting transfers between devices  61.5 us (31%)
  Pallas kernels  42 us (21%)
  matrix products  9.3 us (5%)
  local copies, waits for them, and re-layouts  4.3 us (2%)
    ppermute x23, waiting for transfers between devices, flip(): return lax.ppermute(value, axis, [(i, i ^ bit) for i in range(count)])  48.1 us
    ppermute x23, starting transfers between devices, flip(): return lax.ppermute(value, axis, [(i, i ^ bit) for i in range(count)])  40.7 us
    ppermute x12, waiting for transfers between devices, hop(): return lax.ppermute(value, axis, pairs)  29 us
    ppermute x12, starting transfers between devices, hop(): return lax.ppermute(value, axis, pairs)  20.7 us
    pallas_call x3, Pallas kernels, piece_grad(): pl.pallas_call(functools.partial(piece_grad_kernel, [[len(row) for row in...  10.3 us
    pallas_call x3, Pallas kernels, gather_columns(): pl.pallas_call(gather_kernel, out_shape=[jax.ShapeDtypeStruct((rows, coun...  9.53 us
    dot_general x4, matrix products, rows_for(): jnp.dot(spread, weights[:, n * width:(n + 1) * width], preferred_element_...  9.3 us
    pallas_call x3, Pallas kernels, decoder_part(): pl.pallas_call(functools.partial(decoder_kernel, len(onto)), out_shape=ja...  7.29 us
  transfers between devices with their start and end apart: 35, of which 14 were waited for; matrix products, arithmetic and copies ran while one was open for 6% of the time, Pallas kernels for 16%

profile of v9, /device:TPU:1, one launch (start us, length us, event | category | flops | bytes accessed | tf_op | source)
XLA Modules:
  0.0 197.2 jit_solution(6021205529647155165)
XLA Ops:
  2.2 4.2 %collective-permute-start.2 = (bf16[272,128]{1,0:T(8,128)(2,1)S(1)}, bf16[272,128]{1,0:T(8,128)(2,1)S(1)}, u32[]{:S(2)}, u32[]{:S(2)}) collective-permute-start(bf16[272,128]{1,0:T(8,128)(2,1)S(1)} %fusion.21.refs_0_), channel_id=1, source_target_pairs={{0,6},{2,4},{4,2},{6,0},{1,7},{3,5},{5,3},{7,1},{8,14},{10,12},{12... | collective-permute-start | bytes 208904 | tf_op jit(solution)/shard_map/ppermute | solution.py:103
  9.0 4.0 %collective-permute-start.3 = (bf16[128,2048]{1,0:T(8,128)(2,1)S(1)}, bf16[128,2048]{1,0:T(8,128)(2,1)S(1)}, u32[]{:S(2)}, u32[]{:S(2)}) collective-permute-start(bf16[128,2048]{1,0:T(8,128)(2,1)S(1)} %get-tuple-element.174.refs_0_), channel_id=1, source_target_pairs={{0,2},{2,4},{4,6},{1,3},{3,5},{5,7},{8,10},{10,12},{12,14},{9,11},... | collective-permute-start | bytes 1572872 | tf_op jit(solution)/shard_map/ppermute | solution.py:112
  15.8 3.9 %gather_columns.3 = (bf16[2048,1024]{1,0:T(8,128)(2,1)S(1)}, f32[8,128]{1,0:T(8,128)S(1)}) custom-call(s32[4]{0:T(128)S(1)} %pad_add_fusion.1.scalar_ref, bf16[1,2048,4096]{2,1,0:T(8,128)(2,1)} %weight_ref.5), custom_call_target="tpu_custom_call" | custom-call | flops 3960000000 | bytes 1 | tf_op jit(solution)/shard_map/gather_columns/pallas_call | solution.py:136
  21.7 3.0 %collective-permute-done.refs_1_ = bf16[272,128]{1,0:T(8,128)(2,1)S(1)} collective-permute-done((bf16[272,128]{1,0:T(8,128)(2,1)S(1)}, bf16[272,128]{1,0:T(8,128)(2,1)S(1)}, u32[]{:S(2)}, u32[]{:S(2)}) %collective-permute-start) | collective-permute-done | bytes 69664 | tf_op jit(solution)/shard_map/ppermute | solution.py:103
  27.5 5.9 %collective-permute-start.9 = (bf16[128,2048]{1,0:T(8,128)(2,1)S(1)}, bf16[128,2048]{1,0:T(8,128)(2,1)S(1)}, u32[]{:S(2)}, u32[]{:S(2)}) collective-permute-start(bf16[128,2048]{1,0:T(8,128)(2,1)S(1)} %collective-permute-done.4.refs_1_), channel_id=1, source_target_pairs={{0,2},{2,4},{4,6},{1,3},{3,5},{5,7},{8,10},{10,12},{12,14},{9,11},... | collective-permute-start | bytes 1572872 | tf_op jit(solution)/shard_map/ppermute | solution.py:112
  42.3 4.4 %gather_columns.4 = (bf16[2048,1024]{1,0:T(8,128)(2,1)S(1)}, f32[8,128]{1,0:T(8,128)}) custom-call(s32[4]{0:T(128)S(1)} %pad_add_fusion.scalar_ref, bf16[1,2048,4096]{2,1,0:T(8,128)(2,1)} %weight_ref.5), custom_call_target="tpu_custom_call" | custom-call | flops 3960000000 | bytes 1 | tf_op jit(solution)/shard_map/gather_columns/pallas_call | solution.py:136
  47.4 13.0 %collective-permute-done.12.refs_3_ = bf16[128,2048]{1,0:T(8,128)(2,1)S(1)} collective-permute-done((bf16[128,2048]{1,0:T(8,128)(2,1)S(1)}, bf16[128,2048]{1,0:T(8,128)(2,1)S(1)}, u32[]{:S(2)}, u32[]{:S(2)}) %collective-permute-start.12) | collective-permute-done | bytes 524320 | tf_op jit(solution)/shard_map/ppermute | solution.py:112
  65.4 9.2 %collective-permute-done.13.refs_7_ = bf16[128,2048]{1,0:T(8,128)(2,1)S(1)} collective-permute-done((bf16[128,2048]{1,0:T(8,128)(2,1)S(1)}, bf16[128,2048]{1,0:T(8,128)(2,1)S(1)}, u32[]{:S(2)}, u32[]{:S(2)}) %collective-permute-start.13) | collective-permute-done | bytes 524320 | tf_op jit(solution)/shard_map/ppermute | solution.py:112
  81.5 6.2 %collective-permute-done.15.got_b = bf16[1024,512]{1,0:T(8,128)(2,1)S(1)} collective-permute-done((bf16[1024,512]{1,0:T(8,128)(2,1)S(1)}, bf16[1024,512]{1,0:T(8,128)(2,1)S(1)}, u32[]{:S(2)}, u32[]{:S(2)}) %collective-permute-start.15) | collective-permute-done | bytes 1048608 | tf_op jit(solution)/shard_map/ppermute | solution.py:103
  91.8 2.7 %collective-permute-start.17 = (bf16[128,512]{1,0:T(8,128)(2,1)S(1)}, bf16[128,512]{1,0:T(8,128)(2,1)S(1)}, u32[]{:S(2)}, u32[]{:S(2)}) collective-permute-start(bf16[128,512]{1,0:T(8,128)(2,1)S(1)} %get-tuple-element.199), channel_id=1, source_target_pairs={{0,1},{1,0},{2,3},{3,2},{4,5},{5,4},{6,7},{7,6},{8,9},{9,8},{10,11... | collective-permute-start | bytes 393224 | tf_op jit(solution)/shard_map/ppermute | solution.py:103
  95.5 3.7 %collective-permute-done.16.far_b = bf16[1024,256]{1,0:T(8,128)(2,1)S(1)} collective-permute-done((bf16[1024,256]{1,0:T(8,128)(2,1)S(1)}, bf16[1024,256]{1,0:T(8,128)(2,1)S(1)}, u32[]{:S(2)}, u32[]{:S(2)}) %collective-permute-start.16) | collective-permute-done | bytes 524320 | tf_op jit(solution)/shard_map/ppermute | solution.py:103
  104.5 4.1 %collective-permute-done.20 = bf16[256,512]{1,0:T(8,128)(2,1)S(1)} collective-permute-done((bf16[256,512]{1,0:T(8,128)(2,1)S(1)}, bf16[256,512]{1,0:T(8,128)(2,1)S(1)}, u32[]{:S(2)}, u32[]{:S(2)}) %collective-permute-start.20) | collective-permute-done | bytes 262176 | tf_op jit(solution)/shard_map/ppermute | solution.py:103
  108.6 3.6 %collective-permute-done.21 = bf16[256,512]{1,0:T(8,128)(2,1)S(1)} collective-permute-done((bf16[256,512]{1,0:T(8,128)(2,1)S(1)}, bf16[256,512]{1,0:T(8,128)(2,1)S(1)}, u32[]{:S(2)}, u32[]{:S(2)}) %collective-permute-start.21) | collective-permute-done | bytes 262176 | tf_op jit(solution)/shard_map/ppermute | solution.py:103
  112.2 5.1 %collective-permute-done.22 = bf16[256,512]{1,0:T(8,128)(2,1)S(1)} collective-permute-done((bf16[256,512]{1,0:T(8,128)(2,1)S(1)}, bf16[256,512]{1,0:T(8,128)(2,1)S(1)}, u32[]{:S(2)}, u32[]{:S(2)}) %collective-permute-start.22) | collective-permute-done | bytes 262176 | tf_op jit(solution)/shard_map/ppermute | solution.py:103
  119.7 11.0 %collective-permute-start.26 = (bf16[256,512]{1,0:T(8,128)(2,1)S(1)}, bf16[256,512]{1,0:T(8,128)(2,1)}, u32[]{:S(2)}, u32[]{:S(2)}) collective-permute-start(bf16[256,512]{1,0:T(8,128)(2,1)S(1)} %multiply_convert_fusion.refs_0_), channel_id=1, source_target_pairs={{0,4},{2,6},{4,0},{6,2},{1,5},{3,7},{5,1},{7,3},{8,12},{10,14},{12... | collective-permute-start | bytes 786440 | tf_op jit(solution)/shard_map/ppermute | solution.py:103
  133.1 17.4 %collective-permute-done.26.refs_1_ = bf16[256,512]{1,0:T(8,128)(2,1)} collective-permute-done((bf16[256,512]{1,0:T(8,128)(2,1)S(1)}, bf16[256,512]{1,0:T(8,128)(2,1)}, u32[]{:S(2)}, u32[]{:S(2)}) %collective-permute-start.26) | collective-permute-done | bytes 262176 | tf_op jit(solution)/shard_map/ppermute | solution.py:103
  155.9 2.7 %piece_grad.3 = (bf16[1,16,64,512]{3,2,1,0:T(8,128)(2,1)S(1)}, f32[16,64,128]{2,1,0:T(8,128)S(1)}) custom-call(s32[1]{0:T(128)} %bitcast.21.scalar_ref, bf16[4,256,256]{2,1,0:T(8,128)(2,1)S(1)} %get-tuple-element.148.hot_ref, bf16[1,2048,4096]{2,1,0:T(8,128)(2,1)} %weight_ref.5, bf16[256,512]{1,0:T(8,128)(2,1)S(1)} %multiply_convert_fusion.refs_0_, ...), custom_call_target="tpu_custom_call" | custom-call | flops 3080000000 | bytes 1 | tf_op jit(solution)/shard_map/piece_grad/pallas_call | solution.py:365
  160.7 6.8 %collective-permute-done.31.refs_11_ = bf16[128,2048]{1,0:T(8,128)(2,1)S(1)} collective-permute-done((bf16[128,2048]{1,0:T(8,128)(2,1)S(1)}, bf16[128,2048]{1,0:T(8,128)(2,1)S(1)}, u32[]{:S(2)}, u32[]{:S(2)}) %collective-permute-start.31) | collective-permute-done | bytes 524320 | tf_op jit(solution)/shard_map/ppermute | solution.py:112
  171.3 4.8 %piece_grad.4 = (bf16[2,16,64,512]{3,2,1,0:T(8,128)(2,1)S(1)}, f32[16,64,128]{2,1,0:T(8,128)S(1)}) custom-call(s32[2]{0:T(128)S(1)} %pad_add_fusion.3.scalar_ref, bf16[4,256,256]{2,1,0:T(8,128)(2,1)S(1)} %get-tuple-element.148.hot_ref, bf16[1,2048,4096]{2,1,0:T(8,128)(2,1)} %weight_ref.5, f32[16,64,128]{2,1,0:T(8,128)S(1)} %get-tuple-element.170.refs_0_, ...), custom_call_target="tpu_custom_call" | custom-call | flops 5280000000 | bytes 1 | tf_op jit(solution)/shard_map/piece_grad/pallas_call | solution.py:365
  176.1 3.3 %decoder_part.4.refs_0_ = bf16[2048,2048]{1,0:T(8,128)(2,1)} custom-call(s32[2]{0:T(128)S(1)} %pad_add_fusion.4.scalar_ref, bf16[16,128,64]{2,1,0:T(8,128)(2,1)S(1)} %get-tuple-element.147.code_ref, bf16[2,16,64,512]{3,2,1,0:T(8,128)(2,1)S(1)} %get-tuple-element.172.slots_ref, bf16[2048,2048]{1,0:T(8,128)(2,1)} %decoder_part.3.refs_0_), custom_call_target="tpu_custom_call", output_to_operand_aliasing={{}: (3, {})} | custom-call | flops 3630000128 | bytes 1 | tf_op jit(solution)/shard_map/decoder_part/pallas_call | solution.py:400
  179.4 3.3 %act_slots.1.act_ref = bf16[16,64,2048]{2,1,0:T(8,128)(2,1)S(1)} custom-call(s32[4]{0:T(128)S(1)} %pad_add_fusion.5.scalar_ref, bf16[4,256,256]{2,1,0:T(8,128)(2,1)S(1)} %get-tuple-element.148.hot_ref, bf16[128,2048]{1,0:T(8,128)(2,1)S(1)} %get-tuple-element.174.refs_0_, bf16[128,2048]{1,0:T(8,128)(2,1)S(1)} %collective-permute-done.4.refs_1_, ...), custom_call_target="tpu_custom_call" | custom-call | flops 3630000128 | bytes 1 | tf_op jit(solution)/shard_map/act_slots/pallas_call | solution.py:440
  182.8 2.8 %piece_grad.5 = (bf16[1,16,64,512]{3,2,1,0:T(8,128)(2,1)S(1)}, f32[16,64,128]{2,1,0:T(8,128)S(1)}) custom-call(s32[1]{0:T(128)} %bitcast.23.scalar_ref, bf16[4,256,256]{2,1,0:T(8,128)(2,1)S(1)} %get-tuple-element.148.hot_ref, bf16[1,2048,4096]{2,1,0:T(8,128)(2,1)} %weight_ref.5, f32[16,64,128]{2,1,0:T(8,128)S(1)} %get-tuple-element.188.refs_0_, ...), custom_call_target="tpu_custom_call" | custom-call | flops 3080000000 | bytes 1 | tf_op jit(solution)/shard_map/piece_grad/pallas_call | solution.py:365
  185.5 3.3 %collective-permute-start.34 = (f32[16,64,128]{2,1,0:T(8,128)S(1)}, f32[16,64,128]{2,1,0:T(8,128)S(1)}, u32[]{:S(2)}, u32[]{:S(2)}) collective-permute-start(f32[16,64,128]{2,1,0:T(8,128)S(1)} %get-tuple-element.194.own_ref), channel_id=1, source_target_pairs={{0,1},{1,0},{2,3},{3,2},{4,5},{5,4},{6,7},{7,6},{8,9},{9,8},{10,11... | collective-permute-start | bytes 1572872 | tf_op jit(solution)/shard_map/ppermute | solution.py:103
  190.9 6.3 %encoder_part.1 = bf16[2048,2048]{1,0:T(8,128)(2,1)} custom-call(bf16[16,64,128]{2,1,0:T(8,128)(2,1)S(1)} %get-tuple-element.193.pre_ref, f32[16,64,128]{2,1,0:T(8,128)S(1)} %get-tuple-element.194.own_ref, f32[16,64,128]{2,1,0:T(8,128)S(1)} %collective-permute-done.34.theirs_ref, bf16[16,64,2048]{2,1,0:T(8,128)(2,1)S(1)} %act_slots.1.act_ref), custom_call_target="tpu_custom_call" | custom-call | flops 7150000128 | bytes 1 | tf_op jit(solution)/shard_map/encoder_part/pallas_call | solution.py:476
  (136 shorter events, 61.4 us)
Async XLA Ops:
  2.2 12.5 %collective-permute-start.2 = (bf16[272,128]{1,0:T(8,128)(2,1)S(1)}, bf16[272,128]{1,0:T(8,128)(2,1)S(1)}, u32[]{:S(2)}, u32[]{:S(2)}) collective-permute-start(bf16[272,128]{1,0:T(8,128)(2,1)S(1)} %fusion.21.refs_0_), channel_id=1, source_target_pairs={{0,6},{2,4},{4,2},{6,0},{1,7},{3,5},{5,3},{7,1},{8,14},{10,12},{12... | collective-permute-start | bytes 208904 | tf_op jit(solution)/shard_map/ppermute | solution.py:103
  6.4 15.3 %collective-permute-start.1 = (bf16[272,128]{1,0:T(8,128)(2,1)S(1)}, bf16[272,128]{1,0:T(8,128)(2,1)S(1)}, u32[]{:S(2)}, u32[]{:S(2)}) collective-permute-start(bf16[272,128]{1,0:T(8,128)(2,1)S(1)} %fusion.21.refs_0_), channel_id=1, source_target_pairs={{0,4},{2,6},{4,0},{6,2},{1,5},{3,7},{5,1},{7,3},{8,12},{10,14},{12... | collective-permute-start | bytes 208904 | tf_op jit(solution)/shard_map/ppermute | solution.py:103
  7.7 17.1 %collective-permute-start.5 = (bf16[128,2048]{1,0:T(8,128)(2,1)S(1)}, bf16[128,2048]{1,0:T(8,128)(2,1)S(1)}, u32[]{:S(2)}, u32[]{:S(2)}) collective-permute-start(bf16[128,2048]{1,0:T(8,128)(2,1)S(1)} %get-tuple-element.174.refs_0_), channel_id=1, source_target_pairs={{2,0},{4,2},{6,4},{3,1},{5,3},{7,5},{10,8},{12,10},{14,12},{11,9},... | collective-permute-start | bytes 1572872 | tf_op jit(solution)/shard_map/ppermute | solution.py:112
  9.0 15.8 %collective-permute-start.3 = (bf16[128,2048]{1,0:T(8,128)(2,1)S(1)}, bf16[128,2048]{1,0:T(8,128)(2,1)S(1)}, u32[]{:S(2)}, u32[]{:S(2)}) collective-permute-start(bf16[128,2048]{1,0:T(8,128)(2,1)S(1)} %get-tuple-element.174.refs_0_), channel_id=1, source_target_pairs={{0,2},{2,4},{4,6},{1,3},{3,5},{5,7},{8,10},{10,12},{12,14},{9,11},... | collective-permute-start | bytes 1572872 | tf_op jit(solution)/shard_map/ppermute | solution.py:112
  26.8 37.2 %collective-permute-start.8 = (bf16[128,2048]{1,0:T(8,128)(2,1)S(1)}, bf16[128,2048]{1,0:T(8,128)(2,1)S(1)}, u32[]{:S(2)}, u32[]{:S(2)}) collective-permute-start(bf16[128,2048]{1,0:T(8,128)(2,1)S(1)} %collective-permute-done.3.refs_12_), channel_id=1, source_target_pairs={{2,4},{4,6},{3,5},{5,7},{10,12},{12,14},{11,13},{13,15},{18,20},{2... | collective-permute-start | bytes 1572872 | tf_op jit(solution)/shard_map/ppermute | solution.py:112
  27.5 19.2 %collective-permute-start.9 = (bf16[128,2048]{1,0:T(8,128)(2,1)S(1)}, bf16[128,2048]{1,0:T(8,128)(2,1)S(1)}, u32[]{:S(2)}, u32[]{:S(2)}) collective-permute-start(bf16[128,2048]{1,0:T(8,128)(2,1)S(1)} %collective-permute-done.4.refs_1_), channel_id=1, source_target_pairs={{0,2},{2,4},{4,6},{1,3},{3,5},{5,7},{8,10},{10,12},{12,14},{9,11},... | collective-permute-start | bytes 1572872 | tf_op jit(solution)/shard_map/ppermute | solution.py:112
  33.4 32.0 %collective-permute-start.11 = (bf16[128,2048]{1,0:T(8,128)(2,1)S(1)}, bf16[128,2048]{1,0:T(8,128)(2,1)S(1)}, u32[]{:S(2)}, u32[]{:S(2)}) collective-permute-start(bf16[128,2048]{1,0:T(8,128)(2,1)S(1)} %collective-permute-done.5.refs_2_), channel_id=1, source_target_pairs={{2,0},{4,2},{3,1},{5,3},{10,8},{12,10},{11,9},{13,11},{18,16},{20,... | collective-permute-start | bytes 1572872 | tf_op jit(solution)/shard_map/ppermute | solution.py:112
  34.7 25.7 %collective-permute-start.12 = (bf16[128,2048]{1,0:T(8,128)(2,1)S(1)}, bf16[128,2048]{1,0:T(8,128)(2,1)S(1)}, u32[]{:S(2)}, u32[]{:S(2)}) collective-permute-start(bf16[128,2048]{1,0:T(8,128)(2,1)S(1)} %collective-permute-done.4.refs_1_), channel_id=1, source_target_pairs={{2,0},{4,2},{6,4},{3,1},{5,3},{7,5},{10,8},{12,10},{14,12},{11,9},... | collective-permute-start | bytes 1572872 | tf_op jit(solution)/shard_map/ppermute | solution.py:112
  41.0 48.1 %collective-permute-start.7 = (bf16[1024,512]{1,0:T(8,128)(2,1)S(1)}, bf16[1024,512]{1,0:T(8,128)(2,1)S(1)}, u32[]{:S(2)}, u32[]{:S(2)}) collective-permute-start(bf16[1024,512]{1,0:T(8,128)(2,1)S(1)} %fusion.8), channel_id=1, source_target_pairs={{0,8},{8,0},{16,24},{24,16},{1,9},{9,1},{17,25},{25,17},{2,10},{10... | collective-permute-start | bytes 3145736 | tf_op jit(solution)/shard_map/ppermute | solution.py:103
  46.8 18.6 %collective-permute-start.10 = (bf16[128,2048]{1,0:T(8,128)(2,1)S(1)}, bf16[128,2048]{1,0:T(8,128)(2,1)S(1)}, u32[]{:S(2)}, u32[]{:S(2)}) collective-permute-start(bf16[128,2048]{1,0:T(8,128)(2,1)S(1)} %collective-permute-done.9.refs_13_), channel_id=1, source_target_pairs={{2,4},{4,6},{3,5},{5,7},{10,12},{12,14},{11,13},{13,15},{18,20},{2... | collective-permute-start | bytes 1572872 | tf_op jit(solution)/shard_map/ppermute | solution.py:112
  60.4 14.2 %collective-permute-start.13 = (bf16[128,2048]{1,0:T(8,128)(2,1)S(1)}, bf16[128,2048]{1,0:T(8,128)(2,1)S(1)}, u32[]{:S(2)}, u32[]{:S(2)}) collective-permute-start(bf16[128,2048]{1,0:T(8,128)(2,1)S(1)} %collective-permute-done.12.refs_3_), channel_id=1, source_target_pairs={{2,0},{4,2},{3,1},{5,3},{10,8},{12,10},{11,9},{13,11},{18,16},{20,... | collective-permute-start | bytes 1572872 | tf_op jit(solution)/shard_map/ppermute | solution.py:112
  64.1 23.6 %collective-permute-start.15 = (bf16[1024,512]{1,0:T(8,128)(2,1)S(1)}, bf16[1024,512]{1,0:T(8,128)(2,1)S(1)}, u32[]{:S(2)}, u32[]{:S(2)}) collective-permute-start(bf16[1024,512]{1,0:T(8,128)(2,1)S(1)} %fusion.14), channel_id=1, source_target_pairs={{0,16},{8,24},{16,0},{24,8},{1,17},{9,25},{17,1},{25,9},{2,18},{10... | collective-permute-start | bytes 3145736 | tf_op jit(solution)/shard_map/ppermute | solution.py:103
  74.6 20.9 %collective-permute-start.18 = (bf16[128,2048]{1,0:T(8,128)(2,1)S(1)}, bf16[128,2048]{1,0:T(8,128)(2,1)S(1)}, u32[]{:S(2)}, u32[]{:S(2)}) collective-permute-start(bf16[128,2048]{1,0:T(8,128)(2,1)S(1)} %collective-permute-done.8.refs_8_), channel_id=1, source_target_pairs={{4,6},{5,7},{12,14},{13,15},{20,22},{21,23},{28,30},{29,31}} | collective-permute-start | bytes 1572872 | tf_op jit(solution)/shard_map/ppermute | solution.py:112
  75.3 20.3 %collective-permute-start.19 = (bf16[128,2048]{1,0:T(8,128)(2,1)S(1)}, bf16[128,2048]{1,0:T(8,128)(2,1)S(1)}, u32[]{:S(2)}, u32[]{:S(2)}) collective-permute-start(bf16[128,2048]{1,0:T(8,128)(2,1)S(1)} %collective-permute-done.11.refs_6_), channel_id=1, source_target_pairs={{2,0},{3,1},{10,8},{11,9},{18,16},{19,17},{26,24},{27,25}} | collective-permute-start | bytes 1572872 | tf_op jit(solution)/shard_map/ppermute | solution.py:112
  102.7 14.6 %collective-permute-start.22 = (bf16[256,512]{1,0:T(8,128)(2,1)S(1)}, bf16[256,512]{1,0:T(8,128)(2,1)S(1)}, u32[]{:S(2)}, u32[]{:S(2)}) collective-permute-start(bf16[256,512]{1,0:T(8,128)(2,1)S(1)} %get-tuple-element.130), channel_id=1, source_target_pairs={{0,6},{2,4},{4,2},{6,0},{1,7},{3,5},{5,3},{7,1},{8,14},{10,12},{12... | collective-permute-start | bytes 786440 | tf_op jit(solution)/shard_map/ppermute | solution.py:103
  117.5 15.7 %collective-permute-start.27 = (bf16[256,512]{1,0:T(8,128)(2,1)S(1)}, bf16[256,512]{1,0:T(8,128)(2,1)}, u32[]{:S(2)}, u32[]{:S(2)}) collective-permute-start(bf16[256,512]{1,0:T(8,128)(2,1)S(1)} %multiply_convert_fusion.refs_0_), channel_id=1, source_target_pairs={{0,6},{2,4},{4,2},{6,0},{1,7},{3,5},{5,3},{7,1},{8,14},{10,12},{12... | collective-permute-start | bytes 786440 | tf_op jit(solution)/shard_map/ppermute | solution.py:103
  119.7 30.8 %collective-permute-start.26 = (bf16[256,512]{1,0:T(8,128)(2,1)S(1)}, bf16[256,512]{1,0:T(8,128)(2,1)}, u32[]{:S(2)}, u32[]{:S(2)}) collective-permute-start(bf16[256,512]{1,0:T(8,128)(2,1)S(1)} %multiply_convert_fusion.refs_0_), channel_id=1, source_target_pairs={{0,4},{2,6},{4,0},{6,2},{1,5},{3,7},{5,1},{7,3},{8,12},{10,14},{12... | collective-permute-start | bytes 786440 | tf_op jit(solution)/shard_map/ppermute | solution.py:103
  130.7 19.9 %collective-permute-start.25 = (bf16[256,512]{1,0:T(8,128)(2,1)S(1)}, bf16[256,512]{1,0:T(8,128)(2,1)}, u32[]{:S(2)}, u32[]{:S(2)}) collective-permute-start(bf16[256,512]{1,0:T(8,128)(2,1)S(1)} %multiply_convert_fusion.refs_0_), channel_id=1, source_target_pairs={{0,2},{2,0},{4,6},{6,4},{1,3},{3,1},{5,7},{7,5},{8,10},{10,8},{12,... | collective-permute-start | bytes 786440 | tf_op jit(solution)/shard_map/ppermute | solution.py:103
  130.7 19.9 %collective-permute-start.24 = (bf16[256,512]{1,0:T(8,128)(2,1)S(1)}, bf16[256,512]{1,0:T(8,128)(2,1)S(1)}, u32[]{:S(2)}, u32[]{:S(2)}) collective-permute-start(bf16[256,512]{1,0:T(8,128)(2,1)S(1)} %multiply_convert_fusion.refs_0_), channel_id=1, source_target_pairs={{0,16},{8,24},{16,0},{24,8},{1,17},{9,25},{17,1},{25,9},{2,18},{10... | collective-permute-start | bytes 786440 | tf_op jit(solution)/shard_map/ppermute | solution.py:103
  131.9 18.6 %collective-permute-start.23 = (bf16[256,512]{1,0:T(8,128)(2,1)S(1)}, bf16[256,512]{1,0:T(8,128)(2,1)S(1)}, u32[]{:S(2)}, u32[]{:S(2)}) collective-permute-start(bf16[256,512]{1,0:T(8,128)(2,1)S(1)} %multiply_convert_fusion.refs_0_), channel_id=1, source_target_pairs={{0,8},{8,0},{16,24},{24,16},{1,9},{9,1},{17,25},{25,17},{2,10},{10... | collective-permute-start | bytes 786440 | tf_op jit(solution)/shard_map/ppermute | solution.py:103
  151.9 17.6 %collective-permute-start.29 = (bf16[768,512]{1,0:T(8,128)(2,1)S(1)}, bf16[768,512]{1,0:T(8,128)(2,1)S(1)}, u32[]{:S(2)}, u32[]{:S(2)}) collective-permute-start(bf16[768,512]{1,0:T(8,128)(2,1)S(1)} %join.3.refs_1_), channel_id=1, source_target_pairs={{0,16},{8,24},{16,0},{24,8},{1,17},{9,25},{17,1},{25,9},{2,18},{10... | collective-permute-start | bytes 2359304 | tf_op jit(solution)/shard_map/ppermute | solution.py:103
  153.2 17.2 %collective-permute-start.28 = (bf16[768,512]{1,0:T(8,128)(2,1)S(1)}, bf16[768,512]{1,0:T(8,128)(2,1)S(1)}, u32[]{:S(2)}, u32[]{:S(2)}) collective-permute-start(bf16[768,512]{1,0:T(8,128)(2,1)S(1)} %join.3.refs_1_), channel_id=1, source_target_pairs={{0,8},{8,0},{16,24},{24,16},{1,9},{9,1},{17,25},{25,17},{2,10},{10... | collective-permute-start | bytes 2359304 | tf_op jit(solution)/shard_map/ppermute | solution.py:103
  154.3 13.2 %collective-permute-start.31 = (bf16[128,2048]{1,0:T(8,128)(2,1)S(1)}, bf16[128,2048]{1,0:T(8,128)(2,1)S(1)}, u32[]{:S(2)}, u32[]{:S(2)}) collective-permute-start(bf16[128,2048]{1,0:T(8,128)(2,1)S(1)} %copy-done.18), channel_id=1, source_target_pairs={{2,0},{3,1},{10,8},{11,9},{18,16},{19,17},{26,24},{27,25}} | collective-permute-start | bytes 1572872 | tf_op jit(solution)/shard_map/ppermute | solution.py:112
  170.5 12.2 %collective-permute-start.33 = (bf16[1024,256]{1,0:T(8,128)(2,1)S(1)}, bf16[1024,256]{1,0:T(8,128)(2,1)S(1)}, u32[]{:S(2)}, u32[]{:S(2)}) collective-permute-start(bf16[1024,256]{1,0:T(8,128)(2,1)S(1)} %pad_maximum_fusion.2), channel_id=1, source_target_pairs={{0,16},{8,24},{16,0},{24,8},{1,17},{9,25},{17,1},{25,9},{2,18},{10... | collective-permute-start | bytes 1572872 | tf_op jit(solution)/shard_map/ppermute | solution.py:103
  (36 other events, 383.3 us)

commit v10 on v9

--- a/solution.py
+++ b/solution.py
@@ -525,26 +525,19 @@
     message = [own] + [flip(own, "latent", r) for r in range(1, lat_count)]
 
     own, inputs = lax.optimization_barrier((own, activations[0]))
-    ups = [[columns(inputs, dp_here)]]
-    downs = [[ups[0][0]]]
-    ups.append([flip(columns(inputs, 1 - dp_here), "dp", 1)])
-    downs.append([ups[1][0]])
-
-    def next_hop(part):
-        step = len(ups[part])
-        ups[part].append(hop(ups[part][-1], "latent", 1, step - 1))
-        downs[part].append(hop(downs[part][-1], "latent", -1, step - 1))
-
-    next_hop(0)
-    message = join(message, token)
-    message, ups, downs = lax.optimization_barrier((message, ups, downs))
+    acts = jnp.concatenate([columns(inputs, dp_here), flip(columns(inputs, 1 - dp_here), "dp", 1)])
+    message, acts = lax.optimization_barrier((join(message, token), acts))
     message = message.reshape((lat_count,) + own.shape)
+    up, down = [acts], [acts]
+
+    def next_hops():
+        step = len(up)
+        up.append(hop(up[-1], "latent", 1, step - 1))
+        down.append(hop(down[-1], "latent", -1, step - 1))
+
     message = jnp.stack([message, flip(message, "dp", 1)], axis=1)
     message = message.reshape(lat_count * dp_count, own.shape[0], block_size)
-    next_hop(1)
-    for part in range(2):
-        if lat_count > 2:
-            next_hop(part)
+    next_hops()
 
     codes = spread_codes(message, first, lat_rows)
     at = places((0, 2), dp_here * lay_count, 2, 0) + places((0, 1), dp_here * lay_count, 2, 1)
@@ -564,16 +557,22 @@
         return jnp.dot(spread, weights[:, n * width:(n + 1) * width], preferred_element_type=f32).astype(bf16)
 
     got = flip(rows_for(codes, send_weights, 0), "layer", 1), flip(rows_for(codes, send_weights, 1), "layer", 2)
-    keep_codes, ups, downs = lax.optimization_barrier((codes, ups, downs))
-    for step in range(3, lat_count):
-        next_hop(0)
+    keep_codes, up[1], down[1] = lax.optimization_barrier((codes, up[1], down[1]))
+    if lat_count > 2:
+        next_hops()
     kept = rows_for(keep_codes, keep_weights, 0), rows_for(keep_codes, keep_weights, 1)
 
     def add(one, two):
         return (one[:, side:].astype(f32) + two[:, side:].astype(f32)).astype(bf16)
 
     far = [flip(add(got[n], kept[n]), "layer", 2 - n) for n in range(2)]
-    far, goals, ups, downs = lax.optimization_barrier((far, goals, ups, downs))
+    far, goals, up[-1], down[-1] = lax.optimization_barrier((far, goals, up[-1], down[-1]))
+    while len(up) < lat_count - 1:
+        next_hops()
+    early = group * 11 // 16
+    ends = []
+    if len(up) < lat_count:
+        ends = [(up[-1][rows], down[-1][rows]) for rows in (slice(0, early), slice(early, group))]
 
     total, *sent = layer_sum((got[0], kept[0], far[0]), (got[1], kept[1], far[1]), lat_count)
     for r in range(1, lat_count):
@@ -582,28 +581,27 @@
     others = [flip(errors, "latent", r) for r in range(1, lat_count)]
     one_near, two_near = flip(errors, "layer", 1), flip(errors, "layer", 2)
     made = make_slots(message, first, lat_rows, capacity)
-    one_near, two_near, others, ups, downs, made = lax.optimization_barrier(
-        (one_near, two_near, others, ups, downs, made)
-    )
+    one_near, two_near, others, ends, made = lax.optimization_barrier((one_near, two_near, others, ends, made))
     hot, pre_slots, code_slots = made
     distant = join(others)
     one_far, two_far = flip(distant, "layer", 1), flip(distant, "layer", 2)
-    for step in range(3, lat_count):
-        next_hop(1)
+    ends = [(hop(one, "latent", 1, len(up) - 1), hop(two, "latent", -1, len(up) - 1)) for one, two in ends]
 
     def grads_of(here, names, grad, dec):
         slots, grad = piece_grad(here, hot, decoder, weight_places(names), block_size, grad)
         return grad, decoder_part(slots, code_slots, jnp.stack(places(names, 0)), half, dec)
 
     grad, dec = grads_of([[(errors,), (distant,)]], (0,), None, None)
-    one_far, two_far, grad, dec, ups, downs = lax.optimization_barrier((one_far, two_far, grad, dec, ups, downs))
+    one_far, two_far, grad, dec, ends[:1] = lax.optimization_barrier((one_far, two_far, grad, dec, ends[:1]))
     three_a = flip(jnp.concatenate([two_near[:, :side], two_far[:, :side]]), "layer", 1)
     three_b = flip(jnp.concatenate([one_near[:, side:], one_far[:, side:]]), "layer", 2)
     grad, dec = grads_of([[(one_near,), (one_far,)], [(two_near,), (two_far,)]], (1, 2), grad, dec)
 
-    terms_of = [[[ups[0][0], ups[1][0]]]]
-    for k in range(1, lat_count):
-        terms_of.append([[downs[part][k] for part in range(2)], [ups[part][lat_count - k] for part in range(2)]])
+    ups, downs = [[part] for part in up], [[part] for part in down]
+    if ends:
+        ups.append([part[0] for part in ends])
+        downs.append([part[1] for part in ends])
+    terms_of = [[[acts]]] + [[downs[k], ups[lat_count - k]] for k in range(1, lat_count)]
     shards = [lax.rem(lat_here + k, lat_count) ^ lat_here for k in range(lat_count)]
     slotted = act_slots(terms_of, shards, hot, local_blocks)
     three_a, three_b, grad, dec, slotted = lax.optimization_barrier((three_a, three_b, grad, dec, slotted))

time: 198 us -> 173 us (0.87)
  waiting for transfers between devices: 77 us -> 49.2 us
  local copies, waits for them, and re-layouts: 4.3 us -> 11 us
  starting transfers between devices: 61.5 us -> 55.8 us
  Pallas kernels: 42 us -> 44.2 us
    ppermute x23, waiting for transfers between devices: 48.1 us -> 30.1 us  [flip(): return lax.ppermute(value, axis, [(i, i ^ bit) for i in range(count)])]
    ppermute x12 -> x8, waiting for transfers between devices: 29 us -> 19 us  [hop(): return lax.ppermute(value, axis, pairs)]
    ppermute x12 -> x8, starting transfers between devices: 20.7 us -> 12.5 us  [hop(): return lax.ppermute(value, axis, pairs)]
    slice x0 -> x4, local copies, waits for them, and re-layouts: none -> 5.62 us  [the longest x2 3.84 us: dense_plan(): down[-1][rows]]
    ppermute x23, starting transfers between devices: 40.7 us -> 43.3 us  [flip(): return lax.ppermute(value, axis, [(i, i ^ bit) for i in range(count)])]
  transfers between devices with their start and end apart: 35 -> 31, of which waited for: 14 -> 11; matrix products, arithmetic and copies ran while one was open for 6% -> 10% of each run, Pallas kernels for 16% -> 19%
where the time goes in v10:
time: 173 us; the launch traced here: 172 us
  starting transfers between devices  55.8 us (32%)
  waiting for transfers between devices  49.2 us (28%)
  Pallas kernels  44.2 us (26%)
  local copies, waits for them, and re-layouts  11 us (6%)
  matrix products  9.3 us (5%)
  other arithmetic  1.84 us (1%)
    ppermute x23, starting transfers between devices, flip(): return lax.ppermute(value, axis, [(i, i ^ bit) for i in range(count)])  43.3 us
    ppermute x23, waiting for transfers between devices, flip(): return lax.ppermute(value, axis, [(i, i ^ bit) for i in range(count)])  30.1 us
    ppermute x8, waiting for transfers between devices, hop(): return lax.ppermute(value, axis, pairs)  19 us
    ppermute x8, starting transfers between devices, hop(): return lax.ppermute(value, axis, pairs)  12.5 us
    pallas_call x3, Pallas kernels, piece_grad(): pl.pallas_call(functools.partial(piece_grad_kernel, [[len(row) for row in...  10.5 us
    pallas_call x3, Pallas kernels, gather_columns(): pl.pallas_call(gather_kernel, out_shape=[jax.ShapeDtypeStruct((rows, coun...  9.54 us
    dot_general x4, matrix products, rows_for(): jnp.dot(spread, weights[:, n * width:(n + 1) * width], preferred_element_...  9.3 us
    pallas_call x3, Pallas kernels, decoder_part(): pl.pallas_call(functools.partial(decoder_kernel, len(onto)), out_shape=ja...  7.27 us
  transfers between devices with their start and end apart: 31, of which 11 were waited for; matrix products, arithmetic and copies ran while one was open for 10% of the time, Pallas kernels for 19%

profile of v10, /device:TPU:1, one launch (start us, length us, event | category | flops | bytes accessed | tf_op | source)
XLA Modules:
  0.0 172.5 jit_solution(974319403146634899)
XLA Ops:
  2.2 4.2 %collective-permute-start.2 = (bf16[272,128]{1,0:T(8,128)(2,1)S(1)}, bf16[272,128]{1,0:T(8,128)(2,1)S(1)}, u32[]{:S(2)}, u32[]{:S(2)}) collective-permute-start(bf16[272,128]{1,0:T(8,128)(2,1)S(1)} %fusion.21.refs_0_), channel_id=1, source_target_pairs={{0,6},{2,4},{4,2},{6,0},{1,7},{3,5},{5,3},{7,1},{8,14},{10,12},{12... | collective-permute-start | bytes 208904 | tf_op jit(solution)/shard_map/ppermute | solution.py:103
  9.4 3.9 %gather_columns.3 = (bf16[2048,1024]{1,0:T(8,128)(2,1)S(1)}, f32[8,128]{1,0:T(8,128)S(1)}) custom-call(s32[4]{0:T(128)S(1)} %pad_add_fusion.1.scalar_ref, bf16[1,2048,4096]{2,1,0:T(8,128)(2,1)} %weight_ref.5), custom_call_target="tpu_custom_call" | custom-call | flops 3960000000 | bytes 1 | tf_op jit(solution)/shard_map/gather_columns/pallas_call | solution.py:136
  17.0 4.1 %collective-permute-start.6 = (bf16[256,2048]{1,0:T(8,128)(2,1)S(1)}, bf16[256,2048]{1,0:T(8,128)(2,1)S(1)}, u32[]{:S(2)}, u32[]{:S(2)}) collective-permute-start(bf16[256,2048]{1,0:T(8,128)(2,1)S(1)} %pad_maximum_fusion.refs_0_), channel_id=1, source_target_pairs={{0,2},{2,4},{4,6},{1,3},{3,5},{5,7},{8,10},{10,12},{12,14},{9,11},... | collective-permute-start | bytes 3145736 | tf_op jit(solution)/shard_map/ppermute | solution.py:112
  21.2 2.6 %spread_codes.1 = bf16[1024,2048]{1,0:T(8,128)(2,1)S(1)} custom-call(s32[1]{0:T(128)} %bitcast.5.scalar_ref, bf16[8,272,128]{2,1,0:T(8,128)(2,1)S(1)} %bitcast.43), custom_call_target="tpu_custom_call" | custom-call | flops 2750000128 | bytes 1 | tf_op jit(solution)/shard_map/spread_codes/pallas_call | solution.py:185
  23.8 2.3 %fusion.8 = bf16[1024,512]{1,0:T(8,128)(2,1)S(1)} fusion(bf16[1024,2048]{1,0:T(8,128)(2,1)S(1)} %spread_codes.1, bf16[2048,1024]{1,0:T(8,128)(2,1)S(1)} %copy-done.11), kind=kOutput, calls=%fused_computation.8 | convolution fusion | flops 2148007936 | bytes 7340032 | tf_op jit(solution)/shard_map/dot_general | solution.py:557
  31.2 4.4 %gather_columns.4 = (bf16[2048,1024]{1,0:T(8,128)(2,1)S(1)}, f32[8,128]{1,0:T(8,128)}) custom-call(s32[4]{0:T(128)S(1)} %pad_add_fusion.scalar_ref, bf16[1,2048,4096]{2,1,0:T(8,128)(2,1)} %weight_ref.5), custom_call_target="tpu_custom_call" | custom-call | flops 3960000000 | bytes 1 | tf_op jit(solution)/shard_map/gather_columns/pallas_call | solution.py:136
  35.6 6.2 %collective-permute-done.7.refs_1_ = bf16[256,2048]{1,0:T(8,128)(2,1)S(1)} collective-permute-done((bf16[256,2048]{1,0:T(8,128)(2,1)S(1)}, bf16[256,2048]{1,0:T(8,128)(2,1)S(1)}, u32[]{:S(2)}, u32[]{:S(2)}) %collective-permute-start.7) | collective-permute-done | bytes 1048608 | tf_op jit(solution)/shard_map/ppermute | solution.py:112
  49.6 3.7 %collective-permute-done.9.got_b = bf16[1024,512]{1,0:T(8,128)(2,1)S(1)} collective-permute-done((bf16[1024,512]{1,0:T(8,128)(2,1)S(1)}, bf16[1024,512]{1,0:T(8,128)(2,1)S(1)}, u32[]{:S(2)}, u32[]{:S(2)}) %collective-permute-start.9) | collective-permute-done | bytes 1048608 | tf_op jit(solution)/shard_map/ppermute | solution.py:103
  56.5 2.9 %collective-permute-start.11 = (bf16[128,512]{1,0:T(8,128)(2,1)S(1)}, bf16[128,512]{1,0:T(8,128)(2,1)S(1)}, u32[]{:S(2)}, u32[]{:S(2)}) collective-permute-start(bf16[128,512]{1,0:T(8,128)(2,1)S(1)} %get-tuple-element.115), channel_id=1, source_target_pairs={{0,1},{1,0},{2,3},{3,2},{4,5},{5,4},{6,7},{7,6},{8,9},{9,8},{10,11... | collective-permute-start | bytes 393224 | tf_op jit(solution)/shard_map/ppermute | solution.py:103
  60.4 4.4 %collective-permute-done.10.far_b = bf16[1024,256]{1,0:T(8,128)(2,1)S(1)} collective-permute-done((bf16[1024,256]{1,0:T(8,128)(2,1)S(1)}, bf16[1024,256]{1,0:T(8,128)(2,1)S(1)}, u32[]{:S(2)}, u32[]{:S(2)}) %collective-permute-start.10) | collective-permute-done | bytes 524320 | tf_op jit(solution)/shard_map/ppermute | solution.py:103
  64.8 6.7 %collective-permute-done.13.refs_4_ = bf16[256,2048]{1,0:T(8,128)(2,1)} collective-permute-done((bf16[256,2048]{1,0:T(8,128)(2,1)S(1)}, bf16[256,2048]{1,0:T(8,128)(2,1)}, u32[]{:S(2)}, u32[]{:S(2)}) %collective-permute-start.13) | collective-permute-done | bytes 1048608 | tf_op jit(solution)/shard_map/ppermute | solution.py:112
  73.2 2.4 %collective-permute-start.16 = (bf16[256,512]{1,0:T(8,128)(2,1)S(1)}, bf16[256,512]{1,0:T(8,128)(2,1)S(1)}, u32[]{:S(2)}, u32[]{:S(2)}) collective-permute-start(bf16[256,512]{1,0:T(8,128)(2,1)S(1)} %get-tuple-element.76), channel_id=1, source_target_pairs={{0,6},{2,4},{4,2},{6,0},{1,7},{3,5},{5,3},{7,1},{8,14},{10,12},{12... | collective-permute-start | bytes 786440 | tf_op jit(solution)/shard_map/ppermute | solution.py:103
  75.6 3.3 %collective-permute-done.14 = bf16[256,512]{1,0:T(8,128)(2,1)S(1)} collective-permute-done((bf16[256,512]{1,0:T(8,128)(2,1)S(1)}, bf16[256,512]{1,0:T(8,128)(2,1)S(1)}, u32[]{:S(2)}, u32[]{:S(2)}) %collective-permute-start.14) | collective-permute-done | bytes 262176 | tf_op jit(solution)/shard_map/ppermute | solution.py:103
  78.8 13.0 %collective-permute-done.15 = bf16[256,512]{1,0:T(8,128)(2,1)S(1)} collective-permute-done((bf16[256,512]{1,0:T(8,128)(2,1)S(1)}, bf16[256,512]{1,0:T(8,128)(2,1)S(1)}, u32[]{:S(2)}, u32[]{:S(2)}) %collective-permute-start.15) | collective-permute-done | bytes 262176 | tf_op jit(solution)/shard_map/ppermute | solution.py:103
  92.1 9.9 %collective-permute-start.20 = (bf16[256,512]{1,0:T(8,128)(2,1)S(1)}, bf16[256,512]{1,0:T(8,128)(2,1)S(1)}, u32[]{:S(2)}, u32[]{:S(2)}) collective-permute-start(bf16[256,512]{1,0:T(8,128)(2,1)S(1)} %multiply_convert_fusion.refs_0_), channel_id=1, source_target_pairs={{0,4},{2,6},{4,0},{6,2},{1,5},{3,7},{5,1},{7,3},{8,12},{10,14},{12... | collective-permute-start | bytes 786440 | tf_op jit(solution)/shard_map/ppermute | solution.py:103
  112.1 4.7 %collective-permute-done.20.refs_1_ = bf16[256,512]{1,0:T(8,128)(2,1)S(1)} collective-permute-done((bf16[256,512]{1,0:T(8,128)(2,1)S(1)}, bf16[256,512]{1,0:T(8,128)(2,1)S(1)}, u32[]{:S(2)}, u32[]{:S(2)}) %collective-permute-start.20) | collective-permute-done | bytes 262176 | tf_op jit(solution)/shard_map/ppermute | solution.py:103
  125.1 2.9 %piece_grad.3 = (bf16[1,16,64,512]{3,2,1,0:T(8,128)(2,1)S(1)}, f32[16,64,128]{2,1,0:T(8,128)S(1)}) custom-call(s32[1]{0:T(128)} %bitcast.21.scalar_ref, bf16[4,256,256]{2,1,0:T(8,128)(2,1)S(1)} %get-tuple-element.84.hot_ref, bf16[1,2048,4096]{2,1,0:T(8,128)(2,1)} %weight_ref.5, bf16[256,512]{1,0:T(8,128)(2,1)S(1)} %multiply_convert_fusion.refs_0_, ...), custom_call_target="tpu_custom_call" | custom-call | flops 3080000000 | bytes 1 | tf_op jit(solution)/shard_map/piece_grad/pallas_call | solution.py:365
  131.6 5.2 %collective-permute-done.25.refs_6_ = bf16[176,2048]{1,0:T(8,128)(2,1)} collective-permute-done((bf16[176,2048]{1,0:T(8,128)(2,1)}, bf16[176,2048]{1,0:T(8,128)(2,1)}, u32[]{:S(2)}, u32[]{:S(2)}) %collective-permute-start.25) | collective-permute-done | bytes 720928 | tf_op jit(solution)/shard_map/ppermute | solution.py:112
  137.6 4.8 %piece_grad.4 = (bf16[2,16,64,512]{3,2,1,0:T(8,128)(2,1)S(1)}, f32[16,64,128]{2,1,0:T(8,128)S(1)}) custom-call(s32[2]{0:T(128)S(1)} %pad_add_fusion.3.scalar_ref, bf16[4,256,256]{2,1,0:T(8,128)(2,1)S(1)} %get-tuple-element.84.hot_ref, bf16[1,2048,4096]{2,1,0:T(8,128)(2,1)} %weight_ref.5, f32[16,64,128]{2,1,0:T(8,128)S(1)} %get-tuple-element.96.refs_0_, ...), custom_call_target="tpu_custom_call" | custom-call | flops 5280000000 | bytes 1 | tf_op jit(solution)/shard_map/piece_grad/pallas_call | solution.py:365
  142.5 3.3 %decoder_part.4.refs_0_ = bf16[2048,2048]{1,0:T(8,128)(2,1)} custom-call(s32[2]{0:T(128)S(1)} %pad_add_fusion.4.scalar_ref, bf16[16,128,64]{2,1,0:T(8,128)(2,1)S(1)} %get-tuple-element.83.code_ref, bf16[2,16,64,512]{3,2,1,0:T(8,128)(2,1)S(1)} %get-tuple-element.98.slots_ref, bf16[2048,2048]{1,0:T(8,128)(2,1)} %decoder_part.3.refs_0_), custom_call_target="tpu_custom_call", output_to_operand_aliasing={{}: (3, {})} | custom-call | flops 3630000128 | bytes 1 | tf_op jit(solution)/shard_map/decoder_part/pallas_call | solution.py:400
  145.8 4.6 %act_slots.1.act_ref = bf16[16,64,2048]{2,1,0:T(8,128)(2,1)S(1)} custom-call(s32[4]{0:T(128)S(1)} %pad_add_fusion.5.scalar_ref, bf16[4,256,256]{2,1,0:T(8,128)(2,1)S(1)} %get-tuple-element.84.hot_ref, bf16[256,2048]{1,0:T(8,128)(2,1)S(1)} %copy-done.3, bf16[256,2048]{1,0:T(8,128)(2,1)S(1)} %copy-done.14, bf16[176,2048]{1,0:T(8,128)(2,1)} %collective-permute-done.24.refs_2_, ...), custom_call_target="tpu_custom_call" | custom-call | flops 3630000128 | bytes 1 | tf_op jit(solution)/shard_map/act_slots/pallas_call | solution.py:440
  150.4 2.8 %piece_grad.5 = (bf16[1,16,64,512]{3,2,1,0:T(8,128)(2,1)S(1)}, f32[16,64,128]{2,1,0:T(8,128)S(1)}) custom-call(s32[1]{0:T(128)} %bitcast.23.scalar_ref, bf16[4,256,256]{2,1,0:T(8,128)(2,1)S(1)} %get-tuple-element.84.hot_ref, bf16[1,2048,4096]{2,1,0:T(8,128)(2,1)} %weight_ref.5, f32[16,64,128]{2,1,0:T(8,128)S(1)} %get-tuple-element.104.refs_0_, ...), custom_call_target="tpu_custom_call" | custom-call | flops 3080000000 | bytes 1 | tf_op jit(solution)/shard_map/piece_grad/pallas_call | solution.py:365
  153.2 11.0 %collective-permute-start.30 = (f32[16,64,128]{2,1,0:T(8,128)S(1)}, f32[16,64,128]{2,1,0:T(8,128)S(1)}, u32[]{:S(2)}, u32[]{:S(2)}) collective-permute-start(f32[16,64,128]{2,1,0:T(8,128)S(1)} %get-tuple-element.110.own_ref), channel_id=1, source_target_pairs={{0,1},{1,0},{2,3},{3,2},{4,5},{5,4},{6,7},{7,6},{8,9},{9,8},{10,11... | collective-permute-start | bytes 1572872 | tf_op jit(solution)/shard_map/ppermute | solution.py:103
  166.2 6.3 %encoder_part.1 = bf16[2048,2048]{1,0:T(8,128)(2,1)} custom-call(bf16[16,64,128]{2,1,0:T(8,128)(2,1)S(1)} %copy-done.18, f32[16,64,128]{2,1,0:T(8,128)S(1)} %get-tuple-element.110.own_ref, f32[16,64,128]{2,1,0:T(8,128)S(1)} %collective-permute-done.30.theirs_ref, bf16[16,64,2048]{2,1,0:T(8,128)(2,1)S(1)} %act_slots.1.act_ref), custom_call_target="tpu_custom_call" | custom-call | flops 7150000128 | bytes 1 | tf_op jit(solution)/shard_map/encoder_part/pallas_call | solution.py:476
  (127 shorter events, 51.8 us)
Async XLA Ops:
  2.2 13.1 %collective-permute-start.2 = (bf16[272,128]{1,0:T(8,128)(2,1)S(1)}, bf16[272,128]{1,0:T(8,128)(2,1)S(1)}, u32[]{:S(2)}, u32[]{:S(2)}) collective-permute-start(bf16[272,128]{1,0:T(8,128)(2,1)S(1)} %fusion.21.refs_0_), channel_id=1, source_target_pairs={{0,6},{2,4},{4,2},{6,0},{1,7},{3,5},{5,3},{7,1},{8,14},{10,12},{12... | collective-permute-start | bytes 208904 | tf_op jit(solution)/shard_map/ppermute | solution.py:103
  15.7 26.1 %collective-permute-start.7 = (bf16[256,2048]{1,0:T(8,128)(2,1)S(1)}, bf16[256,2048]{1,0:T(8,128)(2,1)S(1)}, u32[]{:S(2)}, u32[]{:S(2)}) collective-permute-start(bf16[256,2048]{1,0:T(8,128)(2,1)S(1)} %pad_maximum_fusion.refs_0_), channel_id=1, source_target_pairs={{2,0},{4,2},{6,4},{3,1},{5,3},{7,5},{10,8},{12,10},{14,12},{11,9},... | collective-permute-start | bytes 3145736 | tf_op jit(solution)/shard_map/ppermute | solution.py:112
  17.0 25.7 %collective-permute-start.6 = (bf16[256,2048]{1,0:T(8,128)(2,1)S(1)}, bf16[256,2048]{1,0:T(8,128)(2,1)S(1)}, u32[]{:S(2)}, u32[]{:S(2)}) collective-permute-start(bf16[256,2048]{1,0:T(8,128)(2,1)S(1)} %pad_maximum_fusion.refs_0_), channel_id=1, source_target_pairs={{0,2},{2,4},{4,6},{1,3},{3,5},{5,7},{8,10},{10,12},{12,14},{9,11},... | collective-permute-start | bytes 3145736 | tf_op jit(solution)/shard_map/ppermute | solution.py:112
  26.1 27.5 %collective-permute-start.5 = (bf16[1024,512]{1,0:T(8,128)(2,1)S(1)}, bf16[1024,512]{1,0:T(8,128)(2,1)S(1)}, u32[]{:S(2)}, u32[]{:S(2)}) collective-permute-start(bf16[1024,512]{1,0:T(8,128)(2,1)S(1)} %fusion.8), channel_id=1, source_target_pairs={{0,8},{8,0},{16,24},{24,16},{1,9},{9,1},{17,25},{25,17},{2,10},{10... | collective-permute-start | bytes 3145736 | tf_op jit(solution)/shard_map/ppermute | solution.py:103
  29.9 23.4 %collective-permute-start.9 = (bf16[1024,512]{1,0:T(8,128)(2,1)S(1)}, bf16[1024,512]{1,0:T(8,128)(2,1)S(1)}, u32[]{:S(2)}, u32[]{:S(2)}) collective-permute-start(bf16[1024,512]{1,0:T(8,128)(2,1)S(1)} %fusion.14), channel_id=1, source_target_pairs={{0,16},{8,24},{16,0},{24,8},{1,17},{9,25},{17,1},{25,9},{2,18},{10... | collective-permute-start | bytes 3145736 | tf_op jit(solution)/shard_map/ppermute | solution.py:103
  42.7 22.1 %collective-permute-start.12 = (bf16[256,2048]{1,0:T(8,128)(2,1)S(1)}, bf16[256,2048]{1,0:T(8,128)(2,1)S(1)}, u32[]{:S(2)}, u32[]{:S(2)}) collective-permute-start(bf16[256,2048]{1,0:T(8,128)(2,1)S(1)} %collective-permute-done.6.refs_8_), channel_id=1, source_target_pairs={{2,4},{4,6},{3,5},{5,7},{10,12},{12,14},{11,13},{13,15},{18,20},{2... | collective-permute-start | bytes 3145736 | tf_op jit(solution)/shard_map/ppermute | solution.py:112
  43.4 28.1 %collective-permute-start.13 = (bf16[256,2048]{1,0:T(8,128)(2,1)S(1)}, bf16[256,2048]{1,0:T(8,128)(2,1)}, u32[]{:S(2)}, u32[]{:S(2)}) collective-permute-start(bf16[256,2048]{1,0:T(8,128)(2,1)S(1)} %collective-permute-done.7.refs_1_), channel_id=1, source_target_pairs={{2,0},{4,2},{3,1},{5,3},{10,8},{12,10},{11,9},{13,11},{18,16},{20,... | collective-permute-start | bytes 3145736 | tf_op jit(solution)/shard_map/ppermute | solution.py:112
  53.4 11.3 %collective-permute-start.10 = (bf16[1024,256]{1,0:T(8,128)(2,1)S(1)}, bf16[1024,256]{1,0:T(8,128)(2,1)S(1)}, u32[]{:S(2)}, u32[]{:S(2)}) collective-permute-start(bf16[1024,256]{1,0:T(8,128)(2,1)S(1)} %add_convert_fusion), channel_id=1, source_target_pairs={{0,8},{8,0},{16,24},{24,16},{1,9},{9,1},{17,25},{25,17},{2,10},{10... | collective-permute-start | bytes 1572872 | tf_op jit(solution)/shard_map/ppermute | solution.py:103
  53.8 11.1 %collective-permute-start.8 = (bf16[1024,256]{1,0:T(8,128)(2,1)S(1)}, bf16[1024,256]{1,0:T(8,128)(2,1)S(1)}, u32[]{:S(2)}, u32[]{:S(2)}) collective-permute-start(bf16[1024,256]{1,0:T(8,128)(2,1)S(1)} %add_convert_fusion.1), channel_id=1, source_target_pairs={{0,16},{8,24},{16,0},{24,8},{1,17},{9,25},{17,1},{25,9},{2,18},{10... | collective-permute-start | bytes 1572872 | tf_op jit(solution)/shard_map/ppermute | solution.py:103
  73.2 18.7 %collective-permute-start.15 = (bf16[256,512]{1,0:T(8,128)(2,1)S(1)}, bf16[256,512]{1,0:T(8,128)(2,1)S(1)}, u32[]{:S(2)}, u32[]{:S(2)}) collective-permute-start(bf16[256,512]{1,0:T(8,128)(2,1)S(1)} %get-tuple-element.75), channel_id=1, source_target_pairs={{0,4},{2,6},{4,0},{6,2},{1,5},{3,7},{5,1},{7,3},{8,12},{10,14},{12... | collective-permute-start | bytes 786440 | tf_op jit(solution)/shard_map/ppermute | solution.py:103
  73.2 18.7 %collective-permute-start.16 = (bf16[256,512]{1,0:T(8,128)(2,1)S(1)}, bf16[256,512]{1,0:T(8,128)(2,1)S(1)}, u32[]{:S(2)}, u32[]{:S(2)}) collective-permute-start(bf16[256,512]{1,0:T(8,128)(2,1)S(1)} %get-tuple-element.76), channel_id=1, source_target_pairs={{0,6},{2,4},{4,2},{6,0},{1,7},{3,5},{5,3},{7,1},{8,14},{10,12},{12... | collective-permute-start | bytes 786440 | tf_op jit(solution)/shard_map/ppermute | solution.py:103
  92.0 20.1 %collective-permute-start.21 = (bf16[256,512]{1,0:T(8,128)(2,1)S(1)}, bf16[256,512]{1,0:T(8,128)(2,1)S(1)}, u32[]{:S(2)}, u32[]{:S(2)}) collective-permute-start(bf16[256,512]{1,0:T(8,128)(2,1)S(1)} %multiply_convert_fusion.refs_0_), channel_id=1, source_target_pairs={{0,6},{2,4},{4,2},{6,0},{1,7},{3,5},{5,3},{7,1},{8,14},{10,12},{12... | collective-permute-start | bytes 786440 | tf_op jit(solution)/shard_map/ppermute | solution.py:103
  92.1 24.7 %collective-permute-start.20 = (bf16[256,512]{1,0:T(8,128)(2,1)S(1)}, bf16[256,512]{1,0:T(8,128)(2,1)S(1)}, u32[]{:S(2)}, u32[]{:S(2)}) collective-permute-start(bf16[256,512]{1,0:T(8,128)(2,1)S(1)} %multiply_convert_fusion.refs_0_), channel_id=1, source_target_pairs={{0,4},{2,6},{4,0},{6,2},{1,5},{3,7},{5,1},{7,3},{8,12},{10,14},{12... | collective-permute-start | bytes 786440 | tf_op jit(solution)/shard_map/ppermute | solution.py:103
  102.0 14.8 %collective-permute-start.19 = (bf16[256,512]{1,0:T(8,128)(2,1)S(1)}, bf16[256,512]{1,0:T(8,128)(2,1)}, u32[]{:S(2)}, u32[]{:S(2)}) collective-permute-start(bf16[256,512]{1,0:T(8,128)(2,1)S(1)} %multiply_convert_fusion.refs_0_), channel_id=1, source_target_pairs={{0,2},{2,0},{4,6},{6,4},{1,3},{3,1},{5,7},{7,5},{8,10},{10,8},{12,... | collective-permute-start | bytes 786440 | tf_op jit(solution)/shard_map/ppermute | solution.py:103
  102.0 14.8 %collective-permute-start.18 = (bf16[256,512]{1,0:T(8,128)(2,1)S(1)}, bf16[256,512]{1,0:T(8,128)(2,1)S(1)}, u32[]{:S(2)}, u32[]{:S(2)}) collective-permute-start(bf16[256,512]{1,0:T(8,128)(2,1)S(1)} %multiply_convert_fusion.refs_0_), channel_id=1, source_target_pairs={{0,16},{8,24},{16,0},{24,8},{1,17},{9,25},{17,1},{25,9},{2,18},{10... | collective-permute-start | bytes 786440 | tf_op jit(solution)/shard_map/ppermute | solution.py:103
  103.2 13.6 %collective-permute-start.17 = (bf16[256,512]{1,0:T(8,128)(2,1)S(1)}, bf16[256,512]{1,0:T(8,128)(2,1)S(1)}, u32[]{:S(2)}, u32[]{:S(2)}) collective-permute-start(bf16[256,512]{1,0:T(8,128)(2,1)S(1)} %multiply_convert_fusion.refs_0_), channel_id=1, source_target_pairs={{0,8},{8,0},{16,24},{24,16},{1,9},{9,1},{17,25},{25,17},{2,10},{10... | collective-permute-start | bytes 786440 | tf_op jit(solution)/shard_map/ppermute | solution.py:103
  118.9 17.9 %collective-permute-start.23 = (bf16[768,512]{1,0:T(8,128)(2,1)}, bf16[768,512]{1,0:T(8,128)(2,1)S(1)}, u32[]{:S(2)}, u32[]{:S(2)}) collective-permute-start(bf16[768,512]{1,0:T(8,128)(2,1)} %join.3.refs_1_), channel_id=1, source_target_pairs={{0,16},{8,24},{16,0},{24,8},{1,17},{9,25},{17,1},{25,9},{2,18},{10... | collective-permute-start | bytes 2359304 | tf_op jit(solution)/shard_map/ppermute | solution.py:103
  120.1 16.7 %collective-permute-start.22 = (bf16[768,512]{1,0:T(8,128)(2,1)}, bf16[768,512]{1,0:T(8,128)(2,1)S(1)}, u32[]{:S(2)}, u32[]{:S(2)}) collective-permute-start(bf16[768,512]{1,0:T(8,128)(2,1)} %join.3.refs_1_), channel_id=1, source_target_pairs={{0,8},{8,0},{16,24},{24,16},{1,9},{9,1},{17,25},{25,17},{2,10},{10... | collective-permute-start | bytes 2359304 | tf_op jit(solution)/shard_map/ppermute | solution.py:103
  123.0 13.9 %collective-permute-start.25 = (bf16[176,2048]{1,0:T(8,128)(2,1)}, bf16[176,2048]{1,0:T(8,128)(2,1)}, u32[]{:S(2)}, u32[]{:S(2)}) collective-permute-start(bf16[176,2048]{1,0:T(8,128)(2,1)} %slice.65), channel_id=1, source_target_pairs={{2,0},{3,1},{10,8},{11,9},{18,16},{19,17},{26,24},{27,25}} | collective-permute-start | bytes 2162696 | tf_op jit(solution)/shard_map/ppermute | solution.py:112
  124.4 21.3 %collective-permute-start.28 = (bf16[80,2048]{1,0:T(8,128)(2,1)}, bf16[80,2048]{1,0:T(8,128)(2,1)S(1)}, u32[]{:S(2)}, u32[]{:S(2)}) collective-permute-start(bf16[80,2048]{1,0:T(8,128)(2,1)} %slice.66), channel_id=1, source_target_pairs={{4,6},{5,7},{12,14},{13,15},{20,22},{21,23},{28,30},{29,31}} | collective-permute-start | bytes 983048 | tf_op jit(solution)/shard_map/ppermute | solution.py:112
  130.1 15.6 %collective-permute-start.29 = (bf16[80,2048]{1,0:T(8,128)(2,1)S(1)}, bf16[80,2048]{1,0:T(8,128)(2,1)S(1)}, u32[]{:S(2)}, u32[]{:S(2)}) collective-permute-start(bf16[80,2048]{1,0:T(8,128)(2,1)S(1)} %copy-done.19), channel_id=1, source_target_pairs={{2,0},{3,1},{10,8},{11,9},{18,16},{19,17},{26,24},{27,25}} | collective-permute-start | bytes 983048 | tf_op jit(solution)/shard_map/ppermute | solution.py:112
  137.0 13.4 %collective-permute-start.27 = (bf16[1024,256]{1,0:T(8,128)(2,1)S(1)}, bf16[1024,256]{1,0:T(8,128)(2,1)S(1)}, u32[]{:S(2)}, u32[]{:S(2)}) collective-permute-start(bf16[1024,256]{1,0:T(8,128)(2,1)S(1)} %pad_maximum_fusion.3), channel_id=1, source_target_pairs={{0,16},{8,24},{16,0},{24,8},{1,17},{9,25},{17,1},{25,9},{2,18},{10... | collective-permute-start | bytes 1572872 | tf_op jit(solution)/shard_map/ppermute | solution.py:103
  137.3 13.1 %collective-permute-start.26 = (bf16[1024,256]{1,0:T(8,128)(2,1)S(1)}, bf16[1024,256]{1,0:T(8,128)(2,1)S(1)}, u32[]{:S(2)}, u32[]{:S(2)}) collective-permute-start(bf16[1024,256]{1,0:T(8,128)(2,1)S(1)} %pad_maximum_fusion.2), channel_id=1, source_target_pairs={{0,8},{8,0},{16,24},{24,16},{1,9},{9,1},{17,25},{25,17},{2,10},{10... | collective-permute-start | bytes 1572872 | tf_op jit(solution)/shard_map/ppermute | solution.py:103
  153.2 13.0 %collective-permute-start.30 = (f32[16,64,128]{2,1,0:T(8,128)S(1)}, f32[16,64,128]{2,1,0:T(8,128)S(1)}, u32[]{:S(2)}, u32[]{:S(2)}) collective-permute-start(f32[16,64,128]{2,1,0:T(8,128)S(1)} %get-tuple-element.110.own_ref), channel_id=1, source_target_pairs={{0,1},{1,0},{2,3},{3,2},{4,5},{5,4},{6,7},{7,6},{8,9},{9,8},{10,11... | collective-permute-start | bytes 1572872 | tf_op jit(solution)/shard_map/ppermute | solution.py:103
  (29 other events, 214.5 us)

commit v11 on v10

--- a/solution.py
+++ b/solution.py
@@ -136,7 +136,7 @@
     return pl.pallas_call(
         gather_kernel,
         out_shape=[
-            jax.ShapeDtypeStruct((rows, count * width), source.dtype),
+            pltpu.HBM((rows, count * width), source.dtype),
             jax.ShapeDtypeStruct((8, 128), jnp.float32),
         ],
         grid_spec=pltpu.PrefetchScalarGridSpec(
@@ -566,10 +566,11 @@
         return (one[:, side:].astype(f32) + two[:, side:].astype(f32)).astype(bf16)
 
     far = [flip(add(got[n], kept[n]), "layer", 2 - n) for n in range(2)]
-    far, goals, up[-1], down[-1] = lax.optimization_barrier((far, goals, up[-1], down[-1]))
+    made = make_slots(message, first, lat_rows, capacity)
+    far, goals, up[-1], down[-1], made = lax.optimization_barrier((far, goals, up[-1], down[-1], made))
     while len(up) < lat_count - 1:
         next_hops()
-    early = group * 11 // 16
+    early = group * 3 // 8
     ends = []
     if len(up) < lat_count:
         ends = [(up[-1][rows], down[-1][rows]) for rows in (slice(0, early), slice(early, group))]
@@ -580,8 +581,8 @@
     errors = ((total - goals.astype(f32)) / tok_count).astype(bf16)
     others = [flip(errors, "latent", r) for r in range(1, lat_count)]
     one_near, two_near = flip(errors, "layer", 1), flip(errors, "layer", 2)
-    made = make_slots(message, first, lat_rows, capacity)
-    one_near, two_near, others, ends, made = lax.optimization_barrier((one_near, two_near, others, ends, made))
+    ends, others, two_near, one_near = lax.optimization_barrier((ends, others[::-1], two_near, one_near))
+    others = others[::-1]
     hot, pre_slots, code_slots = made
     distant = join(others)
     one_far, two_far = flip(distant, "layer", 1), flip(distant, "layer", 2)

time: 173 us -> 169 us (0.977)
  waiting for transfers between devices: 49.2 us -> 61 us
  starting transfers between devices: 55.8 us -> 44.2 us
  local copies, waits for them, and re-layouts: 11 us -> 5.21 us
  matrix products: 9.3 us -> 11.1 us
    ppermute x23, starting transfers between devices: 43.3 us -> 32.5 us  [flip(): return lax.ppermute(value, axis, [(i, i ^ bit) for i in range(count)])]
    ppermute x23, waiting for transfers between devices: 30.1 us -> 38 us  [flip(): return lax.ppermute(value, axis, [(i, i ^ bit) for i in range(count)])]
    ppermute x8, waiting for transfers between devices: 19 us -> 23 us  [hop(): return lax.ppermute(value, axis, pairs)]
    slice x2, local copies, waits for them, and re-layouts: 3.84 us -> 0.07 us  [dense_plan(): down[-1][rows]]
    unnamed x40 -> x22, local copies, waits for them, and re-layouts: 3.14 us -> 0.05 us
    pallas_call x3, Pallas kernels: 9.54 us -> 11.9 us  [gather_columns(): pl.pallas_call(gather_kernel, out_shape=[pltpu.HBM((rows, count * width),...]
    dot_general x4, matrix products: 9.3 us -> 11.1 us  [rows_for(): jnp.dot(spread, weights[:, n * width:(n + 1) * width], preferred_element_...]
  transfers between devices with their start and end apart: 31 -> 31, of which waited for: 11 -> 11; matrix products, arithmetic and copies ran while one was open for 10% -> 10% of each run, Pallas kernels for 19% -> 20%
where the time goes in v11:
time: 169 us
  waiting for transfers between devices  61 us (36%)
  Pallas kernels  44.3 us (26%)
  starting transfers between devices  44.2 us (26%)
  matrix products  11.1 us (7%)
  local copies, waits for them, and re-layouts  5.21 us (3%)
  other arithmetic  1.86 us (1%)
    ppermute x23, waiting for transfers between devices, flip(): return lax.ppermute(value, axis, [(i, i ^ bit) for i in range(count)])  38 us
    ppermute x23, starting transfers between devices, flip(): return lax.ppermute(value, axis, [(i, i ^ bit) for i in range(count)])  32.5 us
    ppermute x8, waiting for transfers between devices, hop(): return lax.ppermute(value, axis, pairs)  23 us
    pallas_call x3, Pallas kernels, gather_columns(): pl.pallas_call(gather_kernel, out_shape=[pltpu.HBM((rows, count * width),...  11.9 us
    ppermute x8, starting transfers between devices, hop(): return lax.ppermute(value, axis, pairs)  11.7 us
    dot_general x4, matrix products, rows_for(): jnp.dot(spread, weights[:, n * width:(n + 1) * width], preferred_element_...  11.1 us
    pallas_call x3, Pallas kernels, piece_grad(): pl.pallas_call(functools.partial(piece_grad_kernel, [[len(row) for row in...  10.4 us
    pallas_call x3, Pallas kernels, decoder_part(): pl.pallas_call(functools.partial(decoder_kernel, len(onto)), out_shape=ja...  7.29 us
  transfers between devices with their start and end apart: 31, of which 11 were waited for; matrix products, arithmetic and copies ran while one was open for 10% of the time, Pallas kernels for 20%

profile of v11, /device:TPU:1, one launch (start us, length us, event | category | flops | bytes accessed | tf_op | source)
XLA Modules:
  0.0 168.7 jit_solution(15349687079057565437)
XLA Ops:
  2.2 4.2 %collective-permute-start.2 = (bf16[272,128]{1,0:T(8,128)(2,1)S(1)}, bf16[272,128]{1,0:T(8,128)(2,1)S(1)}, u32[]{:S(2)}, u32[]{:S(2)}) collective-permute-start(bf16[272,128]{1,0:T(8,128)(2,1)S(1)} %fusion.21.refs_0_), channel_id=1, source_target_pairs={{0,6},{2,4},{4,2},{6,0},{1,7},{3,5},{5,3},{7,1},{8,14},{10,12},{12... | collective-permute-start | bytes 208904 | tf_op jit(solution)/shard_map/ppermute | solution.py:103
  9.4 5.3 %gather_columns.3 = (bf16[2048,1024]{1,0:T(8,128)(2,1)}, f32[8,128]{1,0:T(8,128)S(1)}) custom-call(s32[4]{0:T(128)S(1)} %pad_add_fusion.1.scalar_ref, bf16[1,2048,4096]{2,1,0:T(8,128)(2,1)} %weight_ref.5), custom_call_target="tpu_custom_call" | custom-call | flops 3960000000 | bytes 1 | tf_op jit(solution)/shard_map/gather_columns/pallas_call | solution.py:136
  16.4 4.1 %collective-permute-start.6 = (bf16[256,2048]{1,0:T(8,128)(2,1)S(1)}, bf16[256,2048]{1,0:T(8,128)(2,1)S(1)}, u32[]{:S(2)}, u32[]{:S(2)}) collective-permute-start(bf16[256,2048]{1,0:T(8,128)(2,1)S(1)} %pad_maximum_fusion.refs_0_), channel_id=1, source_target_pairs={{0,2},{2,4},{4,6},{1,3},{3,5},{5,7},{8,10},{10,12},{12,14},{9,11},... | collective-permute-start | bytes 3145736 | tf_op jit(solution)/shard_map/ppermute | solution.py:112
  20.6 2.6 %spread_codes.1 = bf16[1024,2048]{1,0:T(8,128)(2,1)S(1)} custom-call(s32[1]{0:T(128)} %bitcast.5.scalar_ref, bf16[8,272,128]{2,1,0:T(8,128)(2,1)S(1)} %bitcast.43), custom_call_target="tpu_custom_call" | custom-call | flops 2750000128 | bytes 1 | tf_op jit(solution)/shard_map/spread_codes/pallas_call | solution.py:185
  30.6 5.3 %gather_columns.4 = (bf16[2048,1024]{1,0:T(8,128)(2,1)}, f32[8,128]{1,0:T(8,128)}) custom-call(s32[4]{0:T(128)S(1)} %pad_add_fusion.scalar_ref, bf16[1,2048,4096]{2,1,0:T(8,128)(2,1)} %weight_ref.5), custom_call_target="tpu_custom_call" | custom-call | flops 3960000000 | bytes 1 | tf_op jit(solution)/shard_map/gather_columns/pallas_call | solution.py:136
  35.9 5.4 %collective-permute-done.7.refs_1_ = bf16[256,2048]{1,0:T(8,128)(2,1)S(1)} collective-permute-done((bf16[256,2048]{1,0:T(8,128)(2,1)S(1)}, bf16[256,2048]{1,0:T(8,128)(2,1)S(1)}, u32[]{:S(2)}, u32[]{:S(2)}) %collective-permute-start.7) | collective-permute-done | bytes 1048608 | tf_op jit(solution)/shard_map/ppermute | solution.py:112
  44.3 4.1 %fusion.17.kept_b = bf16[1024,512]{1,0:T(8,128)(2,1)S(1)} fusion(bf16[1024,2048]{1,0:T(8,128)(2,1)S(1)} %spread_codes.1, bf16[2048,1024]{1,0:T(8,128)(2,1)} %get-tuple-element.66), kind=kOutput, calls=%fused_computation.11 | convolution fusion | flops 2148007936 | bytes 7340032 | tf_op jit(solution)/shard_map/dot_general | solution.py:557
  56.9 2.9 %collective-permute-start.11 = (bf16[128,512]{1,0:T(8,128)(2,1)S(1)}, bf16[128,512]{1,0:T(8,128)(2,1)S(1)}, u32[]{:S(2)}, u32[]{:S(2)}) collective-permute-start(bf16[128,512]{1,0:T(8,128)(2,1)S(1)} %get-tuple-element.115), channel_id=1, source_target_pairs={{0,1},{1,0},{2,3},{3,2},{4,5},{5,4},{6,7},{7,6},{8,9},{9,8},{10,11... | collective-permute-start | bytes 393224 | tf_op jit(solution)/shard_map/ppermute | solution.py:103
  60.8 3.3 %collective-permute-done.10.far_b = bf16[1024,256]{1,0:T(8,128)(2,1)S(1)} collective-permute-done((bf16[1024,256]{1,0:T(8,128)(2,1)S(1)}, bf16[1024,256]{1,0:T(8,128)(2,1)S(1)}, u32[]{:S(2)}, u32[]{:S(2)}) %collective-permute-start.10) | collective-permute-done | bytes 524320 | tf_op jit(solution)/shard_map/ppermute | solution.py:103
  64.1 6.7 %collective-permute-done.13.refs_4_ = bf16[256,2048]{1,0:T(8,128)(2,1)S(1)} collective-permute-done((bf16[256,2048]{1,0:T(8,128)(2,1)S(1)}, bf16[256,2048]{1,0:T(8,128)(2,1)S(1)}, u32[]{:S(2)}, u32[]{:S(2)}) %collective-permute-start.13) | collective-permute-done | bytes 1048608 | tf_op jit(solution)/shard_map/ppermute | solution.py:112
  72.5 2.4 %collective-permute-start.16 = (bf16[256,512]{1,0:T(8,128)(2,1)S(1)}, bf16[256,512]{1,0:T(8,128)(2,1)S(1)}, u32[]{:S(2)}, u32[]{:S(2)}) collective-permute-start(bf16[256,512]{1,0:T(8,128)(2,1)S(1)} %get-tuple-element.83), channel_id=1, source_target_pairs={{0,6},{2,4},{4,2},{6,0},{1,7},{3,5},{5,3},{7,1},{8,14},{10,12},{12... | collective-permute-start | bytes 786440 | tf_op jit(solution)/shard_map/ppermute | solution.py:103
  74.9 3.6 %collective-permute-done.14 = bf16[256,512]{1,0:T(8,128)(2,1)S(1)} collective-permute-done((bf16[256,512]{1,0:T(8,128)(2,1)S(1)}, bf16[256,512]{1,0:T(8,128)(2,1)S(1)}, u32[]{:S(2)}, u32[]{:S(2)}) %collective-permute-start.14) | collective-permute-done | bytes 262176 | tf_op jit(solution)/shard_map/ppermute | solution.py:103
  78.5 12.6 %collective-permute-done.15 = bf16[256,512]{1,0:T(8,128)(2,1)S(1)} collective-permute-done((bf16[256,512]{1,0:T(8,128)(2,1)S(1)}, bf16[256,512]{1,0:T(8,128)(2,1)S(1)}, u32[]{:S(2)}, u32[]{:S(2)}) %collective-permute-start.15) | collective-permute-done | bytes 262176 | tf_op jit(solution)/shard_map/ppermute | solution.py:103
  93.8 5.9 %collective-permute-start.19 = (bf16[256,512]{1,0:T(8,128)(2,1)S(1)}, bf16[256,512]{1,0:T(8,128)(2,1)}, u32[]{:S(2)}, u32[]{:S(2)}) collective-permute-start(bf16[256,512]{1,0:T(8,128)(2,1)S(1)} %multiply_convert_fusion.refs_0_), channel_id=1, source_target_pairs={{0,2},{2,0},{4,6},{6,4},{1,3},{3,1},{5,7},{7,5},{8,10},{10,8},{12,... | collective-permute-start | bytes 786440 | tf_op jit(solution)/shard_map/ppermute | solution.py:103
  102.0 2.9 %collective-permute-done.19.refs_0_ = bf16[256,512]{1,0:T(8,128)(2,1)} collective-permute-done((bf16[256,512]{1,0:T(8,128)(2,1)S(1)}, bf16[256,512]{1,0:T(8,128)(2,1)}, u32[]{:S(2)}, u32[]{:S(2)}) %collective-permute-start.19) | collective-permute-done | bytes 262176 | tf_op jit(solution)/shard_map/ppermute | solution.py:103
  105.0 13.5 %collective-permute-done.18.refs_1_ = bf16[256,512]{1,0:T(8,128)(2,1)} collective-permute-done((bf16[256,512]{1,0:T(8,128)(2,1)S(1)}, bf16[256,512]{1,0:T(8,128)(2,1)}, u32[]{:S(2)}, u32[]{:S(2)}) %collective-permute-start.18) | collective-permute-done | bytes 262176 | tf_op jit(solution)/shard_map/ppermute | solution.py:103
  125.0 2.7 %piece_grad.3 = (bf16[1,16,64,512]{3,2,1,0:T(8,128)(2,1)S(1)}, f32[16,64,128]{2,1,0:T(8,128)S(1)}) custom-call(s32[1]{0:T(128)} %bitcast.21.scalar_ref, bf16[4,256,256]{2,1,0:T(8,128)(2,1)S(1)} %get-tuple-element.75.hot_ref, bf16[1,2048,4096]{2,1,0:T(8,128)(2,1)} %weight_ref.5, bf16[256,512]{1,0:T(8,128)(2,1)S(1)} %multiply_convert_fusion.refs_0_, ...), custom_call_target="tpu_custom_call" | custom-call | flops 3080000000 | bytes 1 | tf_op jit(solution)/shard_map/piece_grad/pallas_call | solution.py:365
  131.2 5.5 %collective-permute-done.25.refs_6_ = bf16[96,2048]{1,0:T(8,128)(2,1)S(1)} collective-permute-done((bf16[96,2048]{1,0:T(8,128)(2,1)S(1)}, bf16[96,2048]{1,0:T(8,128)(2,1)S(1)}, u32[]{:S(2)}, u32[]{:S(2)}) %collective-permute-start.25) | collective-permute-done | bytes 393248 | tf_op jit(solution)/shard_map/ppermute | solution.py:112
  139.4 4.9 %piece_grad.4 = (bf16[2,16,64,512]{3,2,1,0:T(8,128)(2,1)S(1)}, f32[16,64,128]{2,1,0:T(8,128)S(1)}) custom-call(s32[2]{0:T(128)S(1)} %pad_add_fusion.3.scalar_ref, bf16[4,256,256]{2,1,0:T(8,128)(2,1)S(1)} %get-tuple-element.75.hot_ref, bf16[1,2048,4096]{2,1,0:T(8,128)(2,1)} %weight_ref.5, f32[16,64,128]{2,1,0:T(8,128)S(1)} %get-tuple-element.96.refs_0_, ...), custom_call_target="tpu_custom_call" | custom-call | flops 5280000000 | bytes 1 | tf_op jit(solution)/shard_map/piece_grad/pallas_call | solution.py:365
  144.4 3.3 %decoder_part.4.refs_0_ = bf16[2048,2048]{1,0:T(8,128)(2,1)} custom-call(s32[2]{0:T(128)S(1)} %pad_add_fusion.4.scalar_ref, bf16[16,128,64]{2,1,0:T(8,128)(2,1)S(1)} %get-tuple-element.74.code_ref, bf16[2,16,64,512]{3,2,1,0:T(8,128)(2,1)S(1)} %get-tuple-element.98.slots_ref, bf16[2048,2048]{1,0:T(8,128)(2,1)} %decoder_part.3.refs_0_), custom_call_target="tpu_custom_call", output_to_operand_aliasing={{}: (3, {})} | custom-call | flops 3630000128 | bytes 1 | tf_op jit(solution)/shard_map/decoder_part/pallas_call | solution.py:400
  147.7 4.6 %collective-permute-done.29.refs_7_ = bf16[160,2048]{1,0:T(8,128)(2,1)S(1)} collective-permute-done((bf16[160,2048]{1,0:T(8,128)(2,1)S(1)}, bf16[160,2048]{1,0:T(8,128)(2,1)S(1)}, u32[]{:S(2)}, u32[]{:S(2)}) %collective-permute-start.29) | collective-permute-done | bytes 655392 | tf_op jit(solution)/shard_map/ppermute | solution.py:112
  152.3 3.3 %act_slots.1.act_ref = bf16[16,64,2048]{2,1,0:T(8,128)(2,1)S(1)} custom-call(s32[4]{0:T(128)S(1)} %pad_add_fusion.5.scalar_ref, bf16[4,256,256]{2,1,0:T(8,128)(2,1)S(1)} %get-tuple-element.75.hot_ref, bf16[256,2048]{1,0:T(8,128)(2,1)S(1)} %copy-done.1, bf16[256,2048]{1,0:T(8,128)(2,1)S(1)} %copy-done.4, ...), custom_call_target="tpu_custom_call" | custom-call | flops 3630000128 | bytes 1 | tf_op jit(solution)/shard_map/act_slots/pallas_call | solution.py:440
  155.6 2.8 %piece_grad.5 = (bf16[1,16,64,512]{3,2,1,0:T(8,128)(2,1)S(1)}, f32[16,64,128]{2,1,0:T(8,128)S(1)}) custom-call(s32[1]{0:T(128)} %bitcast.23.scalar_ref, bf16[4,256,256]{2,1,0:T(8,128)(2,1)S(1)} %get-tuple-element.75.hot_ref, bf16[1,2048,4096]{2,1,0:T(8,128)(2,1)} %weight_ref.5, f32[16,64,128]{2,1,0:T(8,128)S(1)} %get-tuple-element.104.refs_0_, ...), custom_call_target="tpu_custom_call" | custom-call | flops 3080000000 | bytes 1 | tf_op jit(solution)/shard_map/piece_grad/pallas_call | solution.py:365
  162.4 6.3 %encoder_part.1 = bf16[2048,2048]{1,0:T(8,128)(2,1)} custom-call(bf16[16,64,128]{2,1,0:T(8,128)(2,1)S(1)} %copy-done.8, f32[16,64,128]{2,1,0:T(8,128)S(1)} %get-tuple-element.110.own_ref, f32[16,64,128]{2,1,0:T(8,128)S(1)} %collective-permute-done.30.theirs_ref, bf16[16,64,2048]{2,1,0:T(8,128)(2,1)S(1)} %act_slots.1.act_ref), custom_call_target="tpu_custom_call" | custom-call | flops 7150000128 | bytes 1 | tf_op jit(solution)/shard_map/encoder_part/pallas_call | solution.py:476
  (107 shorter events, 49.6 us)
Async XLA Ops:
  2.2 12.6 %collective-permute-start.2 = (bf16[272,128]{1,0:T(8,128)(2,1)S(1)}, bf16[272,128]{1,0:T(8,128)(2,1)S(1)}, u32[]{:S(2)}, u32[]{:S(2)}) collective-permute-start(bf16[272,128]{1,0:T(8,128)(2,1)S(1)} %fusion.21.refs_0_), channel_id=1, source_target_pairs={{0,6},{2,4},{4,2},{6,0},{1,7},{3,5},{5,3},{7,1},{8,14},{10,12},{12... | collective-permute-start | bytes 208904 | tf_op jit(solution)/shard_map/ppermute | solution.py:103
  6.4 8.3 %collective-permute-start.1 = (bf16[272,128]{1,0:T(8,128)(2,1)S(1)}, bf16[272,128]{1,0:T(8,128)(2,1)S(1)}, u32[]{:S(2)}, u32[]{:S(2)}) collective-permute-start(bf16[272,128]{1,0:T(8,128)(2,1)S(1)} %fusion.21.refs_0_), channel_id=1, source_target_pairs={{0,4},{2,6},{4,0},{6,2},{1,5},{3,7},{5,1},{7,3},{8,12},{10,14},{12... | collective-permute-start | bytes 208904 | tf_op jit(solution)/shard_map/ppermute | solution.py:103
  15.1 26.1 %collective-permute-start.7 = (bf16[256,2048]{1,0:T(8,128)(2,1)S(1)}, bf16[256,2048]{1,0:T(8,128)(2,1)S(1)}, u32[]{:S(2)}, u32[]{:S(2)}) collective-permute-start(bf16[256,2048]{1,0:T(8,128)(2,1)S(1)} %pad_maximum_fusion.refs_0_), channel_id=1, source_target_pairs={{2,0},{4,2},{6,4},{3,1},{5,3},{7,5},{10,8},{12,10},{14,12},{11,9},... | collective-permute-start | bytes 3145736 | tf_op jit(solution)/shard_map/ppermute | solution.py:112
  16.4 25.7 %collective-permute-start.6 = (bf16[256,2048]{1,0:T(8,128)(2,1)S(1)}, bf16[256,2048]{1,0:T(8,128)(2,1)S(1)}, u32[]{:S(2)}, u32[]{:S(2)}) collective-permute-start(bf16[256,2048]{1,0:T(8,128)(2,1)S(1)} %pad_maximum_fusion.refs_0_), channel_id=1, source_target_pairs={{0,2},{2,4},{4,6},{1,3},{3,5},{5,7},{8,10},{10,12},{12,14},{9,11},... | collective-permute-start | bytes 3145736 | tf_op jit(solution)/shard_map/ppermute | solution.py:112
  25.5 27.5 %collective-permute-start.5 = (bf16[1024,512]{1,0:T(8,128)(2,1)S(1)}, bf16[1024,512]{1,0:T(8,128)(2,1)S(1)}, u32[]{:S(2)}, u32[]{:S(2)}) collective-permute-start(bf16[1024,512]{1,0:T(8,128)(2,1)S(1)} %fusion.8), channel_id=1, source_target_pairs={{0,8},{8,0},{16,24},{24,16},{1,9},{9,1},{17,25},{25,17},{2,10},{10... | collective-permute-start | bytes 3145736 | tf_op jit(solution)/shard_map/ppermute | solution.py:103
  29.3 23.4 %collective-permute-start.9 = (bf16[1024,512]{1,0:T(8,128)(2,1)S(1)}, bf16[1024,512]{1,0:T(8,128)(2,1)S(1)}, u32[]{:S(2)}, u32[]{:S(2)}) collective-permute-start(bf16[1024,512]{1,0:T(8,128)(2,1)S(1)} %fusion.14), channel_id=1, source_target_pairs={{0,16},{8,24},{16,0},{24,8},{1,17},{9,25},{17,1},{25,9},{2,18},{10... | collective-permute-start | bytes 3145736 | tf_op jit(solution)/shard_map/ppermute | solution.py:103
  42.1 22.0 %collective-permute-start.12 = (bf16[256,2048]{1,0:T(8,128)(2,1)S(1)}, bf16[256,2048]{1,0:T(8,128)(2,1)S(1)}, u32[]{:S(2)}, u32[]{:S(2)}) collective-permute-start(bf16[256,2048]{1,0:T(8,128)(2,1)S(1)} %collective-permute-done.6.refs_8_), channel_id=1, source_target_pairs={{2,4},{4,6},{3,5},{5,7},{10,12},{12,14},{11,13},{13,15},{18,20},{2... | collective-permute-start | bytes 3145736 | tf_op jit(solution)/shard_map/ppermute | solution.py:112
  42.9 28.0 %collective-permute-start.13 = (bf16[256,2048]{1,0:T(8,128)(2,1)S(1)}, bf16[256,2048]{1,0:T(8,128)(2,1)S(1)}, u32[]{:S(2)}, u32[]{:S(2)}) collective-permute-start(bf16[256,2048]{1,0:T(8,128)(2,1)S(1)} %collective-permute-done.7.refs_1_), channel_id=1, source_target_pairs={{2,0},{4,2},{3,1},{5,3},{10,8},{12,10},{11,9},{13,11},{18,16},{20,... | collective-permute-start | bytes 3145736 | tf_op jit(solution)/shard_map/ppermute | solution.py:112
  52.8 11.2 %collective-permute-start.10 = (bf16[1024,256]{1,0:T(8,128)(2,1)S(1)}, bf16[1024,256]{1,0:T(8,128)(2,1)S(1)}, u32[]{:S(2)}, u32[]{:S(2)}) collective-permute-start(bf16[1024,256]{1,0:T(8,128)(2,1)S(1)} %add_convert_fusion), channel_id=1, source_target_pairs={{0,8},{8,0},{16,24},{24,16},{1,9},{9,1},{17,25},{25,17},{2,10},{10... | collective-permute-start | bytes 1572872 | tf_op jit(solution)/shard_map/ppermute | solution.py:103
  53.2 11.0 %collective-permute-start.8 = (bf16[1024,256]{1,0:T(8,128)(2,1)S(1)}, bf16[1024,256]{1,0:T(8,128)(2,1)S(1)}, u32[]{:S(2)}, u32[]{:S(2)}) collective-permute-start(bf16[1024,256]{1,0:T(8,128)(2,1)S(1)} %add_convert_fusion.1), channel_id=1, source_target_pairs={{0,16},{8,24},{16,0},{24,8},{1,17},{9,25},{17,1},{25,9},{2,18},{10... | collective-permute-start | bytes 1572872 | tf_op jit(solution)/shard_map/ppermute | solution.py:103
  72.5 18.6 %collective-permute-start.15 = (bf16[256,512]{1,0:T(8,128)(2,1)S(1)}, bf16[256,512]{1,0:T(8,128)(2,1)S(1)}, u32[]{:S(2)}, u32[]{:S(2)}) collective-permute-start(bf16[256,512]{1,0:T(8,128)(2,1)S(1)} %get-tuple-element.82), channel_id=1, source_target_pairs={{0,4},{2,6},{4,0},{6,2},{1,5},{3,7},{5,1},{7,3},{8,12},{10,14},{12... | collective-permute-start | bytes 786440 | tf_op jit(solution)/shard_map/ppermute | solution.py:103
  72.5 18.6 %collective-permute-start.16 = (bf16[256,512]{1,0:T(8,128)(2,1)S(1)}, bf16[256,512]{1,0:T(8,128)(2,1)S(1)}, u32[]{:S(2)}, u32[]{:S(2)}) collective-permute-start(bf16[256,512]{1,0:T(8,128)(2,1)S(1)} %get-tuple-element.83), channel_id=1, source_target_pairs={{0,6},{2,4},{4,2},{6,0},{1,7},{3,5},{5,3},{7,1},{8,14},{10,12},{12... | collective-permute-start | bytes 786440 | tf_op jit(solution)/shard_map/ppermute | solution.py:103
  91.3 10.7 %collective-permute-start.21 = (bf16[256,512]{1,0:T(8,128)(2,1)S(1)}, bf16[256,512]{1,0:T(8,128)(2,1)}, u32[]{:S(2)}, u32[]{:S(2)}) collective-permute-start(bf16[256,512]{1,0:T(8,128)(2,1)S(1)} %multiply_convert_fusion.refs_0_), channel_id=1, source_target_pairs={{0,8},{8,0},{16,24},{24,16},{1,9},{9,1},{17,25},{25,17},{2,10},{10... | collective-permute-start | bytes 786440 | tf_op jit(solution)/shard_map/ppermute | solution.py:103
  92.6 9.4 %collective-permute-start.20 = (bf16[256,512]{1,0:T(8,128)(2,1)S(1)}, bf16[256,512]{1,0:T(8,128)(2,1)}, u32[]{:S(2)}, u32[]{:S(2)}) collective-permute-start(bf16[256,512]{1,0:T(8,128)(2,1)S(1)} %multiply_convert_fusion.refs_0_), channel_id=1, source_target_pairs={{0,16},{8,24},{16,0},{24,8},{1,17},{9,25},{17,1},{25,9},{2,18},{10... | collective-permute-start | bytes 786440 | tf_op jit(solution)/shard_map/ppermute | solution.py:103
  93.8 11.1 %collective-permute-start.19 = (bf16[256,512]{1,0:T(8,128)(2,1)S(1)}, bf16[256,512]{1,0:T(8,128)(2,1)}, u32[]{:S(2)}, u32[]{:S(2)}) collective-permute-start(bf16[256,512]{1,0:T(8,128)(2,1)S(1)} %multiply_convert_fusion.refs_0_), channel_id=1, source_target_pairs={{0,2},{2,0},{4,6},{6,4},{1,3},{3,1},{5,7},{7,5},{8,10},{10,8},{12,... | collective-permute-start | bytes 786440 | tf_op jit(solution)/shard_map/ppermute | solution.py:103
  99.7 18.7 %collective-permute-start.18 = (bf16[256,512]{1,0:T(8,128)(2,1)S(1)}, bf16[256,512]{1,0:T(8,128)(2,1)}, u32[]{:S(2)}, u32[]{:S(2)}) collective-permute-start(bf16[256,512]{1,0:T(8,128)(2,1)S(1)} %multiply_convert_fusion.refs_0_), channel_id=1, source_target_pairs={{0,4},{2,6},{4,0},{6,2},{1,5},{3,7},{5,1},{7,3},{8,12},{10,14},{12... | collective-permute-start | bytes 786440 | tf_op jit(solution)/shard_map/ppermute | solution.py:103
  99.7 18.7 %collective-permute-start.17 = (bf16[256,512]{1,0:T(8,128)(2,1)S(1)}, bf16[256,512]{1,0:T(8,128)(2,1)}, u32[]{:S(2)}, u32[]{:S(2)}) collective-permute-start(bf16[256,512]{1,0:T(8,128)(2,1)S(1)} %multiply_convert_fusion.refs_0_), channel_id=1, source_target_pairs={{0,6},{2,4},{4,2},{6,0},{1,7},{3,5},{5,3},{7,1},{8,14},{10,12},{12... | collective-permute-start | bytes 786440 | tf_op jit(solution)/shard_map/ppermute | solution.py:103
  119.6 17.1 %collective-permute-start.23 = (bf16[768,512]{1,0:T(8,128)(2,1)S(1)}, bf16[768,512]{1,0:T(8,128)(2,1)S(1)}, u32[]{:S(2)}, u32[]{:S(2)}) collective-permute-start(bf16[768,512]{1,0:T(8,128)(2,1)S(1)} %join.3.refs_1_), channel_id=1, source_target_pairs={{0,16},{8,24},{16,0},{24,8},{1,17},{9,25},{17,1},{25,9},{2,18},{10... | collective-permute-start | bytes 2359304 | tf_op jit(solution)/shard_map/ppermute | solution.py:103
  119.9 16.8 %collective-permute-start.22 = (bf16[768,512]{1,0:T(8,128)(2,1)S(1)}, bf16[768,512]{1,0:T(8,128)(2,1)S(1)}, u32[]{:S(2)}, u32[]{:S(2)}) collective-permute-start(bf16[768,512]{1,0:T(8,128)(2,1)S(1)} %join.3.refs_1_), channel_id=1, source_target_pairs={{0,8},{8,0},{16,24},{24,16},{1,9},{9,1},{17,25},{25,17},{2,10},{10... | collective-permute-start | bytes 2359304 | tf_op jit(solution)/shard_map/ppermute | solution.py:103
  122.9 13.8 %collective-permute-start.25 = (bf16[96,2048]{1,0:T(8,128)(2,1)S(1)}, bf16[96,2048]{1,0:T(8,128)(2,1)S(1)}, u32[]{:S(2)}, u32[]{:S(2)}) collective-permute-start(bf16[96,2048]{1,0:T(8,128)(2,1)S(1)} %slice.65), channel_id=1, source_target_pairs={{2,0},{3,1},{10,8},{11,9},{18,16},{19,17},{26,24},{27,25}} | collective-permute-start | bytes 1179656 | tf_op jit(solution)/shard_map/ppermute | solution.py:112
  124.2 23.4 %collective-permute-start.28 = (bf16[160,2048]{1,0:T(8,128)(2,1)S(1)}, bf16[160,2048]{1,0:T(8,128)(2,1)S(1)}, u32[]{:S(2)}, u32[]{:S(2)}) collective-permute-start(bf16[160,2048]{1,0:T(8,128)(2,1)S(1)} %slice.66), channel_id=1, source_target_pairs={{4,6},{5,7},{12,14},{13,15},{20,22},{21,23},{28,30},{29,31}} | collective-permute-start | bytes 1966088 | tf_op jit(solution)/shard_map/ppermute | solution.py:112
  129.7 22.5 %collective-permute-start.29 = (bf16[160,2048]{1,0:T(8,128)(2,1)S(1)}, bf16[160,2048]{1,0:T(8,128)(2,1)S(1)}, u32[]{:S(2)}, u32[]{:S(2)}) collective-permute-start(bf16[160,2048]{1,0:T(8,128)(2,1)S(1)} %slice.67), channel_id=1, source_target_pairs={{2,0},{3,1},{10,8},{11,9},{18,16},{19,17},{26,24},{27,25}} | collective-permute-start | bytes 1966088 | tf_op jit(solution)/shard_map/ppermute | solution.py:112
  136.8 18.7 %collective-permute-start.27 = (bf16[1024,256]{1,0:T(8,128)(2,1)S(1)}, bf16[1024,256]{1,0:T(8,128)(2,1)S(1)}, u32[]{:S(2)}, u32[]{:S(2)}) collective-permute-start(bf16[1024,256]{1,0:T(8,128)(2,1)S(1)} %pad_maximum_fusion.3), channel_id=1, source_target_pairs={{0,16},{8,24},{16,0},{24,8},{1,17},{9,25},{17,1},{25,9},{2,18},{10... | collective-permute-start | bytes 1572872 | tf_op jit(solution)/shard_map/ppermute | solution.py:103
  138.2 17.4 %collective-permute-start.26 = (bf16[1024,256]{1,0:T(8,128)(2,1)S(1)}, bf16[1024,256]{1,0:T(8,128)(2,1)S(1)}, u32[]{:S(2)}, u32[]{:S(2)}) collective-permute-start(bf16[1024,256]{1,0:T(8,128)(2,1)S(1)} %pad_maximum_fusion.2), channel_id=1, source_target_pairs={{0,8},{8,0},{16,24},{24,16},{1,9},{9,1},{17,25},{25,17},{2,10},{10... | collective-permute-start | bytes 1572872 | tf_op jit(solution)/shard_map/ppermute | solution.py:103
  (18 other events, 113.7 us)

commit v12 on v11

--- a/solution.py
+++ b/solution.py
@@ -414,42 +414,39 @@
     )(columns.astype(jnp.int32), codes, slots, *onto)
 
 
-def act_slots_kernel(layouts, scalar_ref, hot_ref, *refs):
+def act_slots_kernel(scalar_ref, hot_ref, *refs):
     out_ref = refs[-1]
-    per = out_ref.shape[1] // hot_ref.shape[0]
-    at = 0
-    for i, layout in enumerate(layouts):
+    shards = hot_ref.shape[0]
+    per = out_ref.shape[1] // shards
+    for i in range(shards):
         z = scalar_ref[i]
-        total = None
-        for count in layout:
-            rows = [ref[...] for ref in refs[at:at + count]]
-            rows = rows[0] if count == 1 else jnp.concatenate(rows, axis=0)
-            total = rows if total is None else total + rows
-            at += count
-        value = jnp.dot(hot_ref[z], total, preferred_element_type=jnp.float32).astype(jnp.bfloat16)
+        rows, more = refs[2 * i][...], refs[2 * i + 1][...]
+        rows = rows + jnp.where(scalar_ref[shards + i] > 0, more, jnp.zeros((), more.dtype))
+        value = jnp.dot(hot_ref[z], rows, preferred_element_type=jnp.float32).astype(jnp.bfloat16)
         to = pl.ds(pl.multiple_of(z * per, per), per)
         for b in range(out_ref.shape[0]):
             out_ref[b, to, :] = value[b * per:(b + 1) * per]
 
 
-def act_slots(terms_of, places, hot, count):
-    half = terms_of[0][0][0].shape[1]
+def act_slots(terms_of, places, flags, hot, count):
+    group, half = terms_of[0][0].shape
     slots = hot.shape[0] * hot.shape[1] // count
     tile = half // 4
-    flat = [part for terms in terms_of for term in terms for part in term]
-    return pl.pallas_call(
-        functools.partial(act_slots_kernel, [[len(term) for term in terms] for terms in terms_of]),
+    flat = [term for terms in terms_of for term in terms]
+    scalars = jnp.stack([jnp.asarray(x, jnp.int32) for x in (*places, *flags)])
+    return pl.pallas_call(
+        act_slots_kernel,
         out_shape=jax.ShapeDtypeStruct((count, slots, half), jnp.bfloat16),
         grid_spec=pltpu.PrefetchScalarGridSpec(
             num_scalar_prefetch=1,
             grid=(4,),
-            in_specs=[resident(hot.shape)] + [pl.BlockSpec((part.shape[0], tile), lambda i, s: (0, i)) for part in flat],
+            in_specs=[resident(hot.shape)] + [pl.BlockSpec((group, tile), lambda i, s: (0, i)) for _ in flat],
             out_specs=pl.BlockSpec((count, slots, tile), lambda i, s: (0, 0, i)),
         ),
         compiler_params=params(),
         cost_estimate=cost(3.3),
         name="act_slots",
-    )(jnp.stack(places).astype(jnp.int32), hot, *flat)
+    )(scalars, hot, *flat)
 
 
 def encoder_kernel(cap, shared, pre_ref, own_ref, theirs_ref, act_ref, out_ref):
@@ -570,10 +567,7 @@
     far, goals, up[-1], down[-1], made = lax.optimization_barrier((far, goals, up[-1], down[-1], made))
     while len(up) < lat_count - 1:
         next_hops()
-    early = group * 3 // 8
-    ends = []
-    if len(up) < lat_count:
-        ends = [(up[-1][rows], down[-1][rows]) for rows in (slice(0, early), slice(early, group))]
+    relay = jnp.where(lat_here == 1, down[-1], up[-1])
 
     total, *sent = layer_sum((got[0], kept[0], far[0]), (got[1], kept[1], far[1]), lat_count)
     for r in range(1, lat_count):
@@ -581,30 +575,32 @@
     errors = ((total - goals.astype(f32)) / tok_count).astype(bf16)
     others = [flip(errors, "latent", r) for r in range(1, lat_count)]
     one_near, two_near = flip(errors, "layer", 1), flip(errors, "layer", 2)
-    ends, others, two_near, one_near = lax.optimization_barrier((ends, others[::-1], two_near, one_near))
-    others = others[::-1]
+    relay, two_near, one_near, others = lax.optimization_barrier((relay, two_near, one_near, others[::-1]))
+    distant = join(others[::-1])
+    one_far, two_far = flip(distant, "layer", 1), flip(distant, "layer", 2)
+    ends = lax.ppermute(relay, "latent", [(lat_count - 2, lat_count - 1), (1, 0)])
+
     hot, pre_slots, code_slots = made
-    distant = join(others)
-    one_far, two_far = flip(distant, "layer", 1), flip(distant, "layer", 2)
-    ends = [(hop(one, "latent", 1, len(up) - 1), hop(two, "latent", -1, len(up) - 1)) for one, two in ends]
 
     def grads_of(here, names, grad, dec):
         slots, grad = piece_grad(here, hot, decoder, weight_places(names), block_size, grad)
         return grad, decoder_part(slots, code_slots, jnp.stack(places(names, 0)), half, dec)
 
     grad, dec = grads_of([[(errors,), (distant,)]], (0,), None, None)
-    one_far, two_far, grad, dec, ends[:1] = lax.optimization_barrier((one_far, two_far, grad, dec, ends[:1]))
+    grad, dec, two_far, one_far = lax.optimization_barrier((grad, dec, two_far, one_far))
     three_a = flip(jnp.concatenate([two_near[:, :side], two_far[:, :side]]), "layer", 1)
     three_b = flip(jnp.concatenate([one_near[:, side:], one_far[:, side:]]), "layer", 2)
     grad, dec = grads_of([[(one_near,), (one_far,)], [(two_near,), (two_far,)]], (1, 2), grad, dec)
 
-    ups, downs = [[part] for part in up], [[part] for part in down]
-    if ends:
-        ups.append([part[0] for part in ends])
-        downs.append([part[1] for part in ends])
-    terms_of = [[[acts]]] + [[downs[k], ups[lat_count - k]] for k in range(1, lat_count)]
+    down_end, up_end = lat_here == 0, lat_here == lat_count - 1
+    terms_of = [[acts, acts]]
+    flags = [False]
+    for k in range(1, lat_count):
+        last = k == 1 or k == lat_count - 1
+        terms_of.append([(down if k == 1 else up)[1] if last else down[k], ends if last else up[lat_count - k]])
+        flags.append(True if not last else up_end if k == 1 else down_end)
     shards = [lax.rem(lat_here + k, lat_count) ^ lat_here for k in range(lat_count)]
-    slotted = act_slots(terms_of, shards, hot, local_blocks)
+    slotted = act_slots(terms_of, shards, flags, hot, local_blocks)
     three_a, three_b, grad, dec, slotted = lax.optimization_barrier((three_a, three_b, grad, dec, slotted))
     grad, dec = grads_of([[(three_a, three_b)]], (3,), grad, dec)
     enc = encoder_part(pre_slots, grad, flip(grad, "dp", 1), slotted, capacity)
@@ -626,7 +622,7 @@
         and dp_count == 2
         and active_count == 2
         and lay_count == 4
-        and lat_count > 1
+        and lat_count > 3
         and lat_count & (lat_count - 1) == 0
         and tok_count == block_size
         and lat_count * dp_count * 16 <= tok_count

time: 169 us -> 170 us (level)
  other arithmetic: 1.86 us -> 4.78 us
  waiting for transfers between devices: 61 us -> 58.6 us
  local copies, waits for them, and re-layouts: 5.21 us -> 3.35 us
    ppermute x8 -> x4, waiting for transfers between devices: 23 us -> 12.9 us  [hop(): return lax.ppermute(value, axis, pairs)]
    ppermute x0 -> x1, waiting for transfers between devices: none -> 4.64 us  [dense_plan(): lax.ppermute(relay, 'latent', [(lat_count - 2, lat_count - 1), (1, 0)])]
    ppermute x8 -> x4, starting transfers between devices: 11.7 us -> 7.52 us  [hop(): return lax.ppermute(value, axis, pairs)]
    ppermute x23, waiting for transfers between devices: 38 us -> 41 us  [flip(): return lax.ppermute(value, axis, [(i, i ^ bit) for i in range(count)])]
    ppermute x23, starting transfers between devices: 32.5 us -> 34.9 us  [flip(): return lax.ppermute(value, axis, [(i, i ^ bit) for i in range(count)])]
  transfers between devices with their start and end apart: 31 -> 28, of which waited for: 11 -> 12; matrix products, arithmetic and copies ran while one was open for 10% -> 10% of each run, Pallas kernels for 20% -> 21%
where the time goes in v12:
time: 170 us; the launch traced here: 168 us
  waiting for transfers between devices  58.6 us (34%)
  Pallas kernels  45.4 us (27%)
  starting transfers between devices  43.9 us (26%)
  matrix products  11.1 us (7%)
  other arithmetic  4.78 us (3%)
  local copies, waits for them, and re-layouts  3.35 us (2%)
    ppermute x23, waiting for transfers between devices, flip(): return lax.ppermute(value, axis, [(i, i ^ bit) for i in range(count)])  41 us
    ppermute x23, starting transfers between devices, flip(): return lax.ppermute(value, axis, [(i, i ^ bit) for i in range(count)])  34.9 us
    ppermute x4, waiting for transfers between devices, hop(): return lax.ppermute(value, axis, pairs)  12.9 us
    pallas_call x3, Pallas kernels, gather_columns(): pl.pallas_call(gather_kernel, out_shape=[pltpu.HBM((rows, count * width),...  11.9 us
    dot_general x4, matrix products, rows_for(): jnp.dot(spread, weights[:, n * width:(n + 1) * width], preferred_element_...  11.1 us
    pallas_call x3, Pallas kernels, piece_grad(): pl.pallas_call(functools.partial(piece_grad_kernel, [[len(row) for row in...  10.5 us
    ppermute x4, starting transfers between devices, hop(): return lax.ppermute(value, axis, pairs)  7.52 us
    pallas_call x3, Pallas kernels, decoder_part(): pl.pallas_call(functools.partial(decoder_kernel, len(onto)), out_shape=ja...  7.27 us
  transfers between devices with their start and end apart: 28, of which 12 were waited for; matrix products, arithmetic and copies ran while one was open for 10% of the time, Pallas kernels for 21%

profile of v12, /device:TPU:1, one launch (start us, length us, event | category | flops | bytes accessed | tf_op | source)
XLA Modules:
  0.0 168.2 jit_solution(16112136077103541849)
XLA Ops:
  2.2 4.2 %collective-permute-start.2 = (bf16[272,128]{1,0:T(8,128)(2,1)S(1)}, bf16[272,128]{1,0:T(8,128)(2,1)S(1)}, u32[]{:S(2)}, u32[]{:S(2)}) collective-permute-start(bf16[272,128]{1,0:T(8,128)(2,1)S(1)} %fusion.21.refs_0_), channel_id=1, source_target_pairs={{0,6},{2,4},{4,2},{6,0},{1,7},{3,5},{5,3},{7,1},{8,14},{10,12},{12... | collective-permute-start | bytes 208904 | tf_op jit(solution)/shard_map/ppermute | solution.py:103
  9.4 5.3 %gather_columns.3 = (bf16[2048,1024]{1,0:T(8,128)(2,1)}, f32[8,128]{1,0:T(8,128)S(1)}) custom-call(s32[4]{0:T(128)S(1)} %pad_add_fusion.1.scalar_ref, bf16[1,2048,4096]{2,1,0:T(8,128)(2,1)} %weight_ref.5), custom_call_target="tpu_custom_call" | custom-call | flops 3960000000 | bytes 1 | tf_op jit(solution)/shard_map/gather_columns/pallas_call | solution.py:136
  16.4 4.1 %collective-permute-start.6 = (bf16[256,2048]{1,0:T(8,128)(2,1)S(1)}, bf16[256,2048]{1,0:T(8,128)(2,1)S(1)}, u32[]{:S(2)}, u32[]{:S(2)}) collective-permute-start(bf16[256,2048]{1,0:T(8,128)(2,1)S(1)} %pad_maximum_fusion.refs_0_.refs_1_), channel_id=1, source_target_pairs={{0,2},{2,4},{4,6},{1,3},{3,5},{5,7},{8,10},{10,12},{12,14},{9,11},... | collective-permute-start | bytes 3145736 | tf_op jit(solution)/shard_map/ppermute | solution.py:112
  20.6 2.6 %spread_codes.1 = bf16[1024,2048]{1,0:T(8,128)(2,1)S(1)} custom-call(s32[1]{0:T(128)} %bitcast.5.scalar_ref, bf16[8,272,128]{2,1,0:T(8,128)(2,1)S(1)} %bitcast.45), custom_call_target="tpu_custom_call" | custom-call | flops 2750000128 | bytes 1 | tf_op jit(solution)/shard_map/spread_codes/pallas_call | solution.py:185
  30.6 5.3 %gather_columns.4 = (bf16[2048,1024]{1,0:T(8,128)(2,1)}, f32[8,128]{1,0:T(8,128)}) custom-call(s32[4]{0:T(128)S(1)} %pad_add_fusion.scalar_ref, bf16[1,2048,4096]{2,1,0:T(8,128)(2,1)} %weight_ref.5), custom_call_target="tpu_custom_call" | custom-call | flops 3960000000 | bytes 1 | tf_op jit(solution)/shard_map/gather_columns/pallas_call | solution.py:136
  35.9 5.4 %collective-permute-done.7.refs_2_ = bf16[256,2048]{1,0:T(8,128)(2,1)S(1)} collective-permute-done((bf16[256,2048]{1,0:T(8,128)(2,1)S(1)}, bf16[256,2048]{1,0:T(8,128)(2,1)S(1)}, u32[]{:S(2)}, u32[]{:S(2)}) %collective-permute-start.7) | collective-permute-done | bytes 1048608 | tf_op jit(solution)/shard_map/ppermute | solution.py:112
  44.3 4.1 %fusion.17.kept_b = bf16[1024,512]{1,0:T(8,128)(2,1)S(1)} fusion(bf16[1024,2048]{1,0:T(8,128)(2,1)S(1)} %spread_codes.1, bf16[2048,1024]{1,0:T(8,128)(2,1)} %get-tuple-element.61), kind=kOutput, calls=%fused_computation.11 | convolution fusion | flops 2148007936 | bytes 7340032 | tf_op jit(solution)/shard_map/dot_general | solution.py:554
  56.9 2.9 %collective-permute-start.11 = (bf16[128,512]{1,0:T(8,128)(2,1)S(1)}, bf16[128,512]{1,0:T(8,128)(2,1)S(1)}, u32[]{:S(2)}, u32[]{:S(2)}) collective-permute-start(bf16[128,512]{1,0:T(8,128)(2,1)S(1)} %get-tuple-element.105), channel_id=1, source_target_pairs={{0,1},{1,0},{2,3},{3,2},{4,5},{5,4},{6,7},{7,6},{8,9},{9,8},{10,11... | collective-permute-start | bytes 393224 | tf_op jit(solution)/shard_map/ppermute | solution.py:103
  61.5 2.6 %collective-permute-done.10.far_b = bf16[1024,256]{1,0:T(8,128)(2,1)S(1)} collective-permute-done((bf16[1024,256]{1,0:T(8,128)(2,1)S(1)}, bf16[1024,256]{1,0:T(8,128)(2,1)S(1)}, u32[]{:S(2)}, u32[]{:S(2)}) %collective-permute-start.10) | collective-permute-done | bytes 524320 | tf_op jit(solution)/shard_map/ppermute | solution.py:103
  64.3 6.7 %collective-permute-done.13.refs_4_ = bf16[256,2048]{1,0:T(8,128)(2,1)} collective-permute-done((bf16[256,2048]{1,0:T(8,128)(2,1)S(1)}, bf16[256,2048]{1,0:T(8,128)(2,1)}, u32[]{:S(2)}, u32[]{:S(2)}) %collective-permute-start.13) | collective-permute-done | bytes 1048608 | tf_op jit(solution)/shard_map/ppermute | solution.py:112
  72.6 2.4 %collective-permute-start.16 = (bf16[256,512]{1,0:T(8,128)(2,1)S(1)}, bf16[256,512]{1,0:T(8,128)(2,1)}, u32[]{:S(2)}, u32[]{:S(2)}) collective-permute-start(bf16[256,512]{1,0:T(8,128)(2,1)S(1)} %get-tuple-element.78), channel_id=1, source_target_pairs={{0,6},{2,4},{4,2},{6,0},{1,7},{3,5},{5,3},{7,1},{8,14},{10,12},{12... | collective-permute-start | bytes 786440 | tf_op jit(solution)/shard_map/ppermute | solution.py:103
  75.0 3.3 %collective-permute-done.14 = bf16[256,512]{1,0:T(8,128)(2,1)} collective-permute-done((bf16[256,512]{1,0:T(8,128)(2,1)S(1)}, bf16[256,512]{1,0:T(8,128)(2,1)}, u32[]{:S(2)}, u32[]{:S(2)}) %collective-permute-start.14) | collective-permute-done | bytes 262176 | tf_op jit(solution)/shard_map/ppermute | solution.py:103
  78.3 13.1 %collective-permute-done.15 = bf16[256,512]{1,0:T(8,128)(2,1)} collective-permute-done((bf16[256,512]{1,0:T(8,128)(2,1)S(1)}, bf16[256,512]{1,0:T(8,128)(2,1)}, u32[]{:S(2)}, u32[]{:S(2)}) %collective-permute-start.15) | collective-permute-done | bytes 262176 | tf_op jit(solution)/shard_map/ppermute | solution.py:103
  92.8 6.0 %collective-permute-start.21 = (bf16[256,512]{1,0:T(8,128)(2,1)S(1)}, bf16[256,512]{1,0:T(8,128)(2,1)S(1)}, u32[]{:S(2)}, u32[]{:S(2)}) collective-permute-start(bf16[256,512]{1,0:T(8,128)(2,1)S(1)} %multiply_convert_fusion.refs_0_), channel_id=1, source_target_pairs={{0,2},{2,0},{4,6},{6,4},{1,3},{3,1},{5,7},{7,5},{8,10},{10,8},{12,... | collective-permute-start | bytes 786440 | tf_op jit(solution)/shard_map/ppermute | solution.py:103
  104.6 12.8 %collective-permute-done.20.refs_1_ = bf16[256,512]{1,0:T(8,128)(2,1)S(1)} collective-permute-done((bf16[256,512]{1,0:T(8,128)(2,1)S(1)}, bf16[256,512]{1,0:T(8,128)(2,1)S(1)}, u32[]{:S(2)}, u32[]{:S(2)}) %collective-permute-start.20) | collective-permute-done | bytes 262176 | tf_op jit(solution)/shard_map/ppermute | solution.py:103
  122.6 2.9 %piece_grad.3 = (bf16[1,16,64,512]{3,2,1,0:T(8,128)(2,1)S(1)}, f32[16,64,128]{2,1,0:T(8,128)S(1)}) custom-call(s32[1]{0:T(128)} %bitcast.21.scalar_ref, bf16[4,256,256]{2,1,0:T(8,128)(2,1)S(1)} %get-tuple-element.70.hot_ref, bf16[1,2048,4096]{2,1,0:T(8,128)(2,1)} %weight_ref.5, bf16[256,512]{1,0:T(8,128)(2,1)S(1)} %multiply_convert_fusion.refs_0_, ...), custom_call_target="tpu_custom_call" | custom-call | flops 3080000000 | bytes 1 | tf_op jit(solution)/shard_map/piece_grad/pallas_call | solution.py:365
  127.6 6.0 %collective-permute-done.23.refs_2_ = bf16[768,512]{1,0:T(8,128)(2,1)S(1)} collective-permute-done((bf16[768,512]{1,0:T(8,128)(2,1)}, bf16[768,512]{1,0:T(8,128)(2,1)S(1)}, u32[]{:S(2)}, u32[]{:S(2)}) %collective-permute-start.23) | collective-permute-done | bytes 786464 | tf_op jit(solution)/shard_map/ppermute | solution.py:103
  136.4 4.8 %piece_grad.4 = (bf16[2,16,64,512]{3,2,1,0:T(8,128)(2,1)S(1)}, f32[16,64,128]{2,1,0:T(8,128)S(1)}) custom-call(s32[2]{0:T(128)S(1)} %pad_add_fusion.3.scalar_ref, bf16[4,256,256]{2,1,0:T(8,128)(2,1)S(1)} %get-tuple-element.70.hot_ref, bf16[1,2048,4096]{2,1,0:T(8,128)(2,1)} %weight_ref.5, f32[16,64,128]{2,1,0:T(8,128)S(1)} %get-tuple-element.89.refs_0_, ...), custom_call_target="tpu_custom_call" | custom-call | flops 5280000000 | bytes 1 | tf_op jit(solution)/shard_map/piece_grad/pallas_call | solution.py:365
  141.2 3.3 %decoder_part.4.refs_0_ = bf16[2048,2048]{1,0:T(8,128)(2,1)} custom-call(s32[2]{0:T(128)S(1)} %pad_add_fusion.4.scalar_ref, bf16[16,128,64]{2,1,0:T(8,128)(2,1)S(1)} %get-tuple-element.69.code_ref, bf16[2,16,64,512]{3,2,1,0:T(8,128)(2,1)S(1)} %get-tuple-element.91.slots_ref, bf16[2048,2048]{1,0:T(8,128)(2,1)} %decoder_part.3.refs_0_), custom_call_target="tpu_custom_call", output_to_operand_aliasing={{}: (3, {})} | custom-call | flops 3630000128 | bytes 1 | tf_op jit(solution)/shard_map/decoder_part/pallas_call | solution.py:400
  144.5 4.6 %collective-permute-done.26.refs_3_.refs_7_ = bf16[256,2048]{1,0:T(8,128)(2,1)S(1)} collective-permute-done((bf16[256,2048]{1,0:T(8,128)(2,1)}, bf16[256,2048]{1,0:T(8,128)(2,1)S(1)}, u32[]{:S(2)}, u32[]{:S(2)}) %collective-permute-start.26) | collective-permute-done | bytes 1048608 | tf_op jit(solution)/shard_map/ppermute | solution.py:581
  149.2 4.4 %act_slots.1.act_ref = bf16[16,64,2048]{2,1,0:T(8,128)(2,1)S(1)} custom-call(s32[8]{0:T(128)S(1)} %stack.137.scalar_ref, bf16[4,256,256]{2,1,0:T(8,128)(2,1)S(1)} %get-tuple-element.70.hot_ref, bf16[256,2048]{1,0:T(8,128)(2,1)S(1)} %copy-done.1, bf16[256,2048]{1,0:T(8,128)(2,1)S(1)} %copy-done.1, bf16[256,2048]{1,0:T(8,128)(2,1)S(1)} %copy-done.10, ...), custom_call_target="tpu_custom_call" | custom-call | flops 3630000128 | bytes 1 | tf_op jit(solution)/shard_map/act_slots/pallas_call | solution.py:437
  153.6 2.8 %piece_grad.5 = (bf16[1,16,64,512]{3,2,1,0:T(8,128)(2,1)S(1)}, f32[16,64,128]{2,1,0:T(8,128)S(1)}) custom-call(s32[1]{0:T(128)} %bitcast.23.scalar_ref, bf16[4,256,256]{2,1,0:T(8,128)(2,1)S(1)} %get-tuple-element.70.hot_ref, bf16[1,2048,4096]{2,1,0:T(8,128)(2,1)} %weight_ref.5, f32[16,64,128]{2,1,0:T(8,128)S(1)} %get-tuple-element.94.refs_0_, ...), custom_call_target="tpu_custom_call" | custom-call | flops 3080000000 | bytes 1 | tf_op jit(solution)/shard_map/piece_grad/pallas_call | solution.py:365
  156.4 3.5 %collective-permute-start.27 = (f32[16,64,128]{2,1,0:T(8,128)S(1)}, f32[16,64,128]{2,1,0:T(8,128)S(1)}, u32[]{:S(2)}, u32[]{:S(2)}) collective-permute-start(f32[16,64,128]{2,1,0:T(8,128)S(1)} %get-tuple-element.100.own_ref), channel_id=1, source_target_pairs={{0,1},{1,0},{2,3},{3,2},{4,5},{5,4},{6,7},{7,6},{8,9},{9,8},{10,11... | collective-permute-start | bytes 1572872 | tf_op jit(solution)/shard_map/ppermute | solution.py:103
  161.9 6.3 %encoder_part.1 = bf16[2048,2048]{1,0:T(8,128)(2,1)} custom-call(bf16[16,64,128]{2,1,0:T(8,128)(2,1)S(1)} %copy-done.14, f32[16,64,128]{2,1,0:T(8,128)S(1)} %get-tuple-element.100.own_ref, f32[16,64,128]{2,1,0:T(8,128)S(1)} %collective-permute-done.27.theirs_ref, bf16[16,64,2048]{2,1,0:T(8,128)(2,1)S(1)} %act_slots.1.act_ref), custom_call_target="tpu_custom_call" | custom-call | flops 7150000128 | bytes 1 | tf_op jit(solution)/shard_map/encoder_part/pallas_call | solution.py:473
  (112 shorter events, 47.8 us)
Async XLA Ops:
  2.2 12.6 %collective-permute-start.2 = (bf16[272,128]{1,0:T(8,128)(2,1)S(1)}, bf16[272,128]{1,0:T(8,128)(2,1)S(1)}, u32[]{:S(2)}, u32[]{:S(2)}) collective-permute-start(bf16[272,128]{1,0:T(8,128)(2,1)S(1)} %fusion.21.refs_0_), channel_id=1, source_target_pairs={{0,6},{2,4},{4,2},{6,0},{1,7},{3,5},{5,3},{7,1},{8,14},{10,12},{12... | collective-permute-start | bytes 208904 | tf_op jit(solution)/shard_map/ppermute | solution.py:103
  6.4 8.3 %collective-permute-start.1 = (bf16[272,128]{1,0:T(8,128)(2,1)S(1)}, bf16[272,128]{1,0:T(8,128)(2,1)S(1)}, u32[]{:S(2)}, u32[]{:S(2)}) collective-permute-start(bf16[272,128]{1,0:T(8,128)(2,1)S(1)} %fusion.21.refs_0_), channel_id=1, source_target_pairs={{0,4},{2,6},{4,0},{6,2},{1,5},{3,7},{5,1},{7,3},{8,12},{10,14},{12... | collective-permute-start | bytes 208904 | tf_op jit(solution)/shard_map/ppermute | solution.py:103
  6.4 8.3 %collective-permute-start = (bf16[272,128]{1,0:T(8,128)(2,1)S(1)}, bf16[272,128]{1,0:T(8,128)(2,1)S(1)}, u32[]{:S(2)}, u32[]{:S(2)}) collective-permute-start(bf16[272,128]{1,0:T(8,128)(2,1)S(1)} %fusion.21.refs_0_), channel_id=1, source_target_pairs={{0,2},{2,0},{4,6},{6,4},{1,3},{3,1},{5,7},{7,5},{8,10},{10,8},{12,... | collective-permute-start | bytes 208904 | tf_op jit(solution)/shard_map/ppermute | solution.py:103
  15.1 26.1 %collective-permute-start.7 = (bf16[256,2048]{1,0:T(8,128)(2,1)S(1)}, bf16[256,2048]{1,0:T(8,128)(2,1)S(1)}, u32[]{:S(2)}, u32[]{:S(2)}) collective-permute-start(bf16[256,2048]{1,0:T(8,128)(2,1)S(1)} %pad_maximum_fusion.refs_0_.refs_1_), channel_id=1, source_target_pairs={{2,0},{4,2},{6,4},{3,1},{5,3},{7,5},{10,8},{12,10},{14,12},{11,9},... | collective-permute-start | bytes 3145736 | tf_op jit(solution)/shard_map/ppermute | solution.py:112
  16.4 25.7 %collective-permute-start.6 = (bf16[256,2048]{1,0:T(8,128)(2,1)S(1)}, bf16[256,2048]{1,0:T(8,128)(2,1)S(1)}, u32[]{:S(2)}, u32[]{:S(2)}) collective-permute-start(bf16[256,2048]{1,0:T(8,128)(2,1)S(1)} %pad_maximum_fusion.refs_0_.refs_1_), channel_id=1, source_target_pairs={{0,2},{2,4},{4,6},{1,3},{3,5},{5,7},{8,10},{10,12},{12,14},{9,11},... | collective-permute-start | bytes 3145736 | tf_op jit(solution)/shard_map/ppermute | solution.py:112
  25.5 27.5 %collective-permute-start.5 = (bf16[1024,512]{1,0:T(8,128)(2,1)S(1)}, bf16[1024,512]{1,0:T(8,128)(2,1)S(1)}, u32[]{:S(2)}, u32[]{:S(2)}) collective-permute-start(bf16[1024,512]{1,0:T(8,128)(2,1)S(1)} %fusion.8), channel_id=1, source_target_pairs={{0,8},{8,0},{16,24},{24,16},{1,9},{9,1},{17,25},{25,17},{2,10},{10... | collective-permute-start | bytes 3145736 | tf_op jit(solution)/shard_map/ppermute | solution.py:103
  29.3 23.4 %collective-permute-start.9 = (bf16[1024,512]{1,0:T(8,128)(2,1)S(1)}, bf16[1024,512]{1,0:T(8,128)(2,1)S(1)}, u32[]{:S(2)}, u32[]{:S(2)}) collective-permute-start(bf16[1024,512]{1,0:T(8,128)(2,1)S(1)} %fusion.14), channel_id=1, source_target_pairs={{0,16},{8,24},{16,0},{24,8},{1,17},{9,25},{17,1},{25,9},{2,18},{10... | collective-permute-start | bytes 3145736 | tf_op jit(solution)/shard_map/ppermute | solution.py:103
  42.1 22.1 %collective-permute-start.12 = (bf16[256,2048]{1,0:T(8,128)(2,1)S(1)}, bf16[256,2048]{1,0:T(8,128)(2,1)S(1)}, u32[]{:S(2)}, u32[]{:S(2)}) collective-permute-start(bf16[256,2048]{1,0:T(8,128)(2,1)S(1)} %collective-permute-done.6.refs_6_), channel_id=1, source_target_pairs={{2,4},{4,6},{3,5},{5,7},{10,12},{12,14},{11,13},{13,15},{18,20},{2... | collective-permute-start | bytes 3145736 | tf_op jit(solution)/shard_map/ppermute | solution.py:112
  42.9 28.1 %collective-permute-start.13 = (bf16[256,2048]{1,0:T(8,128)(2,1)S(1)}, bf16[256,2048]{1,0:T(8,128)(2,1)}, u32[]{:S(2)}, u32[]{:S(2)}) collective-permute-start(bf16[256,2048]{1,0:T(8,128)(2,1)S(1)} %collective-permute-done.7.refs_2_), channel_id=1, source_target_pairs={{2,0},{4,2},{3,1},{5,3},{10,8},{12,10},{11,9},{13,11},{18,16},{20,... | collective-permute-start | bytes 3145736 | tf_op jit(solution)/shard_map/ppermute | solution.py:112
  52.8 11.3 %collective-permute-start.10 = (bf16[1024,256]{1,0:T(8,128)(2,1)S(1)}, bf16[1024,256]{1,0:T(8,128)(2,1)S(1)}, u32[]{:S(2)}, u32[]{:S(2)}) collective-permute-start(bf16[1024,256]{1,0:T(8,128)(2,1)S(1)} %add_convert_fusion), channel_id=1, source_target_pairs={{0,8},{8,0},{16,24},{24,16},{1,9},{9,1},{17,25},{25,17},{2,10},{10... | collective-permute-start | bytes 1572872 | tf_op jit(solution)/shard_map/ppermute | solution.py:103
  53.2 11.1 %collective-permute-start.8 = (bf16[1024,256]{1,0:T(8,128)(2,1)S(1)}, bf16[1024,256]{1,0:T(8,128)(2,1)S(1)}, u32[]{:S(2)}, u32[]{:S(2)}) collective-permute-start(bf16[1024,256]{1,0:T(8,128)(2,1)S(1)} %add_convert_fusion.1), channel_id=1, source_target_pairs={{0,16},{8,24},{16,0},{24,8},{1,17},{9,25},{17,1},{25,9},{2,18},{10... | collective-permute-start | bytes 1572872 | tf_op jit(solution)/shard_map/ppermute | solution.py:103
  71.3 6.9 %collective-permute-start.14 = (bf16[256,512]{1,0:T(8,128)(2,1)S(1)}, bf16[256,512]{1,0:T(8,128)(2,1)}, u32[]{:S(2)}, u32[]{:S(2)}) collective-permute-start(bf16[256,512]{1,0:T(8,128)(2,1)S(1)} %get-tuple-element.76), channel_id=1, source_target_pairs={{0,2},{2,0},{4,6},{6,4},{1,3},{3,1},{5,7},{7,5},{8,10},{10,8},{12,... | collective-permute-start | bytes 786440 | tf_op jit(solution)/shard_map/ppermute | solution.py:103
  72.6 18.8 %collective-permute-start.15 = (bf16[256,512]{1,0:T(8,128)(2,1)S(1)}, bf16[256,512]{1,0:T(8,128)(2,1)}, u32[]{:S(2)}, u32[]{:S(2)}) collective-permute-start(bf16[256,512]{1,0:T(8,128)(2,1)S(1)} %get-tuple-element.77), channel_id=1, source_target_pairs={{0,4},{2,6},{4,0},{6,2},{1,5},{3,7},{5,1},{7,3},{8,12},{10,14},{12... | collective-permute-start | bytes 786440 | tf_op jit(solution)/shard_map/ppermute | solution.py:103
  72.6 18.8 %collective-permute-start.16 = (bf16[256,512]{1,0:T(8,128)(2,1)S(1)}, bf16[256,512]{1,0:T(8,128)(2,1)}, u32[]{:S(2)}, u32[]{:S(2)}) collective-permute-start(bf16[256,512]{1,0:T(8,128)(2,1)S(1)} %get-tuple-element.78), channel_id=1, source_target_pairs={{0,6},{2,4},{4,2},{6,0},{1,7},{3,5},{5,3},{7,1},{8,14},{10,12},{12... | collective-permute-start | bytes 786440 | tf_op jit(solution)/shard_map/ppermute | solution.py:103
  92.8 11.8 %collective-permute-start.21 = (bf16[256,512]{1,0:T(8,128)(2,1)S(1)}, bf16[256,512]{1,0:T(8,128)(2,1)S(1)}, u32[]{:S(2)}, u32[]{:S(2)}) collective-permute-start(bf16[256,512]{1,0:T(8,128)(2,1)S(1)} %multiply_convert_fusion.refs_0_), channel_id=1, source_target_pairs={{0,2},{2,0},{4,6},{6,4},{1,3},{3,1},{5,7},{7,5},{8,10},{10,8},{12,... | collective-permute-start | bytes 786440 | tf_op jit(solution)/shard_map/ppermute | solution.py:103
  98.8 18.6 %collective-permute-start.20 = (bf16[256,512]{1,0:T(8,128)(2,1)S(1)}, bf16[256,512]{1,0:T(8,128)(2,1)S(1)}, u32[]{:S(2)}, u32[]{:S(2)}) collective-permute-start(bf16[256,512]{1,0:T(8,128)(2,1)S(1)} %multiply_convert_fusion.refs_0_), channel_id=1, source_target_pairs={{0,4},{2,6},{4,0},{6,2},{1,5},{3,7},{5,1},{7,3},{8,12},{10,14},{12... | collective-permute-start | bytes 786440 | tf_op jit(solution)/shard_map/ppermute | solution.py:103
  98.8 18.6 %collective-permute-start.19 = (bf16[256,512]{1,0:T(8,128)(2,1)S(1)}, bf16[256,512]{1,0:T(8,128)(2,1)S(1)}, u32[]{:S(2)}, u32[]{:S(2)}) collective-permute-start(bf16[256,512]{1,0:T(8,128)(2,1)S(1)} %multiply_convert_fusion.refs_0_), channel_id=1, source_target_pairs={{0,6},{2,4},{4,2},{6,0},{1,7},{3,5},{5,3},{7,1},{8,14},{10,12},{12... | collective-permute-start | bytes 786440 | tf_op jit(solution)/shard_map/ppermute | solution.py:103
  100.9 16.5 %collective-permute-start.18 = (bf16[256,512]{1,0:T(8,128)(2,1)S(1)}, bf16[256,512]{1,0:T(8,128)(2,1)S(1)}, u32[]{:S(2)}, u32[]{:S(2)}) collective-permute-start(bf16[256,512]{1,0:T(8,128)(2,1)S(1)} %multiply_convert_fusion.refs_0_), channel_id=1, source_target_pairs={{0,8},{8,0},{16,24},{24,16},{1,9},{9,1},{17,25},{25,17},{2,10},{10... | collective-permute-start | bytes 786440 | tf_op jit(solution)/shard_map/ppermute | solution.py:103
  102.1 15.3 %collective-permute-start.17 = (bf16[256,512]{1,0:T(8,128)(2,1)S(1)}, bf16[256,512]{1,0:T(8,128)(2,1)S(1)}, u32[]{:S(2)}, u32[]{:S(2)}) collective-permute-start(bf16[256,512]{1,0:T(8,128)(2,1)S(1)} %multiply_convert_fusion.refs_0_), channel_id=1, source_target_pairs={{0,16},{8,24},{16,0},{24,8},{1,17},{9,25},{17,1},{25,9},{2,18},{10... | collective-permute-start | bytes 786440 | tf_op jit(solution)/shard_map/ppermute | solution.py:103
  118.5 15.2 %collective-permute-start.23 = (bf16[768,512]{1,0:T(8,128)(2,1)}, bf16[768,512]{1,0:T(8,128)(2,1)S(1)}, u32[]{:S(2)}, u32[]{:S(2)}) collective-permute-start(bf16[768,512]{1,0:T(8,128)(2,1)} %join.3.refs_1_), channel_id=1, source_target_pairs={{0,8},{8,0},{16,24},{24,16},{1,9},{9,1},{17,25},{25,17},{2,10},{10... | collective-permute-start | bytes 2359304 | tf_op jit(solution)/shard_map/ppermute | solution.py:103
  119.6 14.9 %collective-permute-start.22 = (bf16[768,512]{1,0:T(8,128)(2,1)}, bf16[768,512]{1,0:T(8,128)(2,1)S(1)}, u32[]{:S(2)}, u32[]{:S(2)}) collective-permute-start(bf16[768,512]{1,0:T(8,128)(2,1)} %join.3.refs_1_), channel_id=1, source_target_pairs={{0,16},{8,24},{16,0},{24,8},{1,17},{9,25},{17,1},{25,9},{2,18},{10... | collective-permute-start | bytes 2359304 | tf_op jit(solution)/shard_map/ppermute | solution.py:103
  121.1 28.0 %collective-permute-start.26 = (bf16[256,2048]{1,0:T(8,128)(2,1)}, bf16[256,2048]{1,0:T(8,128)(2,1)S(1)}, u32[]{:S(2)}, u32[]{:S(2)}) collective-permute-start(bf16[256,2048]{1,0:T(8,128)(2,1)} %broadcast_select_fusion), channel_id=1, source_target_pairs={{4,6},{2,0},{5,7},{3,1},{12,14},{10,8},{13,15},{11,9},{20,22},{18,... | collective-permute-start | bytes 3145736 | tf_op jit(solution)/shard_map/ppermute | solution.py:581
  134.7 18.9 %collective-permute-start.25 = (bf16[1024,256]{1,0:T(8,128)(2,1)S(1)}, bf16[1024,256]{1,0:T(8,128)(2,1)S(1)}, u32[]{:S(2)}, u32[]{:S(2)}) collective-permute-start(bf16[1024,256]{1,0:T(8,128)(2,1)S(1)} %pad_maximum_fusion.3), channel_id=1, source_target_pairs={{0,16},{8,24},{16,0},{24,8},{1,17},{9,25},{17,1},{25,9},{2,18},{10... | collective-permute-start | bytes 1572872 | tf_op jit(solution)/shard_map/ppermute | solution.py:103
  136.0 17.6 %collective-permute-start.24 = (bf16[1024,256]{1,0:T(8,128)(2,1)S(1)}, bf16[1024,256]{1,0:T(8,128)(2,1)S(1)}, u32[]{:S(2)}, u32[]{:S(2)}) collective-permute-start(bf16[1024,256]{1,0:T(8,128)(2,1)S(1)} %pad_maximum_fusion.2), channel_id=1, source_target_pairs={{0,8},{8,0},{16,24},{24,16},{1,9},{9,1},{17,25},{25,17},{2,10},{10... | collective-permute-start | bytes 1572872 | tf_op jit(solution)/shard_map/ppermute | solution.py:103
  (23 other events, 199.4 us)

commit v13 on v12

--- a/solution.py
+++ b/solution.py
@@ -146,12 +146,12 @@
             out_specs=[pl.BlockSpec((rows, width), lambda i, s: (0, i)), resident((8, 128))],
         ),
         compiler_params=params(),
-        cost_estimate=cost(0.9 * count),
+        cost_estimate=cost(0.01 * count),
         name="gather_columns",
     )(columns.astype(jnp.int32), source)
 
 
-def codes_kernel(groups, blocks, scalar_ref, message_ref, codes, id_map, pre):
+def codes_kernel(groups, blocks, scalar_ref, message_ref, own_ref, rest_ref, id_map, pre):
     tok = message_ref.shape[2]
     pad = message_ref.shape[1] - 2 * tok
     first = scalar_ref[0].astype(jnp.float32)
@@ -173,7 +173,8 @@
         for g in range(groups):
             value = jnp.where(id_map[g, tok:2 * tok, :] == block, pre[g, tok:2 * tok, :], jnp.zeros((), jnp.bfloat16))
             value = jnp.where(id_map[g, 0:tok, :] == block, pre[g, 0:tok, :], value)
-            codes[g * tok:(g + 1) * tok, pl.ds(at, tok)] = value
+            to, n = (own_ref, g) if g < 2 else (rest_ref, g - 2)
+            to[n * tok:(n + 1) * tok, pl.ds(at, tok)] = value
         return carry
 
     lax.fori_loop(0, blocks, block_step, 0)
@@ -181,15 +182,15 @@
 
 def spread_codes(message, first, lat_rows):
     groups, _, tok = message.shape
-    rows = groups * tok
+    shapes = [(2 * tok, lat_rows), ((groups - 2) * tok, lat_rows)]
     return pl.pallas_call(
         functools.partial(codes_kernel, groups, lat_rows // tok),
-        out_shape=jax.ShapeDtypeStruct((rows, lat_rows), jnp.bfloat16),
+        out_shape=[jax.ShapeDtypeStruct(shape, jnp.bfloat16) for shape in shapes],
         grid_spec=pltpu.PrefetchScalarGridSpec(
             num_scalar_prefetch=1,
             grid=(1,),
             in_specs=[resident(message.shape)],
-            out_specs=resident((rows, lat_rows)),
+            out_specs=[resident(shape) for shape in shapes],
             scratch_shapes=[
                 pltpu.VMEM((groups, 2 * tok, tok), jnp.bfloat16),
                 pltpu.VMEM((groups, 2 * tok, tok), jnp.bfloat16),
@@ -201,30 +202,27 @@
     )(first[None].astype(jnp.int32), message)
 
 
-def layer_sum_kernel(got_a, kept_a, far_a, got_b, kept_b, far_b, own_ref, *sent_refs):
+def layer_sum_kernel(got_a, kept_a, far_a, got_b, kept_b, far_b, *sent_refs):
     half = far_a.shape[1]
-    rows = own_ref.shape[0]
+    rows = sent_refs[0].shape[0]
     for side, (got, kept, far) in enumerate(((got_a, kept_a, far_a), (got_b, kept_b, far_b))):
         lanes = slice(side * half, (side + 1) * half)
-        for n in range(1 + len(sent_refs)):
+        for n, sent_ref in enumerate(sent_refs):
             at = slice(n * rows, (n + 1) * rows)
             total = got[at, :half].astype(jnp.float32) + kept[at, :half].astype(jnp.float32)
             total = total + far[at, :].astype(jnp.float32)
-            if n:
-                sent_refs[n - 1][:, lanes] = total.astype(jnp.bfloat16)
-            else:
-                own_ref[:, lanes] = total
+            sent_ref[:, lanes] = total.astype(jnp.bfloat16)
 
 
 def layer_sum(terms_a, terms_b, blocks):
     rows, half = terms_a[2].shape
     cut = (rows // blocks, 2 * half)
+    vmem = pl.BlockSpec(memory_space=pltpu.VMEM)
     return pl.pallas_call(
         layer_sum_kernel,
-        out_shape=[jax.ShapeDtypeStruct(cut, jnp.float32)] + [jax.ShapeDtypeStruct(cut, jnp.bfloat16)] * (blocks - 1),
-        grid=(1,),
-        in_specs=[pl.BlockSpec((rows, half), lambda i: (0, 0)) for _ in range(6)],
-        out_specs=[pl.BlockSpec(cut, lambda i: (0, 0))] * blocks,
+        out_shape=[jax.ShapeDtypeStruct(cut, jnp.bfloat16)] * blocks,
+        in_specs=[vmem] * 6,
+        out_specs=[vmem] * blocks,
         compiler_params=params(),
         cost_estimate=cost(0.5),
         name="layer_sum",
@@ -306,7 +304,7 @@
             out_specs=[resident(shape) for shape in shapes],
         ),
         compiler_params=params(),
-        cost_estimate=cost(1),
+        cost_estimate=cost(0.01),
         name="make_slots",
     )(first[None].astype(jnp.int32), message)
 
@@ -414,33 +412,37 @@
     )(columns.astype(jnp.int32), codes, slots, *onto)
 
 
-def act_slots_kernel(scalar_ref, hot_ref, *refs):
-    out_ref = refs[-1]
-    shards = hot_ref.shape[0]
-    per = out_ref.shape[1] // shards
-    for i in range(shards):
+def act_slots_kernel(scalar_ref, hot_ref, own_ref, down_ref, up_ref, *refs):
+    middle, ends, out_ref = refs[:2], refs[2:4], refs[4]
+    per = out_ref.shape[1] // hot_ref.shape[0]
+    last = jnp.concatenate([ref[...] for ref in ends], axis=0)
+    zero = jnp.zeros((), last.dtype)
+    rows = [
+        own_ref[...],
+        down_ref[...] + jnp.where(scalar_ref[4] > 0, last, zero),
+        jnp.concatenate([ref[...] for ref in middle], axis=0),
+        up_ref[...] + jnp.where(scalar_ref[5] > 0, last, zero),
+    ]
+    for i in range(4):
         z = scalar_ref[i]
-        rows, more = refs[2 * i][...], refs[2 * i + 1][...]
-        rows = rows + jnp.where(scalar_ref[shards + i] > 0, more, jnp.zeros((), more.dtype))
-        value = jnp.dot(hot_ref[z], rows, preferred_element_type=jnp.float32).astype(jnp.bfloat16)
+        value = jnp.dot(hot_ref[z], rows[i], preferred_element_type=jnp.float32).astype(jnp.bfloat16)
         to = pl.ds(pl.multiple_of(z * per, per), per)
         for b in range(out_ref.shape[0]):
             out_ref[b, to, :] = value[b * per:(b + 1) * per]
 
 
-def act_slots(terms_of, places, flags, hot, count):
-    group, half = terms_of[0][0].shape
+def act_slots(own, down, up, middle, ends, scalars, hot, count):
+    half = own.shape[1]
     slots = hot.shape[0] * hot.shape[1] // count
     tile = half // 4
-    flat = [term for terms in terms_of for term in terms]
-    scalars = jnp.stack([jnp.asarray(x, jnp.int32) for x in (*places, *flags)])
+    flat = [own, down, up, *middle, *ends]
     return pl.pallas_call(
         act_slots_kernel,
         out_shape=jax.ShapeDtypeStruct((count, slots, half), jnp.bfloat16),
         grid_spec=pltpu.PrefetchScalarGridSpec(
             num_scalar_prefetch=1,
             grid=(4,),
-            in_specs=[resident(hot.shape)] + [pl.BlockSpec((group, tile), lambda i, s: (0, i)) for _ in flat],
+            in_specs=[resident(hot.shape)] + [pl.BlockSpec((part.shape[0], tile), lambda i, s: (0, i)) for part in flat],
             out_specs=pl.BlockSpec((count, slots, tile), lambda i, s: (0, 0, i)),
         ),
         compiler_params=params(),
@@ -525,27 +527,20 @@
     acts = jnp.concatenate([columns(inputs, dp_here), flip(columns(inputs, 1 - dp_here), "dp", 1)])
     message, acts = lax.optimization_barrier((join(message, token), acts))
     message = message.reshape((lat_count,) + own.shape)
-    up, down = [acts], [acts]
-
-    def next_hops():
-        step = len(up)
-        up.append(hop(up[-1], "latent", 1, step - 1))
-        down.append(hop(down[-1], "latent", -1, step - 1))
-
     message = jnp.stack([message, flip(message, "dp", 1)], axis=1)
     message = message.reshape(lat_count * dp_count, own.shape[0], block_size)
-    next_hops()
-
-    codes = spread_codes(message, first, lat_rows)
+    up, down = hop(acts, "latent", 1, 0), hop(acts, "latent", -1, 0)
+
+    here, rest = spread_codes(message, first, lat_rows)
     at = places((0, 2), dp_here * lay_count, 2, 0) + places((0, 1), dp_here * lay_count, 2, 1)
-    at, codes, target = lax.optimization_barrier((jnp.stack(at), codes, target))
+    at, rest, target = lax.optimization_barrier((jnp.stack(at), rest, target))
     keep_weights, _ = gather_columns(decoder, at, side)
     goals, _ = gather_columns(target, jnp.stack([which * lay_count + lay_here for which in (dp_here, 1 - dp_here)]), width)
     goals = jnp.concatenate([goals[:, :width], flip(goals[:, width:], "dp", 1)])
 
-    codes = spread_codes(message, first, lat_rows)
+    here, rest = spread_codes(message, first, lat_rows)
     at = places((0, 2), dp_here * lay_count, 2, 0) + places((0, 1), dp_here * lay_count, 2, 1)
-    at, codes, target = lax.optimization_barrier((jnp.stack(at), codes, target))
+    at, rest, target = lax.optimization_barrier((jnp.stack(at), rest, target))
     keep_weights, _ = gather_columns(decoder, at, side)
     goals, _ = gather_columns(target, jnp.stack([which * lay_count + lay_here for which in (dp_here, 1 - dp_here)]), width)
     goals = jnp.concatenate([goals[:, :width], flip(goals[:, width:], "dp", 1)])
@@ -553,33 +548,48 @@
     def rows_for(spread, weights, n):
         return jnp.dot(spread, weights[:, n * width:(n + 1) * width], preferred_element_type=f32).astype(bf16)
 
-    got = flip(rows_for(codes, send_weights, 0), "layer", 1), flip(rows_for(codes, send_weights, 1), "layer", 2)
-    keep_codes, up[1], down[1] = lax.optimization_barrier((codes, up[1], down[1]))
-    if lat_count > 2:
-        next_hops()
-    kept = rows_for(keep_codes, keep_weights, 0), rows_for(keep_codes, keep_weights, 1)
-
     def add(one, two):
         return (one[:, side:].astype(f32) + two[:, side:].astype(f32)).astype(bf16)
 
+    got = flip(rows_for(rest, send_weights, 0), "layer", 1), flip(rows_for(rest, send_weights, 1), "layer", 2)
+    keep_rest, up, down = lax.optimization_barrier((rest, up, down))
+    cuts = slice(0, tok_count), slice(tok_count, group)
+    ups, downs = [up[cut] for cut in cuts], [down[cut] for cut in cuts]
+    up_two, down_two = [hop(ups[0], "latent", 1, 1)], [hop(downs[0], "latent", -1, 1)]
+    kept = rows_for(keep_rest, keep_weights, 0), rows_for(keep_rest, keep_weights, 1)
     far = [flip(add(got[n], kept[n]), "layer", 2 - n) for n in range(2)]
+    sent_here = rows_for(here, send_weights, 0), rows_for(here, send_weights, 1)
+    kept_here = rows_for(here, keep_weights, 0), rows_for(here, keep_weights, 1)
     made = make_slots(message, first, lat_rows, capacity)
-    far, goals, up[-1], down[-1], made = lax.optimization_barrier((far, goals, up[-1], down[-1], made))
-    while len(up) < lat_count - 1:
-        next_hops()
-    relay = jnp.where(lat_here == 1, down[-1], up[-1])
-
-    total, *sent = layer_sum((got[0], kept[0], far[0]), (got[1], kept[1], far[1]), lat_count)
-    for r in range(1, lat_count):
-        total = total + flip(sent[r - 1], "latent", r).astype(f32)
+    made, goals, sent_here, kept_here, up_two, down_two, ups[1], downs[1], far = lax.optimization_barrier(
+        (made, goals, sent_here, kept_here, up_two, down_two, ups[1], downs[1], far)
+    )
+
+    sent = layer_sum((got[0], kept[0], far[0]), (got[1], kept[1], far[1]), lat_count - 1)
+    came = [flip(sent[r - 1], "latent", r) for r in range(1, lat_count)]
+    got_here = flip(sent_here[0], "layer", 1), flip(sent_here[1], "layer", 2)
+    far = [flip(add(got_here[n], kept_here[n]), "layer", 2 - n) for n in range(2)]
+    relay = jnp.where(lat_here == 1, down_two[0], up_two[0])
+    far, relay, came = lax.optimization_barrier((far, relay, came[::-1]))
+    total = [got_here[n][:, :side].astype(f32) + kept_here[n][:, :side].astype(f32) + far[n].astype(f32) for n in range(2)]
+    total = jnp.concatenate(total, axis=1)
+    for block in came:
+        total = total + block.astype(f32)
     errors = ((total - goals.astype(f32)) / tok_count).astype(bf16)
     others = [flip(errors, "latent", r) for r in range(1, lat_count)]
     one_near, two_near = flip(errors, "layer", 1), flip(errors, "layer", 2)
-    relay, two_near, one_near, others = lax.optimization_barrier((relay, two_near, one_near, others[::-1]))
-    distant = join(others[::-1])
+    others, one_near, two_near, relay, ups[1], downs[1] = lax.optimization_barrier(
+        (others, one_near, two_near, relay, ups[1], downs[1])
+    )
+    distant = join(others)
     one_far, two_far = flip(distant, "layer", 1), flip(distant, "layer", 2)
-    ends = lax.ppermute(relay, "latent", [(lat_count - 2, lat_count - 1), (1, 0)])
-
+    up_two.append(hop(ups[1], "latent", 1, 1))
+    down_two.append(hop(downs[1], "latent", -1, 1))
+
+    def last_hop(value):
+        return lax.ppermute(value, "latent", [(lat_count - 2, lat_count - 1), (1, 0)])
+
+    ends = [last_hop(relay)]
     hot, pre_slots, code_slots = made
 
     def grads_of(here, names, grad, dec):
@@ -587,21 +597,19 @@
         return grad, decoder_part(slots, code_slots, jnp.stack(places(names, 0)), half, dec)
 
     grad, dec = grads_of([[(errors,), (distant,)]], (0,), None, None)
-    grad, dec, two_far, one_far = lax.optimization_barrier((grad, dec, two_far, one_far))
+    grad, dec, up_two[1], down_two[1], two_far, one_far = lax.optimization_barrier(
+        (grad, dec, up_two[1], down_two[1], two_far, one_far)
+    )
+    ends.append(last_hop(jnp.where(lat_here == 1, down_two[1], up_two[1])))
     three_a = flip(jnp.concatenate([two_near[:, :side], two_far[:, :side]]), "layer", 1)
     three_b = flip(jnp.concatenate([one_near[:, side:], one_far[:, side:]]), "layer", 2)
     grad, dec = grads_of([[(one_near,), (one_far,)], [(two_near,), (two_far,)]], (1, 2), grad, dec)
 
-    down_end, up_end = lat_here == 0, lat_here == lat_count - 1
-    terms_of = [[acts, acts]]
-    flags = [False]
-    for k in range(1, lat_count):
-        last = k == 1 or k == lat_count - 1
-        terms_of.append([(down if k == 1 else up)[1] if last else down[k], ends if last else up[lat_count - k]])
-        flags.append(True if not last else up_end if k == 1 else down_end)
-    shards = [lax.rem(lat_here + k, lat_count) ^ lat_here for k in range(lat_count)]
-    slotted = act_slots(terms_of, shards, flags, hot, local_blocks)
-    three_a, three_b, grad, dec, slotted = lax.optimization_barrier((three_a, three_b, grad, dec, slotted))
+    middle = [down_two[part] + up_two[part] for part in range(2)]
+    scalars = [lax.rem(lat_here + k, lat_count) ^ lat_here for k in range(lat_count)]
+    scalars = jnp.stack(scalars + [(lat_here == lat_count - 1).astype(jnp.int32), (lat_here == 0).astype(jnp.int32)])
+    slotted = act_slots(acts, down, up, middle, ends, scalars, hot, local_blocks)
+    grad, dec, three_b, three_a = lax.optimization_barrier((grad, dec, three_b, three_a))
     grad, dec = grads_of([[(three_a, three_b)]], (3,), grad, dec)
     enc = encoder_part(pre_slots, grad, flip(grad, "dp", 1), slotted, capacity)
     return dec[None], enc[None]
@@ -622,8 +630,7 @@
         and dp_count == 2
         and active_count == 2
         and lay_count == 4
-        and lat_count > 3
-        and lat_count & (lat_count - 1) == 0
+        and lat_count == 4
         and tok_count == block_size
         and lat_count * dp_count * 16 <= tok_count
         and model_width % (dp_count * 2 * lay_count * 128) == 0

time: 170 us -> 180 us (1.059)
  local copies, waits for them, and re-layouts: 3.35 us -> 12.1 us
  waiting for transfers between devices: 58.6 us -> 54.3 us
  matrix products: 11.1 us -> 14.7 us
  other arithmetic: 4.78 us -> 6.75 us
    unnamed x34 -> x58, local copies, waits for them, and re-layouts: 0.08 us -> 7.03 us
    ppermute x1 -> x2, waiting for transfers between devices: 4.64 us -> 0.01 us  [last_hop(): lax.ppermute(value, 'latent', [(lat_count - 2, lat_count - 1), (1, 0)])]
    dot_general x4 -> x8, matrix products: 11.1 us -> 14.7 us  [rows_for(): jnp.dot(spread, weights[:, n * width:(n + 1) * width], preferred_element_...]
    add x0 -> x2, other arithmetic: none -> 2.04 us  [the longest x1 1.05 us: dense_plan(): middle = [down_two[part] + up_two[part] for part in range(2)]]
    ppermute x23 -> x27, starting transfers between devices: 34.9 us -> 33 us  [flip(): return lax.ppermute(value, axis, [(i, i ^ bit) for i in range(count)])]
    ppermute x4 -> x6, waiting for transfers between devices: 12.9 us -> 14.8 us  [hop(): return lax.ppermute(value, axis, pairs)]
    ppermute x4 -> x6, starting transfers between devices: 7.52 us -> 9.36 us  [hop(): return lax.ppermute(value, axis, pairs)]
    ppermute x23 -> x27, waiting for transfers between devices: 41 us -> 39.5 us  [flip(): return lax.ppermute(value, axis, [(i, i ^ bit) for i in range(count)])]
  transfers between devices with their start and end apart: 28 -> 35, of which waited for: 12 -> 9; matrix products, arithmetic and copies ran while one was open for 10% -> 13% of each run, Pallas kernels for 21% -> 21%
where the time goes in v13:
time: 180 us; the launch traced here: 178 us
  waiting for transfers between devices  54.3 us (30%)
  starting transfers between devices  44.9 us (25%)
  Pallas kernels  44 us (24%)
  matrix products  14.7 us (8%)
  local copies, waits for them, and re-layouts  12.1 us (7%)
  other arithmetic  6.75 us (4%)
    ppermute x27, waiting for transfers between devices, flip(): return lax.ppermute(value, axis, [(i, i ^ bit) for i in range(count)])  39.5 us
    ppermute x27, starting transfers between devices, flip(): return lax.ppermute(value, axis, [(i, i ^ bit) for i in range(count)])  33 us
    ppermute x6, waiting for transfers between devices, hop(): return lax.ppermute(value, axis, pairs)  14.8 us
    dot_general x8, matrix products, rows_for(): jnp.dot(spread, weights[:, n * width:(n + 1) * width], preferred_element_...  14.7 us
    pallas_call x3, Pallas kernels, gather_columns(): pl.pallas_call(gather_kernel, out_shape=[pltpu.HBM((rows, count * width),...  11.9 us
    pallas_call x3, Pallas kernels, piece_grad(): pl.pallas_call(functools.partial(piece_grad_kernel, [[len(row) for row in...  10.5 us
    ppermute x6, starting transfers between devices, hop(): return lax.ppermute(value, axis, pairs)  9.36 us
    pallas_call x3, Pallas kernels, decoder_part(): pl.pallas_call(functools.partial(decoder_kernel, len(onto)), out_shape=ja...  7.28 us
  transfers between devices with their start and end apart: 35, of which 9 were waited for; matrix products, arithmetic and copies ran while one was open for 13% of the time, Pallas kernels for 21%

profile of v13, /device:TPU:1, one launch (start us, length us, event | category | flops | bytes accessed | tf_op | source)
XLA Modules:
  0.0 177.9 jit_solution(16401765658059986596)
XLA Ops:
  3.6 2.8 %collective-permute-start = (bf16[272,128]{1,0:T(8,128)(2,1)S(1)}, bf16[272,128]{1,0:T(8,128)(2,1)S(1)}, u32[]{:S(2)}, u32[]{:S(2)}) collective-permute-start(bf16[272,128]{1,0:T(8,128)(2,1)S(1)} %fusion.46.refs_0_), channel_id=1, source_target_pairs={{0,2},{2,0},{4,6},{6,4},{1,3},{3,1},{5,7},{7,5},{8,10},{10,8},{12,... | collective-permute-start | bytes 208904 | tf_op jit(solution)/shard_map/ppermute | solution.py:103
  6.4 2.3 %collective-permute-start.1 = (bf16[272,128]{1,0:T(8,128)(2,1)S(1)}, bf16[272,128]{1,0:T(8,128)(2,1)S(1)}, u32[]{:S(2)}, u32[]{:S(2)}) collective-permute-start(bf16[272,128]{1,0:T(8,128)(2,1)S(1)} %fusion.46.refs_0_), channel_id=1, source_target_pairs={{0,4},{2,6},{4,0},{6,2},{1,5},{3,7},{5,1},{7,3},{8,12},{10,14},{12... | collective-permute-start | bytes 208904 | tf_op jit(solution)/shard_map/ppermute | solution.py:103
  8.8 5.3 %gather_columns.3 = (bf16[2048,1024]{1,0:T(8,128)(2,1)}, f32[8,128]{1,0:T(8,128)S(1)}) custom-call(s32[4]{0:T(128)S(1)} %pad_add_fusion.scalar_ref, bf16[1,2048,4096]{2,1,0:T(8,128)(2,1)} %weight_ref.5), custom_call_target="tpu_custom_call" | custom-call | flops 44000000 | bytes 1 | tf_op jit(solution)/shard_map/gather_columns/pallas_call | solution.py:136
  15.8 3.2 %collective-permute-start.6 = (bf16[256,2048]{1,0:T(8,128)(2,1)S(1)}, bf16[256,2048]{1,0:T(8,128)(2,1)S(1)}, u32[]{:S(2)}, u32[]{:S(2)}) collective-permute-start(bf16[256,2048]{1,0:T(8,128)(2,1)S(1)} %pad_maximum_fusion.own_ref), channel_id=1, source_target_pairs={{0,2},{2,4},{4,6},{1,3},{3,5},{5,7},{8,10},{10,12},{12,14},{9,11},... | collective-permute-start | bytes 3145736 | tf_op jit(solution)/shard_map/ppermute | solution.py:112
  20.4 2.6 %spread_codes.1 = (bf16[256,2048]{1,0:T(8,128)(2,1)S(1)}, bf16[768,2048]{1,0:T(8,128)(2,1)S(1)}) custom-call(s32[1]{0:T(128)} %bitcast.1.scalar_ref, bf16[8,272,128]{2,1,0:T(8,128)(2,1)S(1)} %bitcast.49), custom_call_target="tpu_custom_call" | custom-call | flops 2750000128 | bytes 1 | tf_op jit(solution)/shard_map/spread_codes/pallas_call | solution.py:186
  24.8 1.8 %fusion.16 = bf16[768,512]{1,0:T(8,128)(2,1)S(1)} fusion(bf16[768,2048]{1,0:T(8,128)(2,1)S(1)} %get-tuple-element.86, bf16[2048,1024]{1,0:T(8,128)(2,1)S(1)} %copy-done.27), kind=kOutput, calls=%fused_computation.16 | convolution fusion | flops 1611005952 | bytes 6029312 | tf_op jit(solution)/shard_map/dot_general | solution.py:549
  32.4 5.3 %gather_columns.5 = (bf16[2048,1024]{1,0:T(8,128)(2,1)}, f32[8,128]{1,0:T(8,128)}) custom-call(s32[4]{0:T(128)S(1)} %pad_add_fusion.2.scalar_ref, bf16[1,2048,4096]{2,1,0:T(8,128)(2,1)} %weight_ref.5), custom_call_target="tpu_custom_call" | custom-call | flops 44000000 | bytes 1 | tf_op jit(solution)/shard_map/gather_columns/pallas_call | solution.py:136
  37.7 3.2 %fusion.37 = bf16[256,512]{1,0:T(8,128)(2,1)} fusion(bf16[256,2048]{1,0:T(8,128)(2,1)S(1)} %get-tuple-element.78, bf16[2048,1024]{1,0:T(8,128)(2,1)} %get-tuple-element.81), kind=kOutput, calls=%fused_computation.23 | convolution fusion | flops 537001984 | bytes 3407872 | tf_op jit(solution)/shard_map/dot_general | solution.py:549
  59.0 3.6 %collective-permute-done.13.far_b = bf16[768,256]{1,0:T(8,128)(2,1)S(1)} collective-permute-done((bf16[768,256]{1,0:T(8,128)(2,1)S(1)}, bf16[768,256]{1,0:T(8,128)(2,1)S(1)}, u32[]{:S(2)}, u32[]{:S(2)}) %collective-permute-start.13) | collective-permute-done | bytes 393248 | tf_op jit(solution)/shard_map/ppermute | solution.py:103
  73.5 3.0 %collective-permute-start.19 = (bf16[256,512]{1,0:T(8,128)(2,1)S(1)}, bf16[256,512]{1,0:T(8,128)(2,1)S(1)}, u32[]{:S(2)}, u32[]{:S(2)}) collective-permute-start(bf16[256,512]{1,0:T(8,128)(2,1)S(1)} %get-tuple-element.98), channel_id=1, source_target_pairs={{0,4},{2,6},{4,0},{6,2},{1,5},{3,7},{5,1},{7,3},{8,12},{10,14},{12... | collective-permute-start | bytes 786440 | tf_op jit(solution)/shard_map/ppermute | solution.py:103
  79.6 19.6 %collective-permute-done.19 = bf16[256,512]{1,0:T(8,128)(2,1)S(1)} collective-permute-done((bf16[256,512]{1,0:T(8,128)(2,1)S(1)}, bf16[256,512]{1,0:T(8,128)(2,1)S(1)}, u32[]{:S(2)}, u32[]{:S(2)}) %collective-permute-start.19) | collective-permute-done | bytes 262176 | tf_op jit(solution)/shard_map/ppermute | solution.py:103
  101.9 2.1 %collective-permute-start.23 = (bf16[256,512]{1,0:T(8,128)(2,1)S(1)}, bf16[256,512]{1,0:T(8,128)(2,1)S(1)}, u32[]{:S(2)}, u32[]{:S(2)}) collective-permute-start(bf16[256,512]{1,0:T(8,128)(2,1)S(1)} %fusion.44.refs_0_), channel_id=1, source_target_pairs={{0,6},{2,4},{4,2},{6,0},{1,7},{3,5},{5,3},{7,1},{8,14},{10,12},{12... | collective-permute-start | bytes 786440 | tf_op jit(solution)/shard_map/ppermute | solution.py:103
  104.3 7.8 %collective-permute-done.21.refs_0_ = bf16[256,512]{1,0:T(8,128)(2,1)S(1)} collective-permute-done((bf16[256,512]{1,0:T(8,128)(2,1)S(1)}, bf16[256,512]{1,0:T(8,128)(2,1)S(1)}, u32[]{:S(2)}, u32[]{:S(2)}) %collective-permute-start.21) | collective-permute-done | bytes 262176 | tf_op jit(solution)/shard_map/ppermute | solution.py:103
  112.1 7.8 %collective-permute-done.22.refs_1_ = bf16[256,512]{1,0:T(8,128)(2,1)S(1)} collective-permute-done((bf16[256,512]{1,0:T(8,128)(2,1)S(1)}, bf16[256,512]{1,0:T(8,128)(2,1)S(1)}, u32[]{:S(2)}, u32[]{:S(2)}) %collective-permute-start.22) | collective-permute-done | bytes 262176 | tf_op jit(solution)/shard_map/ppermute | solution.py:103
  126.8 2.9 %piece_grad.3 = (bf16[1,16,64,512]{3,2,1,0:T(8,128)(2,1)S(1)}, f32[16,64,128]{2,1,0:T(8,128)S(1)}) custom-call(s32[1]{0:T(128)} %bitcast.17.scalar_ref, bf16[4,256,256]{2,1,0:T(8,128)(2,1)S(1)} %get-tuple-element.88.hot_ref, bf16[1,2048,4096]{2,1,0:T(8,128)(2,1)} %weight_ref.5, bf16[256,512]{1,0:T(8,128)(2,1)S(1)} %fusion.44.refs_0_, ...), custom_call_target="tpu_custom_call" | custom-call | flops 3080000000 | bytes 1 | tf_op jit(solution)/shard_map/piece_grad/pallas_call | solution.py:363
  129.7 2.0 %decoder_part.3.refs_0_ = bf16[2048,2048]{1,0:T(8,128)(2,1)} custom-call(s32[1]{0:T(128)} %bitcast.26.scalar_ref, bf16[16,128,64]{2,1,0:T(8,128)(2,1)S(1)} %get-tuple-element.87.code_ref, bf16[1,16,64,512]{3,2,1,0:T(8,128)(2,1)S(1)} %get-tuple-element.113.slots_ref), custom_call_target="tpu_custom_call" | custom-call | flops 2200000000 | bytes 1 | tf_op jit(solution)/shard_map/decoder_part/pallas_call | solution.py:398
  131.7 12.9 %collective-permute-done.27 = bf16[128,2048]{1,0:T(8,128)(2,1)} collective-permute-done((bf16[128,2048]{1,0:T(8,128)(2,1)}, bf16[128,2048]{1,0:T(8,128)(2,1)}, u32[]{:S(2)}, u32[]{:S(2)}) %collective-permute-start.27) | collective-permute-done | bytes 524320 | tf_op jit(solution)/shard_map/ppermute | solution.py:112
  148.2 4.8 %piece_grad.4 = (bf16[2,16,64,512]{3,2,1,0:T(8,128)(2,1)S(1)}, f32[16,64,128]{2,1,0:T(8,128)S(1)}) custom-call(s32[2]{0:T(128)S(1)} %pad_add_fusion.3.scalar_ref, bf16[4,256,256]{2,1,0:T(8,128)(2,1)S(1)} %get-tuple-element.88.hot_ref, bf16[1,2048,4096]{2,1,0:T(8,128)(2,1)} %weight_ref.5, f32[16,64,128]{2,1,0:T(8,128)S(1)} %get-tuple-element.116.refs_0_, ...), custom_call_target="tpu_custom_call" | custom-call | flops 5280000000 | bytes 1 | tf_op jit(solution)/shard_map/piece_grad/pallas_call | solution.py:363
  153.0 3.3 %decoder_part.4.refs_0_ = bf16[2048,2048]{1,0:T(8,128)(2,1)} custom-call(s32[2]{0:T(128)S(1)} %pad_add_fusion.4.scalar_ref, bf16[16,128,64]{2,1,0:T(8,128)(2,1)S(1)} %get-tuple-element.87.code_ref, bf16[2,16,64,512]{3,2,1,0:T(8,128)(2,1)S(1)} %get-tuple-element.122.slots_ref, bf16[2048,2048]{1,0:T(8,128)(2,1)} %decoder_part.3.refs_0_), custom_call_target="tpu_custom_call", output_to_operand_aliasing={{}: (3, {})} | custom-call | flops 3630000128 | bytes 1 | tf_op jit(solution)/shard_map/decoder_part/pallas_call | solution.py:398
  156.5 2.8 %piece_grad.5 = (bf16[1,16,64,512]{3,2,1,0:T(8,128)(2,1)S(1)}, f32[16,64,128]{2,1,0:T(8,128)S(1)}) custom-call(s32[1]{0:T(128)} %bitcast.23.scalar_ref, bf16[4,256,256]{2,1,0:T(8,128)(2,1)S(1)} %get-tuple-element.88.hot_ref, bf16[1,2048,4096]{2,1,0:T(8,128)(2,1)} %weight_ref.5, f32[16,64,128]{2,1,0:T(8,128)S(1)} %get-tuple-element.124.refs_0_, ...), custom_call_target="tpu_custom_call" | custom-call | flops 3080000000 | bytes 1 | tf_op jit(solution)/shard_map/piece_grad/pallas_call | solution.py:363
  159.3 6.4 %collective-permute-start.32 = (f32[16,64,128]{2,1,0:T(8,128)S(1)}, f32[16,64,128]{2,1,0:T(8,128)S(1)}, u32[]{:S(2)}, u32[]{:S(2)}) collective-permute-start(f32[16,64,128]{2,1,0:T(8,128)S(1)} %get-tuple-element.130.own_ref), channel_id=1, source_target_pairs={{0,1},{1,0},{2,3},{3,2},{4,5},{5,4},{6,7},{7,6},{8,9},{9,8},{10,11... | collective-permute-start | bytes 1572872 | tf_op jit(solution)/shard_map/ppermute | solution.py:103
  165.7 2.0 %decoder_part.5 = bf16[2048,2048]{1,0:T(8,128)(2,1)} custom-call(s32[1]{0:T(128)} %bitcast.scalar_ref, bf16[16,128,64]{2,1,0:T(8,128)(2,1)S(1)} %get-tuple-element.87.code_ref, bf16[1,16,64,512]{3,2,1,0:T(8,128)(2,1)S(1)} %get-tuple-element.127.slots_ref, bf16[2048,2048]{1,0:T(8,128)(2,1)} %decoder_part.4.refs_0_), custom_call_target="tpu_custom_call", output_to_operand_aliasing={{}: (3, {})} | custom-call | flops 2200000000 | bytes 1 | tf_op jit(solution)/shard_map/decoder_part/pallas_call | solution.py:398
  168.5 3.1 %act_slots.1.act_ref = bf16[16,64,2048]{2,1,0:T(8,128)(2,1)S(1)} custom-call(s32[6]{0:T(128)S(1)} %stack.137.scalar_ref, bf16[4,256,256]{2,1,0:T(8,128)(2,1)S(1)} %get-tuple-element.88.hot_ref, bf16[256,2048]{1,0:T(8,128)(2,1)S(1)} %copy-done.4, bf16[256,2048]{1,0:T(8,128)(2,1)S(1)} %copy-done.8, bf16[256,2048]{1,0:T(8,128)(2,1)S(1)} %copy-done.6, ...), custom_call_target="tpu_custom_call" | custom-call | flops 3630000128 | bytes 1 | tf_op jit(solution)/shard_map/act_slots/pallas_call | solution.py:439
  171.6 6.3 %encoder_part.1 = bf16[2048,2048]{1,0:T(8,128)(2,1)} custom-call(bf16[16,64,128]{2,1,0:T(8,128)(2,1)S(1)} %copy-done.19, f32[16,64,128]{2,1,0:T(8,128)S(1)} %get-tuple-element.130.own_ref, f32[16,64,128]{2,1,0:T(8,128)S(1)} %collective-permute-done.32.theirs_ref, bf16[16,64,2048]{2,1,0:T(8,128)(2,1)S(1)} %act_slots.1.act_ref), custom_call_target="tpu_custom_call" | custom-call | flops 7150000128 | bytes 1 | tf_op jit(solution)/shard_map/encoder_part/pallas_call | solution.py:475
  (160 shorter events, 59.8 us)
Async XLA Ops:
  3.5 10.6 %collective-permute-start.3 = (bf16[128,2048]{1,0:T(8,128)(2,1)S(1)}, bf16[128,2048]{1,0:T(8,128)(2,1)S(1)}, u32[]{:S(2)}, u32[]{:S(2)}) collective-permute-start(bf16[128,2048]{1,0:T(8,128)(2,1)S(1)} %get-tuple-element.143), channel_id=1, source_target_pairs={{0,1},{1,0},{2,3},{3,2},{4,5},{5,4},{6,7},{7,6},{8,9},{9,8},{10,11... | collective-permute-start | bytes 1572872 | tf_op jit(solution)/shard_map/ppermute | solution.py:103
  15.8 28.0 %collective-permute-start.6 = (bf16[256,2048]{1,0:T(8,128)(2,1)S(1)}, bf16[256,2048]{1,0:T(8,128)(2,1)S(1)}, u32[]{:S(2)}, u32[]{:S(2)}) collective-permute-start(bf16[256,2048]{1,0:T(8,128)(2,1)S(1)} %pad_maximum_fusion.own_ref), channel_id=1, source_target_pairs={{0,2},{2,4},{4,6},{1,3},{3,5},{5,7},{8,10},{10,12},{12,14},{9,11},... | collective-permute-start | bytes 3145736 | tf_op jit(solution)/shard_map/ppermute | solution.py:112
  19.0 26.3 %collective-permute-start.7 = (bf16[256,2048]{1,0:T(8,128)(2,1)S(1)}, bf16[256,2048]{1,0:T(8,128)(2,1)S(1)}, u32[]{:S(2)}, u32[]{:S(2)}) collective-permute-start(bf16[256,2048]{1,0:T(8,128)(2,1)S(1)} %pad_maximum_fusion.own_ref), channel_id=1, source_target_pairs={{2,0},{4,2},{6,4},{3,1},{5,3},{7,5},{10,8},{12,10},{14,12},{11,9},... | collective-permute-start | bytes 3145736 | tf_op jit(solution)/shard_map/ppermute | solution.py:112
  26.7 26.3 %collective-permute-start.12 = (bf16[768,512]{1,0:T(8,128)(2,1)S(1)}, bf16[768,512]{1,0:T(8,128)(2,1)S(1)}, u32[]{:S(2)}, u32[]{:S(2)}) collective-permute-start(bf16[768,512]{1,0:T(8,128)(2,1)S(1)} %fusion.19), channel_id=1, source_target_pairs={{0,16},{8,24},{16,0},{24,8},{1,17},{9,25},{17,1},{25,9},{2,18},{10... | collective-permute-start | bytes 2359304 | tf_op jit(solution)/shard_map/ppermute | solution.py:103
  28.0 26.4 %collective-permute-start.10 = (bf16[768,512]{1,0:T(8,128)(2,1)S(1)}, bf16[768,512]{1,0:T(8,128)(2,1)S(1)}, u32[]{:S(2)}, u32[]{:S(2)}) collective-permute-start(bf16[768,512]{1,0:T(8,128)(2,1)S(1)} %fusion.16), channel_id=1, source_target_pairs={{0,8},{8,0},{16,24},{24,16},{1,9},{9,1},{17,25},{25,17},{2,10},{10... | collective-permute-start | bytes 2359304 | tf_op jit(solution)/shard_map/ppermute | solution.py:103
  31.5 26.7 %collective-permute-start.5 = (bf16[128,512]{1,0:T(8,128)(2,1)S(1)}, bf16[128,512]{1,0:T(8,128)(2,1)S(1)}, u32[]{:S(2)}, u32[]{:S(2)}) collective-permute-start(bf16[128,512]{1,0:T(8,128)(2,1)S(1)} %get-tuple-element.145), channel_id=1, source_target_pairs={{0,1},{1,0},{2,3},{3,2},{4,5},{5,4},{6,7},{7,6},{8,9},{9,8},{10,11... | collective-permute-start | bytes 393224 | tf_op jit(solution)/shard_map/ppermute | solution.py:103
  48.1 16.4 %collective-permute-start.8 = (bf16[128,2048]{1,0:T(8,128)(2,1)S(1)}, bf16[128,2048]{1,0:T(8,128)(2,1)S(1)}, u32[]{:S(2)}, u32[]{:S(2)}) collective-permute-start(bf16[128,2048]{1,0:T(8,128)(2,1)S(1)} %get-tuple-element.141), channel_id=1, source_target_pairs={{2,4},{4,6},{3,5},{5,7},{10,12},{12,14},{11,13},{13,15},{18,20},{2... | collective-permute-start | bytes 1572872 | tf_op jit(solution)/shard_map/ppermute | solution.py:112
  49.6 16.0 %collective-permute-start.9 = (bf16[128,2048]{1,0:T(8,128)(2,1)S(1)}, bf16[128,2048]{1,0:T(8,128)(2,1)S(1)}, u32[]{:S(2)}, u32[]{:S(2)}) collective-permute-start(bf16[128,2048]{1,0:T(8,128)(2,1)S(1)} %get-tuple-element.139), channel_id=1, source_target_pairs={{2,0},{4,2},{3,1},{5,3},{10,8},{12,10},{11,9},{13,11},{18,16},{20,... | collective-permute-start | bytes 1572872 | tf_op jit(solution)/shard_map/ppermute | solution.py:112
  67.7 10.5 %collective-permute-start.14 = (bf16[256,512]{1,0:T(8,128)(2,1)}, bf16[256,512]{1,0:T(8,128)(2,1)S(1)}, u32[]{:S(2)}, u32[]{:S(2)}) collective-permute-start(bf16[256,512]{1,0:T(8,128)(2,1)} %fusion.28), channel_id=1, source_target_pairs={{0,8},{8,0},{16,24},{24,16},{1,9},{9,1},{17,25},{25,17},{2,10},{10... | collective-permute-start | bytes 786440 | tf_op jit(solution)/shard_map/ppermute | solution.py:103
  73.5 25.7 %collective-permute-start.19 = (bf16[256,512]{1,0:T(8,128)(2,1)S(1)}, bf16[256,512]{1,0:T(8,128)(2,1)S(1)}, u32[]{:S(2)}, u32[]{:S(2)}) collective-permute-start(bf16[256,512]{1,0:T(8,128)(2,1)S(1)} %get-tuple-element.98), channel_id=1, source_target_pairs={{0,4},{2,6},{4,0},{6,2},{1,5},{3,7},{5,1},{7,3},{8,12},{10,14},{12... | collective-permute-start | bytes 786440 | tf_op jit(solution)/shard_map/ppermute | solution.py:103
  76.5 22.6 %collective-permute-start.20 = (bf16[256,512]{1,0:T(8,128)(2,1)S(1)}, bf16[256,512]{1,0:T(8,128)(2,1)S(1)}, u32[]{:S(2)}, u32[]{:S(2)}) collective-permute-start(bf16[256,512]{1,0:T(8,128)(2,1)S(1)} %get-tuple-element.99), channel_id=1, source_target_pairs={{0,2},{2,0},{4,6},{6,4},{1,3},{3,1},{5,7},{7,5},{8,10},{10,8},{12,... | collective-permute-start | bytes 786440 | tf_op jit(solution)/shard_map/ppermute | solution.py:103
  77.5 21.7 %collective-permute-start.17 = (bf16[256,256]{1,0:T(8,128)(2,1)S(1)}, bf16[256,256]{1,0:T(8,128)(2,1)S(1)}, u32[]{:S(2)}, u32[]{:S(2)}) collective-permute-start(bf16[256,256]{1,0:T(8,128)(2,1)S(1)} %add_convert_fusion.2), channel_id=1, source_target_pairs={{0,8},{8,0},{16,24},{24,16},{1,9},{9,1},{17,25},{25,17},{2,10},{10... | collective-permute-start | bytes 393224 | tf_op jit(solution)/shard_map/ppermute | solution.py:103
  78.2 20.9 %collective-permute-start.15 = (bf16[256,256]{1,0:T(8,128)(2,1)S(1)}, bf16[256,256]{1,0:T(8,128)(2,1)S(1)}, u32[]{:S(2)}, u32[]{:S(2)}) collective-permute-start(bf16[256,256]{1,0:T(8,128)(2,1)S(1)} %add_convert_fusion.3), channel_id=1, source_target_pairs={{0,16},{8,24},{16,0},{24,8},{1,17},{9,25},{17,1},{25,9},{2,18},{10... | collective-permute-start | bytes 393224 | tf_op jit(solution)/shard_map/ppermute | solution.py:103
  100.4 11.8 %collective-permute-start.21 = (bf16[256,512]{1,0:T(8,128)(2,1)S(1)}, bf16[256,512]{1,0:T(8,128)(2,1)S(1)}, u32[]{:S(2)}, u32[]{:S(2)}) collective-permute-start(bf16[256,512]{1,0:T(8,128)(2,1)S(1)} %fusion.44.refs_0_), channel_id=1, source_target_pairs={{0,2},{2,0},{4,6},{6,4},{1,3},{3,1},{5,7},{7,5},{8,10},{10,8},{12,... | collective-permute-start | bytes 786440 | tf_op jit(solution)/shard_map/ppermute | solution.py:103
  100.4 19.5 %collective-permute-start.22 = (bf16[256,512]{1,0:T(8,128)(2,1)S(1)}, bf16[256,512]{1,0:T(8,128)(2,1)S(1)}, u32[]{:S(2)}, u32[]{:S(2)}) collective-permute-start(bf16[256,512]{1,0:T(8,128)(2,1)S(1)} %fusion.44.refs_0_), channel_id=1, source_target_pairs={{0,4},{2,6},{4,0},{6,2},{1,5},{3,7},{5,1},{7,3},{8,12},{10,14},{12... | collective-permute-start | bytes 786440 | tf_op jit(solution)/shard_map/ppermute | solution.py:103
  101.9 18.1 %collective-permute-start.23 = (bf16[256,512]{1,0:T(8,128)(2,1)S(1)}, bf16[256,512]{1,0:T(8,128)(2,1)S(1)}, u32[]{:S(2)}, u32[]{:S(2)}) collective-permute-start(bf16[256,512]{1,0:T(8,128)(2,1)S(1)} %fusion.44.refs_0_), channel_id=1, source_target_pairs={{0,6},{2,4},{4,2},{6,0},{1,7},{3,5},{5,3},{7,1},{8,14},{10,12},{12... | collective-permute-start | bytes 786440 | tf_op jit(solution)/shard_map/ppermute | solution.py:103
  104.0 16.0 %collective-permute-start.24 = (bf16[256,512]{1,0:T(8,128)(2,1)S(1)}, bf16[256,512]{1,0:T(8,128)(2,1)S(1)}, u32[]{:S(2)}, u32[]{:S(2)}) collective-permute-start(bf16[256,512]{1,0:T(8,128)(2,1)S(1)} %fusion.44.refs_0_), channel_id=1, source_target_pairs={{0,8},{8,0},{16,24},{24,16},{1,9},{9,1},{17,25},{25,17},{2,10},{10... | collective-permute-start | bytes 786440 | tf_op jit(solution)/shard_map/ppermute | solution.py:103
  104.1 15.9 %collective-permute-start.25 = (bf16[256,512]{1,0:T(8,128)(2,1)S(1)}, bf16[256,512]{1,0:T(8,128)(2,1)S(1)}, u32[]{:S(2)}, u32[]{:S(2)}) collective-permute-start(bf16[256,512]{1,0:T(8,128)(2,1)S(1)} %fusion.44.refs_0_), channel_id=1, source_target_pairs={{0,16},{8,24},{16,0},{24,8},{1,17},{9,25},{17,1},{25,9},{2,18},{10... | collective-permute-start | bytes 786440 | tf_op jit(solution)/shard_map/ppermute | solution.py:103
  121.0 23.6 %collective-permute-start.28 = (bf16[768,512]{1,0:T(8,128)(2,1)}, bf16[768,512]{1,0:T(8,128)(2,1)S(1)}, u32[]{:S(2)}, u32[]{:S(2)}) collective-permute-start(bf16[768,512]{1,0:T(8,128)(2,1)} %join.3.refs_1_), channel_id=1, source_target_pairs={{0,16},{8,24},{16,0},{24,8},{1,17},{9,25},{17,1},{25,9},{2,18},{10... | collective-permute-start | bytes 2359304 | tf_op jit(solution)/shard_map/ppermute | solution.py:103
  121.7 23.0 %collective-permute-start.29 = (bf16[768,512]{1,0:T(8,128)(2,1)}, bf16[768,512]{1,0:T(8,128)(2,1)S(1)}, u32[]{:S(2)}, u32[]{:S(2)}) collective-permute-start(bf16[768,512]{1,0:T(8,128)(2,1)} %join.3.refs_1_), channel_id=1, source_target_pairs={{0,8},{8,0},{16,24},{24,16},{1,9},{9,1},{17,25},{25,17},{2,10},{10... | collective-permute-start | bytes 2359304 | tf_op jit(solution)/shard_map/ppermute | solution.py:103
  124.0 20.6 %collective-permute-start.27 = (bf16[128,2048]{1,0:T(8,128)(2,1)}, bf16[128,2048]{1,0:T(8,128)(2,1)}, u32[]{:S(2)}, u32[]{:S(2)}) collective-permute-start(bf16[128,2048]{1,0:T(8,128)(2,1)} %get-tuple-element.115), channel_id=1, source_target_pairs={{2,0},{4,2},{3,1},{5,3},{10,8},{12,10},{11,9},{13,11},{18,16},{20,... | collective-permute-start | bytes 1572872 | tf_op jit(solution)/shard_map/ppermute | solution.py:112
  125.5 42.3 %collective-permute-start.33 = (bf16[128,2048]{1,0:T(8,128)(2,1)}, bf16[128,2048]{1,0:T(8,128)(2,1)S(1)}, u32[]{:S(2)}, u32[]{:S(2)}) collective-permute-start(bf16[128,2048]{1,0:T(8,128)(2,1)} %get-tuple-element.133), channel_id=1, source_target_pairs={{4,6},{2,0},{5,7},{3,1},{12,14},{10,8},{13,15},{11,9},{20,22},{18,... | collective-permute-start | bytes 1572872 | tf_op jit(solution)/shard_map/ppermute | solution.py:590
  145.9 21.8 %collective-permute-start.34 = (bf16[128,2048]{1,0:T(8,128)(2,1)S(1)}, bf16[128,2048]{1,0:T(8,128)(2,1)S(1)}, u32[]{:S(2)}, u32[]{:S(2)}) collective-permute-start(bf16[128,2048]{1,0:T(8,128)(2,1)S(1)} %get-tuple-element.134), channel_id=1, source_target_pairs={{4,6},{2,0},{5,7},{3,1},{12,14},{10,8},{13,15},{11,9},{20,22},{18,... | collective-permute-start | bytes 1572872 | tf_op jit(solution)/shard_map/ppermute | solution.py:590
  159.3 12.3 %collective-permute-start.32 = (f32[16,64,128]{2,1,0:T(8,128)S(1)}, f32[16,64,128]{2,1,0:T(8,128)S(1)}, u32[]{:S(2)}, u32[]{:S(2)}) collective-permute-start(f32[16,64,128]{2,1,0:T(8,128)S(1)} %get-tuple-element.130.own_ref), channel_id=1, source_target_pairs={{0,1},{1,0},{2,3},{3,2},{4,5},{5,4},{6,7},{7,6},{8,9},{9,8},{10,11... | collective-permute-start | bytes 1572872 | tf_op jit(solution)/shard_map/ppermute | solution.py:103
  (42 other events, 284.7 us)

commit v14 on v12

--- a/solution.py
+++ b/solution.py
@@ -414,39 +414,41 @@
     )(columns.astype(jnp.int32), codes, slots, *onto)
 
 
-def act_slots_kernel(scalar_ref, hot_ref, *refs):
-    out_ref = refs[-1]
-    shards = hot_ref.shape[0]
-    per = out_ref.shape[1] // shards
-    for i in range(shards):
+def act_slots_kernel(scalar_ref, hot_ref, own_ref, down_ref, up_ref, down_two_ref, up_two_ref, end_ref, out_ref):
+    per = out_ref.shape[1] // hot_ref.shape[0]
+    last = end_ref[...]
+    zero = jnp.zeros((), last.dtype)
+    rows = [
+        own_ref[...],
+        down_ref[...] + jnp.where(scalar_ref[4] > 0, last, zero),
+        down_two_ref[...] + up_two_ref[...],
+        up_ref[...] + jnp.where(scalar_ref[5] > 0, last, zero),
+    ]
+    for i in range(4):
         z = scalar_ref[i]
-        rows, more = refs[2 * i][...], refs[2 * i + 1][...]
-        rows = rows + jnp.where(scalar_ref[shards + i] > 0, more, jnp.zeros((), more.dtype))
-        value = jnp.dot(hot_ref[z], rows, preferred_element_type=jnp.float32).astype(jnp.bfloat16)
+        value = jnp.dot(hot_ref[z], rows[i], preferred_element_type=jnp.float32).astype(jnp.bfloat16)
         to = pl.ds(pl.multiple_of(z * per, per), per)
         for b in range(out_ref.shape[0]):
             out_ref[b, to, :] = value[b * per:(b + 1) * per]
 
 
-def act_slots(terms_of, places, flags, hot, count):
-    group, half = terms_of[0][0].shape
+def act_slots(parts, scalars, hot, count):
+    half = parts[0].shape[1]
     slots = hot.shape[0] * hot.shape[1] // count
     tile = half // 4
-    flat = [term for terms in terms_of for term in terms]
-    scalars = jnp.stack([jnp.asarray(x, jnp.int32) for x in (*places, *flags)])
     return pl.pallas_call(
         act_slots_kernel,
         out_shape=jax.ShapeDtypeStruct((count, slots, half), jnp.bfloat16),
         grid_spec=pltpu.PrefetchScalarGridSpec(
             num_scalar_prefetch=1,
             grid=(4,),
-            in_specs=[resident(hot.shape)] + [pl.BlockSpec((group, tile), lambda i, s: (0, i)) for _ in flat],
+            in_specs=[resident(hot.shape)] + [pl.BlockSpec((part.shape[0], tile), lambda i, s: (0, i)) for part in parts],
             out_specs=pl.BlockSpec((count, slots, tile), lambda i, s: (0, 0, i)),
         ),
         compiler_params=params(),
         cost_estimate=cost(3.3),
         name="act_slots",
-    )(scalars, hot, *flat)
+    )(scalars, hot, *parts)
 
 
 def encoder_kernel(cap, shared, pre_ref, own_ref, theirs_ref, act_ref, out_ref):
@@ -575,8 +577,12 @@
     errors = ((total - goals.astype(f32)) / tok_count).astype(bf16)
     others = [flip(errors, "latent", r) for r in range(1, lat_count)]
     one_near, two_near = flip(errors, "layer", 1), flip(errors, "layer", 2)
-    relay, two_near, one_near, others = lax.optimization_barrier((relay, two_near, one_near, others[::-1]))
-    distant = join(others[::-1])
+    next_block, *others = others
+    one_next, two_next = flip(next_block, "layer", 1), flip(next_block, "layer", 2)
+    others, two_next, one_next, two_near, one_near, next_block, relay = lax.optimization_barrier(
+        (others, two_next, one_next, two_near, one_near, next_block, relay)
+    )
+    distant = join(others)
     one_far, two_far = flip(distant, "layer", 1), flip(distant, "layer", 2)
     ends = lax.ppermute(relay, "latent", [(lat_count - 2, lat_count - 1), (1, 0)])
 
@@ -586,21 +592,16 @@
         slots, grad = piece_grad(here, hot, decoder, weight_places(names), block_size, grad)
         return grad, decoder_part(slots, code_slots, jnp.stack(places(names, 0)), half, dec)
 
-    grad, dec = grads_of([[(errors,), (distant,)]], (0,), None, None)
+    grad, dec = grads_of([[(errors,), (next_block,), (distant,)]], (0,), None, None)
     grad, dec, two_far, one_far = lax.optimization_barrier((grad, dec, two_far, one_far))
-    three_a = flip(jnp.concatenate([two_near[:, :side], two_far[:, :side]]), "layer", 1)
-    three_b = flip(jnp.concatenate([one_near[:, side:], one_far[:, side:]]), "layer", 2)
-    grad, dec = grads_of([[(one_near,), (one_far,)], [(two_near,), (two_far,)]], (1, 2), grad, dec)
-
-    down_end, up_end = lat_here == 0, lat_here == lat_count - 1
-    terms_of = [[acts, acts]]
-    flags = [False]
-    for k in range(1, lat_count):
-        last = k == 1 or k == lat_count - 1
-        terms_of.append([(down if k == 1 else up)[1] if last else down[k], ends if last else up[lat_count - k]])
-        flags.append(True if not last else up_end if k == 1 else down_end)
-    shards = [lax.rem(lat_here + k, lat_count) ^ lat_here for k in range(lat_count)]
-    slotted = act_slots(terms_of, shards, flags, hot, local_blocks)
+    one, two = (one_near, one_next, one_far), (two_near, two_next, two_far)
+    three_a = flip(jnp.concatenate([rows[:, :side] for rows in two]), "layer", 1)
+    three_b = flip(jnp.concatenate([rows[:, side:] for rows in one]), "layer", 2)
+    grad, dec = grads_of([[(rows,) for rows in one], [(rows,) for rows in two]], (1, 2), grad, dec)
+
+    scalars = [lax.rem(lat_here + k, lat_count) ^ lat_here for k in range(lat_count)]
+    scalars = jnp.stack(scalars + [(lat_here == lat_count - 1).astype(jnp.int32), (lat_here == 0).astype(jnp.int32)])
+    slotted = act_slots((acts, down[1], up[1], down[2], up[2], ends), scalars, hot, local_blocks)
     three_a, three_b, grad, dec, slotted = lax.optimization_barrier((three_a, three_b, grad, dec, slotted))
     grad, dec = grads_of([[(three_a, three_b)]], (3,), grad, dec)
     enc = encoder_part(pre_slots, grad, flip(grad, "dp", 1), slotted, capacity)
@@ -622,8 +623,7 @@
         and dp_count == 2
         and active_count == 2
         and lay_count == 4
-        and lat_count > 3
-        and lat_count & (lat_count - 1) == 0
+        and lat_count == 4
         and tok_count == block_size
         and lat_count * dp_count * 16 <= tok_count
         and model_width % (dp_count * 2 * lay_count * 128) == 0

time: 170 us -> 170 us (level)
  local copies, waits for them, and re-layouts: 3.35 us -> 5.84 us
  other arithmetic: 4.78 us -> 2.85 us
    slice x6 -> x8, local copies, waits for them, and re-layouts: 0.06 us -> 1.88 us  [the longest x4 0.94 us: dense_plan(): rows[:, side:]]
    ppermute x23 -> x25, waiting for transfers between devices: 41 us -> 42.2 us  [flip(): return lax.ppermute(value, axis, [(i, i ^ bit) for i in range(count)])]
    ppermute x23 -> x25, starting transfers between devices: 34.9 us -> 34.8 us  [flip(): return lax.ppermute(value, axis, [(i, i ^ bit) for i in range(count)])]
  transfers between devices with their start and end apart: 28 -> 30, of which waited for: 12 -> 13; matrix products, arithmetic and copies ran while one was open for 10% -> 10% of each run, Pallas kernels for 21% -> 21%
where the time goes in v14:
time: 170 us; the launch traced here: 169 us
  waiting for transfers between devices  59.7 us (35%)
  Pallas kernels  45.1 us (27%)
  starting transfers between devices  43.8 us (26%)
  matrix products  11 us (6%)
  local copies, waits for them, and re-layouts  5.84 us (3%)
  other arithmetic  2.85 us (2%)
    ppermute x25, waiting for transfers between devices, flip(): return lax.ppermute(value, axis, [(i, i ^ bit) for i in range(count)])  42.2 us
    ppermute x25, starting transfers between devices, flip(): return lax.ppermute(value, axis, [(i, i ^ bit) for i in range(count)])  34.8 us
    ppermute x4, waiting for transfers between devices, hop(): return lax.ppermute(value, axis, pairs)  13 us
    pallas_call x3, Pallas kernels, gather_columns(): pl.pallas_call(gather_kernel, out_shape=[pltpu.HBM((rows, count * width),...  11.9 us
    dot_general x4, matrix products, rows_for(): jnp.dot(spread, weights[:, n * width:(n + 1) * width], preferred_element_...  11 us
    pallas_call x3, Pallas kernels, piece_grad(): pl.pallas_call(functools.partial(piece_grad_kernel, [[len(row) for row in...  10.6 us
    ppermute x4, starting transfers between devices, hop(): return lax.ppermute(value, axis, pairs)  7.52 us
    pallas_call x3, Pallas kernels, decoder_part(): pl.pallas_call(functools.partial(decoder_kernel, len(onto)), out_shape=ja...  7.29 us
  transfers between devices with their start and end apart: 30, of which 13 were waited for; matrix products, arithmetic and copies ran while one was open for 10% of the time, Pallas kernels for 21%

profile of v14, /device:TPU:1, one launch (start us, length us, event | category | flops | bytes accessed | tf_op | source)
XLA Modules:
  0.0 169.4 jit_solution(2074749905762254237)
XLA Ops:
  2.2 4.2 %collective-permute-start.2 = (bf16[272,128]{1,0:T(8,128)(2,1)S(1)}, bf16[272,128]{1,0:T(8,128)(2,1)S(1)}, u32[]{:S(2)}, u32[]{:S(2)}) collective-permute-start(bf16[272,128]{1,0:T(8,128)(2,1)S(1)} %fusion.21.refs_0_), channel_id=1, source_target_pairs={{0,6},{2,4},{4,2},{6,0},{1,7},{3,5},{5,3},{7,1},{8,14},{10,12},{12... | collective-permute-start | bytes 208904 | tf_op jit(solution)/shard_map/ppermute | solution.py:103
  9.4 5.3 %gather_columns.3 = (bf16[2048,1024]{1,0:T(8,128)(2,1)}, f32[8,128]{1,0:T(8,128)S(1)}) custom-call(s32[4]{0:T(128)S(1)} %pad_add_fusion.1.scalar_ref, bf16[1,2048,4096]{2,1,0:T(8,128)(2,1)} %weight_ref.5), custom_call_target="tpu_custom_call" | custom-call | flops 3960000000 | bytes 1 | tf_op jit(solution)/shard_map/gather_columns/pallas_call | solution.py:136
  16.4 4.1 %collective-permute-start.6 = (bf16[256,2048]{1,0:T(8,128)(2,1)S(1)}, bf16[256,2048]{1,0:T(8,128)(2,1)S(1)}, u32[]{:S(2)}, u32[]{:S(2)}) collective-permute-start(bf16[256,2048]{1,0:T(8,128)(2,1)S(1)} %pad_maximum_fusion.own_ref), channel_id=1, source_target_pairs={{0,2},{2,4},{4,6},{1,3},{3,5},{5,7},{8,10},{10,12},{12,14},{9,11},... | collective-permute-start | bytes 3145736 | tf_op jit(solution)/shard_map/ppermute | solution.py:112
  20.5 2.6 %spread_codes.1 = bf16[1024,2048]{1,0:T(8,128)(2,1)S(1)} custom-call(s32[1]{0:T(128)} %bitcast.5.scalar_ref, bf16[8,272,128]{2,1,0:T(8,128)(2,1)S(1)} %bitcast.45), custom_call_target="tpu_custom_call" | custom-call | flops 2750000128 | bytes 1 | tf_op jit(solution)/shard_map/spread_codes/pallas_call | solution.py:185
  30.5 5.3 %gather_columns.4 = (bf16[2048,1024]{1,0:T(8,128)(2,1)}, f32[8,128]{1,0:T(8,128)}) custom-call(s32[4]{0:T(128)S(1)} %pad_add_fusion.scalar_ref, bf16[1,2048,4096]{2,1,0:T(8,128)(2,1)} %weight_ref.5), custom_call_target="tpu_custom_call" | custom-call | flops 3960000000 | bytes 1 | tf_op jit(solution)/shard_map/gather_columns/pallas_call | solution.py:136
  35.8 5.4 %collective-permute-done.7.down_ref = bf16[256,2048]{1,0:T(8,128)(2,1)S(1)} collective-permute-done((bf16[256,2048]{1,0:T(8,128)(2,1)S(1)}, bf16[256,2048]{1,0:T(8,128)(2,1)S(1)}, u32[]{:S(2)}, u32[]{:S(2)}) %collective-permute-start.7) | collective-permute-done | bytes 1048608 | tf_op jit(solution)/shard_map/ppermute | solution.py:112
  44.3 4.1 %fusion.17.kept_b = bf16[1024,512]{1,0:T(8,128)(2,1)S(1)} fusion(bf16[1024,2048]{1,0:T(8,128)(2,1)S(1)} %spread_codes.1, bf16[2048,1024]{1,0:T(8,128)(2,1)} %get-tuple-element.63), kind=kOutput, calls=%fused_computation.11 | convolution fusion | flops 2148007936 | bytes 7340032 | tf_op jit(solution)/shard_map/dot_general | solution.py:556
  56.9 2.9 %collective-permute-start.11 = (bf16[128,512]{1,0:T(8,128)(2,1)S(1)}, bf16[128,512]{1,0:T(8,128)(2,1)S(1)}, u32[]{:S(2)}, u32[]{:S(2)}) collective-permute-start(bf16[128,512]{1,0:T(8,128)(2,1)S(1)} %get-tuple-element.109), channel_id=1, source_target_pairs={{0,1},{1,0},{2,3},{3,2},{4,5},{5,4},{6,7},{7,6},{8,9},{9,8},{10,11... | collective-permute-start | bytes 393224 | tf_op jit(solution)/shard_map/ppermute | solution.py:103
  60.7 3.4 %collective-permute-done.10.far_b = bf16[1024,256]{1,0:T(8,128)(2,1)S(1)} collective-permute-done((bf16[1024,256]{1,0:T(8,128)(2,1)S(1)}, bf16[1024,256]{1,0:T(8,128)(2,1)S(1)}, u32[]{:S(2)}, u32[]{:S(2)}) %collective-permute-start.10) | collective-permute-done | bytes 524320 | tf_op jit(solution)/shard_map/ppermute | solution.py:103
  64.2 6.7 %collective-permute-done.13.down_two_ref = bf16[256,2048]{1,0:T(8,128)(2,1)} collective-permute-done((bf16[256,2048]{1,0:T(8,128)(2,1)S(1)}, bf16[256,2048]{1,0:T(8,128)(2,1)}, u32[]{:S(2)}, u32[]{:S(2)}) %collective-permute-start.13) | collective-permute-done | bytes 1048608 | tf_op jit(solution)/shard_map/ppermute | solution.py:112
  72.5 2.4 %collective-permute-start.16 = (bf16[256,512]{1,0:T(8,128)(2,1)S(1)}, bf16[256,512]{1,0:T(8,128)(2,1)S(1)}, u32[]{:S(2)}, u32[]{:S(2)}) collective-permute-start(bf16[256,512]{1,0:T(8,128)(2,1)S(1)} %get-tuple-element.78), channel_id=1, source_target_pairs={{0,6},{2,4},{4,2},{6,0},{1,7},{3,5},{5,3},{7,1},{8,14},{10,12},{12... | collective-permute-start | bytes 786440 | tf_op jit(solution)/shard_map/ppermute | solution.py:103
  74.9 3.2 %collective-permute-done.14 = bf16[256,512]{1,0:T(8,128)(2,1)S(1)} collective-permute-done((bf16[256,512]{1,0:T(8,128)(2,1)S(1)}, bf16[256,512]{1,0:T(8,128)(2,1)S(1)}, u32[]{:S(2)}, u32[]{:S(2)}) %collective-permute-start.14) | collective-permute-done | bytes 262176 | tf_op jit(solution)/shard_map/ppermute | solution.py:103
  78.1 13.1 %collective-permute-done.15 = bf16[256,512]{1,0:T(8,128)(2,1)S(1)} collective-permute-done((bf16[256,512]{1,0:T(8,128)(2,1)S(1)}, bf16[256,512]{1,0:T(8,128)(2,1)S(1)}, u32[]{:S(2)}, u32[]{:S(2)}) %collective-permute-start.15) | collective-permute-done | bytes 262176 | tf_op jit(solution)/shard_map/ppermute | solution.py:103
  91.4 6.0 %collective-permute-start.19 = (bf16[256,512]{1,0:T(8,128)(2,1)S(1)}, bf16[256,512]{1,0:T(8,128)(2,1)}, u32[]{:S(2)}, u32[]{:S(2)}) collective-permute-start(bf16[256,512]{1,0:T(8,128)(2,1)S(1)} %multiply_convert_fusion.refs_0_), channel_id=1, source_target_pairs={{0,2},{2,0},{4,6},{6,4},{1,3},{3,1},{5,7},{7,5},{8,10},{10,8},{12,... | collective-permute-start | bytes 786440 | tf_op jit(solution)/shard_map/ppermute | solution.py:103
  107.0 15.6 %collective-permute-done.17.refs_0_ = bf16[256,512]{1,0:T(8,128)(2,1)S(1)} collective-permute-done((bf16[256,512]{1,0:T(8,128)(2,1)S(1)}, bf16[256,512]{1,0:T(8,128)(2,1)S(1)}, u32[]{:S(2)}, u32[]{:S(2)}) %collective-permute-start.17) | collective-permute-done | bytes 262176 | tf_op jit(solution)/shard_map/ppermute | solution.py:103
  127.8 2.9 %piece_grad.3 = (bf16[1,16,64,512]{3,2,1,0:T(8,128)(2,1)S(1)}, f32[16,64,128]{2,1,0:T(8,128)S(1)}) custom-call(s32[1]{0:T(128)} %bitcast.21.scalar_ref, bf16[4,256,256]{2,1,0:T(8,128)(2,1)S(1)} %get-tuple-element.72.hot_ref, bf16[1,2048,4096]{2,1,0:T(8,128)(2,1)} %weight_ref.5, bf16[256,512]{1,0:T(8,128)(2,1)S(1)} %multiply_convert_fusion.refs_0_, ...), custom_call_target="tpu_custom_call" | custom-call | flops 3080000000 | bytes 1 | tf_op jit(solution)/shard_map/piece_grad/pallas_call | solution.py:365
  132.8 2.5 %collective-permute-done.25.refs_3_ = bf16[512,512]{1,0:T(8,128)(2,1)S(1)} collective-permute-done((bf16[512,512]{1,0:T(8,128)(2,1)}, bf16[512,512]{1,0:T(8,128)(2,1)S(1)}, u32[]{:S(2)}, u32[]{:S(2)}) %collective-permute-start.25) | collective-permute-done | bytes 524320 | tf_op jit(solution)/shard_map/ppermute | solution.py:103
  136.7 4.9 %piece_grad.4 = (bf16[2,16,64,512]{3,2,1,0:T(8,128)(2,1)S(1)}, f32[16,64,128]{2,1,0:T(8,128)S(1)}) custom-call(s32[2]{0:T(128)S(1)} %pad_add_fusion.3.scalar_ref, bf16[4,256,256]{2,1,0:T(8,128)(2,1)S(1)} %get-tuple-element.72.hot_ref, bf16[1,2048,4096]{2,1,0:T(8,128)(2,1)} %weight_ref.5, f32[16,64,128]{2,1,0:T(8,128)S(1)} %get-tuple-element.93.refs_0_, ...), custom_call_target="tpu_custom_call" | custom-call | flops 5280000000 | bytes 1 | tf_op jit(solution)/shard_map/piece_grad/pallas_call | solution.py:365
  141.7 3.3 %decoder_part.4.refs_0_ = bf16[2048,2048]{1,0:T(8,128)(2,1)} custom-call(s32[2]{0:T(128)S(1)} %pad_add_fusion.4.scalar_ref, bf16[16,128,64]{2,1,0:T(8,128)(2,1)S(1)} %get-tuple-element.71.code_ref, bf16[2,16,64,512]{3,2,1,0:T(8,128)(2,1)S(1)} %get-tuple-element.95.slots_ref, bf16[2048,2048]{1,0:T(8,128)(2,1)} %decoder_part.3.refs_0_), custom_call_target="tpu_custom_call", output_to_operand_aliasing={{}: (3, {})} | custom-call | flops 3630000128 | bytes 1 | tf_op jit(solution)/shard_map/decoder_part/pallas_call | solution.py:400
  144.9 4.5 %collective-permute-done.28.end_ref = bf16[256,2048]{1,0:T(8,128)(2,1)S(1)} collective-permute-done((bf16[256,2048]{1,0:T(8,128)(2,1)}, bf16[256,2048]{1,0:T(8,128)(2,1)S(1)}, u32[]{:S(2)}, u32[]{:S(2)}) %collective-permute-start.28) | collective-permute-done | bytes 1048608 | tf_op jit(solution)/shard_map/ppermute | solution.py:587
  149.4 4.3 %act_slots.1.act_ref = bf16[16,64,2048]{2,1,0:T(8,128)(2,1)S(1)} custom-call(s32[6]{0:T(128)S(1)} %stack.137.scalar_ref, bf16[4,256,256]{2,1,0:T(8,128)(2,1)S(1)} %get-tuple-element.72.hot_ref, bf16[256,2048]{1,0:T(8,128)(2,1)S(1)} %pad_maximum_fusion.own_ref, bf16[256,2048]{1,0:T(8,128)(2,1)S(1)} %copy-done.8, bf16[256,2048]{1,0:T(8,128)(2,1)S(1)} %copy-done.10, ...), custom_call_target="tpu_custom_call" | custom-call | flops 3630000128 | bytes 1 | tf_op jit(solution)/shard_map/act_slots/pallas_call | solution.py:439
  153.8 2.8 %piece_grad.5 = (bf16[1,16,64,512]{3,2,1,0:T(8,128)(2,1)S(1)}, f32[16,64,128]{2,1,0:T(8,128)S(1)}) custom-call(s32[1]{0:T(128)} %bitcast.23.scalar_ref, bf16[4,256,256]{2,1,0:T(8,128)(2,1)S(1)} %get-tuple-element.72.hot_ref, bf16[1,2048,4096]{2,1,0:T(8,128)(2,1)} %weight_ref.5, f32[16,64,128]{2,1,0:T(8,128)S(1)} %get-tuple-element.98.refs_0_, ...), custom_call_target="tpu_custom_call" | custom-call | flops 3080000000 | bytes 1 | tf_op jit(solution)/shard_map/piece_grad/pallas_call | solution.py:365
  156.5 4.6 %collective-permute-start.29 = (f32[16,64,128]{2,1,0:T(8,128)S(1)}, f32[16,64,128]{2,1,0:T(8,128)S(1)}, u32[]{:S(2)}, u32[]{:S(2)}) collective-permute-start(f32[16,64,128]{2,1,0:T(8,128)S(1)} %get-tuple-element.104.own_ref), channel_id=1, source_target_pairs={{0,1},{1,0},{2,3},{3,2},{4,5},{5,4},{6,7},{7,6},{8,9},{9,8},{10,11... | collective-permute-start | bytes 1572872 | tf_op jit(solution)/shard_map/ppermute | solution.py:103
  163.1 6.3 %encoder_part.1 = bf16[2048,2048]{1,0:T(8,128)(2,1)} custom-call(bf16[16,64,128]{2,1,0:T(8,128)(2,1)S(1)} %copy-done.12, f32[16,64,128]{2,1,0:T(8,128)S(1)} %get-tuple-element.104.own_ref, f32[16,64,128]{2,1,0:T(8,128)S(1)} %collective-permute-done.29.theirs_ref, bf16[16,64,2048]{2,1,0:T(8,128)(2,1)S(1)} %act_slots.1.act_ref), custom_call_target="tpu_custom_call" | custom-call | flops 7150000128 | bytes 1 | tf_op jit(solution)/shard_map/encoder_part/pallas_call | solution.py:475
  (114 shorter events, 48.2 us)
Async XLA Ops:
  2.2 12.5 %collective-permute-start.2 = (bf16[272,128]{1,0:T(8,128)(2,1)S(1)}, bf16[272,128]{1,0:T(8,128)(2,1)S(1)}, u32[]{:S(2)}, u32[]{:S(2)}) collective-permute-start(bf16[272,128]{1,0:T(8,128)(2,1)S(1)} %fusion.21.refs_0_), channel_id=1, source_target_pairs={{0,6},{2,4},{4,2},{6,0},{1,7},{3,5},{5,3},{7,1},{8,14},{10,12},{12... | collective-permute-start | bytes 208904 | tf_op jit(solution)/shard_map/ppermute | solution.py:103
  6.4 8.3 %collective-permute-start.1 = (bf16[272,128]{1,0:T(8,128)(2,1)S(1)}, bf16[272,128]{1,0:T(8,128)(2,1)S(1)}, u32[]{:S(2)}, u32[]{:S(2)}) collective-permute-start(bf16[272,128]{1,0:T(8,128)(2,1)S(1)} %fusion.21.refs_0_), channel_id=1, source_target_pairs={{0,4},{2,6},{4,0},{6,2},{1,5},{3,7},{5,1},{7,3},{8,12},{10,14},{12... | collective-permute-start | bytes 208904 | tf_op jit(solution)/shard_map/ppermute | solution.py:103
  6.4 8.3 %collective-permute-start = (bf16[272,128]{1,0:T(8,128)(2,1)S(1)}, bf16[272,128]{1,0:T(8,128)(2,1)S(1)}, u32[]{:S(2)}, u32[]{:S(2)}) collective-permute-start(bf16[272,128]{1,0:T(8,128)(2,1)S(1)} %fusion.21.refs_0_), channel_id=1, source_target_pairs={{0,2},{2,0},{4,6},{6,4},{1,3},{3,1},{5,7},{7,5},{8,10},{10,8},{12,... | collective-permute-start | bytes 208904 | tf_op jit(solution)/shard_map/ppermute | solution.py:103
  15.1 26.1 %collective-permute-start.7 = (bf16[256,2048]{1,0:T(8,128)(2,1)S(1)}, bf16[256,2048]{1,0:T(8,128)(2,1)S(1)}, u32[]{:S(2)}, u32[]{:S(2)}) collective-permute-start(bf16[256,2048]{1,0:T(8,128)(2,1)S(1)} %pad_maximum_fusion.own_ref), channel_id=1, source_target_pairs={{2,0},{4,2},{6,4},{3,1},{5,3},{7,5},{10,8},{12,10},{14,12},{11,9},... | collective-permute-start | bytes 3145736 | tf_op jit(solution)/shard_map/ppermute | solution.py:112
  16.4 25.7 %collective-permute-start.6 = (bf16[256,2048]{1,0:T(8,128)(2,1)S(1)}, bf16[256,2048]{1,0:T(8,128)(2,1)S(1)}, u32[]{:S(2)}, u32[]{:S(2)}) collective-permute-start(bf16[256,2048]{1,0:T(8,128)(2,1)S(1)} %pad_maximum_fusion.own_ref), channel_id=1, source_target_pairs={{0,2},{2,4},{4,6},{1,3},{3,5},{5,7},{8,10},{10,12},{12,14},{9,11},... | collective-permute-start | bytes 3145736 | tf_op jit(solution)/shard_map/ppermute | solution.py:112
  25.5 27.5 %collective-permute-start.5 = (bf16[1024,512]{1,0:T(8,128)(2,1)S(1)}, bf16[1024,512]{1,0:T(8,128)(2,1)S(1)}, u32[]{:S(2)}, u32[]{:S(2)}) collective-permute-start(bf16[1024,512]{1,0:T(8,128)(2,1)S(1)} %fusion.8), channel_id=1, source_target_pairs={{0,8},{8,0},{16,24},{24,16},{1,9},{9,1},{17,25},{25,17},{2,10},{10... | collective-permute-start | bytes 3145736 | tf_op jit(solution)/shard_map/ppermute | solution.py:103
  29.2 23.4 %collective-permute-start.9 = (bf16[1024,512]{1,0:T(8,128)(2,1)S(1)}, bf16[1024,512]{1,0:T(8,128)(2,1)S(1)}, u32[]{:S(2)}, u32[]{:S(2)}) collective-permute-start(bf16[1024,512]{1,0:T(8,128)(2,1)S(1)} %fusion.14), channel_id=1, source_target_pairs={{0,16},{8,24},{16,0},{24,8},{1,17},{9,25},{17,1},{25,9},{2,18},{10... | collective-permute-start | bytes 3145736 | tf_op jit(solution)/shard_map/ppermute | solution.py:103
  42.1 22.1 %collective-permute-start.12 = (bf16[256,2048]{1,0:T(8,128)(2,1)S(1)}, bf16[256,2048]{1,0:T(8,128)(2,1)S(1)}, u32[]{:S(2)}, u32[]{:S(2)}) collective-permute-start(bf16[256,2048]{1,0:T(8,128)(2,1)S(1)} %collective-permute-done.6.up_ref), channel_id=1, source_target_pairs={{2,4},{4,6},{3,5},{5,7},{10,12},{12,14},{11,13},{13,15},{18,20},{2... | collective-permute-start | bytes 3145736 | tf_op jit(solution)/shard_map/ppermute | solution.py:112
  42.8 28.1 %collective-permute-start.13 = (bf16[256,2048]{1,0:T(8,128)(2,1)S(1)}, bf16[256,2048]{1,0:T(8,128)(2,1)}, u32[]{:S(2)}, u32[]{:S(2)}) collective-permute-start(bf16[256,2048]{1,0:T(8,128)(2,1)S(1)} %collective-permute-done.7.down_ref), channel_id=1, source_target_pairs={{2,0},{4,2},{3,1},{5,3},{10,8},{12,10},{11,9},{13,11},{18,16},{20,... | collective-permute-start | bytes 3145736 | tf_op jit(solution)/shard_map/ppermute | solution.py:112
  52.8 11.3 %collective-permute-start.10 = (bf16[1024,256]{1,0:T(8,128)(2,1)S(1)}, bf16[1024,256]{1,0:T(8,128)(2,1)S(1)}, u32[]{:S(2)}, u32[]{:S(2)}) collective-permute-start(bf16[1024,256]{1,0:T(8,128)(2,1)S(1)} %add_convert_fusion), channel_id=1, source_target_pairs={{0,8},{8,0},{16,24},{24,16},{1,9},{9,1},{17,25},{25,17},{2,10},{10... | collective-permute-start | bytes 1572872 | tf_op jit(solution)/shard_map/ppermute | solution.py:103
  53.1 11.1 %collective-permute-start.8 = (bf16[1024,256]{1,0:T(8,128)(2,1)S(1)}, bf16[1024,256]{1,0:T(8,128)(2,1)S(1)}, u32[]{:S(2)}, u32[]{:S(2)}) collective-permute-start(bf16[1024,256]{1,0:T(8,128)(2,1)S(1)} %add_convert_fusion.1), channel_id=1, source_target_pairs={{0,16},{8,24},{16,0},{24,8},{1,17},{9,25},{17,1},{25,9},{2,18},{10... | collective-permute-start | bytes 1572872 | tf_op jit(solution)/shard_map/ppermute | solution.py:103
  71.3 6.8 %collective-permute-start.14 = (bf16[256,512]{1,0:T(8,128)(2,1)S(1)}, bf16[256,512]{1,0:T(8,128)(2,1)S(1)}, u32[]{:S(2)}, u32[]{:S(2)}) collective-permute-start(bf16[256,512]{1,0:T(8,128)(2,1)S(1)} %get-tuple-element.76), channel_id=1, source_target_pairs={{0,2},{2,0},{4,6},{6,4},{1,3},{3,1},{5,7},{7,5},{8,10},{10,8},{12,... | collective-permute-start | bytes 786440 | tf_op jit(solution)/shard_map/ppermute | solution.py:103
  72.5 18.7 %collective-permute-start.15 = (bf16[256,512]{1,0:T(8,128)(2,1)S(1)}, bf16[256,512]{1,0:T(8,128)(2,1)S(1)}, u32[]{:S(2)}, u32[]{:S(2)}) collective-permute-start(bf16[256,512]{1,0:T(8,128)(2,1)S(1)} %get-tuple-element.77), channel_id=1, source_target_pairs={{0,4},{2,6},{4,0},{6,2},{1,5},{3,7},{5,1},{7,3},{8,12},{10,14},{12... | collective-permute-start | bytes 786440 | tf_op jit(solution)/shard_map/ppermute | solution.py:103
  72.5 18.7 %collective-permute-start.16 = (bf16[256,512]{1,0:T(8,128)(2,1)S(1)}, bf16[256,512]{1,0:T(8,128)(2,1)S(1)}, u32[]{:S(2)}, u32[]{:S(2)}) collective-permute-start(bf16[256,512]{1,0:T(8,128)(2,1)S(1)} %get-tuple-element.78), channel_id=1, source_target_pairs={{0,6},{2,4},{4,2},{6,0},{1,7},{3,5},{5,3},{7,1},{8,14},{10,12},{12... | collective-permute-start | bytes 786440 | tf_op jit(solution)/shard_map/ppermute | solution.py:103
  91.4 10.5 %collective-permute-start.19 = (bf16[256,512]{1,0:T(8,128)(2,1)S(1)}, bf16[256,512]{1,0:T(8,128)(2,1)}, u32[]{:S(2)}, u32[]{:S(2)}) collective-permute-start(bf16[256,512]{1,0:T(8,128)(2,1)S(1)} %multiply_convert_fusion.refs_0_), channel_id=1, source_target_pairs={{0,2},{2,0},{4,6},{6,4},{1,3},{3,1},{5,7},{7,5},{8,10},{10,8},{12,... | collective-permute-start | bytes 786440 | tf_op jit(solution)/shard_map/ppermute | solution.py:103
  99.9 7.2 %collective-permute-start.18 = (bf16[256,512]{1,0:T(8,128)(2,1)S(1)}, bf16[256,512]{1,0:T(8,128)(2,1)S(1)}, u32[]{:S(2)}, u32[]{:S(2)}) collective-permute-start(bf16[256,512]{1,0:T(8,128)(2,1)S(1)} %multiply_convert_fusion.refs_0_), channel_id=1, source_target_pairs={{0,6},{2,4},{4,2},{6,0},{1,7},{3,5},{5,3},{7,1},{8,14},{10,12},{12... | collective-permute-start | bytes 786440 | tf_op jit(solution)/shard_map/ppermute | solution.py:103
  100.0 22.6 %collective-permute-start.17 = (bf16[256,512]{1,0:T(8,128)(2,1)S(1)}, bf16[256,512]{1,0:T(8,128)(2,1)S(1)}, u32[]{:S(2)}, u32[]{:S(2)}) collective-permute-start(bf16[256,512]{1,0:T(8,128)(2,1)S(1)} %multiply_convert_fusion.refs_0_), channel_id=1, source_target_pairs={{0,4},{2,6},{4,0},{6,2},{1,5},{3,7},{5,1},{7,3},{8,12},{10,14},{12... | collective-permute-start | bytes 786440 | tf_op jit(solution)/shard_map/ppermute | solution.py:103
  102.0 20.7 %collective-permute-start.21 = (bf16[256,512]{1,0:T(8,128)(2,1)}, bf16[256,512]{1,0:T(8,128)(2,1)S(1)}, u32[]{:S(2)}, u32[]{:S(2)}) collective-permute-start(bf16[256,512]{1,0:T(8,128)(2,1)} %collective-permute-done.19.refs_1_), channel_id=1, source_target_pairs={{0,8},{8,0},{16,24},{24,16},{1,9},{9,1},{17,25},{25,17},{2,10},{10... | collective-permute-start | bytes 786440 | tf_op jit(solution)/shard_map/ppermute | solution.py:103
  103.1 20.3 %collective-permute-start.20 = (bf16[256,512]{1,0:T(8,128)(2,1)}, bf16[256,512]{1,0:T(8,128)(2,1)}, u32[]{:S(2)}, u32[]{:S(2)}) collective-permute-start(bf16[256,512]{1,0:T(8,128)(2,1)} %collective-permute-done.19.refs_1_), channel_id=1, source_target_pairs={{0,16},{8,24},{16,0},{24,8},{1,17},{9,25},{17,1},{25,9},{2,18},{10... | collective-permute-start | bytes 786440 | tf_op jit(solution)/shard_map/ppermute | solution.py:103
  124.2 11.0 %collective-permute-start.25 = (bf16[512,512]{1,0:T(8,128)(2,1)}, bf16[512,512]{1,0:T(8,128)(2,1)S(1)}, u32[]{:S(2)}, u32[]{:S(2)}) collective-permute-start(bf16[512,512]{1,0:T(8,128)(2,1)} %join.3.refs_2_), channel_id=1, source_target_pairs={{0,8},{8,0},{16,24},{24,16},{1,9},{9,1},{17,25},{25,17},{2,10},{10... | collective-permute-start | bytes 1572872 | tf_op jit(solution)/shard_map/ppermute | solution.py:103
  124.2 11.0 %collective-permute-start.24 = (bf16[512,512]{1,0:T(8,128)(2,1)}, bf16[512,512]{1,0:T(8,128)(2,1)S(1)}, u32[]{:S(2)}, u32[]{:S(2)}) collective-permute-start(bf16[512,512]{1,0:T(8,128)(2,1)} %join.3.refs_2_), channel_id=1, source_target_pairs={{0,16},{8,24},{16,0},{24,8},{1,17},{9,25},{17,1},{25,9},{2,18},{10... | collective-permute-start | bytes 1572872 | tf_op jit(solution)/shard_map/ppermute | solution.py:103
  126.3 23.1 %collective-permute-start.28 = (bf16[256,2048]{1,0:T(8,128)(2,1)}, bf16[256,2048]{1,0:T(8,128)(2,1)S(1)}, u32[]{:S(2)}, u32[]{:S(2)}) collective-permute-start(bf16[256,2048]{1,0:T(8,128)(2,1)} %broadcast_select_fusion), channel_id=1, source_target_pairs={{4,6},{2,0},{5,7},{3,1},{12,14},{10,8},{13,15},{11,9},{20,22},{18,... | collective-permute-start | bytes 3145736 | tf_op jit(solution)/shard_map/ppermute | solution.py:587
  135.3 18.4 %collective-permute-start.27 = (bf16[1024,256]{1,0:T(8,128)(2,1)S(1)}, bf16[1024,256]{1,0:T(8,128)(2,1)S(1)}, u32[]{:S(2)}, u32[]{:S(2)}) collective-permute-start(bf16[1024,256]{1,0:T(8,128)(2,1)S(1)} %pad_maximum_fusion.3), channel_id=1, source_target_pairs={{0,16},{8,24},{16,0},{24,8},{1,17},{9,25},{17,1},{25,9},{2,18},{10... | collective-permute-start | bytes 1572872 | tf_op jit(solution)/shard_map/ppermute | solution.py:103
  135.5 18.3 %collective-permute-start.26 = (bf16[1024,256]{1,0:T(8,128)(2,1)S(1)}, bf16[1024,256]{1,0:T(8,128)(2,1)S(1)}, u32[]{:S(2)}, u32[]{:S(2)}) collective-permute-start(bf16[1024,256]{1,0:T(8,128)(2,1)S(1)} %pad_maximum_fusion.2), channel_id=1, source_target_pairs={{0,8},{8,0},{16,24},{24,16},{1,9},{9,1},{17,25},{25,17},{2,10},{10... | collective-permute-start | bytes 1572872 | tf_op jit(solution)/shard_map/ppermute | solution.py:103
  (23 other events, 177.5 us)

commit v15 on v14

--- a/solution.py
+++ b/solution.py
@@ -602,7 +602,7 @@
     scalars = [lax.rem(lat_here + k, lat_count) ^ lat_here for k in range(lat_count)]
     scalars = jnp.stack(scalars + [(lat_here == lat_count - 1).astype(jnp.int32), (lat_here == 0).astype(jnp.int32)])
     slotted = act_slots((acts, down[1], up[1], down[2], up[2], ends), scalars, hot, local_blocks)
-    three_a, three_b, grad, dec, slotted = lax.optimization_barrier((three_a, three_b, grad, dec, slotted))
+    three_a, three_b, grad, dec = lax.optimization_barrier((three_a, three_b, grad, dec))
     grad, dec = grads_of([[(three_a, three_b)]], (3,), grad, dec)
     enc = encoder_part(pre_slots, grad, flip(grad, "dp", 1), slotted, capacity)
     return dec[None], enc[None]

time: 170 us -> 167 us (0.982)
  waiting for transfers between devices: 59.7 us -> 56 us
    ppermute x1, waiting for transfers between devices: 4.48 us -> 0.01 us  [dense_plan(): lax.ppermute(relay, 'latent', [(lat_count - 2, lat_count - 1), (1, 0)])]
  transfers between devices with their start and end apart: 30 -> 30, of which waited for: 13 -> 13; matrix products, arithmetic and copies ran while one was open for 10% -> 10% of each run, Pallas kernels for 21% -> 23%
where the time goes in v15:
time: 167 us; the launch traced here: 166 us
  waiting for transfers between devices  56 us (34%)
  Pallas kernels  45.1 us (27%)
  starting transfers between devices  43.7 us (26%)
  matrix products  11 us (7%)
  local copies, waits for them, and re-layouts  6.25 us (4%)
  other arithmetic  2.85 us (2%)
    ppermute x25, waiting for transfers between devices, flip(): return lax.ppermute(value, axis, [(i, i ^ bit) for i in range(count)])  42.9 us
    ppermute x25, starting transfers between devices, flip(): return lax.ppermute(value, axis, [(i, i ^ bit) for i in range(count)])  34.6 us
    ppermute x4, waiting for transfers between devices, hop(): return lax.ppermute(value, axis, pairs)  13 us
    pallas_call x3, Pallas kernels, gather_columns(): pl.pallas_call(gather_kernel, out_shape=[pltpu.HBM((rows, count * width),...  11.9 us
    dot_general x4, matrix products, rows_for(): jnp.dot(spread, weights[:, n * width:(n + 1) * width], preferred_element_...  11 us
    pallas_call x3, Pallas kernels, piece_grad(): pl.pallas_call(functools.partial(piece_grad_kernel, [[len(row) for row in...  10.6 us
    ppermute x4, starting transfers between devices, hop(): return lax.ppermute(value, axis, pairs)  7.52 us
    pallas_call x3, Pallas kernels, decoder_part(): pl.pallas_call(functools.partial(decoder_kernel, len(onto)), out_shape=ja...  7.29 us
  transfers between devices with their start and end apart: 30, of which 13 were waited for; matrix products, arithmetic and copies ran while one was open for 10% of the time, Pallas kernels for 23%

profile of v15, /device:TPU:1, one launch (start us, length us, event | category | flops | bytes accessed | tf_op | source)
XLA Modules:
  0.0 165.9 jit_solution(9409860620713155120)
XLA Ops:
  2.2 4.2 %collective-permute-start.2 = (bf16[272,128]{1,0:T(8,128)(2,1)S(1)}, bf16[272,128]{1,0:T(8,128)(2,1)S(1)}, u32[]{:S(2)}, u32[]{:S(2)}) collective-permute-start(bf16[272,128]{1,0:T(8,128)(2,1)S(1)} %fusion.21.refs_0_), channel_id=1, source_target_pairs={{0,6},{2,4},{4,2},{6,0},{1,7},{3,5},{5,3},{7,1},{8,14},{10,12},{12... | collective-permute-start | bytes 208904 | tf_op jit(solution)/shard_map/ppermute | solution.py:103
  9.4 5.3 %gather_columns.3 = (bf16[2048,1024]{1,0:T(8,128)(2,1)}, f32[8,128]{1,0:T(8,128)S(1)}) custom-call(s32[4]{0:T(128)S(1)} %pad_add_fusion.1.scalar_ref, bf16[1,2048,4096]{2,1,0:T(8,128)(2,1)} %weight_ref.5), custom_call_target="tpu_custom_call" | custom-call | flops 3960000000 | bytes 1 | tf_op jit(solution)/shard_map/gather_columns/pallas_call | solution.py:136
  16.4 4.1 %collective-permute-start.6 = (bf16[256,2048]{1,0:T(8,128)(2,1)S(1)}, bf16[256,2048]{1,0:T(8,128)(2,1)S(1)}, u32[]{:S(2)}, u32[]{:S(2)}) collective-permute-start(bf16[256,2048]{1,0:T(8,128)(2,1)S(1)} %pad_maximum_fusion.own_ref), channel_id=1, source_target_pairs={{0,2},{2,4},{4,6},{1,3},{3,5},{5,7},{8,10},{10,12},{12,14},{9,11},... | collective-permute-start | bytes 3145736 | tf_op jit(solution)/shard_map/ppermute | solution.py:112
  20.5 2.6 %spread_codes.1 = bf16[1024,2048]{1,0:T(8,128)(2,1)S(1)} custom-call(s32[1]{0:T(128)} %bitcast.5.scalar_ref, bf16[8,272,128]{2,1,0:T(8,128)(2,1)S(1)} %bitcast.45), custom_call_target="tpu_custom_call" | custom-call | flops 2750000128 | bytes 1 | tf_op jit(solution)/shard_map/spread_codes/pallas_call | solution.py:185
  23.1 2.3 %fusion.8 = bf16[1024,512]{1,0:T(8,128)(2,1)S(1)} fusion(bf16[1024,2048]{1,0:T(8,128)(2,1)S(1)} %spread_codes.1, bf16[2048,1024]{1,0:T(8,128)(2,1)S(1)} %copy-done.13), kind=kOutput, calls=%fused_computation.8 | convolution fusion | flops 2148007936 | bytes 7340032 | tf_op jit(solution)/shard_map/dot_general | solution.py:556
  30.5 5.3 %gather_columns.4 = (bf16[2048,1024]{1,0:T(8,128)(2,1)}, f32[8,128]{1,0:T(8,128)}) custom-call(s32[4]{0:T(128)S(1)} %pad_add_fusion.scalar_ref, bf16[1,2048,4096]{2,1,0:T(8,128)(2,1)} %weight_ref.5), custom_call_target="tpu_custom_call" | custom-call | flops 3960000000 | bytes 1 | tf_op jit(solution)/shard_map/gather_columns/pallas_call | solution.py:136
  35.8 5.4 %collective-permute-done.7.down_ref = bf16[256,2048]{1,0:T(8,128)(2,1)S(1)} collective-permute-done((bf16[256,2048]{1,0:T(8,128)(2,1)S(1)}, bf16[256,2048]{1,0:T(8,128)(2,1)S(1)}, u32[]{:S(2)}, u32[]{:S(2)}) %collective-permute-start.7) | collective-permute-done | bytes 1048608 | tf_op jit(solution)/shard_map/ppermute | solution.py:112
  44.3 4.1 %fusion.17.kept_b = bf16[1024,512]{1,0:T(8,128)(2,1)S(1)} fusion(bf16[1024,2048]{1,0:T(8,128)(2,1)S(1)} %spread_codes.1, bf16[2048,1024]{1,0:T(8,128)(2,1)} %get-tuple-element.62), kind=kOutput, calls=%fused_computation.11 | convolution fusion | flops 2148007936 | bytes 7340032 | tf_op jit(solution)/shard_map/dot_general | solution.py:556
  56.9 2.9 %collective-permute-start.11 = (bf16[128,512]{1,0:T(8,128)(2,1)S(1)}, bf16[128,512]{1,0:T(8,128)(2,1)S(1)}, u32[]{:S(2)}, u32[]{:S(2)}) collective-permute-start(bf16[128,512]{1,0:T(8,128)(2,1)S(1)} %get-tuple-element.107), channel_id=1, source_target_pairs={{0,1},{1,0},{2,3},{3,2},{4,5},{5,4},{6,7},{7,6},{8,9},{9,8},{10,11... | collective-permute-start | bytes 393224 | tf_op jit(solution)/shard_map/ppermute | solution.py:103
  60.7 3.4 %collective-permute-done.10.far_b = bf16[1024,256]{1,0:T(8,128)(2,1)S(1)} collective-permute-done((bf16[1024,256]{1,0:T(8,128)(2,1)S(1)}, bf16[1024,256]{1,0:T(8,128)(2,1)S(1)}, u32[]{:S(2)}, u32[]{:S(2)}) %collective-permute-start.10) | collective-permute-done | bytes 524320 | tf_op jit(solution)/shard_map/ppermute | solution.py:103
  64.2 6.7 %collective-permute-done.13.down_two_ref = bf16[256,2048]{1,0:T(8,128)(2,1)} collective-permute-done((bf16[256,2048]{1,0:T(8,128)(2,1)S(1)}, bf16[256,2048]{1,0:T(8,128)(2,1)}, u32[]{:S(2)}, u32[]{:S(2)}) %collective-permute-start.13) | collective-permute-done | bytes 1048608 | tf_op jit(solution)/shard_map/ppermute | solution.py:112
  72.5 2.4 %collective-permute-start.16 = (bf16[256,512]{1,0:T(8,128)(2,1)S(1)}, bf16[256,512]{1,0:T(8,128)(2,1)S(1)}, u32[]{:S(2)}, u32[]{:S(2)}) collective-permute-start(bf16[256,512]{1,0:T(8,128)(2,1)S(1)} %get-tuple-element.77), channel_id=1, source_target_pairs={{0,6},{2,4},{4,2},{6,0},{1,7},{3,5},{5,3},{7,1},{8,14},{10,12},{12... | collective-permute-start | bytes 786440 | tf_op jit(solution)/shard_map/ppermute | solution.py:103
  74.9 3.2 %collective-permute-done.14 = bf16[256,512]{1,0:T(8,128)(2,1)S(1)} collective-permute-done((bf16[256,512]{1,0:T(8,128)(2,1)S(1)}, bf16[256,512]{1,0:T(8,128)(2,1)S(1)}, u32[]{:S(2)}, u32[]{:S(2)}) %collective-permute-start.14) | collective-permute-done | bytes 262176 | tf_op jit(solution)/shard_map/ppermute | solution.py:103
  78.1 13.1 %collective-permute-done.15 = bf16[256,512]{1,0:T(8,128)(2,1)S(1)} collective-permute-done((bf16[256,512]{1,0:T(8,128)(2,1)S(1)}, bf16[256,512]{1,0:T(8,128)(2,1)S(1)}, u32[]{:S(2)}, u32[]{:S(2)}) %collective-permute-start.15) | collective-permute-done | bytes 262176 | tf_op jit(solution)/shard_map/ppermute | solution.py:103
  91.4 6.0 %collective-permute-start.19 = (bf16[256,512]{1,0:T(8,128)(2,1)S(1)}, bf16[256,512]{1,0:T(8,128)(2,1)}, u32[]{:S(2)}, u32[]{:S(2)}) collective-permute-start(bf16[256,512]{1,0:T(8,128)(2,1)S(1)} %multiply_convert_fusion.refs_0_), channel_id=1, source_target_pairs={{0,2},{2,0},{4,6},{6,4},{1,3},{3,1},{5,7},{7,5},{8,10},{10,8},{12,... | collective-permute-start | bytes 786440 | tf_op jit(solution)/shard_map/ppermute | solution.py:103
  107.0 15.6 %collective-permute-done.17.refs_0_ = bf16[256,512]{1,0:T(8,128)(2,1)S(1)} collective-permute-done((bf16[256,512]{1,0:T(8,128)(2,1)S(1)}, bf16[256,512]{1,0:T(8,128)(2,1)S(1)}, u32[]{:S(2)}, u32[]{:S(2)}) %collective-permute-start.17) | collective-permute-done | bytes 262176 | tf_op jit(solution)/shard_map/ppermute | solution.py:103
  127.8 2.9 %piece_grad.3 = (bf16[1,16,64,512]{3,2,1,0:T(8,128)(2,1)S(1)}, f32[16,64,128]{2,1,0:T(8,128)S(1)}) custom-call(s32[1]{0:T(128)} %bitcast.21.scalar_ref, bf16[4,256,256]{2,1,0:T(8,128)(2,1)S(1)} %get-tuple-element.71.hot_ref, bf16[1,2048,4096]{2,1,0:T(8,128)(2,1)} %weight_ref.5, bf16[256,512]{1,0:T(8,128)(2,1)S(1)} %multiply_convert_fusion.refs_0_, ...), custom_call_target="tpu_custom_call" | custom-call | flops 3080000000 | bytes 1 | tf_op jit(solution)/shard_map/piece_grad/pallas_call | solution.py:365
  132.8 2.5 %collective-permute-done.25.refs_3_ = bf16[512,512]{1,0:T(8,128)(2,1)S(1)} collective-permute-done((bf16[512,512]{1,0:T(8,128)(2,1)}, bf16[512,512]{1,0:T(8,128)(2,1)S(1)}, u32[]{:S(2)}, u32[]{:S(2)}) %collective-permute-start.25) | collective-permute-done | bytes 524320 | tf_op jit(solution)/shard_map/ppermute | solution.py:103
  136.7 4.9 %piece_grad.4 = (bf16[2,16,64,512]{3,2,1,0:T(8,128)(2,1)S(1)}, f32[16,64,128]{2,1,0:T(8,128)S(1)}) custom-call(s32[2]{0:T(128)S(1)} %pad_add_fusion.3.scalar_ref, bf16[4,256,256]{2,1,0:T(8,128)(2,1)S(1)} %get-tuple-element.71.hot_ref, bf16[1,2048,4096]{2,1,0:T(8,128)(2,1)} %weight_ref.5, f32[16,64,128]{2,1,0:T(8,128)S(1)} %get-tuple-element.92.refs_0_, ...), custom_call_target="tpu_custom_call" | custom-call | flops 5280000000 | bytes 1 | tf_op jit(solution)/shard_map/piece_grad/pallas_call | solution.py:365
  141.6 3.3 %decoder_part.4.refs_0_ = bf16[2048,2048]{1,0:T(8,128)(2,1)} custom-call(s32[2]{0:T(128)S(1)} %pad_add_fusion.4.scalar_ref, bf16[16,128,64]{2,1,0:T(8,128)(2,1)S(1)} %get-tuple-element.70.code_ref, bf16[2,16,64,512]{3,2,1,0:T(8,128)(2,1)S(1)} %get-tuple-element.94.slots_ref, bf16[2048,2048]{1,0:T(8,128)(2,1)} %decoder_part.3.refs_0_), custom_call_target="tpu_custom_call", output_to_operand_aliasing={{}: (3, {})} | custom-call | flops 3630000128 | bytes 1 | tf_op jit(solution)/shard_map/decoder_part/pallas_call | solution.py:400
  145.6 2.8 %piece_grad.5 = (bf16[1,16,64,512]{3,2,1,0:T(8,128)(2,1)S(1)}, f32[16,64,128]{2,1,0:T(8,128)S(1)}) custom-call(s32[1]{0:T(128)} %bitcast.23.scalar_ref, bf16[4,256,256]{2,1,0:T(8,128)(2,1)S(1)} %get-tuple-element.71.hot_ref, bf16[1,2048,4096]{2,1,0:T(8,128)(2,1)} %weight_ref.5, f32[16,64,128]{2,1,0:T(8,128)S(1)} %get-tuple-element.96.refs_0_, ...), custom_call_target="tpu_custom_call" | custom-call | flops 3080000000 | bytes 1 | tf_op jit(solution)/shard_map/piece_grad/pallas_call | solution.py:365
  148.4 4.4 %collective-permute-start.28 = (f32[16,64,128]{2,1,0:T(8,128)S(1)}, f32[16,64,128]{2,1,0:T(8,128)S(1)}, u32[]{:S(2)}, u32[]{:S(2)}) collective-permute-start(f32[16,64,128]{2,1,0:T(8,128)S(1)} %get-tuple-element.102.own_ref), channel_id=1, source_target_pairs={{0,1},{1,0},{2,3},{3,2},{4,5},{5,4},{6,7},{7,6},{8,9},{9,8},{10,11... | collective-permute-start | bytes 1572872 | tf_op jit(solution)/shard_map/ppermute | solution.py:103
  155.3 4.3 %act_slots.1.act_ref = bf16[16,64,2048]{2,1,0:T(8,128)(2,1)S(1)} custom-call(s32[6]{0:T(128)S(1)} %stack.137.scalar_ref, bf16[4,256,256]{2,1,0:T(8,128)(2,1)S(1)} %get-tuple-element.71.hot_ref, bf16[256,2048]{1,0:T(8,128)(2,1)S(1)} %pad_maximum_fusion.own_ref, bf16[256,2048]{1,0:T(8,128)(2,1)S(1)} %copy-done.8, bf16[256,2048]{1,0:T(8,128)(2,1)S(1)} %copy-done.10, ...), custom_call_target="tpu_custom_call" | custom-call | flops 3630000128 | bytes 1 | tf_op jit(solution)/shard_map/act_slots/pallas_call | solution.py:439
  159.6 6.3 %encoder_part.1 = bf16[2048,2048]{1,0:T(8,128)(2,1)} custom-call(bf16[16,64,128]{2,1,0:T(8,128)(2,1)S(1)} %copy-done.12, f32[16,64,128]{2,1,0:T(8,128)S(1)} %get-tuple-element.102.own_ref, f32[16,64,128]{2,1,0:T(8,128)S(1)} %collective-permute-done.28.theirs_ref, bf16[16,64,2048]{2,1,0:T(8,128)(2,1)S(1)} %act_slots.1.act_ref), custom_call_target="tpu_custom_call" | custom-call | flops 7150000128 | bytes 1 | tf_op jit(solution)/shard_map/encoder_part/pallas_call | solution.py:475
  (114 shorter events, 47.0 us)
Async XLA Ops:
  2.2 12.5 %collective-permute-start.2 = (bf16[272,128]{1,0:T(8,128)(2,1)S(1)}, bf16[272,128]{1,0:T(8,128)(2,1)S(1)}, u32[]{:S(2)}, u32[]{:S(2)}) collective-permute-start(bf16[272,128]{1,0:T(8,128)(2,1)S(1)} %fusion.21.refs_0_), channel_id=1, source_target_pairs={{0,6},{2,4},{4,2},{6,0},{1,7},{3,5},{5,3},{7,1},{8,14},{10,12},{12... | collective-permute-start | bytes 208904 | tf_op jit(solution)/shard_map/ppermute | solution.py:103
  6.4 8.3 %collective-permute-start.1 = (bf16[272,128]{1,0:T(8,128)(2,1)S(1)}, bf16[272,128]{1,0:T(8,128)(2,1)S(1)}, u32[]{:S(2)}, u32[]{:S(2)}) collective-permute-start(bf16[272,128]{1,0:T(8,128)(2,1)S(1)} %fusion.21.refs_0_), channel_id=1, source_target_pairs={{0,4},{2,6},{4,0},{6,2},{1,5},{3,7},{5,1},{7,3},{8,12},{10,14},{12... | collective-permute-start | bytes 208904 | tf_op jit(solution)/shard_map/ppermute | solution.py:103
  6.4 8.3 %collective-permute-start = (bf16[272,128]{1,0:T(8,128)(2,1)S(1)}, bf16[272,128]{1,0:T(8,128)(2,1)S(1)}, u32[]{:S(2)}, u32[]{:S(2)}) collective-permute-start(bf16[272,128]{1,0:T(8,128)(2,1)S(1)} %fusion.21.refs_0_), channel_id=1, source_target_pairs={{0,2},{2,0},{4,6},{6,4},{1,3},{3,1},{5,7},{7,5},{8,10},{10,8},{12,... | collective-permute-start | bytes 208904 | tf_op jit(solution)/shard_map/ppermute | solution.py:103
  15.1 26.1 %collective-permute-start.7 = (bf16[256,2048]{1,0:T(8,128)(2,1)S(1)}, bf16[256,2048]{1,0:T(8,128)(2,1)S(1)}, u32[]{:S(2)}, u32[]{:S(2)}) collective-permute-start(bf16[256,2048]{1,0:T(8,128)(2,1)S(1)} %pad_maximum_fusion.own_ref), channel_id=1, source_target_pairs={{2,0},{4,2},{6,4},{3,1},{5,3},{7,5},{10,8},{12,10},{14,12},{11,9},... | collective-permute-start | bytes 3145736 | tf_op jit(solution)/shard_map/ppermute | solution.py:112
  16.4 25.7 %collective-permute-start.6 = (bf16[256,2048]{1,0:T(8,128)(2,1)S(1)}, bf16[256,2048]{1,0:T(8,128)(2,1)S(1)}, u32[]{:S(2)}, u32[]{:S(2)}) collective-permute-start(bf16[256,2048]{1,0:T(8,128)(2,1)S(1)} %pad_maximum_fusion.own_ref), channel_id=1, source_target_pairs={{0,2},{2,4},{4,6},{1,3},{3,5},{5,7},{8,10},{10,12},{12,14},{9,11},... | collective-permute-start | bytes 3145736 | tf_op jit(solution)/shard_map/ppermute | solution.py:112
  25.5 27.5 %collective-permute-start.5 = (bf16[1024,512]{1,0:T(8,128)(2,1)S(1)}, bf16[1024,512]{1,0:T(8,128)(2,1)S(1)}, u32[]{:S(2)}, u32[]{:S(2)}) collective-permute-start(bf16[1024,512]{1,0:T(8,128)(2,1)S(1)} %fusion.8), channel_id=1, source_target_pairs={{0,8},{8,0},{16,24},{24,16},{1,9},{9,1},{17,25},{25,17},{2,10},{10... | collective-permute-start | bytes 3145736 | tf_op jit(solution)/shard_map/ppermute | solution.py:103
  29.2 23.4 %collective-permute-start.9 = (bf16[1024,512]{1,0:T(8,128)(2,1)S(1)}, bf16[1024,512]{1,0:T(8,128)(2,1)S(1)}, u32[]{:S(2)}, u32[]{:S(2)}) collective-permute-start(bf16[1024,512]{1,0:T(8,128)(2,1)S(1)} %fusion.14), channel_id=1, source_target_pairs={{0,16},{8,24},{16,0},{24,8},{1,17},{9,25},{17,1},{25,9},{2,18},{10... | collective-permute-start | bytes 3145736 | tf_op jit(solution)/shard_map/ppermute | solution.py:103
  42.1 22.1 %collective-permute-start.12 = (bf16[256,2048]{1,0:T(8,128)(2,1)S(1)}, bf16[256,2048]{1,0:T(8,128)(2,1)S(1)}, u32[]{:S(2)}, u32[]{:S(2)}) collective-permute-start(bf16[256,2048]{1,0:T(8,128)(2,1)S(1)} %collective-permute-done.6.up_ref), channel_id=1, source_target_pairs={{2,4},{4,6},{3,5},{5,7},{10,12},{12,14},{11,13},{13,15},{18,20},{2... | collective-permute-start | bytes 3145736 | tf_op jit(solution)/shard_map/ppermute | solution.py:112
  42.8 28.1 %collective-permute-start.13 = (bf16[256,2048]{1,0:T(8,128)(2,1)S(1)}, bf16[256,2048]{1,0:T(8,128)(2,1)}, u32[]{:S(2)}, u32[]{:S(2)}) collective-permute-start(bf16[256,2048]{1,0:T(8,128)(2,1)S(1)} %collective-permute-done.7.down_ref), channel_id=1, source_target_pairs={{2,0},{4,2},{3,1},{5,3},{10,8},{12,10},{11,9},{13,11},{18,16},{20,... | collective-permute-start | bytes 3145736 | tf_op jit(solution)/shard_map/ppermute | solution.py:112
  52.8 11.3 %collective-permute-start.10 = (bf16[1024,256]{1,0:T(8,128)(2,1)S(1)}, bf16[1024,256]{1,0:T(8,128)(2,1)S(1)}, u32[]{:S(2)}, u32[]{:S(2)}) collective-permute-start(bf16[1024,256]{1,0:T(8,128)(2,1)S(1)} %add_convert_fusion), channel_id=1, source_target_pairs={{0,8},{8,0},{16,24},{24,16},{1,9},{9,1},{17,25},{25,17},{2,10},{10... | collective-permute-start | bytes 1572872 | tf_op jit(solution)/shard_map/ppermute | solution.py:103
  53.1 11.1 %collective-permute-start.8 = (bf16[1024,256]{1,0:T(8,128)(2,1)S(1)}, bf16[1024,256]{1,0:T(8,128)(2,1)S(1)}, u32[]{:S(2)}, u32[]{:S(2)}) collective-permute-start(bf16[1024,256]{1,0:T(8,128)(2,1)S(1)} %add_convert_fusion.1), channel_id=1, source_target_pairs={{0,16},{8,24},{16,0},{24,8},{1,17},{9,25},{17,1},{25,9},{2,18},{10... | collective-permute-start | bytes 1572872 | tf_op jit(solution)/shard_map/ppermute | solution.py:103
  72.5 18.7 %collective-permute-start.15 = (bf16[256,512]{1,0:T(8,128)(2,1)S(1)}, bf16[256,512]{1,0:T(8,128)(2,1)S(1)}, u32[]{:S(2)}, u32[]{:S(2)}) collective-permute-start(bf16[256,512]{1,0:T(8,128)(2,1)S(1)} %get-tuple-element.76), channel_id=1, source_target_pairs={{0,4},{2,6},{4,0},{6,2},{1,5},{3,7},{5,1},{7,3},{8,12},{10,14},{12... | collective-permute-start | bytes 786440 | tf_op jit(solution)/shard_map/ppermute | solution.py:103
  72.5 18.7 %collective-permute-start.16 = (bf16[256,512]{1,0:T(8,128)(2,1)S(1)}, bf16[256,512]{1,0:T(8,128)(2,1)S(1)}, u32[]{:S(2)}, u32[]{:S(2)}) collective-permute-start(bf16[256,512]{1,0:T(8,128)(2,1)S(1)} %get-tuple-element.77), channel_id=1, source_target_pairs={{0,6},{2,4},{4,2},{6,0},{1,7},{3,5},{5,3},{7,1},{8,14},{10,12},{12... | collective-permute-start | bytes 786440 | tf_op jit(solution)/shard_map/ppermute | solution.py:103
  91.4 10.5 %collective-permute-start.19 = (bf16[256,512]{1,0:T(8,128)(2,1)S(1)}, bf16[256,512]{1,0:T(8,128)(2,1)}, u32[]{:S(2)}, u32[]{:S(2)}) collective-permute-start(bf16[256,512]{1,0:T(8,128)(2,1)S(1)} %multiply_convert_fusion.refs_0_), channel_id=1, source_target_pairs={{0,2},{2,0},{4,6},{6,4},{1,3},{3,1},{5,7},{7,5},{8,10},{10,8},{12,... | collective-permute-start | bytes 786440 | tf_op jit(solution)/shard_map/ppermute | solution.py:103
  99.9 7.2 %collective-permute-start.18 = (bf16[256,512]{1,0:T(8,128)(2,1)S(1)}, bf16[256,512]{1,0:T(8,128)(2,1)S(1)}, u32[]{:S(2)}, u32[]{:S(2)}) collective-permute-start(bf16[256,512]{1,0:T(8,128)(2,1)S(1)} %multiply_convert_fusion.refs_0_), channel_id=1, source_target_pairs={{0,6},{2,4},{4,2},{6,0},{1,7},{3,5},{5,3},{7,1},{8,14},{10,12},{12... | collective-permute-start | bytes 786440 | tf_op jit(solution)/shard_map/ppermute | solution.py:103
  100.0 22.6 %collective-permute-start.17 = (bf16[256,512]{1,0:T(8,128)(2,1)S(1)}, bf16[256,512]{1,0:T(8,128)(2,1)S(1)}, u32[]{:S(2)}, u32[]{:S(2)}) collective-permute-start(bf16[256,512]{1,0:T(8,128)(2,1)S(1)} %multiply_convert_fusion.refs_0_), channel_id=1, source_target_pairs={{0,4},{2,6},{4,0},{6,2},{1,5},{3,7},{5,1},{7,3},{8,12},{10,14},{12... | collective-permute-start | bytes 786440 | tf_op jit(solution)/shard_map/ppermute | solution.py:103
  102.0 20.7 %collective-permute-start.21 = (bf16[256,512]{1,0:T(8,128)(2,1)}, bf16[256,512]{1,0:T(8,128)(2,1)S(1)}, u32[]{:S(2)}, u32[]{:S(2)}) collective-permute-start(bf16[256,512]{1,0:T(8,128)(2,1)} %collective-permute-done.19.refs_1_), channel_id=1, source_target_pairs={{0,8},{8,0},{16,24},{24,16},{1,9},{9,1},{17,25},{25,17},{2,10},{10... | collective-permute-start | bytes 786440 | tf_op jit(solution)/shard_map/ppermute | solution.py:103
  103.1 20.3 %collective-permute-start.20 = (bf16[256,512]{1,0:T(8,128)(2,1)}, bf16[256,512]{1,0:T(8,128)(2,1)}, u32[]{:S(2)}, u32[]{:S(2)}) collective-permute-start(bf16[256,512]{1,0:T(8,128)(2,1)} %collective-permute-done.19.refs_1_), channel_id=1, source_target_pairs={{0,16},{8,24},{16,0},{24,8},{1,17},{9,25},{17,1},{25,9},{2,18},{10... | collective-permute-start | bytes 786440 | tf_op jit(solution)/shard_map/ppermute | solution.py:103
  124.2 11.0 %collective-permute-start.25 = (bf16[512,512]{1,0:T(8,128)(2,1)}, bf16[512,512]{1,0:T(8,128)(2,1)S(1)}, u32[]{:S(2)}, u32[]{:S(2)}) collective-permute-start(bf16[512,512]{1,0:T(8,128)(2,1)} %join.3.refs_2_), channel_id=1, source_target_pairs={{0,8},{8,0},{16,24},{24,16},{1,9},{9,1},{17,25},{25,17},{2,10},{10... | collective-permute-start | bytes 1572872 | tf_op jit(solution)/shard_map/ppermute | solution.py:103
  124.2 11.0 %collective-permute-start.24 = (bf16[512,512]{1,0:T(8,128)(2,1)}, bf16[512,512]{1,0:T(8,128)(2,1)S(1)}, u32[]{:S(2)}, u32[]{:S(2)}) collective-permute-start(bf16[512,512]{1,0:T(8,128)(2,1)} %join.3.refs_2_), channel_id=1, source_target_pairs={{0,16},{8,24},{16,0},{24,8},{1,17},{9,25},{17,1},{25,9},{2,18},{10... | collective-permute-start | bytes 1572872 | tf_op jit(solution)/shard_map/ppermute | solution.py:103
  126.3 28.6 %collective-permute-start.29 = (bf16[256,2048]{1,0:T(8,128)(2,1)}, bf16[256,2048]{1,0:T(8,128)(2,1)S(1)}, u32[]{:S(2)}, u32[]{:S(2)}) collective-permute-start(bf16[256,2048]{1,0:T(8,128)(2,1)} %broadcast_select_fusion), channel_id=1, source_target_pairs={{4,6},{2,0},{5,7},{3,1},{12,14},{10,8},{13,15},{11,9},{20,22},{18,... | collective-permute-start | bytes 3145736 | tf_op jit(solution)/shard_map/ppermute | solution.py:587
  135.3 10.3 %collective-permute-start.27 = (bf16[1024,256]{1,0:T(8,128)(2,1)S(1)}, bf16[1024,256]{1,0:T(8,128)(2,1)S(1)}, u32[]{:S(2)}, u32[]{:S(2)}) collective-permute-start(bf16[1024,256]{1,0:T(8,128)(2,1)S(1)} %pad_maximum_fusion.3), channel_id=1, source_target_pairs={{0,16},{8,24},{16,0},{24,8},{1,17},{9,25},{17,1},{25,9},{2,18},{10... | collective-permute-start | bytes 1572872 | tf_op jit(solution)/shard_map/ppermute | solution.py:103
  135.5 10.1 %collective-permute-start.26 = (bf16[1024,256]{1,0:T(8,128)(2,1)S(1)}, bf16[1024,256]{1,0:T(8,128)(2,1)S(1)}, u32[]{:S(2)}, u32[]{:S(2)}) collective-permute-start(bf16[1024,256]{1,0:T(8,128)(2,1)S(1)} %pad_maximum_fusion.2), channel_id=1, source_target_pairs={{0,8},{8,0},{16,24},{24,16},{1,9},{9,1},{17,25},{25,17},{2,10},{10... | collective-permute-start | bytes 1572872 | tf_op jit(solution)/shard_map/ppermute | solution.py:103
  148.4 11.2 %collective-permute-start.28 = (f32[16,64,128]{2,1,0:T(8,128)S(1)}, f32[16,64,128]{2,1,0:T(8,128)S(1)}, u32[]{:S(2)}, u32[]{:S(2)}) collective-permute-start(f32[16,64,128]{2,1,0:T(8,128)S(1)} %get-tuple-element.102.own_ref), channel_id=1, source_target_pairs={{0,1},{1,0},{2,3},{3,2},{4,5},{5,4},{6,7},{7,6},{8,9},{9,8},{10,11... | collective-permute-start | bytes 1572872 | tf_op jit(solution)/shard_map/ppermute | solution.py:103
  (23 other events, 163.6 us)
